TPU v7x, 32 devices: a whole 2x2x4 slice. The times are simulated.
32 devices in a mesh: orb: 8 (over y, x, core), band: 4 (over z).
Axes of the slice: x: 2, y: 2, z: 4, core: 2. Of those that a mesh axis runs over, the one named last changes fastest.
Arguments:
- blocks: float32 [192, 32, 64, 64], P('orb'), may hold values from -0.125 to 0.125
- columns: int32 [192, 32], P('orb'), may hold values from 0 to 191, as said below
- counts: int32 [192], P('orb'), may hold values from 8 to 32
- vectors: float32 [12288, 1536], P('orb', 'band'), may hold values from -6 to 6
Outputs:
- filtered: float32 [12288, 1536], P('orb', 'band')
- gram: float32 [1536, 1536], P('band', 'orb')
Inputs may be any that keep to these rules, and one draw needn't show every extreme that they name: `columns`: block column indices of row r lie within 24 block rows of r, counted cyclically modulo 192, are distinct within a row, and slot 0 holds r itself.
All inputs are finite; a program needn't handle non-finite values.
Results may differ from a plain program's by a relative error of at most 0.000088.
Values sent between devices are 32-bit elements; how exact they have to be, the bound alone decides.
No kernel may reach another device: no remote copies, remote signals or barrier semaphores. Data moves between devices by JAX's collectives and lax.ppermute only.
A program may use at most 192 MiB of HBM per device.

v0:
```python
import math

import jax
import jax.numpy as jnp
from jax import lax
from jax.sharding import PartitionSpec as P


def with_halo(shard, sides, width):
    for axis, dim in sides:
        size, length = (lax.axis_size(axis), shard.shape[dim])
        up = [(i, (i + 1) % size) for i in range(size)]
        down = [(j, i) for i, j in up]
        last = lax.slice_in_dim(shard, length - width, length, axis=dim)
        first = lax.slice_in_dim(shard, 0, width, axis=dim)
        before = lax.ppermute(last, axis, up)
        after = lax.ppermute(first, axis, down)
        shard = jnp.concatenate([before, shard, after], axis=dim)
    return shard


def apply_hamiltonian(blocks, columns, counts, vec):
    rows_dev = blocks.shape[0]
    slots = blocks.shape[1]
    blk = blocks.shape[2]
    width = vec.shape[1]
    total_rows = rows_dev * lax.axis_size("orb")
    extended = with_halo(vec, (("orb", 0),), vec.shape[0])
    stacked = extended.reshape(3 * rows_dev, blk, width)
    offset = lax.axis_index("orb") * rows_dev - rows_dev
    local_cols = (columns - offset) % total_rows
    live = (jnp.arange(slots, dtype=jnp.int32)[None, :] < counts[:, None]).astype(jnp.float32)
    group = math.gcd(rows_dev, 8)
    grouped_blocks = blocks.reshape(rows_dev // group, group, slots, blk, blk)
    grouped_cols = local_cols.reshape(rows_dev // group, group, slots)
    grouped_live = live.reshape(rows_dev // group, group, slots)

    def one_group(item):
        gblk, gcol, galive = item
        picked = stacked[gcol]
        return jnp.einsum(
            "gkij,gkjm->gim",
            gblk * galive[:, :, None, None],
            picked,
            precision=lax.Precision.HIGHEST,
        )

    out = lax.map(one_group, (grouped_blocks, grouped_cols, grouped_live))
    return out.reshape(rows_dev * blk, width)


def body(blocks, columns, counts, vectors):
    order_total = vectors.shape[0] * lax.axis_size("orb")
    first = (apply_hamiltonian(blocks, columns, counts, vectors) - 0.1 * vectors) / 0.9
    filtered = (
        2.0 * (apply_hamiltonian(blocks, columns, counts, first) - 0.1 * first) / 0.9 - vectors
    )
    partial_gram = jnp.dot(
        filtered.T,
        lax.all_gather(filtered, "band", axis=1, tiled=True),
        precision=lax.Precision.HIGHEST,
        preferred_element_type=jnp.float32,
    )
    gram = lax.psum_scatter(partial_gram, "orb", scatter_dimension=1, tiled=True)
    return (filtered, gram / order_total)


def solution(mesh):
    placed = (P("orb", None, None, None), P("orb", None), P("orb"), P("orb", "band"))
    return jax.shard_map(
        body,
        mesh=mesh,
        in_specs=placed,
        out_specs=(P("orb", "band"), P("band", "orb")),
        check_vma=False,
    )
```

profile of v0, /device:TPU:3, one launch (start us, length us, event | category | flops | bytes accessed | tf_op | source)
XLA Modules:
  0.0 601.7 jit_solution(12091619328351801009)
XLA Ops:
  10.6 49.0 %collective-permute-done = f32[1536,384]{1,0:T(8,128)S(1)} collective-permute-done((f32[1536,384]{1,0:T(8,128)}, f32[1536,384]{1,0:T(8,128)S(1)}, u32[]{:S(2)}, u32[]{:S(2)}) %collective-permute-start) | collective-permute-done | bytes 2359328 | tf_op jit(solution)/shard_map/ppermute | solution.py:16
  59.6 2.5 collective-permute-done.1
  62.1 5.8 pad_maximum_fusion
  69.5 116.3 %while.20 = (s32[]{:T(128)}, f32[3,8,64,384]{3,2,1,0:T(8,128)}, f32[3,8,32,64,64]{4,3,2,1,0:T(8,128)}, f32[3,8,32]{2,1,0:T(8,128)S(1)}, s32[3,8,32]{2,1,0:T(8,128)S(1)}, /*index=5*/f32[72,64,384]{2,1,0:T(8,128)}, s32[]{:T(128)}) while((s32[]{:T(128)}, f32[3,8,64,384]{3,2,1,0:T(8,128)}, f32[3,8,32,64,64]{4,3,2,1,0:T(8,128)}, ...), condition=%wide.region_1.2_spmd, body=%wide.region_0.1_spmd.sunk | while | flops 4832888832 | bytes 84686928 | solution.py:48
  69.6 18.6 %gather_fusion = f32[256,64,384]{2,1,0:T(8,128)} fusion(f32[72,64,384]{2,1,0:T(8,128)} %get-tuple-element.185, s32[1024]{0:T(1024)S(1)} %pad_clamp_fusion.4), kind=kCustom, calls=%fused_computation.clone.1 | custom fusion | bytes 50332672 | tf_op jit(solution)/shard_map/while/body/eval_jaxpr/gather | solution.py:40
  88.2 20.2 %fusion.27 = f32[3,8,64,384]{3,2,1,0:T(8,128)} fusion(f32[3,8,64,384]{3,2,1,0:T(8,128)} %get-tuple-element.174, s32[]{:T(128)} %get-tuple-element.173, f32[8,32,64,384]{3,2,1,0:T(8,128)} %bitcast.85, f32[3,8,32,64,64]{4,3,2,1,0:T(8,128)} %get-tuple-element.182, f32[8,32]{1,0:T(8,128)S(1)} %dynamic-slice_bitcast_fusion.4), kind=kOutput, calls=%fused_computation.7.clone.1 | convolution fusion | flops 4832886784 | bytes 34342912 | tf_op jit(solution)/shard_map/while/body/eval_jaxpr/gkij,gkjm->gim/dot_general | solution.py:41
  108.5 18.5 %gather_fusion = f32[256,64,384]{2,1,0:T(8,128)} fusion(f32[72,64,384]{2,1,0:T(8,128)} %get-tuple-element.185, s32[1024]{0:T(1024)S(1)} %pad_clamp_fusion.4), kind=kCustom, calls=%fused_computation.clone.1 | custom fusion | bytes 50332672 | tf_op jit(solution)/shard_map/while/body/eval_jaxpr/gather | solution.py:40
  126.9 20.2 %fusion.27 = f32[3,8,64,384]{3,2,1,0:T(8,128)} fusion(f32[3,8,64,384]{3,2,1,0:T(8,128)} %get-tuple-element.174, s32[]{:T(128)} %get-tuple-element.173, f32[8,32,64,384]{3,2,1,0:T(8,128)} %bitcast.85, f32[3,8,32,64,64]{4,3,2,1,0:T(8,128)} %get-tuple-element.182, f32[8,32]{1,0:T(8,128)S(1)} %dynamic-slice_bitcast_fusion.4), kind=kOutput, calls=%fused_computation.7.clone.1 | convolution fusion | flops 4832886784 | bytes 34342912 | tf_op jit(solution)/shard_map/while/body/eval_jaxpr/gkij,gkjm->gim/dot_general | solution.py:41
  147.2 18.4 %gather_fusion = f32[256,64,384]{2,1,0:T(8,128)} fusion(f32[72,64,384]{2,1,0:T(8,128)} %get-tuple-element.185, s32[1024]{0:T(1024)S(1)} %pad_clamp_fusion.4), kind=kCustom, calls=%fused_computation.clone.1 | custom fusion | bytes 50332672 | tf_op jit(solution)/shard_map/while/body/eval_jaxpr/gather | solution.py:40
  165.7 20.2 %fusion.27 = f32[3,8,64,384]{3,2,1,0:T(8,128)} fusion(f32[3,8,64,384]{3,2,1,0:T(8,128)} %get-tuple-element.174, s32[]{:T(128)} %get-tuple-element.173, f32[8,32,64,384]{3,2,1,0:T(8,128)} %bitcast.85, f32[3,8,32,64,64]{4,3,2,1,0:T(8,128)} %get-tuple-element.182, f32[8,32]{1,0:T(8,128)S(1)} %dynamic-slice_bitcast_fusion.4), kind=kOutput, calls=%fused_computation.7.clone.1 | convolution fusion | flops 4832886784 | bytes 34342912 | tf_op jit(solution)/shard_map/while/body/eval_jaxpr/gkij,gkjm->gim/dot_general | solution.py:41
  185.8 2.0 fusion.14
  188.7 50.8 %collective-permute-done.2 = f32[1536,384]{1,0:T(8,128)S(1)} collective-permute-done((f32[1536,384]{1,0:T(8,128)S(1)}, f32[1536,384]{1,0:T(8,128)S(1)}, u32[]{:S(2)}, u32[]{:S(2)}) %collective-permute-start.2) | collective-permute-done | bytes 2359328 | tf_op jit(solution)/shard_map/ppermute | solution.py:16
  239.6 3.4 pad_maximum_fusion.1
  244.6 116.2 %while.21 = (s32[]{:T(128)}, f32[3,8,64,384]{3,2,1,0:T(8,128)}, f32[3,8,32,64,64]{4,3,2,1,0:T(8,128)}, f32[3,8,32]{2,1,0:T(8,128)S(1)}, s32[3,8,32]{2,1,0:T(8,128)S(1)}, /*index=5*/f32[72,64,384]{2,1,0:T(8,128)}, s32[]{:T(128)}) while((s32[]{:T(128)}, f32[3,8,64,384]{3,2,1,0:T(8,128)}, f32[3,8,32,64,64]{4,3,2,1,0:T(8,128)}, ...), condition=%wide.region_3.4_spmd, body=%wide.region_2.3_spmd.sunk | while | flops 4832888832 | bytes 84686928 | solution.py:48
  244.7 18.4 %gather_fusion.1 = f32[256,64,384]{2,1,0:T(8,128)} fusion(f32[72,64,384]{2,1,0:T(8,128)} %get-tuple-element.206, s32[1024]{0:T(1024)S(1)} %pad_clamp_fusion.5), kind=kCustom, calls=%fused_computation.1.clone.1 | custom fusion | bytes 50332672 | tf_op jit(solution)/shard_map/while/body/eval_jaxpr/gather | solution.py:40
  263.1 20.2 %fusion.29 = f32[3,8,64,384]{3,2,1,0:T(8,128)} fusion(f32[3,8,64,384]{3,2,1,0:T(8,128)} %get-tuple-element.195, s32[]{:T(128)} %get-tuple-element.194, f32[8,32,64,384]{3,2,1,0:T(8,128)} %bitcast.86, f32[3,8,32,64,64]{4,3,2,1,0:T(8,128)} %get-tuple-element.203, f32[8,32]{1,0:T(8,128)S(1)} %dynamic-slice_bitcast_fusion.5), kind=kOutput, calls=%fused_computation.17.clone.1 | convolution fusion | flops 4832886784 | bytes 34342912 | tf_op jit(solution)/shard_map/while/body/eval_jaxpr/gkij,gkjm->gim/dot_general | solution.py:41
  283.4 18.5 %gather_fusion.1 = f32[256,64,384]{2,1,0:T(8,128)} fusion(f32[72,64,384]{2,1,0:T(8,128)} %get-tuple-element.206, s32[1024]{0:T(1024)S(1)} %pad_clamp_fusion.5), kind=kCustom, calls=%fused_computation.1.clone.1 | custom fusion | bytes 50332672 | tf_op jit(solution)/shard_map/while/body/eval_jaxpr/gather | solution.py:40
  301.9 20.2 %fusion.29 = f32[3,8,64,384]{3,2,1,0:T(8,128)} fusion(f32[3,8,64,384]{3,2,1,0:T(8,128)} %get-tuple-element.195, s32[]{:T(128)} %get-tuple-element.194, f32[8,32,64,384]{3,2,1,0:T(8,128)} %bitcast.86, f32[3,8,32,64,64]{4,3,2,1,0:T(8,128)} %get-tuple-element.203, f32[8,32]{1,0:T(8,128)S(1)} %dynamic-slice_bitcast_fusion.5), kind=kOutput, calls=%fused_computation.17.clone.1 | convolution fusion | flops 4832886784 | bytes 34342912 | tf_op jit(solution)/shard_map/while/body/eval_jaxpr/gkij,gkjm->gim/dot_general | solution.py:41
  322.2 18.4 %gather_fusion.1 = f32[256,64,384]{2,1,0:T(8,128)} fusion(f32[72,64,384]{2,1,0:T(8,128)} %get-tuple-element.206, s32[1024]{0:T(1024)S(1)} %pad_clamp_fusion.5), kind=kCustom, calls=%fused_computation.1.clone.1 | custom fusion | bytes 50332672 | tf_op jit(solution)/shard_map/while/body/eval_jaxpr/gather | solution.py:40
  340.6 20.2 %fusion.29 = f32[3,8,64,384]{3,2,1,0:T(8,128)} fusion(f32[3,8,64,384]{3,2,1,0:T(8,128)} %get-tuple-element.195, s32[]{:T(128)} %get-tuple-element.194, f32[8,32,64,384]{3,2,1,0:T(8,128)} %bitcast.86, f32[3,8,32,64,64]{4,3,2,1,0:T(8,128)} %get-tuple-element.203, f32[8,32]{1,0:T(8,128)S(1)} %dynamic-slice_bitcast_fusion.5), kind=kOutput, calls=%fused_computation.17.clone.1 | convolution fusion | flops 4832886784 | bytes 34342912 | tf_op jit(solution)/shard_map/while/body/eval_jaxpr/gkij,gkjm->gim/dot_general | solution.py:41
  360.8 4.3 fusion.13
  365.4 168.7 %all-gather.2.cloned.1.call-done = f32[1536,1536]{1,0:T(8,128)} async-done(((f32[1536,384]{1,0:T(8,128)}), f32[1536,1536]{1,0:T(8,128)}) %all-gather.2.cloned.1.call-update) | async-done | bytes 9437200 | tf_op jit(solution)/shard_map/all_gather | solution.py:60
  534.1 18.4 %fusion.17 = f32[384,1536]{0,1:T(8,128)} fusion(f32[1536,384]{1,0:T(8,128)S(1)} %copy-done.1, f32[1536,1536]{1,0:T(8,128)} %all-gather.2.cloned.1.call-done), kind=kOutput, calls=%fused_computation.35 | convolution fusion | flops 10871635968 | bytes 14155776 | tf_op jit(solution)/shard_map/dot_general | solution.py:58
  552.6 40.6 %reduce-scatter.2.cloned.1.call-done = f32[384,192]{0,1:T(8,128)} async-done(((f32[384,1536]{0,1:T(8,128)}), f32[384,192]{0,1:T(8,128)}) %reduce-scatter.2.cloned.1.call-update) | async-done | bytes 294928 | tf_op jit(solution)/shard_map/reduce_scatter | solution.py:64
  (43 shorter events, 10.2 us)
Async XLA Ops:
  7.2 527.0 %all-gather.2.cloned.1.call-start = ((), (), s32[]{:S(2)}) async-start(), calls=%async_computation.1 | async-start | bytes 11796480 | tf_op jit(solution)/shard_map/all_gather | solution.py:60
  7.2 52.4 %collective-permute-start = (f32[1536,384]{1,0:T(8,128)}, f32[1536,384]{1,0:T(8,128)S(1)}, u32[]{:S(2)}, u32[]{:S(2)}) collective-permute-start(f32[1536,384]{1,0:T(8,128)} %param.11), channel_id=1, source_target_pairs={{0,4},{4,8},{8,12},{12,16},{16,20},{20,24},{24,28},{28,0},{1,5},{5... | collective-permute-start | bytes 7077896 | tf_op jit(solution)/shard_map/ppermute | solution.py:16
  9.0 53.0 %collective-permute-start.1 = (f32[1536,384]{1,0:T(8,128)}, f32[1536,384]{1,0:T(8,128)}, u32[]{:S(2)}, u32[]{:S(2)}) collective-permute-start(f32[1536,384]{1,0:T(8,128)} %param.11), channel_id=1, source_target_pairs={{4,0},{8,4},{12,8},{16,12},{20,16},{24,20},{28,24},{0,28},{5,1},{9... | collective-permute-start | bytes 7077896 | tf_op jit(solution)/shard_map/ppermute | solution.py:17
  69.5 116.3 %copy-start = (f32[1536,384]{1,0:T(8,128)S(1)}, f32[1536,384]{1,0:T(8,128)}, u32[]{:S(2)}) copy-start(f32[1536,384]{1,0:T(8,128)} %param.11) | copy-start | bytes 7077892
  187.9 51.6 %collective-permute-start.2 = (f32[1536,384]{1,0:T(8,128)S(1)}, f32[1536,384]{1,0:T(8,128)S(1)}, u32[]{:S(2)}, u32[]{:S(2)}) collective-permute-start(f32[1536,384]{1,0:T(8,128)S(1)} %fusion.14), channel_id=1, source_target_pairs={{0,4},{4,8},{8,12},{12,16},{16,20},{20,24},{24,28},{28,0},{1,5},{5... | collective-permute-start | bytes 7077896 | tf_op jit(solution)/shard_map/ppermute | solution.py:16
  188.7 50.8 %collective-permute-start.3 = (f32[1536,384]{1,0:T(8,128)S(1)}, f32[1536,384]{1,0:T(8,128)S(1)}, u32[]{:S(2)}, u32[]{:S(2)}) collective-permute-start(f32[1536,384]{1,0:T(8,128)S(1)} %fusion.14), channel_id=1, source_target_pairs={{4,0},{8,4},{12,8},{16,12},{20,16},{24,20},{28,24},{0,28},{5,1},{9... | collective-permute-start | bytes 7077896 | tf_op jit(solution)/shard_map/ppermute | solution.py:17
  365.1 169.0 %copy-start.1 = (f32[1536,384]{1,0:T(8,128)S(1)}, f32[1536,384]{1,0:T(8,128)}, u32[]{:S(2)}) copy-start(f32[1536,384]{1,0:T(8,128)} %fusion.13) | copy-start | bytes 7077892
  365.1 228.0 %reduce-scatter.2.cloned.1.call-start = ((), (), s32[]{:S(2)}) async-start(), calls=%async_computation.2 | async-start | bytes 2654208 | tf_op jit(solution)/shard_map/reduce_scatter | solution.py:64
Sparse Core Ops, SparseCore 0:
  365.3 168.8 all-gather.1
  552.7 40.4 reduce-scatter.1
where the time goes:
time: 604 us; the launch traced here: 602 us
  waiting for transfers between devices  312 us (52%)
  matrix products  140 us (23%)
  local copies, waits for them, and re-layouts  115 us (19%)
  other arithmetic  18 us (3%)
  between operations  14.1 us (2%)
    all_gather x1, waiting for transfers between devices, body(): lax.all_gather(filtered, 'band', axis=1, tiled=True)  169 us
    dot_general x6, matrix products, one_group(): jnp.einsum('gkij,gkjm->gim', gblk * galive[:, :, None, None], picked, pre...  121 us
    gather x6, local copies, waits for them, and re-layouts, one_group(): picked = stacked[gcol]  111 us
    ppermute x2, waiting for transfers between devices, with_halo(): before = lax.ppermute(last, axis, up)  99.8 us
    reduce_scatter x1, waiting for transfers between devices, body(): lax.psum_scatter(partial_gram, 'orb', scatter_dimension=1, tiled=True)  40.6 us
    dot_general x1, matrix products, body(): jnp.dot(filtered.T, lax.all_gather(filtered, 'band', axis=1, tiled=True),...  18.4 us
  transfers between devices with their start and end apart: 6, of which 6 were waited for; matrix products, arithmetic and copies ran while one was open for 0% of the time, Pallas kernels for 0%

commit v1 on v0

v1 whole, which is shorter than its diff:
```python
import functools

import jax
import jax.numpy as jnp
from jax import lax
from jax.experimental import pallas as pl
from jax.experimental.pallas import tpu as pltpu
from jax.sharding import PartitionSpec as P

GROUP = 4
LANES = 128
VMEM = 40 * 1024 * 1024


def split(x):
    hi = x.astype(jnp.bfloat16)
    lo = (x - hi.astype(jnp.float32)).astype(jnp.bfloat16)
    return hi, lo


def densify_kernel(slot_ref, blocks_ref, hi_ref, lo_ref, *, spread):
    blk = blocks_ref.shape[2]
    step = pl.program_id(0)

    def one_row(i, carry):
        row = step * GROUP + i
        start = pl.multiple_of(i * blk, blk)
        for pair in range(spread // 2):
            left = slot_ref[row, 2 * pair]
            right = slot_ref[row, 2 * pair + 1]
            lblk = jnp.where(left >= 0, blocks_ref[i, jnp.maximum(left, 0)], 0.0)
            rblk = jnp.where(right >= 0, blocks_ref[i, jnp.maximum(right, 0)], 0.0)
            hi, lo = split(jnp.concatenate([lblk, rblk], axis=1))
            hi_ref[pl.ds(start, blk), pl.ds(pair * 2 * blk, 2 * blk)] = hi
            lo_ref[pl.ds(start, blk), pl.ds(pair * 2 * blk, 2 * blk)] = lo
        return carry

    lax.fori_loop(0, GROUP, one_row, 0)


def densify(slot_of, blocks):
    rows, slots, blk, _ = blocks.shape
    spread = slot_of.shape[1]
    shape = jax.ShapeDtypeStruct((rows * blk, spread * blk), jnp.bfloat16)
    out = pl.BlockSpec((GROUP * blk, spread * blk), lambda g, _: (g, 0))
    return pl.pallas_call(
        functools.partial(densify_kernel, spread=spread),
        grid_spec=pltpu.PrefetchScalarGridSpec(
            num_scalar_prefetch=1,
            grid=(rows // GROUP,),
            in_specs=[pl.BlockSpec((GROUP, slots, blk, blk), lambda g, _: (g, 0, 0, 0))],
            out_specs=[out, out],
        ),
        out_shape=[shape, shape],
        compiler_params=pltpu.CompilerParams(vmem_limit_bytes=VMEM),
        cost_estimate=pl.CostEstimate(flops=0, bytes_accessed=60_000_000, transcendentals=0),
    )(slot_of, blocks)


def apply_kernel(hi_ref, lo_ref, before_ref, own_ref, after_ref, *rest, second):
    old_ref = rest[0] if second else None
    out_ref, parts = rest[-2:]
    step = pl.program_id(0)
    rows, width = own_ref.shape
    tall, wide = hi_ref.shape

    @pl.when(step == 0)
    def _():
        for place, ref in enumerate((before_ref, own_ref, after_ref)):
            hi, lo = split(ref[...])
            parts[pl.ds(place * rows, rows), pl.ds(0, width)] = hi
            parts[pl.ds(place * rows, rows), pl.ds(width, width)] = lo

    start = pl.multiple_of(step * tall, tall)
    both = jnp.dot(hi_ref[...], parts[pl.ds(start, wide), :], preferred_element_type=jnp.float32)
    rest_ = jnp.dot(
        lo_ref[...], parts[pl.ds(start, wide), pl.ds(0, width)], preferred_element_type=jnp.float32
    )
    product = both[:, :width] + (both[:, width:] + rest_)
    own = own_ref[pl.ds(start, tall), :]
    if second:
        out_ref[...] = 2.0 * (product - 0.1 * own) / 0.9 - old_ref[...]
    else:
        out_ref[...] = (product - 0.1 * own) / 0.9


def apply_step(hi, lo, before, own, after, old=None):
    rows, width = own.shape
    wide = hi.shape[1]
    tall = wide - 2 * rows
    steps = rows // tall
    band = pl.BlockSpec((tall, wide), lambda g: (g, 0))
    whole = pl.BlockSpec((rows, width), lambda g: (0, 0))
    piece = pl.BlockSpec((tall, width), lambda g: (g, 0))
    second = old is not None
    return pl.pallas_call(
        functools.partial(apply_kernel, second=second),
        grid=(steps,),
        in_specs=[band, band, whole, whole, whole] + ([piece] if second else []),
        out_specs=piece,
        out_shape=jax.ShapeDtypeStruct((rows, width), jnp.float32),
        scratch_shapes=[pltpu.VMEM((3 * rows, 2 * width), jnp.bfloat16)],
        compiler_params=pltpu.CompilerParams(vmem_limit_bytes=VMEM),
        cost_estimate=pl.CostEstimate(
            flops=8 * rows * wide * width, bytes_accessed=4 * rows * wide, transcendentals=0
        ),
    )(hi, lo, before, own, after, *([old] if second else []))


def slot_table(columns, counts):
    rows, slots = columns.shape
    total = rows * lax.axis_size("orb")
    spread = GROUP + 2 * rows
    ids = jnp.arange(rows, dtype=jnp.int32)
    offset = lax.axis_index("orb") * rows - rows
    place = (columns - offset) % total - (ids // GROUP * GROUP)[:, None]
    number = jnp.arange(slots, dtype=jnp.int32)
    place = jnp.where(number[None, :] < counts[:, None], place, -1)
    hit = place[:, :, None] == jnp.arange(spread, dtype=jnp.int32)[None, None, :]
    return jnp.max(jnp.where(hit, number[None, :, None], -1), axis=1)


def neighbours(x):
    size = lax.axis_size("orb")
    up = [(i, (i + 1) % size) for i in range(size)]
    down = [(j, i) for i, j in up]
    return lax.ppermute(x, "orb", up), lax.ppermute(x, "orb", down)


def after_that(x, done):
    return lax.optimization_barrier((x, done))[0]


def body(blocks, columns, counts, vectors):
    rows, width = vectors.shape
    order_total = rows * lax.axis_size("orb")
    cuts = [(c, min(c + LANES, width)) for c in range(0, width, LANES)]
    hi, lo = densify(slot_table(columns, counts), blocks)
    old = [vectors[:, a:b] for a, b in cuts]
    halo, done = [], None
    for x in old:
        x = x if done is None else after_that(x, done)
        halo.append(neighbours(x))
        done = halo[-1]
    first = [apply_step(hi, lo, h[0], x, h[1]) for x, h in zip(old, halo)]
    halo = []
    for x in first:
        x = after_that(x, done)
        halo.append(neighbours(x))
        done = halo[-1]
    filtered = jnp.concatenate(
        [apply_step(hi, lo, h[0], x, h[1], v) for x, h, v in zip(first, halo, old)], axis=1
    )
    partial_gram = jnp.dot(
        filtered.T,
        lax.all_gather(filtered, "band", axis=1, tiled=True),
        precision=lax.Precision.HIGH,
        preferred_element_type=jnp.float32,
    )
    gram = lax.psum_scatter(partial_gram, "orb", scatter_dimension=1, tiled=True)
    return (filtered, gram / order_total)


def solution(mesh):
    placed = (P("orb", None, None, None), P("orb", None), P("orb"), P("orb", "band"))
    return jax.shard_map(
        body,
        mesh=mesh,
        in_specs=placed,
        out_specs=(P("orb", "band"), P("band", "orb")),
        check_vma=False,
    )
```

time: 604 us -> 380 us (0.63)
  matrix products: 140 us -> 11.1 us
  local copies, waits for them, and re-layouts: 115 us -> 8.12 us
  Pallas kernels: 0 us -> 71.5 us
  waiting for transfers between devices: 312 us -> 253 us
  other arithmetic: 18 us -> 3.54 us
  starting transfers between devices: 2.99 us -> 16.2 us
    dot_general x6 -> x0, matrix products: 121 us -> none  [one_group(): jnp.einsum('gkij,gkjm->gim', gblk * galive[:, :, None, None], picked, pre...]
    gather x6 -> x0, local copies, waits for them, and re-layouts: 111 us -> none  [one_group(): picked = stacked[gcol]]
    pallas_call x0 -> x7, Pallas kernels: none -> 71.5 us  [the longest x6 55.7 us: apply_step(): pl.pallas_call(functools.partial(apply_kernel, second=second), grid=(step...]
    ppermute x4 -> x12, waiting for transfers between devices: 102 us -> 45.4 us  [neighbours(): return (lax.ppermute(x, 'orb', up), lax.ppermute(x, 'orb', down))]
    ppermute x4 -> x12, starting transfers between devices: 2.69 us -> 15.9 us  [neighbours(): return (lax.ppermute(x, 'orb', up), lax.ppermute(x, 'orb', down))]
    concatenate x2 -> x1, other arithmetic: 9.14 us -> 1.56 us  [body(): jnp.concatenate([apply_step(hi, lo, h[0], x, h[1], v) for x, h, v in zip(...]
    dot_general x1, matrix products: 18.4 us -> 11.1 us  [body(): jnp.dot(filtered.T, lax.all_gather(filtered, 'band', axis=1, tiled=True),...]
  transfers between devices with their start and end apart: 6 -> 14, of which waited for: 6 -> 6; matrix products, arithmetic and copies ran while one was open for 0% -> 0% of each run, Pallas kernels for 0% -> 17%
where the time goes in v1:
time: 380 us; the launch traced here: 377 us
  waiting for transfers between devices  253 us (67%)
  Pallas kernels  71.5 us (19%)
  starting transfers between devices  16.2 us (4%)
  between operations  14.2 us (4%)
  matrix products  11.1 us (3%)
  local copies, waits for them, and re-layouts  8.12 us (2%)
    all_gather x1, waiting for transfers between devices, body(): lax.all_gather(filtered, 'band', axis=1, tiled=True)  167 us
    pallas_call x6, Pallas kernels, apply_step(): pl.pallas_call(functools.partial(apply_kernel, second=second), grid=(step...  55.7 us
    ppermute x12, waiting for transfers between devices, neighbours(): return (lax.ppermute(x, 'orb', up), lax.ppermute(x, 'orb', down))  45.4 us
    reduce_scatter x1, waiting for transfers between devices, body(): lax.psum_scatter(partial_gram, 'orb', scatter_dimension=1, tiled=True)  40.6 us
    ppermute x12, starting transfers between devices, neighbours(): return (lax.ppermute(x, 'orb', up), lax.ppermute(x, 'orb', down))  15.9 us
    pallas_call x1, Pallas kernels, densify(): pl.pallas_call(functools.partial(densify_kernel, spread=spread), grid_spe...  15.9 us
    dot_general x1, matrix products, body(): jnp.dot(filtered.T, lax.all_gather(filtered, 'band', axis=1, tiled=True),...  11.1 us
  transfers between devices with their start and end apart: 14, of which 6 were waited for; matrix products, arithmetic and copies ran while one was open for 0% of the time, Pallas kernels for 17%

profile of v1, /device:TPU:3, one launch (start us, length us, event | category | flops | bytes accessed | tf_op | source)
XLA Modules:
  0.0 377.4 jit_solution(17979417064891390519)
XLA Ops:
  7.2 2.7 fusion.3
  10.6 2.0 collective-permute-start
  13.4 17.2 %collective-permute-done.1.after_ref = f32[1536,128]{1,0:T(8,128)S(1)} collective-permute-done((f32[1536,128]{1,0:T(8,128)S(1)}, f32[1536,128]{1,0:T(8,128)S(1)}, u32[]{:S(2)}, u32[]{:S(2)}) %collective-permute-start.1) | collective-permute-done | bytes 786464 | tf_op jit(solution)/shard_map/ppermute | solution.py:127
  31.5 1.0 copy-done.10
  32.4 2.6 collective-permute-start.2
  36.0 15.5 %collective-permute-done.3.after_ref = f32[1536,128]{1,0:T(8,128)S(1)} collective-permute-done((f32[1536,128]{1,0:T(8,128)S(1)}, f32[1536,128]{1,0:T(8,128)S(1)}, u32[]{:S(2)}, u32[]{:S(2)}) %collective-permute-start.3) | collective-permute-done | bytes 786464 | tf_op jit(solution)/shard_map/ppermute | solution.py:127
  53.3 2.6 collective-permute-start.4
  56.2 15.9 %shard_map.59 = (bf16[1536,3328]{1,0:T(8,128)(2,1)S(1)}, bf16[1536,3328]{1,0:T(8,128)(2,1)}) custom-call(s32[24,52]{1,0:T(8,128)S(1)} %select_reduce_fusion.slot_ref, f32[24,32,64,64]{3,2,1,0:T(8,128)} %blocks_ref.1), custom_call_target="tpu_custom_call" | custom-call | bytes 60000000 | tf_op jit(solution)/shard_map/pallas_call | solution.py:46
  72.1 9.4 %shard_map.60.own_ref = f32[1536,128]{1,0:T(8,128)S(1)} custom-call(bf16[1536,3328]{1,0:T(8,128)(2,1)S(1)} %get-tuple-element.9.hi_ref, bf16[1536,3328]{1,0:T(8,128)(2,1)} %get-tuple-element.10.lo_ref, f32[1536,128]{1,0:T(8,128)S(1)} %copy-done.11, f32[1536,128]{1,0:T(8,128)S(1)} %copy-done.3, f32[1536,128]{1,0:T(8,128)S(1)} %copy-done.7), custom_call_target="tpu_custom_call" | custom-call | flops 5234491392 | bytes 20447232 | tf_op jit(solution)/shard_map/pallas_call | solution.py:96
  81.6 2.6 collective-permute-start.6
  84.2 9.2 %shard_map.62.own_ref = f32[1536,128]{1,0:T(8,128)S(1)} custom-call(bf16[1536,3328]{1,0:T(8,128)(2,1)S(1)} %get-tuple-element.9.hi_ref, bf16[1536,3328]{1,0:T(8,128)(2,1)} %get-tuple-element.10.lo_ref, f32[1536,128]{1,0:T(8,128)S(1)} %copy-done.9, f32[1536,128]{1,0:T(8,128)S(1)} %copy-done.1, f32[1536,128]{1,0:T(8,128)S(1)} %copy-done.5), custom_call_target="tpu_custom_call" | custom-call | flops 5234491392 | bytes 20447232 | tf_op jit(solution)/shard_map/pallas_call | solution.py:96
  93.4 6.1 %collective-permute-done.7.after_ref = f32[1536,128]{1,0:T(8,128)S(1)} collective-permute-done((f32[1536,128]{1,0:T(8,128)S(1)}, f32[1536,128]{1,0:T(8,128)S(1)}, u32[]{:S(2)}, u32[]{:S(2)}) %collective-permute-start.7) | collective-permute-done | bytes 786464 | tf_op jit(solution)/shard_map/ppermute | solution.py:127
  99.5 2.6 collective-permute-start.8
  102.1 9.4 %shard_map.64.own_ref = f32[1536,128]{1,0:T(8,128)S(1)} custom-call(bf16[1536,3328]{1,0:T(8,128)(2,1)S(1)} %get-tuple-element.9.hi_ref, bf16[1536,3328]{1,0:T(8,128)(2,1)} %get-tuple-element.10.lo_ref, f32[1536,128]{1,0:T(8,128)S(1)} %collective-permute-done.4.before_ref, f32[1536,128]{1,0:T(8,128)} %get-tuple-element.12.own_ref.rest_0_, ...), custom_call_target="tpu_custom_call" | custom-call | flops 5234491392 | bytes 20447232 | tf_op jit(solution)/shard_map/pallas_call | solution.py:96
  111.5 6.7 %collective-permute-done.9.after_ref = f32[1536,128]{1,0:T(8,128)S(1)} collective-permute-done((f32[1536,128]{1,0:T(8,128)S(1)}, f32[1536,128]{1,0:T(8,128)S(1)}, u32[]{:S(2)}, u32[]{:S(2)}) %collective-permute-start.9) | collective-permute-done | bytes 786464 | tf_op jit(solution)/shard_map/ppermute | solution.py:127
  118.3 2.6 collective-permute-start.10
  120.9 9.2 %shard_map.61 = f32[1536,128]{1,0:T(8,128)S(1)} custom-call(bf16[1536,3328]{1,0:T(8,128)(2,1)S(1)} %get-tuple-element.9.hi_ref, bf16[1536,3328]{1,0:T(8,128)(2,1)} %get-tuple-element.10.lo_ref, f32[1536,128]{1,0:T(8,128)S(1)} %collective-permute-done.6.before_ref, f32[1536,128]{1,0:T(8,128)S(1)} %shard_map.60.own_ref, ...), custom_call_target="tpu_custom_call" | custom-call | flops 5234491392 | bytes 20447232 | tf_op jit(solution)/shard_map/pallas_call | solution.py:96
  130.1 9.2 %shard_map.63 = f32[1536,128]{1,0:T(8,128)S(1)} custom-call(bf16[1536,3328]{1,0:T(8,128)(2,1)S(1)} %get-tuple-element.9.hi_ref, bf16[1536,3328]{1,0:T(8,128)(2,1)} %get-tuple-element.10.lo_ref, f32[1536,128]{1,0:T(8,128)S(1)} %collective-permute-done.8.before_ref, f32[1536,128]{1,0:T(8,128)S(1)} %shard_map.62.own_ref, ...), custom_call_target="tpu_custom_call" | custom-call | flops 5234491392 | bytes 20447232 | tf_op jit(solution)/shard_map/pallas_call | solution.py:96
  139.4 9.3 %shard_map.65 = f32[1536,128]{1,0:T(8,128)S(1)} custom-call(bf16[1536,3328]{1,0:T(8,128)(2,1)S(1)} %get-tuple-element.9.hi_ref, bf16[1536,3328]{1,0:T(8,128)(2,1)} %get-tuple-element.10.lo_ref, f32[1536,128]{1,0:T(8,128)S(1)} %collective-permute-done.10.before_ref, f32[1536,128]{1,0:T(8,128)S(1)} %shard_map.64.own_ref, ...), custom_call_target="tpu_custom_call" | custom-call | flops 5234491392 | bytes 20447232 | tf_op jit(solution)/shard_map/pallas_call | solution.py:96
  148.7 1.6 pad_maximum_fusion
  150.5 166.7 %all-gather.2.cloned.1.call-done = f32[1536,1536]{1,0:T(8,128)} async-done(((f32[1536,384]{1,0:T(8,128)}), f32[1536,1536]{1,0:T(8,128)}) %all-gather.2.cloned.1.call-update) | async-done | bytes 9437200 | tf_op jit(solution)/shard_map/all_gather | solution.py:156
  317.2 11.1 %fusion.4 = f32[384,1536]{0,1:T(8,128)} fusion(f32[1536,384]{1,0:T(8,128)S(1)} %copy-done.12, f32[1536,1536]{1,0:T(8,128)} %all-gather.2.cloned.1.call-done), kind=kOutput, calls=%fused_computation.15 | convolution fusion | flops 5435817984 | bytes 14155776 | tf_op jit(solution)/shard_map/dot_general | solution.py:154
  328.3 40.6 %reduce-scatter.2.cloned.1.call-done = f32[384,192]{0,1:T(8,128)} async-done(((f32[384,1536]{0,1:T(8,128)}), f32[384,192]{0,1:T(8,128)}) %reduce-scatter.2.cloned.1.call-update) | async-done | bytes 294928 | tf_op jit(solution)/shard_map/reduce_scatter | solution.py:160
  368.9 1.7 broadcast_multiply_fusion
  (50 shorter events, 5.8 us)
Async XLA Ops:
  7.2 48.7 %copy-start.14 = (s32[24]{0:T(128)S(1)}, s32[24]{0:T(128)}, u32[]{:S(2)}) copy-start(s32[24]{0:T(128)} %param.6) | copy-start | bytes 292
  7.2 48.7 %copy-start.13 = (s32[24,32]{1,0:T(8,128)S(1)}, s32[24,32]{1,0:T(8,128)}, u32[]{:S(2)}) copy-start(s32[24,32]{1,0:T(8,128)} %param.5) | copy-start | bytes 9220
  7.2 310.0 %all-gather.2.cloned.1.call-start = ((), (), s32[]{:S(2)}) async-start(), calls=%async_computation.1 | async-start | bytes 11796480 | tf_op jit(solution)/shard_map/all_gather | solution.py:156
  9.9 20.7 %collective-permute-start.1 = (f32[1536,128]{1,0:T(8,128)S(1)}, f32[1536,128]{1,0:T(8,128)S(1)}, u32[]{:S(2)}, u32[]{:S(2)}) collective-permute-start(f32[1536,128]{1,0:T(8,128)S(1)} %get-tuple-element.16.own_ref.rest_0_), channel_id=1, source_target_pairs={{4,0},{8,4},{12,8},{16,12},{20,16},{24,20},{28,24},{0,28},{5,1},{9... | collective-permute-start | bytes 2359304 | tf_op jit(solution)/shard_map/ppermute | solution.py:127
  10.6 20.9 %collective-permute-start = (f32[1536,128]{1,0:T(8,128)S(1)}, f32[1536,128]{1,0:T(8,128)S(1)}, u32[]{:S(2)}, u32[]{:S(2)}) collective-permute-start(f32[1536,128]{1,0:T(8,128)S(1)} %get-tuple-element.16.own_ref.rest_0_), channel_id=1, source_target_pairs={{0,4},{4,8},{8,12},{12,16},{16,20},{20,24},{24,28},{28,0},{1,5},{5... | collective-permute-start | bytes 2359304 | tf_op jit(solution)/shard_map/ppermute | solution.py:127
  31.5 1.0 copy-start.10
  32.4 19.0 %collective-permute-start.3 = (f32[1536,128]{1,0:T(8,128)S(1)}, f32[1536,128]{1,0:T(8,128)S(1)}, u32[]{:S(2)}, u32[]{:S(2)}) collective-permute-start(f32[1536,128]{1,0:T(8,128)S(1)} %get-tuple-element.11.own_ref.rest_0_), channel_id=1, source_target_pairs={{4,0},{8,4},{12,8},{16,12},{20,16},{24,20},{28,24},{0,28},{5,1},{9... | collective-permute-start | bytes 2359304 | tf_op jit(solution)/shard_map/ppermute | solution.py:127
  32.4 19.9 %collective-permute-start.2 = (f32[1536,128]{1,0:T(8,128)S(1)}, f32[1536,128]{1,0:T(8,128)S(1)}, u32[]{:S(2)}, u32[]{:S(2)}) collective-permute-start(f32[1536,128]{1,0:T(8,128)S(1)} %get-tuple-element.11.own_ref.rest_0_), channel_id=1, source_target_pairs={{0,4},{4,8},{8,12},{12,16},{16,20},{20,24},{24,28},{28,0},{1,5},{5... | collective-permute-start | bytes 2359304 | tf_op jit(solution)/shard_map/ppermute | solution.py:127
  53.3 28.2 %collective-permute-start.5 = (f32[1536,128]{1,0:T(8,128)}, f32[1536,128]{1,0:T(8,128)S(1)}, u32[]{:S(2)}, u32[]{:S(2)}) collective-permute-start(f32[1536,128]{1,0:T(8,128)} %get-tuple-element.12.own_ref.rest_0_), channel_id=1, source_target_pairs={{4,0},{8,4},{12,8},{16,12},{20,16},{24,20},{28,24},{0,28},{5,1},{9... | collective-permute-start | bytes 2359304 | tf_op jit(solution)/shard_map/ppermute | solution.py:127
  53.3 28.2 %collective-permute-start.4 = (f32[1536,128]{1,0:T(8,128)}, f32[1536,128]{1,0:T(8,128)S(1)}, u32[]{:S(2)}, u32[]{:S(2)}) collective-permute-start(f32[1536,128]{1,0:T(8,128)} %get-tuple-element.12.own_ref.rest_0_), channel_id=1, source_target_pairs={{0,4},{4,8},{8,12},{12,16},{16,20},{20,24},{24,28},{28,0},{1,5},{5... | collective-permute-start | bytes 2359304 | tf_op jit(solution)/shard_map/ppermute | solution.py:127
  56.2 15.9 %copy-start.3 = (f32[1536,128]{1,0:T(8,128)S(1)}, f32[1536,128]{1,0:T(8,128)}, u32[]{:S(2)}) copy-start(f32[1536,128]{1,0:T(8,128)} %copy-done.2) | copy-start | bytes 2359300
  56.2 15.9 %copy-start.7 = (f32[1536,128]{1,0:T(8,128)S(1)}, f32[1536,128]{1,0:T(8,128)}, u32[]{:S(2)}) copy-start(f32[1536,128]{1,0:T(8,128)} %copy-done.6) | copy-start | bytes 2359300
  56.2 15.9 %copy-start.11 = (f32[1536,128]{1,0:T(8,128)S(1)}, f32[1536,128]{1,0:T(8,128)}, u32[]{:S(2)}) copy-start(f32[1536,128]{1,0:T(8,128)} %copy-done.10) | copy-start | bytes 2359300
  72.1 12.1 %copy-start.1 = (f32[1536,128]{1,0:T(8,128)S(1)}, f32[1536,128]{1,0:T(8,128)}, u32[]{:S(2)}) copy-start(f32[1536,128]{1,0:T(8,128)} %copy-done) | copy-start | bytes 2359300
  72.1 12.1 %copy-start.5 = (f32[1536,128]{1,0:T(8,128)S(1)}, f32[1536,128]{1,0:T(8,128)}, u32[]{:S(2)}) copy-start(f32[1536,128]{1,0:T(8,128)} %copy-done.4) | copy-start | bytes 2359300
  72.1 12.1 %copy-start.9 = (f32[1536,128]{1,0:T(8,128)S(1)}, f32[1536,128]{1,0:T(8,128)}, u32[]{:S(2)}) copy-start(f32[1536,128]{1,0:T(8,128)} %copy-done.8) | copy-start | bytes 2359300
  81.5 18.0 %collective-permute-start.7 = (f32[1536,128]{1,0:T(8,128)S(1)}, f32[1536,128]{1,0:T(8,128)S(1)}, u32[]{:S(2)}, u32[]{:S(2)}) collective-permute-start(f32[1536,128]{1,0:T(8,128)S(1)} %shard_map.60.own_ref), channel_id=1, source_target_pairs={{4,0},{8,4},{12,8},{16,12},{20,16},{24,20},{28,24},{0,28},{5,1},{9... | collective-permute-start | bytes 2359304 | tf_op jit(solution)/shard_map/ppermute | solution.py:127
  81.6 17.9 %collective-permute-start.6 = (f32[1536,128]{1,0:T(8,128)S(1)}, f32[1536,128]{1,0:T(8,128)S(1)}, u32[]{:S(2)}, u32[]{:S(2)}) collective-permute-start(f32[1536,128]{1,0:T(8,128)S(1)} %shard_map.60.own_ref), channel_id=1, source_target_pairs={{0,4},{4,8},{8,12},{12,16},{16,20},{20,24},{24,28},{28,0},{1,5},{5... | collective-permute-start | bytes 2359304 | tf_op jit(solution)/shard_map/ppermute | solution.py:127
  99.5 18.8 %collective-permute-start.9 = (f32[1536,128]{1,0:T(8,128)S(1)}, f32[1536,128]{1,0:T(8,128)S(1)}, u32[]{:S(2)}, u32[]{:S(2)}) collective-permute-start(f32[1536,128]{1,0:T(8,128)S(1)} %shard_map.62.own_ref), channel_id=1, source_target_pairs={{4,0},{8,4},{12,8},{16,12},{20,16},{24,20},{28,24},{0,28},{5,1},{9... | collective-permute-start | bytes 2359304 | tf_op jit(solution)/shard_map/ppermute | solution.py:127
  99.5 18.8 %collective-permute-start.8 = (f32[1536,128]{1,0:T(8,128)S(1)}, f32[1536,128]{1,0:T(8,128)S(1)}, u32[]{:S(2)}, u32[]{:S(2)}) collective-permute-start(f32[1536,128]{1,0:T(8,128)S(1)} %shard_map.62.own_ref), channel_id=1, source_target_pairs={{0,4},{4,8},{8,12},{12,16},{16,20},{20,24},{24,28},{28,0},{1,5},{5... | collective-permute-start | bytes 2359304 | tf_op jit(solution)/shard_map/ppermute | solution.py:127
  118.3 21.1 %collective-permute-start.11 = (f32[1536,128]{1,0:T(8,128)S(1)}, f32[1536,128]{1,0:T(8,128)S(1)}, u32[]{:S(2)}, u32[]{:S(2)}) collective-permute-start(f32[1536,128]{1,0:T(8,128)S(1)} %shard_map.64.own_ref), channel_id=1, source_target_pairs={{4,0},{8,4},{12,8},{16,12},{20,16},{24,20},{28,24},{0,28},{5,1},{9... | collective-permute-start | bytes 2359304 | tf_op jit(solution)/shard_map/ppermute | solution.py:127
  118.3 21.1 %collective-permute-start.10 = (f32[1536,128]{1,0:T(8,128)S(1)}, f32[1536,128]{1,0:T(8,128)S(1)}, u32[]{:S(2)}, u32[]{:S(2)}) collective-permute-start(f32[1536,128]{1,0:T(8,128)S(1)} %shard_map.64.own_ref), channel_id=1, source_target_pairs={{0,4},{4,8},{8,12},{12,16},{16,20},{20,24},{24,28},{28,0},{1,5},{5... | collective-permute-start | bytes 2359304 | tf_op jit(solution)/shard_map/ppermute | solution.py:127
  150.2 166.9 %copy-start.12 = (f32[1536,384]{1,0:T(8,128)S(1)}, f32[1536,384]{1,0:T(8,128)}, u32[]{:S(2)}) copy-start(f32[1536,384]{1,0:T(8,128)} %pad_maximum_fusion) | copy-start | bytes 7077892
  150.3 218.6 %reduce-scatter.2.cloned.1.call-start = ((), (), s32[]{:S(2)}) async-start(), calls=%async_computation.2 | async-start | bytes 2654208 | tf_op jit(solution)/shard_map/reduce_scatter | solution.py:160
  (5 other events, 4.5 us)
Sparse Core Ops, SparseCore 0:
  150.4 166.7 all-gather.1
  328.4 40.4 reduce-scatter.1

commit v2 on v1

--- a/solution.py
+++ b/solution.py
@@ -127,44 +127,198 @@
     return lax.ppermute(x, "orb", up), lax.ppermute(x, "orb", down)
 
 
-def after_that(x, done):
+def after_that(x, *done):
     return lax.optimization_barrier((x, done))[0]
 
 
-def body(blocks, columns, counts, vectors):
-    rows, width = vectors.shape
-    order_total = rows * lax.axis_size("orb")
-    cuts = [(c, min(c + LANES, width)) for c in range(0, width, LANES)]
-    hi, lo = densify(slot_table(columns, counts), blocks)
-    old = [vectors[:, a:b] for a, b in cuts]
-    halo, done = [], None
-    for x in old:
-        x = x if done is None else after_that(x, done)
-        halo.append(neighbours(x))
-        done = halo[-1]
-    first = [apply_step(hi, lo, h[0], x, h[1]) for x, h in zip(old, halo)]
-    halo = []
-    for x in first:
-        x = after_that(x, done)
-        halo.append(neighbours(x))
-        done = halo[-1]
-    filtered = jnp.concatenate(
-        [apply_step(hi, lo, h[0], x, h[1], v) for x, h, v in zip(first, halo, old)], axis=1
-    )
+def prep_kernel(band_ref, *refs):
+    ins, (hi_ref, lo_ref, thi_ref, tlo_ref) = refs[:4], refs[4:]
+    for place, ref in enumerate(ins):
+        band = band_ref[place]
+        x = ref[...]
+        hi_ref[band], lo_ref[band] = split(x)
+        thi_ref[band], tlo_ref[band] = split(x.T)
+
+
+def prep(bands, parts):
+    rows, width = parts[0].shape
+    plain = jax.ShapeDtypeStruct((4, rows, width), jnp.bfloat16)
+    turned = jax.ShapeDtypeStruct((4, width, rows), jnp.bfloat16)
+    return pl.pallas_call(
+        prep_kernel,
+        in_specs=[pl.BlockSpec(memory_space=pltpu.SMEM)] + [pl.BlockSpec(memory_space=pltpu.VMEM)] * 4,
+        out_specs=[pl.BlockSpec(memory_space=pltpu.VMEM)] * 4,
+        out_shape=[plain, plain, turned, turned],
+        compiler_params=pltpu.CompilerParams(vmem_limit_bytes=VMEM),
+        cost_estimate=pl.CostEstimate(flops=0, bytes_accessed=32 * rows * width, transcendentals=0),
+    )(bands, *parts)
+
+
+def product_kernel(target_ref, thi_ref, tlo_ref, *rest):
+    *ins, out_ref = rest
+    count = len(ins) // 2
+    four, width, rows = thi_ref.shape
+    thi = thi_ref[...].reshape(four * width, rows)
+    tlo = tlo_ref[...].reshape(four * width, rows)
+    his = jnp.concatenate([ref[0] for ref in ins[:count]], axis=1)
+    both = jnp.concatenate([his] + [ref[0] for ref in ins[count:]], axis=1)
+    size = his.shape[1]
+    big = jnp.dot(thi, both, preferred_element_type=jnp.float32)
+    small = jnp.dot(tlo, his, preferred_element_type=jnp.float32)
+    out_ref[0] = big[:, :size] + (big[:, size:] + small)
+
+
+def products(targets, thi, tlo, his, los):
+    four, width, rows = thi.shape
+    size = sum(x.shape[2] for x in his)
+    whole = pl.BlockSpec((four, width, rows), lambda g, t: (0, 0, 0))
+    picked = [pl.BlockSpec((1, rows, x.shape[2]), lambda g, t: (t[g], 0, 0)) for x in his]
+    return pl.pallas_call(
+        product_kernel,
+        grid_spec=pltpu.PrefetchScalarGridSpec(
+            num_scalar_prefetch=1,
+            grid=(targets.shape[0],),
+            in_specs=[whole, whole] + picked + picked,
+            out_specs=pl.BlockSpec((1, four * width, size), lambda g, t: (g, 0, 0)),
+        ),
+        out_shape=jax.ShapeDtypeStruct((targets.shape[0], four * width, size), jnp.float32),
+        compiler_params=pltpu.CompilerParams(vmem_limit_bytes=VMEM),
+        cost_estimate=pl.CostEstimate(
+            flops=targets.shape[0] * 8 * four * width * rows * size,
+            bytes_accessed=8 * four * width * rows,
+            transcendentals=0,
+        ),
+    )(targets, thi, tlo, *his, *los)
+
+
+def linear(chip, core, z):
+    return (chip * 2 + core) * 4 + z
+
+
+def send(x, pairs):
+    return lax.ppermute(x, ("orb", "band"), pairs)
+
+
+def mirrored(pairs):
+    out = []
+    for chip in range(4):
+        for a, b in pairs:
+            out.append((linear(chip, 0, a), linear(chip, 0, b)))
+            out.append((linear(chip, 1, 3 - a), linear(chip, 1, 3 - b)))
+    return out
+
+
+def gather_bands(x):
+    return [x] + [send(x, mirrored([(source, 2)])) for source in (0, 1, 3)]
+
+
+def over_chips(flip):
+    return [
+        (linear(chip, core, 2 - core), linear(chip ^ flip, core, 2 - core))
+        for chip in range(4)
+        for core in range(2)
+    ]
+
+
+class GramPlan:
+    def __init__(self):
+        orb, self.z = lax.axis_index("orb"), lax.axis_index("band")
+        self.chip, self.core = orb // 2, orb % 2
+        order = jnp.asarray([[2, 0, 1, 3], [1, 3, 2, 0]], jnp.int32)
+        self.bands = order[self.core]
+        self.holder = self.z == 2 - self.core
+        self.his, self.los = [], []
+
+    def add_chunk(self, parts):
+        hi, lo, thi, tlo = prep(self.bands, parts)
+        self.his.append(hi)
+        self.los.append(lo)
+        far = jnp.stack([self.chip ^ 2, self.chip ^ 3])
+        near = jnp.stack([self.chip, self.chip ^ 1])
+        theirs = products(far, thi, tlo, self.his, self.los)
+        got = send(theirs, over_chips(2))
+        ours = products(near, thi, tlo, self.his, self.los)
+        return got, ours
+
+    def reduce(self, got, ours):
+        got_x = send(got[1] + ours[1], over_chips(1))
+        total = got[0] + ours[0] + got_x
+        total = total.reshape(4, total.shape[0] // 4, total.shape[1])
+        piece = jnp.where(self.holder, lax.dynamic_index_in_dim(total, self.z, 0, False), 0.0)
+        for z in (0, 1, 3):
+            goal = jnp.where(self.core == 0, z, 3 - z)
+            moved = lax.dynamic_index_in_dim(total, goal, 0, False)
+            piece = piece + send(moved, mirrored([(2, z)]))
+        swap = [(linear(q, c, z), linear(q, 1 - c, z)) for q in range(4) for c in range(2) for z in range(4)]
+        piece = piece + send(piece, swap)
+        turn = [(linear(q, c, z), linear(z, c, q)) for q in range(4) for c in range(2) for z in range(4)]
+        return piece, send(piece, turn).T
+
+    def assemble(self, pieces, widths):
+        rows = []
+        for r in range(len(widths)):
+            row = [pieces[r][0]]
+            start = sum(widths[:r])
+            for c in range(r + 1, len(widths)):
+                row.append(pieces[c][1][start : start + widths[r], :])
+            rows.append(jnp.concatenate(row, axis=1))
+        gram = jnp.concatenate(rows, axis=0)
+        half = gram.shape[1] // 2
+        return jnp.where(self.core == 0, gram[:, :half], gram[:, half:])
+
+
+def simple_gram(filtered):
     partial_gram = jnp.dot(
         filtered.T,
         lax.all_gather(filtered, "band", axis=1, tiled=True),
         precision=lax.Precision.HIGH,
         preferred_element_type=jnp.float32,
     )
-    gram = lax.psum_scatter(partial_gram, "orb", scatter_dimension=1, tiled=True)
-    return (filtered, gram / order_total)
+    return lax.psum_scatter(partial_gram, "orb", scatter_dimension=1, tiled=True)
+
+
+def body(blocks, columns, counts, vectors, by_symmetry):
+    rows, width = vectors.shape
+    order_total = rows * lax.axis_size("orb")
+    widths = [min(LANES, width - c) for c in range(0, width, LANES)]
+    starts = [sum(widths[:c]) for c in range(len(widths))]
+    hi, lo = densify(slot_table(columns, counts), blocks)
+    old = [vectors[:, a : a + w] for a, w in zip(starts, widths)]
+    count = len(widths)
+    halos, first, filtered = {}, [], []
+    order = [("v", 0)]
+    for c in range(count):
+        if c + 1 < count:
+            order.append(("v", c + 1))
+        order.append(("f", c))
+    done = None
+    for kind, c in order:
+        if kind == "v":
+            x = old[c]
+        else:
+            first.append(apply_step(hi, lo, halos["v", c][0], old[c], halos["v", c][1]))
+            x = first[c]
+        if done is not None:
+            x = after_that(x, *done)
+        halos[kind, c] = neighbours(x)
+        done = halos[kind, c] if done is not None else halos[kind, c] + (hi,)
+    for c in range(count):
+        h = halos["f", c]
+        filtered.append(apply_step(hi, lo, h[0], first[c], h[1], old[c]))
+    if by_symmetry:
+        plan = GramPlan()
+        partial = [plan.add_chunk(gather_bands(x)) for x in filtered]
+        gram = plan.assemble([plan.reduce(*p) for p in partial], widths)
+    else:
+        gram = simple_gram(jnp.concatenate(filtered, axis=1))
+    return (jnp.concatenate(filtered, axis=1), gram / order_total)
 
 
 def solution(mesh):
     placed = (P("orb", None, None, None), P("orb", None), P("orb"), P("orb", "band"))
+    by_symmetry = mesh.shape["orb"] == 8 and mesh.shape["band"] == 4
     return jax.shard_map(
-        body,
+        functools.partial(body, by_symmetry=by_symmetry),
         mesh=mesh,
         in_specs=placed,
         out_specs=(P("orb", "band"), P("band", "orb")),

time: 380 us -> 292 us (0.77)
  waiting for transfers between devices: 253 us -> 86.8 us
  starting transfers between devices: 16.2 us -> 60.2 us
  Pallas kernels: 71.5 us -> 102 us
  local copies, waits for them, and re-layouts: 8.12 us -> 26 us
  between operations: 14.2 us -> 1.45 us
  matrix products: 11.1 us -> 0 us
  other arithmetic: 3.54 us -> 13 us
    all_gather x1 -> x0, waiting for transfers between devices: 167 us -> none  [body(): lax.all_gather(filtered, 'band', axis=1, tiled=True)]
    ppermute x0 -> x29, waiting for transfers between devices: none -> 46.3 us  [send(): return lax.ppermute(x, ('orb', 'band'), pairs)]
    ppermute x0 -> x29, starting transfers between devices: none -> 44.3 us  [send(): return lax.ppermute(x, ('orb', 'band'), pairs)]
    reduce_scatter x1 -> x0, waiting for transfers between devices: 40.6 us -> none  [body(): lax.psum_scatter(partial_gram, 'orb', scatter_dimension=1, tiled=True)]
    pallas_call x0 -> x9, Pallas kernels: none -> 28.9 us  [the longest x6 22.8 us: products(): pl.pallas_call(product_kernel, grid_spec=pltpu.PrefetchScalarGridSpec(num...]
    unnamed x30 -> x68, local copies, waits for them, and re-layouts: 5.46 us -> 21.9 us
    dot_general x1 -> x0, matrix products: 11.1 us -> none  [body(): jnp.dot(filtered.T, lax.all_gather(filtered, 'band', axis=1, tiled=True),...]
    add x0 -> x12, other arithmetic: none -> 8.87 us  [the longest x3 4.03 us: reduce(): got_x = send(got[1] + ours[1], over_chips(1))]
  transfers between devices with their start and end apart: 14 -> 41, of which waited for: 6 -> 11; matrix products, arithmetic and copies ran while one was open for 0% -> 5% of each run, Pallas kernels for 17% -> 35%
where the time goes in v2:
time: 292 us; the launch traced here: 290 us
  Pallas kernels  102 us (35%)
  waiting for transfers between devices  86.8 us (30%)
  starting transfers between devices  60.2 us (21%)
  local copies, waits for them, and re-layouts  26 us (9%)
  other arithmetic  13 us (4%)
    pallas_call x6, Pallas kernels, apply_step(): pl.pallas_call(functools.partial(apply_kernel, second=second), grid=(step...  57.6 us
    ppermute x29, waiting for transfers between devices, send(): return lax.ppermute(x, ('orb', 'band'), pairs)  46.3 us
    ppermute x29, starting transfers between devices, send(): return lax.ppermute(x, ('orb', 'band'), pairs)  44.3 us
    ppermute x12, waiting for transfers between devices, neighbours(): return (lax.ppermute(x, 'orb', up), lax.ppermute(x, 'orb', down))  40.5 us
    pallas_call x6, Pallas kernels, products(): pl.pallas_call(product_kernel, grid_spec=pltpu.PrefetchScalarGridSpec(num...  22.8 us
    unnamed x68, local copies, waits for them, and re-layouts  21.9 us
    ppermute x12, starting transfers between devices, neighbours(): return (lax.ppermute(x, 'orb', up), lax.ppermute(x, 'orb', down))  15.9 us
    pallas_call x1, Pallas kernels, densify(): pl.pallas_call(functools.partial(densify_kernel, spread=spread), grid_spe...  15.8 us
  transfers between devices with their start and end apart: 41, of which 11 were waited for; matrix products, arithmetic and copies ran while one was open for 5% of the time, Pallas kernels for 35%

profile of v2, /device:TPU:3, one launch (start us, length us, event | category | flops | bytes accessed | tf_op | source)
XLA Modules:
  0.0 289.9 jit_solution(15458691113639595212)
XLA Ops:
  0.7 3.1 %fusion.20 = (f32[1536,128]{1,0:T(8,128)}, f32[1536,128]{1,0:T(8,128)}, f32[1536,128]{1,0:T(8,128)}) fusion(f32[1536,384]{1,0:T(8,128)} %param.8), kind=kLoop, calls=%fused_computation.56 | loop fusion | bytes 4718592 | tf_op jit(solution)/shard_map/slice | solution.py:286
  6.7 15.8 %shard_map.68 = (bf16[1536,3328]{1,0:T(8,128)(2,1)S(1)}, bf16[1536,3328]{1,0:T(8,128)(2,1)}) custom-call(s32[24,52]{1,0:T(8,128)S(1)} %select_reduce_fusion.slot_ref, f32[24,32,64,64]{3,2,1,0:T(8,128)} %blocks_ref.1), custom_call_target="tpu_custom_call" | custom-call | bytes 60000000 | tf_op jit(solution)/shard_map/pallas_call | solution.py:46
  27.4 10.0 %shard_map.69.own_ref = f32[1536,128]{1,0:T(8,128)S(1)} custom-call(bf16[1536,3328]{1,0:T(8,128)(2,1)S(1)} %get-tuple-element.21.hi_ref, bf16[1536,3328]{1,0:T(8,128)(2,1)} %get-tuple-element.22.lo_ref, f32[1536,128]{1,0:T(8,128)} %collective-permute-done.before_ref, f32[1536,128]{1,0:T(8,128)} %get-tuple-element.41.own_ref.rest_0_, ...), custom_call_target="tpu_custom_call" | custom-call | flops 5234491392 | bytes 20447232 | tf_op jit(solution)/shard_map/pallas_call | solution.py:96
  37.4 7.3 %collective-permute-done.3.after_ref = f32[1536,128]{1,0:T(8,128)S(1)} collective-permute-done((f32[1536,128]{1,0:T(8,128)S(1)}, f32[1536,128]{1,0:T(8,128)S(1)}, u32[]{:S(2)}, u32[]{:S(2)}) %collective-permute-start.3) | collective-permute-done | bytes 786464 | tf_op jit(solution)/shard_map/ppermute | solution.py:127
  44.7 2.6 collective-permute-start.4
  47.3 16.4 %collective-permute-done.5.after_ref = f32[1536,128]{1,0:T(8,128)S(1)} collective-permute-done((f32[1536,128]{1,0:T(8,128)S(1)}, f32[1536,128]{1,0:T(8,128)S(1)}, u32[]{:S(2)}, u32[]{:S(2)}) %collective-permute-start.5) | collective-permute-done | bytes 786464 | tf_op jit(solution)/shard_map/ppermute | solution.py:127
  66.3 9.2 %shard_map.71.own_ref = f32[1536,128]{1,0:T(8,128)S(1)} custom-call(bf16[1536,3328]{1,0:T(8,128)(2,1)S(1)} %get-tuple-element.21.hi_ref, bf16[1536,3328]{1,0:T(8,128)(2,1)} %get-tuple-element.22.lo_ref, f32[1536,128]{1,0:T(8,128)S(1)} %collective-permute-done.2.before_ref, f32[1536,128]{1,0:T(8,128)S(1)} %copy-done.1, ...), custom_call_target="tpu_custom_call" | custom-call | flops 5234491392 | bytes 20447232 | tf_op jit(solution)/shard_map/pallas_call | solution.py:96
  75.6 6.6 %collective-permute-done.7.after_ref = f32[1536,128]{1,0:T(8,128)S(1)} collective-permute-done((f32[1536,128]{1,0:T(8,128)S(1)}, f32[1536,128]{1,0:T(8,128)S(1)}, u32[]{:S(2)}, u32[]{:S(2)}) %collective-permute-start.7) | collective-permute-done | bytes 786464 | tf_op jit(solution)/shard_map/ppermute | solution.py:127
  84.9 9.2 %shard_map.73.own_ref = f32[1536,128]{1,0:T(8,128)S(1)} custom-call(bf16[1536,3328]{1,0:T(8,128)(2,1)S(1)} %get-tuple-element.21.hi_ref, bf16[1536,3328]{1,0:T(8,128)(2,1)} %get-tuple-element.22.lo_ref, f32[1536,128]{1,0:T(8,128)S(1)} %collective-permute-done.6.before_ref, f32[1536,128]{1,0:T(8,128)S(1)} %copy-done, ...), custom_call_target="tpu_custom_call" | custom-call | flops 5234491392 | bytes 20447232 | tf_op jit(solution)/shard_map/pallas_call | solution.py:96
  94.1 8.0 %collective-permute-done.9.after_ref = f32[1536,128]{1,0:T(8,128)S(1)} collective-permute-done((f32[1536,128]{1,0:T(8,128)S(1)}, f32[1536,128]{1,0:T(8,128)S(1)}, u32[]{:S(2)}, u32[]{:S(2)}) %collective-permute-start.9) | collective-permute-done | bytes 786464 | tf_op jit(solution)/shard_map/ppermute | solution.py:127
  104.7 9.2 %shard_map.70.refs_0_ = f32[1536,128]{1,0:T(8,128)S(1)} custom-call(bf16[1536,3328]{1,0:T(8,128)(2,1)S(1)} %get-tuple-element.21.hi_ref, bf16[1536,3328]{1,0:T(8,128)(2,1)} %get-tuple-element.22.lo_ref, f32[1536,128]{1,0:T(8,128)S(1)} %collective-permute-done.4.before_ref, f32[1536,128]{1,0:T(8,128)S(1)} %shard_map.69.own_ref, ...), custom_call_target="tpu_custom_call" | custom-call | flops 5234491392 | bytes 20447232 | tf_op jit(solution)/shard_map/pallas_call | solution.py:96
  114.0 3.2 %collective-permute-start.14 = (f32[1536,128]{1,0:T(8,128)S(1)}, f32[1536,128]{1,0:T(8,128)S(1)}, u32[]{:S(2)}, u32[]{:S(2)}) collective-permute-start(f32[1536,128]{1,0:T(8,128)S(1)} %shard_map.70.refs_0_), channel_id=1, source_target_pairs={{3,2},{4,5},{11,10},{12,13},{19,18},{20,21},{27,26},{28,29}} | collective-permute-start | bytes 2359304 | tf_op jit(solution)/shard_map/ppermute | solution.py:199
  118.7 10.0 %shard_map.72.refs_0_ = f32[1536,128]{1,0:T(8,128)} custom-call(bf16[1536,3328]{1,0:T(8,128)(2,1)S(1)} %get-tuple-element.21.hi_ref, bf16[1536,3328]{1,0:T(8,128)(2,1)} %get-tuple-element.22.lo_ref, f32[1536,128]{1,0:T(8,128)S(1)} %collective-permute-done.8.before_ref, f32[1536,128]{1,0:T(8,128)S(1)} %shard_map.71.own_ref, ...), custom_call_target="tpu_custom_call" | custom-call | flops 5234491392 | bytes 20447232 | tf_op jit(solution)/shard_map/pallas_call | solution.py:96
  132.7 10.0 %shard_map.74.refs_0_ = f32[1536,128]{1,0:T(8,128)} custom-call(bf16[1536,3328]{1,0:T(8,128)(2,1)S(1)} %get-tuple-element.21.hi_ref, bf16[1536,3328]{1,0:T(8,128)(2,1)} %get-tuple-element.22.lo_ref, f32[1536,128]{1,0:T(8,128)S(1)} %collective-permute-done.10.before_ref, f32[1536,128]{1,0:T(8,128)S(1)} %shard_map.73.own_ref, ...), custom_call_target="tpu_custom_call" | custom-call | flops 5234491392 | bytes 20447232 | tf_op jit(solution)/shard_map/pallas_call | solution.py:96
  176.7 5.9 %shard_map.82 = f32[2,512,384]{2,1,0:T(8,128)} custom-call(s32[2]{0:T(128)S(1)} %pad_add_fusion.target_ref, bf16[4,128,1536]{2,1,0:T(8,128)(2,1)S(1)} %copy-done.26, bf16[4,128,1536]{2,1,0:T(8,128)(2,1)S(1)} %get-tuple-element.37.tlo_ref, bf16[4,1536,128]{2,1,0:T(8,128)(2,1)S(1)} %get-tuple-element.30.rest_0_, bf16[4,1536,128]{2,1,0:T(8,128)(2,1)S(1)} %copy-done.14, ...), custom_call_target="tpu_custom_call" | custom-call | flops 4831838208 | bytes 6291456 | tf_op jit(solution)/shard_map/pallas_call | solution.py:176
  185.8 3.4 %shard_map.79 = f32[2,512,256]{2,1,0:T(8,128)S(1)} custom-call(s32[2]{0:T(128)S(1)} %pad_add_fusion.target_ref, bf16[4,128,1536]{2,1,0:T(8,128)(2,1)S(1)} %copy-done.18, bf16[4,128,1536]{2,1,0:T(8,128)(2,1)S(1)} %copy-done.20, bf16[4,1536,128]{2,1,0:T(8,128)(2,1)S(1)} %get-tuple-element.30.rest_0_, bf16[4,1536,128]{2,1,0:T(8,128)(2,1)S(1)} %copy-done.15, ...), custom_call_target="tpu_custom_call" | custom-call | flops 3221225472 | bytes 6291456 | tf_op jit(solution)/shard_map/pallas_call | solution.py:176
  195.0 3.4 %shard_map.80 = f32[2,512,256]{2,1,0:T(8,128)S(1)} custom-call(s32[2]{0:T(128)S(1)} %pad_add_fusion.1.target_ref, bf16[4,128,1536]{2,1,0:T(8,128)(2,1)S(1)} %copy-done.18, bf16[4,128,1536]{2,1,0:T(8,128)(2,1)S(1)} %copy-done.20, bf16[4,1536,128]{2,1,0:T(8,128)(2,1)S(1)} %get-tuple-element.30.rest_0_, bf16[4,1536,128]{2,1,0:T(8,128)(2,1)S(1)} %copy-done.15, ...), custom_call_target="tpu_custom_call" | custom-call | flops 3221225472 | bytes 6291456 | tf_op jit(solution)/shard_map/pallas_call | solution.py:176
  198.4 5.1 %shard_map.83 = f32[2,512,384]{2,1,0:T(8,128)S(1)} custom-call(s32[2]{0:T(128)S(1)} %pad_add_fusion.1.target_ref, bf16[4,128,1536]{2,1,0:T(8,128)(2,1)S(1)} %copy-done.26, bf16[4,128,1536]{2,1,0:T(8,128)(2,1)S(1)} %copy-done.28, bf16[4,1536,128]{2,1,0:T(8,128)(2,1)S(1)} %get-tuple-element.30.rest_0_, bf16[4,1536,128]{2,1,0:T(8,128)(2,1)S(1)} %copy-done.16, ...), custom_call_target="tpu_custom_call" | custom-call | flops 4831838208 | bytes 6291456 | tf_op jit(solution)/shard_map/pallas_call | solution.py:176
  221.3 28.0 %collective-permute-done.28 = f32[128,256]{0,1:T(8,128)S(1)} collective-permute-done((f32[128,256]{0,1:T(8,128)S(1)}, f32[128,256]{0,1:T(8,128)S(1)}, u32[]{:S(2)}, u32[]{:S(2)}) %collective-permute-start.28) | collective-permute-done | bytes 131104 | tf_op jit(solution)/shard_map/ppermute | solution.py:199
  251.6 5.5 %collective-permute-start.29 = (f32[128,256]{0,1:T(8,128)S(1)}, f32[128,256]{0,1:T(8,128)S(1)}, u32[]{:S(2)}, u32[]{:S(2)}) collective-permute-start(f32[128,256]{0,1:T(8,128)S(1)} %fusion.13), channel_id=1, source_target_pairs={{0,4},{1,5},{2,6},{3,7},{4,0},{5,1},{6,2},{7,3},{8,12},{9,13},{10,... | collective-permute-start | bytes 393224 | tf_op jit(solution)/shard_map/ppermute | solution.py:199
  260.2 7.1 %collective-permute-start.30 = (f32[128,256]{0,1:T(8,128)S(1)}, f32[128,256]{0,1:T(8,128)S(1)}, u32[]{:S(2)}, u32[]{:S(2)}) collective-permute-start(f32[128,256]{0,1:T(8,128)S(1)} %add.142), channel_id=1, source_target_pairs={{0,0},{1,8},{2,16},{3,24},{4,4},{5,12},{6,20},{7,28},{8,1},{9,9},{... | collective-permute-start | bytes 393224 | tf_op jit(solution)/shard_map/ppermute | solution.py:199
  269.3 2.9 %pad_maximum_fusion = f32[1536,384]{1,0:T(8,128)} fusion(f32[1536,128]{1,0:T(8,128)} %shard_map.74.refs_0_, f32[1536,128]{1,0:T(8,128)} %shard_map.72.refs_0_, f32[1536,128]{1,0:T(8,128)S(1)} %copy-done.4), kind=kLoop, calls=%fused_computation | loop fusion | flops 1179648 | bytes 4718592 | tf_op jit(solution)/shard_map/concatenate | solution.py:314
  272.2 12.4 %collective-permute-done.30 = f32[128,256]{0,1:T(8,128)S(1)} collective-permute-done((f32[128,256]{0,1:T(8,128)S(1)}, f32[128,256]{0,1:T(8,128)S(1)}, u32[]{:S(2)}, u32[]{:S(2)}) %collective-permute-start.30) | collective-permute-done | bytes 131104 | tf_op jit(solution)/shard_map/ppermute | solution.py:199
  284.6 4.2 %collective-permute-done.40 = f32[128,384]{0,1:T(8,128)S(1)} collective-permute-done((f32[128,384]{0,1:T(8,128)S(1)}, f32[128,384]{0,1:T(8,128)S(1)}, u32[]{:S(2)}, u32[]{:S(2)}) %collective-permute-start.40) | collective-permute-done | bytes 196640 | tf_op jit(solution)/shard_map/ppermute | solution.py:199
  (178 shorter events, 89.9 us)
Async XLA Ops:
  3.8 21.0 %collective-permute-start.1 = (f32[1536,128]{1,0:T(8,128)}, f32[1536,128]{1,0:T(8,128)}, u32[]{:S(2)}, u32[]{:S(2)}) collective-permute-start(f32[1536,128]{1,0:T(8,128)} %get-tuple-element.41.own_ref.rest_0_), channel_id=1, source_target_pairs={{4,0},{8,4},{12,8},{16,12},{20,16},{24,20},{28,24},{0,28},{5,1},{9... | collective-permute-start | bytes 2359304 | tf_op jit(solution)/shard_map/ppermute | solution.py:127
  4.5 20.3 %collective-permute-start = (f32[1536,128]{1,0:T(8,128)}, f32[1536,128]{1,0:T(8,128)}, u32[]{:S(2)}, u32[]{:S(2)}) collective-permute-start(f32[1536,128]{1,0:T(8,128)} %get-tuple-element.41.own_ref.rest_0_), channel_id=1, source_target_pairs={{0,4},{4,8},{8,12},{12,16},{16,20},{20,24},{24,28},{28,0},{1,5},{5... | collective-permute-start | bytes 2359304 | tf_op jit(solution)/shard_map/ppermute | solution.py:127
  24.8 19.9 %collective-permute-start.3 = (f32[1536,128]{1,0:T(8,128)S(1)}, f32[1536,128]{1,0:T(8,128)S(1)}, u32[]{:S(2)}, u32[]{:S(2)}) collective-permute-start(f32[1536,128]{1,0:T(8,128)S(1)} %copy-done.1), channel_id=1, source_target_pairs={{4,0},{8,4},{12,8},{16,12},{20,16},{24,20},{28,24},{0,28},{5,1},{9... | collective-permute-start | bytes 2359304 | tf_op jit(solution)/shard_map/ppermute | solution.py:127
  24.8 19.9 %collective-permute-start.2 = (f32[1536,128]{1,0:T(8,128)S(1)}, f32[1536,128]{1,0:T(8,128)S(1)}, u32[]{:S(2)}, u32[]{:S(2)}) collective-permute-start(f32[1536,128]{1,0:T(8,128)S(1)} %copy-done.1), channel_id=1, source_target_pairs={{0,4},{4,8},{8,12},{12,16},{16,20},{20,24},{24,28},{28,0},{1,5},{5... | collective-permute-start | bytes 2359304 | tf_op jit(solution)/shard_map/ppermute | solution.py:127
  44.7 19.0 %collective-permute-start.5 = (f32[1536,128]{1,0:T(8,128)S(1)}, f32[1536,128]{1,0:T(8,128)S(1)}, u32[]{:S(2)}, u32[]{:S(2)}) collective-permute-start(f32[1536,128]{1,0:T(8,128)S(1)} %shard_map.69.own_ref), channel_id=1, source_target_pairs={{4,0},{8,4},{12,8},{16,12},{20,16},{24,20},{28,24},{0,28},{5,1},{9... | collective-permute-start | bytes 2359304 | tf_op jit(solution)/shard_map/ppermute | solution.py:127
  82.2 19.9 %collective-permute-start.9 = (f32[1536,128]{1,0:T(8,128)S(1)}, f32[1536,128]{1,0:T(8,128)S(1)}, u32[]{:S(2)}, u32[]{:S(2)}) collective-permute-start(f32[1536,128]{1,0:T(8,128)S(1)} %shard_map.71.own_ref), channel_id=1, source_target_pairs={{4,0},{8,4},{12,8},{16,12},{20,16},{24,20},{28,24},{0,28},{5,1},{9... | collective-permute-start | bytes 2359304 | tf_op jit(solution)/shard_map/ppermute | solution.py:127
  82.2 19.9 %collective-permute-start.8 = (f32[1536,128]{1,0:T(8,128)S(1)}, f32[1536,128]{1,0:T(8,128)S(1)}, u32[]{:S(2)}, u32[]{:S(2)}) collective-permute-start(f32[1536,128]{1,0:T(8,128)S(1)} %shard_map.71.own_ref), channel_id=1, source_target_pairs={{0,4},{4,8},{8,12},{12,16},{16,20},{20,24},{24,28},{28,0},{1,5},{5... | collective-permute-start | bytes 2359304 | tf_op jit(solution)/shard_map/ppermute | solution.py:127
  102.1 26.6 %collective-permute-start.11 = (f32[1536,128]{1,0:T(8,128)S(1)}, f32[1536,128]{1,0:T(8,128)S(1)}, u32[]{:S(2)}, u32[]{:S(2)}) collective-permute-start(f32[1536,128]{1,0:T(8,128)S(1)} %shard_map.73.own_ref), channel_id=1, source_target_pairs={{4,0},{8,4},{12,8},{16,12},{20,16},{24,20},{28,24},{0,28},{5,1},{9... | collective-permute-start | bytes 2359304 | tf_op jit(solution)/shard_map/ppermute | solution.py:127
  102.1 29.1 %collective-permute-start.10 = (f32[1536,128]{1,0:T(8,128)S(1)}, f32[1536,128]{1,0:T(8,128)S(1)}, u32[]{:S(2)}, u32[]{:S(2)}) collective-permute-start(f32[1536,128]{1,0:T(8,128)S(1)} %shard_map.73.own_ref), channel_id=1, source_target_pairs={{0,4},{4,8},{8,12},{12,16},{16,20},{20,24},{24,28},{28,0},{1,5},{5... | collective-permute-start | bytes 2359304 | tf_op jit(solution)/shard_map/ppermute | solution.py:127
  114.0 28.7 %collective-permute-start.14 = (f32[1536,128]{1,0:T(8,128)S(1)}, f32[1536,128]{1,0:T(8,128)S(1)}, u32[]{:S(2)}, u32[]{:S(2)}) collective-permute-start(f32[1536,128]{1,0:T(8,128)S(1)} %shard_map.70.refs_0_), channel_id=1, source_target_pairs={{3,2},{4,5},{11,10},{12,13},{19,18},{20,21},{27,26},{28,29}} | collective-permute-start | bytes 2359304 | tf_op jit(solution)/shard_map/ppermute | solution.py:199
  117.2 27.1 %collective-permute-start.13 = (f32[1536,128]{1,0:T(8,128)S(1)}, f32[1536,128]{1,0:T(8,128)S(1)}, u32[]{:S(2)}, u32[]{:S(2)}) collective-permute-start(f32[1536,128]{1,0:T(8,128)S(1)} %shard_map.70.refs_0_), channel_id=1, source_target_pairs={{1,2},{6,5},{9,10},{14,13},{17,18},{22,21},{25,26},{30,29}} | collective-permute-start | bytes 2359304 | tf_op jit(solution)/shard_map/ppermute | solution.py:199
  118.0 29.0 %collective-permute-start.12 = (f32[1536,128]{1,0:T(8,128)S(1)}, f32[1536,128]{1,0:T(8,128)S(1)}, u32[]{:S(2)}, u32[]{:S(2)}) collective-permute-start(f32[1536,128]{1,0:T(8,128)S(1)} %shard_map.70.refs_0_), channel_id=1, source_target_pairs={{0,2},{7,5},{8,10},{15,13},{16,18},{23,21},{24,26},{31,29}} | collective-permute-start | bytes 2359304 | tf_op jit(solution)/shard_map/ppermute | solution.py:199
  128.7 20.0 %collective-permute-start.23 = (f32[1536,128]{1,0:T(8,128)}, f32[1536,128]{1,0:T(8,128)S(1)}, u32[]{:S(2)}, u32[]{:S(2)}) collective-permute-start(f32[1536,128]{1,0:T(8,128)} %shard_map.72.refs_0_), channel_id=1, source_target_pairs={{3,2},{4,5},{11,10},{12,13},{19,18},{20,21},{27,26},{28,29}} | collective-permute-start | bytes 2359304 | tf_op jit(solution)/shard_map/ppermute | solution.py:199
  131.2 27.8 %collective-permute-start.22 = (f32[1536,128]{1,0:T(8,128)}, f32[1536,128]{1,0:T(8,128)}, u32[]{:S(2)}, u32[]{:S(2)}) collective-permute-start(f32[1536,128]{1,0:T(8,128)} %shard_map.72.refs_0_), channel_id=1, source_target_pairs={{1,2},{6,5},{9,10},{14,13},{17,18},{22,21},{25,26},{30,29}} | collective-permute-start | bytes 2359304 | tf_op jit(solution)/shard_map/ppermute | solution.py:199
  145.3 19.3 %collective-permute-start.33 = (f32[1536,128]{1,0:T(8,128)}, f32[1536,128]{1,0:T(8,128)S(1)}, u32[]{:S(2)}, u32[]{:S(2)}) collective-permute-start(f32[1536,128]{1,0:T(8,128)} %shard_map.74.refs_0_), channel_id=1, source_target_pairs={{3,2},{4,5},{11,10},{12,13},{19,18},{20,21},{27,26},{28,29}} | collective-permute-start | bytes 2359304 | tf_op jit(solution)/shard_map/ppermute | solution.py:199
  159.0 34.4 %collective-permute-start.15 = (f32[2,512,128]{2,1,0:T(8,128)S(1)}, f32[2,512,128]{2,1,0:T(8,128)S(1)}, u32[]{:S(2)}, u32[]{:S(2)}) collective-permute-start(f32[2,512,128]{2,1,0:T(8,128)S(1)} %shard_map.76), channel_id=1, source_target_pairs={{2,18},{5,21},{10,26},{13,29},{18,2},{21,5},{26,10},{29,13}} | collective-permute-start | bytes 1572872 | tf_op jit(solution)/shard_map/ppermute | solution.py:199
  182.6 24.3 %collective-permute-start.34 = (f32[2,512,384]{2,1,0:T(8,128)}, f32[2,512,384]{2,1,0:T(8,128)}, u32[]{:S(2)}, u32[]{:S(2)}) collective-permute-start(f32[2,512,384]{2,1,0:T(8,128)} %shard_map.82), channel_id=1, source_target_pairs={{2,18},{5,21},{10,26},{13,29},{18,2},{21,5},{26,10},{29,13}} | collective-permute-start | bytes 4718600 | tf_op jit(solution)/shard_map/ppermute | solution.py:199
  211.6 46.2 %collective-permute-start.17 = (f32[128,128]{1,0:T(8,128)S(1)}, f32[128,128]{1,0:T(8,128)S(1)}, u32[]{:S(2)}, u32[]{:S(2)}) collective-permute-start(f32[128,128]{1,0:T(8,128)S(1)} %get-tuple-element.51), channel_id=1, source_target_pairs={{2,0},{5,7},{10,8},{13,15},{18,16},{21,23},{26,24},{29,31}} | collective-permute-start | bytes 196616 | tf_op jit(solution)/shard_map/ppermute | solution.py:199
  212.3 45.6 %collective-permute-start.19 = (f32[128,128]{1,0:T(8,128)S(1)}, f32[128,128]{1,0:T(8,128)}, u32[]{:S(2)}, u32[]{:S(2)}) collective-permute-start(f32[128,128]{1,0:T(8,128)S(1)} %get-tuple-element.52), channel_id=1, source_target_pairs={{2,3},{5,4},{10,11},{13,12},{18,19},{21,20},{26,27},{29,28}} | collective-permute-start | bytes 196616 | tf_op jit(solution)/shard_map/ppermute | solution.py:199
  216.7 32.6 %collective-permute-start.28 = (f32[128,256]{0,1:T(8,128)S(1)}, f32[128,256]{0,1:T(8,128)S(1)}, u32[]{:S(2)}, u32[]{:S(2)}) collective-permute-start(f32[128,256]{0,1:T(8,128)S(1)} %bitcast.66), channel_id=1, source_target_pairs={{2,3},{5,4},{10,11},{13,12},{18,19},{21,20},{26,27},{29,28}} | collective-permute-start | bytes 393224 | tf_op jit(solution)/shard_map/ppermute | solution.py:199
  220.0 30.8 %collective-permute-start.36 = (f32[128,384]{0,1:T(8,128)S(1)}, f32[128,384]{0,1:T(8,128)S(1)}, u32[]{:S(2)}, u32[]{:S(2)}) collective-permute-start(f32[128,384]{0,1:T(8,128)S(1)} %bitcast.65), channel_id=1, source_target_pairs={{2,0},{5,7},{10,8},{13,15},{18,16},{21,23},{26,24},{29,31}} | collective-permute-start | bytes 589832 | tf_op jit(solution)/shard_map/ppermute | solution.py:199
  220.7 31.0 %collective-permute-start.37 = (f32[128,384]{0,1:T(8,128)S(1)}, f32[128,384]{0,1:T(8,128)S(1)}, u32[]{:S(2)}, u32[]{:S(2)}) collective-permute-start(f32[128,384]{0,1:T(8,128)S(1)} %bitcast.64), channel_id=1, source_target_pairs={{2,1},{5,6},{10,9},{13,14},{18,17},{21,22},{26,25},{29,30}} | collective-permute-start | bytes 589832 | tf_op jit(solution)/shard_map/ppermute | solution.py:199
  260.2 24.4 %collective-permute-start.30 = (f32[128,256]{0,1:T(8,128)S(1)}, f32[128,256]{0,1:T(8,128)S(1)}, u32[]{:S(2)}, u32[]{:S(2)}) collective-permute-start(f32[128,256]{0,1:T(8,128)S(1)} %add.142), channel_id=1, source_target_pairs={{0,0},{1,8},{2,16},{3,24},{4,4},{5,12},{6,20},{7,28},{8,1},{9,9},{... | collective-permute-start | bytes 393224 | tf_op jit(solution)/shard_map/ppermute | solution.py:199
  267.3 21.4 %collective-permute-start.40 = (f32[128,384]{0,1:T(8,128)S(1)}, f32[128,384]{0,1:T(8,128)S(1)}, u32[]{:S(2)}, u32[]{:S(2)}) collective-permute-start(f32[128,384]{0,1:T(8,128)S(1)} %add.151), channel_id=1, source_target_pairs={{0,0},{1,8},{2,16},{3,24},{4,4},{5,12},{6,20},{7,28},{8,1},{9,9},{... | collective-permute-start | bytes 589832 | tf_op jit(solution)/shard_map/ppermute | solution.py:199
  (50 other events, 386.2 us)

commit v3 on v1

v3 whole, which is shorter than its diff:
```python
import functools

import jax
import jax.numpy as jnp
from jax import lax
from jax.experimental import pallas as pl
from jax.experimental.pallas import tpu as pltpu
from jax.sharding import PartitionSpec as P

GROUP = 4
LANES = 128
MIB = 1024 * 1024


def split(x):
    hi = x.astype(jnp.bfloat16)
    lo = (x - hi.astype(jnp.float32)).astype(jnp.bfloat16)
    return hi, lo


def folds(rows, width):
    count = LANES // width if LANES % width == 0 else 1
    return count if rows % (count * 256) == 0 else 1


def fold(x, count):
    return jnp.concatenate(jnp.split(x, count, axis=0), axis=1) if count > 1 else x


def unfold(x, count):
    return jnp.concatenate(jnp.split(x, count, axis=1), axis=0) if count > 1 else x


def densify_kernel(slot_ref, blocks_ref, hi_ref, lo_ref, *, spread, reach):
    blk = blocks_ref.shape[2]
    step = pl.program_id(0)
    tile = (blk, 2 * blk)
    shift = lax.broadcasted_iota(jnp.int32, tile, 1) - lax.broadcasted_iota(jnp.int32, tile, 0)

    def one_row(i, carry):
        row = step * GROUP + i
        start = pl.multiple_of(i * blk, blk)
        for pair in range(spread // 2):
            left = slot_ref[row, 2 * pair]
            right = slot_ref[row, 2 * pair + 1]
            lblk = jnp.where(left >= 0, blocks_ref[i, jnp.maximum(left, 0)], 0.0)
            rblk = jnp.where(right >= 0, blocks_ref[i, jnp.maximum(right, 0)], 0.0)
            both = jnp.concatenate([lblk, rblk], axis=1)
            if reach <= 2 * pair + 1 and 2 * pair < reach + GROUP:
                both = both - jnp.where(shift == (reach + i - 2 * pair) * blk, 0.1, 0.0)
            hi, lo = split(both / 0.9)
            hi_ref[pl.ds(start, blk), pl.ds(pair * 2 * blk, 2 * blk)] = hi
            lo_ref[pl.ds(start, blk), pl.ds(pair * 2 * blk, 2 * blk)] = lo
        return carry

    lax.fori_loop(0, GROUP, one_row, 0)


def densify(slot_of, blocks):
    rows, slots, blk, _ = blocks.shape
    spread = slot_of.shape[1]
    shape = jax.ShapeDtypeStruct((rows * blk, spread * blk), jnp.bfloat16)
    out = pl.BlockSpec((GROUP * blk, spread * blk), lambda g, _: (g, 0))
    return pl.pallas_call(
        functools.partial(densify_kernel, spread=spread, reach=rows),
        grid_spec=pltpu.PrefetchScalarGridSpec(
            num_scalar_prefetch=1,
            grid=(rows // GROUP,),
            in_specs=[pl.BlockSpec((GROUP, slots, blk, blk), lambda g, _: (g, 0, 0, 0))],
            out_specs=[out, out],
        ),
        out_shape=[shape, shape],
        compiler_params=pltpu.CompilerParams(vmem_limit_bytes=20 * MIB),
        cost_estimate=pl.CostEstimate(flops=0, bytes_accessed=60_000_000, transcendentals=0),
    )(slot_of, blocks)


def apply_kernel(hi_ref, lo_ref, before_ref, own_ref, after_ref, *rest, second, count):
    old_ref = rest[0] if second else None
    out_ref, parts = rest[-2:]
    step = pl.program_id(0)
    rows, width = own_ref.shape[0] * count, own_ref.shape[1] // count
    tall, wide = hi_ref.shape
    short = rows // count

    @pl.when(step == 0)
    def _():
        for place, ref in enumerate((before_ref, own_ref, after_ref)):
            for k in range(count):
                hi, lo = split(ref[:, pl.ds(k * width, width)])
                there = pl.ds(place * rows + k * short, short)
                parts[there, pl.ds(0, width)] = hi
                parts[there, pl.ds(width, width)] = lo

    start = pl.multiple_of(step * tall, tall)
    both = jnp.dot(hi_ref[...], parts[pl.ds(start, wide), :], preferred_element_type=jnp.float32)
    other = jnp.dot(
        lo_ref[...], parts[pl.ds(start, wide), pl.ds(0, width)], preferred_element_type=jnp.float32
    )
    product = both[:, :width] + (both[:, width:] + other)
    for k in range(count):

        @pl.when((step * tall) // short == k)
        def _():
            there = pl.ds(pl.multiple_of(step * tall - k * short, tall), tall)
            lanes = pl.ds(k * width, width)
            if second:
                out_ref[there, lanes] = 2.0 * product - old_ref[there, lanes]
            else:
                out_ref[there, lanes] = product


def apply_step(hi, lo, before, own, after, count, old=None):
    short, lanes = own.shape
    rows, width = short * count, lanes // count
    wide = hi.shape[1]
    tall = wide - 2 * rows
    band = pl.BlockSpec((tall, wide), lambda g: (g, 0))
    whole = pl.BlockSpec((short, lanes), lambda g: (0, 0))
    second = old is not None
    return pl.pallas_call(
        functools.partial(apply_kernel, second=second, count=count),
        grid=(rows // tall,),
        in_specs=[band, band, whole, whole, whole] + ([whole] if second else []),
        out_specs=whole,
        out_shape=jax.ShapeDtypeStruct((short, lanes), jnp.float32),
        scratch_shapes=[pltpu.VMEM((3 * rows, 2 * width), jnp.bfloat16)],
        compiler_params=pltpu.CompilerParams(vmem_limit_bytes=22 * MIB),
        cost_estimate=pl.CostEstimate(
            flops=8 * rows * wide * width, bytes_accessed=4 * rows * wide, transcendentals=0
        ),
    )(hi, lo, before, own, after, *([old] if second else []))


def slot_table(columns, counts):
    rows, slots = columns.shape
    total = rows * lax.axis_size("orb")
    spread = GROUP + 2 * rows
    ids = jnp.arange(rows, dtype=jnp.int32)
    offset = lax.axis_index("orb") * rows - rows
    place = (columns - offset) % total - (ids // GROUP * GROUP)[:, None]
    number = jnp.arange(slots, dtype=jnp.int32)
    place = jnp.where(number[None, :] < counts[:, None], place, -1)
    hit = place[:, :, None] == jnp.arange(spread, dtype=jnp.int32)[None, None, :]
    return jnp.max(jnp.where(hit, number[None, :, None], -1), axis=1)


def neighbours(x):
    size = lax.axis_size("orb")
    up = [(i, (i + 1) % size) for i in range(size)]
    down = [(j, i) for i, j in up]
    return lax.ppermute(x, "orb", up), lax.ppermute(x, "orb", down)


def after_that(x, *done):
    return lax.optimization_barrier((x, done))[0]


def prep_kernel(band_ref, *refs, count):
    ins, (hi_ref, lo_ref, thi_ref, tlo_ref) = refs[:4], refs[4:]
    for place, ref in enumerate(ins):
        band = band_ref[place]
        short, width = ref.shape[0], ref.shape[1] // count
        for k in range(count):
            x = ref[:, pl.ds(k * width, width)]
            there = pl.ds(k * short, short)
            hi_ref[band, there, :], lo_ref[band, there, :] = split(x)
            thi_ref[band, :, there], tlo_ref[band, :, there] = split(x.T)


def prep(bands, parts, count):
    short, lanes = parts[0].shape
    rows, width = short * count, lanes // count
    plain = jax.ShapeDtypeStruct((4, rows, width), jnp.bfloat16)
    turned = jax.ShapeDtypeStruct((4, width, rows), jnp.bfloat16)
    return pl.pallas_call(
        functools.partial(prep_kernel, count=count),
        in_specs=[pl.BlockSpec(memory_space=pltpu.SMEM)] + [pl.BlockSpec(memory_space=pltpu.VMEM)] * 4,
        out_specs=[pl.BlockSpec(memory_space=pltpu.VMEM)] * 4,
        out_shape=[plain, plain, turned, turned],
        compiler_params=pltpu.CompilerParams(vmem_limit_bytes=16 * MIB),
        cost_estimate=pl.CostEstimate(flops=0, bytes_accessed=32 * rows * width, transcendentals=0),
    )(bands, *parts)


def product_kernel(target_ref, *refs, shapes):
    refs, out_ref = list(refs[:-1]), refs[-1]
    start = 0
    for columns in shapes:
        thi_ref, tlo_ref = refs[:2]
        ins, refs = refs[2 : 2 + 2 * columns], refs[2 + 2 * columns :]
        four, width, rows = thi_ref.shape
        thi = thi_ref[...].reshape(four * width, rows)
        tlo = tlo_ref[...].reshape(four * width, rows)
        his = jnp.concatenate([ref[0] for ref in ins[:columns]], axis=1)
        los = jnp.concatenate([ref[0] for ref in ins[columns:]], axis=1)
        total = jnp.dot(thi, los, preferred_element_type=jnp.float32)
        total += jnp.dot(tlo, his, preferred_element_type=jnp.float32)
        total += jnp.dot(thi, his, preferred_element_type=jnp.float32)
        out_ref[0, :, pl.ds(start, his.shape[1])] = total
        start += his.shape[1]


def products(targets, chunks, lines):
    ins, specs, shapes, size, flops = [], [], [], 0, 0
    for line in lines:
        hi, lo, thi, tlo = chunks[line]
        four, width, rows = thi.shape
        ins += [thi, tlo]
        specs += [pl.BlockSpec((four, width, rows), lambda g, t: (0, 0, 0))] * 2
        for part in (0, 1):
            for c in range(line + 1):
                x = chunks[c][part]
                ins.append(x)
                specs.append(pl.BlockSpec((1, rows, x.shape[2]), lambda g, t: (t[g], 0, 0)))
        wide = sum(chunks[c][0].shape[2] for c in range(line + 1))
        shapes.append(line + 1)
        size += wide
        flops += 6 * four * width * rows * wide
    return pl.pallas_call(
        functools.partial(product_kernel, shapes=shapes),
        grid_spec=pltpu.PrefetchScalarGridSpec(
            num_scalar_prefetch=1,
            grid=(targets.shape[0],),
            in_specs=specs,
            out_specs=pl.BlockSpec((1, four * width, size), lambda g, t: (g, 0, 0)),
        ),
        out_shape=jax.ShapeDtypeStruct((targets.shape[0], four * width, size), jnp.float32),
        compiler_params=pltpu.CompilerParams(vmem_limit_bytes=28 * MIB),
        cost_estimate=pl.CostEstimate(
            flops=targets.shape[0] * flops, bytes_accessed=8_000_000, transcendentals=0
        ),
    )(targets, *ins)


def linear(chip, core, z):
    return (chip * 2 + core) * 4 + z


def send(x, pairs):
    return lax.ppermute(x, ("orb", "band"), pairs)


def mirrored(pairs):
    out = []
    for chip in range(4):
        for a, b in pairs:
            out.append((linear(chip, 0, a), linear(chip, 0, b)))
            out.append((linear(chip, 1, 3 - a), linear(chip, 1, 3 - b)))
    return out


def gather_bands(x):
    return [x] + [send(x, mirrored([(source, 2)])) for source in (0, 1, 3)]


def over_chips(flip):
    return [
        (linear(chip, core, 2 - core), linear(chip ^ flip, core, 2 - core))
        for chip in range(4)
        for core in range(2)
    ]


class GramPlan:
    def __init__(self, rows, widths, counts):
        orb, self.z = lax.axis_index("orb"), lax.axis_index("band")
        self.chip, self.core = orb // 2, orb % 2
        order = jnp.asarray([[2, 0, 1, 3], [1, 3, 2, 0]], jnp.int32)
        self.bands = order[self.core]
        self.holder = self.z == 2 - self.core
        self.widths, self.counts = widths, counts
        self.chunks = []

    def add(self, parts):
        self.chunks.append(prep(self.bands, parts, self.counts[len(self.chunks)]))

    def far(self, lines, flip):
        targets = jnp.stack([self.chip ^ flip, self.chip ^ 3])
        theirs = products(targets, self.chunks, lines)
        return send(theirs, over_chips(flip)), theirs

    def near(self, lines, flip, theirs):
        targets = after_that(jnp.stack([self.chip, self.chip ^ flip ^ 3]), theirs)
        return products(targets, self.chunks, lines)

    def total(self, got, ours, flip):
        last = send(got[1] + ours[1], over_chips(flip ^ 3))
        out = got[0] + ours[0] + last
        return out.reshape(4, out.shape[0] // 4, out.shape[1])

    def finish(self, totals):
        total = jnp.concatenate(
            [jnp.pad(t, ((0, 0), (0, 0), (0, totals[0].shape[2] - t.shape[2]))) for t in totals], axis=1
        )
        piece = jnp.where(self.holder, lax.dynamic_index_in_dim(total, self.z, 0, False), 0.0)
        for z in (0, 1, 3):
            goal = jnp.where(self.core == 0, z, 3 - z)
            moved = lax.dynamic_index_in_dim(total, goal, 0, False)
            piece = piece + send(moved, mirrored([(2, z)]))
        swap = [(linear(q, c, z), linear(q, 1 - c, z)) for q in range(4) for c in range(2) for z in range(4)]
        piece = piece + send(piece, swap)
        w0, w1, w2, w3 = self.widths
        high = piece[:w0]
        own = [high[:, :w0], high[:, w0:], piece[w0 : w0 + w2, : w0 + w1 + w2], piece[w0 + w2 :]]
        half = w1 // 2
        small = jnp.where(self.core == 0, own[1][:half, :w0], own[1][half:, :w0])
        turn = [[(linear(q, c, z), linear(z, c, q)) for q in range(4) for z in range(4)] for c in range(2)]
        small = send(small, turn[0] + turn[1])
        large = send(piece[w0:], turn[1])
        first = jnp.concatenate([own[0], own[1][:, :w0], own[2][:, :w0], own[3][:, :w0]], axis=0)
        middle = [small.T, own[1][:, w0:], own[2][:, w0 : w0 + w1], own[3][:, w0 : w0 + w1]]
        left = [x if x is middle[0] else x[:, :half] for x in middle]
        right = [x if x is middle[0] else x[:, half:] for x in middle]
        left = jnp.concatenate([first, jnp.concatenate(left, axis=0)], axis=1)
        turned = large.T
        second = [turned[: w0 + w1, :w2], own[2][:, w0 + w1 :], own[3][:, w0 + w1 : w0 + w1 + w2]]
        third = [turned[: w0 + w1 + w2, w2:], own[3][:, w0 + w1 + w2 :]]
        right = jnp.concatenate(
            [jnp.concatenate(x, axis=0) for x in (right, second, third)], axis=1
        )
        return jnp.where(self.core == 0, left, right)


def simple_gram(filtered):
    partial_gram = jnp.dot(
        filtered.T,
        lax.all_gather(filtered, "band", axis=1, tiled=True),
        precision=lax.Precision.HIGH,
        preferred_element_type=jnp.float32,
    )
    return lax.psum_scatter(partial_gram, "orb", scatter_dimension=1, tiled=True)


def in_turn(hi, lo, old, counts, rows):
    first, filtered = [], []
    for x, count in zip(old, counts):
        before, after = neighbours(x)
        first.append(apply_step(hi, lo, before, x, after, count))
    for x, v, count in zip(first, old, counts):
        before, after = neighbours(x)
        filtered.append(apply_step(hi, lo, before, x, after, count, v))
    return filtered, simple_gram(
        jnp.concatenate([unfold(x, count) for x, count in zip(filtered, counts)], axis=1)
    )


def by_symmetry(hi, lo, old, counts, rows, widths):
    def one(x, halo, c, v=None):
        return apply_step(hi, lo, halo[0], x, halo[1], counts[c], v)

    plan = GramPlan(rows, widths, counts)
    v0, v1, v2, v3 = old
    hv0 = neighbours(v0)
    hv1 = neighbours(after_that(v1, hi, *hv0))
    f0 = one(v0, hv0, 0)
    hf0 = neighbours(f0)
    f1 = one(v1, hv1, 1)
    hv2 = neighbours(after_that(v2, f1, *hf0))
    g0 = one(f0, hf0, 0, v0)
    z0 = gather_bands(g0)
    f1 = after_that(f1, g0)
    hf1 = neighbours(f1)
    f2 = one(after_that(v2, g0), hv2, 2)
    hv3 = neighbours(after_that(v3, f2, *hf1))
    g1 = one(after_that(f1, f2), hf1, 1, v1)
    z1 = gather_bands(g1)
    f2 = after_that(f2, g1)
    hf2 = neighbours(f2)
    f3 = one(after_that(v3, g1), hv3, 3)
    hf3 = neighbours(f3)
    z0[0] = after_that(z0[0], f3)
    plan.add(z0)
    g2 = one(after_that(f2, plan.chunks[0][0]), hf2, 2, v2)
    z2 = gather_bands(g2)
    g3 = one(after_that(f3, g2), hf3, 3, v3)
    z3 = gather_bands(g3)
    z1[0] = after_that(z1[0], g3)
    plan.add(z1)
    got_a, theirs = plan.far([0, 1], 2)
    ours_a = plan.near([0, 1], 2, theirs)
    z2[0] = after_that(z2[0], ours_a)
    plan.add(z2)
    got_b, theirs = plan.far([2], 1)
    ours_b = plan.near([2], 1, theirs)
    z3[0] = after_that(z3[0], ours_b)
    plan.add(z3)
    got_c, theirs = plan.far([3], 1)
    ours_c = plan.near([3], 1, theirs)
    totals = [plan.total(got_a, ours_a, 2), plan.total(got_b, ours_b, 1), plan.total(got_c, ours_c, 1)]
    return [g0, g1, g2, after_that(g3, ours_c)], plan.finish(totals)


def body(blocks, columns, counts, vectors, symmetric):
    rows, width = vectors.shape
    order_total = rows * lax.axis_size("orb")
    if symmetric:
        widths = [LANES, LANES, LANES // 2, LANES // 2]
    else:
        widths = [min(LANES, width - c) for c in range(0, width, LANES)]
    counts_of = [folds(rows, w) for w in widths]
    slot_of = slot_table(columns, counts)
    hi, lo = densify(slot_of, blocks)
    old = []
    for c, (w, count) in enumerate(zip(widths, counts_of)):
        start = sum(widths[:c])
        source = after_that(vectors, slot_of) if c else vectors
        old.append(fold(source[:, start : start + w], count))
    if symmetric:
        filtered, gram = by_symmetry(hi, lo, old, counts_of, rows, widths)
    else:
        filtered, gram = in_turn(hi, lo, old, counts_of, rows)
    filtered = jnp.concatenate([unfold(x, n) for x, n in zip(filtered, counts_of)], axis=1)
    return (filtered, gram / order_total)


def solution(mesh):
    placed = (P("orb", None, None, None), P("orb", None), P("orb"), P("orb", "band"))
    return jax.shard_map(
        lambda blocks, columns, counts, vectors: body(
            blocks,
            columns,
            counts,
            vectors,
            mesh.shape["orb"] == 8 and mesh.shape["band"] == 4 and vectors.shape[1] == 3 * LANES,
        ),
        mesh=mesh,
        in_specs=placed,
        out_specs=(P("orb", "band"), P("band", "orb")),
        check_vma=False,
    )
```

time: 380 us -> 339 us (0.89)
  waiting for transfers between devices: 253 us -> 65.9 us
  starting transfers between devices: 16.2 us -> 72.4 us
  local copies, waits for them, and re-layouts: 8.12 us -> 58.8 us
  Pallas kernels: 71.5 us -> 117 us
  other arithmetic: 3.54 us -> 18.7 us
  between operations: 14.2 us -> 1.61 us
  matrix products: 11.1 us -> 0 us
    all_gather x1 -> x0, waiting for transfers between devices: 167 us -> none  [body(): lax.all_gather(filtered, 'band', axis=1, tiled=True)]
    ppermute x0 -> x24, starting transfers between devices: none -> 56 us  [send(): return lax.ppermute(x, ('orb', 'band'), pairs)]
    pallas_call x7 -> x19, Pallas kernels: 71.5 us -> 117 us  [the longest x8 65.5 us: apply_step(): pl.pallas_call(functools.partial(apply_kernel, second=second, count=count...]
    unnamed x30 -> x100, local copies, waits for them, and re-layouts: 5.46 us -> 47.9 us
    reduce_scatter x1 -> x0, waiting for transfers between devices: 40.6 us -> none  [body(): lax.psum_scatter(partial_gram, 'orb', scatter_dimension=1, tiled=True)]
    ppermute x0 -> x24, waiting for transfers between devices: none -> 22 us  [send(): return lax.ppermute(x, ('orb', 'band'), pairs)]
    add x0 -> x8, other arithmetic: none -> 12.5 us  [the longest x3 5.78 us: total(): last = send(got[1] + ours[1], over_chips(flip ^ 3))]
    dot_general x1 -> x0, matrix products: 11.1 us -> none  [body(): jnp.dot(filtered.T, lax.all_gather(filtered, 'band', axis=1, tiled=True),...]
  transfers between devices with their start and end apart: 14 -> 40, of which waited for: 6 -> 8; matrix products, arithmetic and copies ran while one was open for 0% -> 7% of each run, Pallas kernels for 17% -> 33%
where the time goes in v3:
time: 339 us; the launch traced here: 334 us
  Pallas kernels  117 us (35%)
  starting transfers between devices  72.4 us (21%)
  waiting for transfers between devices  65.9 us (19%)
  local copies, waits for them, and re-layouts  58.8 us (17%)
  other arithmetic  18.7 us (6%)
    pallas_call x8, Pallas kernels, apply_step(): pl.pallas_call(functools.partial(apply_kernel, second=second, count=count...  65.5 us
    ppermute x24, starting transfers between devices, send(): return lax.ppermute(x, ('orb', 'band'), pairs)  56 us
    unnamed x100, local copies, waits for them, and re-layouts  47.9 us
    ppermute x16, waiting for transfers between devices, neighbours(): return (lax.ppermute(x, 'orb', up), lax.ppermute(x, 'orb', down))  43.9 us
    pallas_call x6, Pallas kernels, products(): pl.pallas_call(functools.partial(product_kernel, shapes=shapes), grid_spe...  27.1 us
    ppermute x24, waiting for transfers between devices, send(): return lax.ppermute(x, ('orb', 'band'), pairs)  22 us
    ppermute x16, starting transfers between devices, neighbours(): return (lax.ppermute(x, 'orb', up), lax.ppermute(x, 'orb', down))  16.4 us
    pallas_call x1, Pallas kernels, densify(): pl.pallas_call(functools.partial(densify_kernel, spread=spread, reach=row...  12.8 us
  transfers between devices with their start and end apart: 40, of which 8 were waited for; matrix products, arithmetic and copies ran while one was open for 7% of the time, Pallas kernels for 33%

profile of v3, /device:TPU:3, one launch (start us, length us, event | category | flops | bytes accessed | tf_op | source)
XLA Modules:
  0.0 334.3 jit_solution(7531112101145994103)
XLA Ops:
  4.0 12.8 %shard_map.68 = (bf16[1536,3328]{1,0:T(8,128)(2,1)S(1)}, bf16[1536,3328]{1,0:T(8,128)(2,1)S(1)}) custom-call(s32[24,52]{1,0:T(8,128)S(1)} %select_reduce_fusion.slot_ref, f32[24,32,64,64]{3,2,1,0:T(8,128)} %blocks_ref.1), custom_call_target="tpu_custom_call" | custom-call | bytes 60000000 | tf_op jit(solution)/shard_map/pallas_call | solution.py:64
  23.6 6.8 %shard_map.69.own_ref = f32[1536,128]{1,0:T(8,128)S(1)} custom-call(bf16[1536,3328]{1,0:T(8,128)(2,1)S(1)} %get-tuple-element.39.hi_ref, bf16[1536,3328]{1,0:T(8,128)(2,1)S(1)} %get-tuple-element.40.lo_ref, f32[1536,128]{1,0:T(8,128)S(1)} %collective-permute-done.before_ref, f32[1536,128]{1,0:T(8,128)S(1)} %slice.124.own_ref.rest_0_, ...), custom_call_target="tpu_custom_call" | custom-call | flops 5234491392 | bytes 20447232 | tf_op jit(solution)/shard_map/pallas_call | solution.py:121
  33.4 7.6 %collective-permute-done.4.before_ref = f32[1536,128]{1,0:T(8,128)S(1)} collective-permute-done((f32[1536,128]{1,0:T(8,128)S(1)}, f32[1536,128]{1,0:T(8,128)S(1)}, u32[]{:S(2)}, u32[]{:S(2)}) %collective-permute-start.4) | collective-permute-done | bytes 786464 | tf_op jit(solution)/shard_map/ppermute | solution.py:152
  44.4 6.8 %shard_map.71.own_ref = f32[1536,128]{1,0:T(8,128)S(1)} custom-call(bf16[1536,3328]{1,0:T(8,128)(2,1)S(1)} %get-tuple-element.39.hi_ref, bf16[1536,3328]{1,0:T(8,128)(2,1)S(1)} %get-tuple-element.40.lo_ref, f32[1536,128]{1,0:T(8,128)S(1)} %collective-permute-done.4.before_ref, f32[1536,128]{1,0:T(8,128)S(1)} %slice.125.own_ref.rest_0_, ...), custom_call_target="tpu_custom_call" | custom-call | flops 5234491392 | bytes 20447232 | tf_op jit(solution)/shard_map/pallas_call | solution.py:121
  51.2 6.6 %collective-permute-done.2.before_ref = f32[1536,128]{1,0:T(8,128)S(1)} collective-permute-done((f32[1536,128]{1,0:T(8,128)S(1)}, f32[1536,128]{1,0:T(8,128)S(1)}, u32[]{:S(2)}, u32[]{:S(2)}) %collective-permute-start.2) | collective-permute-done | bytes 786464 | tf_op jit(solution)/shard_map/ppermute | solution.py:152
  57.8 6.8 %shard_map.70.refs_0_ = f32[1536,128]{1,0:T(8,128)S(1)} custom-call(bf16[1536,3328]{1,0:T(8,128)(2,1)S(1)} %get-tuple-element.39.hi_ref, bf16[1536,3328]{1,0:T(8,128)(2,1)S(1)} %get-tuple-element.40.lo_ref, f32[1536,128]{1,0:T(8,128)S(1)} %collective-permute-done.2.before_ref, f32[1536,128]{1,0:T(8,128)S(1)} %shard_map.69.own_ref, ...), custom_call_target="tpu_custom_call" | custom-call | flops 5234491392 | bytes 20447232 | tf_op jit(solution)/shard_map/pallas_call | solution.py:121
  72.5 20.4 %collective-permute-done.7.before_ref = f32[768,128]{1,0:T(8,128)S(1)} collective-permute-done((f32[768,128]{1,0:T(8,128)S(1)}, f32[768,128]{1,0:T(8,128)S(1)}, u32[]{:S(2)}, u32[]{:S(2)}) %collective-permute-start.7) | collective-permute-done | bytes 393248 | tf_op jit(solution)/shard_map/ppermute | solution.py:152
  100.0 3.9 %copy-done.1 = bf16[1536,3328]{1,0:T(8,128)(2,1)S(1)} copy-done((bf16[1536,3328]{1,0:T(8,128)(2,1)S(1)}, bf16[1536,3328]{1,0:T(8,128)(2,1)}, u32[]{:S(2)}) %copy-start.1) | copy-done | bytes 10223640
  103.9 3.9 %copy-done.5 = bf16[1536,3328]{1,0:T(8,128)(2,1)S(1)} copy-done((bf16[1536,3328]{1,0:T(8,128)(2,1)S(1)}, bf16[1536,3328]{1,0:T(8,128)(2,1)}, u32[]{:S(2)}) %copy-start.5) | copy-done | bytes 10223640
  109.8 8.1 %shard_map.72.own_ref = f32[768,128]{1,0:T(8,128)S(1)} custom-call(bf16[1536,3328]{1,0:T(8,128)(2,1)S(1)} %copy-done.1, bf16[1536,3328]{1,0:T(8,128)(2,1)S(1)} %copy-done.5, f32[768,128]{1,0:T(8,128)S(1)} %copy-done.41, f32[768,128]{1,0:T(8,128)S(1)} %pad_maximum_fusion.own_ref.rest_0_, f32[768,128]{1,0:T(8,128)S(1)} %copy-done.43), custom_call_target="tpu_custom_call" | custom-call | flops 2617245696 | bytes 20447232 | tf_op jit(solution)/shard_map/pallas_call | solution.py:121
  119.1 9.1 %shard_map.73.refs_0_ = f32[1536,128]{1,0:T(8,128)} custom-call(bf16[1536,3328]{1,0:T(8,128)(2,1)S(1)} %copy-done.1, bf16[1536,3328]{1,0:T(8,128)(2,1)S(1)} %copy-done.5, f32[1536,128]{1,0:T(8,128)} %collective-permute-done.6.before_ref, f32[1536,128]{1,0:T(8,128)S(1)} %shard_map.71.own_ref, f32[1536,128]{1,0:T(8,128)} %collective-permute-done.9.after_ref, ...), custom_call_target="tpu_custom_call" | custom-call | flops 5234491392 | bytes 20447232 | tf_op jit(solution)/shard_map/pallas_call | solution.py:121
  134.2 6.6 %collective-permute-start.21 = (f32[1536,128]{1,0:T(8,128)}, f32[1536,128]{1,0:T(8,128)}, u32[]{:S(2)}, u32[]{:S(2)}) collective-permute-start(f32[1536,128]{1,0:T(8,128)} %shard_map.73.refs_0_), channel_id=1, source_target_pairs={{3,2},{4,5},{11,10},{12,13},{19,18},{20,21},{27,26},{28,29}} | collective-permute-start | bytes 2359304 | tf_op jit(solution)/shard_map/ppermute | solution.py:241
  140.9 3.9 %copy-done.2 = bf16[1536,3328]{1,0:T(8,128)(2,1)S(1)} copy-done((bf16[1536,3328]{1,0:T(8,128)(2,1)S(1)}, bf16[1536,3328]{1,0:T(8,128)(2,1)}, u32[]{:S(2)}) %copy-start.2) | copy-done | bytes 10223640
  148.7 10.0 %shard_map.74.own_ref = f32[768,128]{1,0:T(8,128)} custom-call(bf16[1536,3328]{1,0:T(8,128)(2,1)S(1)} %copy-done.2, bf16[1536,3328]{1,0:T(8,128)(2,1)S(1)} %copy-done.6, f32[768,128]{1,0:T(8,128)} %collective-permute-done.11.before_ref, f32[768,128]{1,0:T(8,128)S(1)} %pad_maximum_fusion.1.own_ref.rest_0_, f32[768,128]{1,0:T(8,128)} %collective-permute-done.12.after_ref), custom_call_target="tpu_custom_call" | custom-call | flops 2617245696 | bytes 20447232 | tf_op jit(solution)/shard_map/pallas_call | solution.py:121
  165.1 3.9 %copy-done.3 = bf16[1536,3328]{1,0:T(8,128)(2,1)S(1)} copy-done((bf16[1536,3328]{1,0:T(8,128)(2,1)S(1)}, bf16[1536,3328]{1,0:T(8,128)(2,1)}, u32[]{:S(2)}) %copy-start.3) | copy-done | bytes 10223640
  173.0 8.3 %shard_map.76.refs_0_ = f32[768,128]{1,0:T(8,128)S(1)} custom-call(bf16[1536,3328]{1,0:T(8,128)(2,1)S(1)} %copy-done.3, bf16[1536,3328]{1,0:T(8,128)(2,1)S(1)} %copy-done.7, f32[768,128]{1,0:T(8,128)S(1)} %copy-done.37, f32[768,128]{1,0:T(8,128)S(1)} %copy-done.35, f32[768,128]{1,0:T(8,128)S(1)} %copy-done.39, f32[768,128]{1,0:T(8,128)S(1)} %pad_maximum_fusion.own_ref.rest_0_), custom_call_target="tpu_custom_call" | custom-call | flops 2617245696 | bytes 20447232 | tf_op jit(solution)/shard_map/pallas_call | solution.py:121
  182.7 9.6 %shard_map.77.refs_0_ = f32[768,128]{1,0:T(8,128)S(1)} custom-call(bf16[1536,3328]{1,0:T(8,128)(2,1)S(1)} %copy-done.3, bf16[1536,3328]{1,0:T(8,128)(2,1)S(1)} %copy-done.7, f32[768,128]{1,0:T(8,128)} %collective-permute-done.17.before_ref, f32[768,128]{1,0:T(8,128)} %shard_map.74.own_ref, f32[768,128]{1,0:T(8,128)} %collective-permute-done.18.after_ref, ...), custom_call_target="tpu_custom_call" | custom-call | flops 2617245696 | bytes 20447232 | tf_op jit(solution)/shard_map/pallas_call | solution.py:121
  192.3 4.6 %collective-permute-start.24 = (f32[768,128]{1,0:T(8,128)S(1)}, f32[768,128]{1,0:T(8,128)S(1)}, u32[]{:S(2)}, u32[]{:S(2)}) collective-permute-start(f32[768,128]{1,0:T(8,128)S(1)} %shard_map.76.refs_0_), channel_id=1, source_target_pairs={{3,2},{4,5},{11,10},{12,13},{19,18},{20,21},{27,26},{28,29}} | collective-permute-start | bytes 1179656 | tf_op jit(solution)/shard_map/ppermute | solution.py:241
  201.1 6.7 %shard_map.79 = f32[2,512,384]{2,1,0:T(8,128)} custom-call(s32[2]{0:T(128)S(1)} %pad_add_fusion.3.target_ref, bf16[4,128,1536]{2,1,0:T(8,128)(2,1)S(1)} %get-tuple-element.54.refs_0_, bf16[4,128,1536]{2,1,0:T(8,128)(2,1)S(1)} %get-tuple-element.55.refs_1_, bf16[4,1536,128]{2,1,0:T(8,128)(2,1)S(1)} %get-tuple-element.51.refs_2_.refs_6_, ...), custom_call_target="tpu_custom_call" | custom-call | flops 3623878656 | bytes 8000000 | tf_op jit(solution)/shard_map/pallas_call | solution.py:220
  209.7 5.8 %shard_map.80 = f32[2,512,384]{2,1,0:T(8,128)S(1)} custom-call(s32[2]{0:T(128)S(1)} %get-tuple-element.62.target_ref, bf16[4,128,1536]{2,1,0:T(8,128)(2,1)S(1)} %get-tuple-element.54.refs_0_, bf16[4,128,1536]{2,1,0:T(8,128)(2,1)S(1)} %get-tuple-element.55.refs_1_, bf16[4,1536,128]{2,1,0:T(8,128)(2,1)S(1)} %get-tuple-element.51.refs_2_.refs_6_, ...), custom_call_target="tpu_custom_call" | custom-call | flops 3623878656 | bytes 8000000 | tf_op jit(solution)/shard_map/pallas_call | solution.py:220
  218.1 11.6 %collective-permute-start.27 = (f32[768,128]{1,0:T(8,128)S(1)}, f32[768,128]{1,0:T(8,128)}, u32[]{:S(2)}, u32[]{:S(2)}) collective-permute-start(f32[768,128]{1,0:T(8,128)S(1)} %shard_map.77.refs_0_), channel_id=1, source_target_pairs={{3,2},{4,5},{11,10},{12,13},{19,18},{20,21},{27,26},{28,29}} | collective-permute-start | bytes 1179656 | tf_op jit(solution)/shard_map/ppermute | solution.py:241
  259.4 4.3 %shard_map.85 = f32[2,256,384]{2,1,0:T(8,128)} custom-call(s32[2]{0:T(128)S(1)} %pad_add_fusion.1.target_ref, bf16[4,64,1536]{2,1,0:T(8,128)(2,1)S(1)} %get-tuple-element.70.refs_0_, bf16[4,64,1536]{2,1,0:T(8,128)(2,1)S(1)} %get-tuple-element.71.refs_1_, bf16[4,1536,128]{2,1,0:T(8,128)(2,1)S(1)} %get-tuple-element.51.refs_2_.refs_6_, ...), custom_call_target="tpu_custom_call" | custom-call | flops 1811939328 | bytes 8000000 | tf_op jit(solution)/shard_map/pallas_call | solution.py:220
  299.8 15.1 %collective-permute-done.36 = f32[256,384]{0,1:T(8,128)} collective-permute-done((f32[256,384]{0,1:T(8,128)S(1)}, f32[256,384]{0,1:T(8,128)}, u32[]{:S(2)}, u32[]{:S(2)}) %collective-permute-start.36) | collective-permute-done | bytes 393248 | tf_op jit(solution)/shard_map/ppermute | solution.py:241
  326.1 6.8 %collective-permute-done.39 = f32[128,384]{0,1:T(8,128)S(1)} collective-permute-done((f32[128,384]{0,1:T(8,128)S(1)}, f32[128,384]{0,1:T(8,128)S(1)}, u32[]{:S(2)}, u32[]{:S(2)}) %collective-permute-start.39) | collective-permute-done | bytes 196640 | tf_op jit(solution)/shard_map/ppermute | solution.py:241
  (218 shorter events, 142.6 us)
Async XLA Ops:
  23.6 20.8 %collective-permute-start.5 = (f32[1536,128]{1,0:T(8,128)S(1)}, f32[1536,128]{1,0:T(8,128)S(1)}, u32[]{:S(2)}, u32[]{:S(2)}) collective-permute-start(f32[1536,128]{1,0:T(8,128)S(1)} %slice.125.own_ref.rest_0_), channel_id=1, source_target_pairs={{4,0},{8,4},{12,8},{16,12},{20,16},{24,20},{28,24},{0,28},{5,1},{9... | collective-permute-start | bytes 2359304 | tf_op jit(solution)/shard_map/ppermute | solution.py:152
  30.4 27.4 %collective-permute-start.2 = (f32[1536,128]{1,0:T(8,128)S(1)}, f32[1536,128]{1,0:T(8,128)S(1)}, u32[]{:S(2)}, u32[]{:S(2)}) collective-permute-start(f32[1536,128]{1,0:T(8,128)S(1)} %shard_map.69.own_ref), channel_id=1, source_target_pairs={{0,4},{4,8},{8,12},{12,16},{16,20},{20,24},{24,28},{28,0},{1,5},{5... | collective-permute-start | bytes 2359304 | tf_op jit(solution)/shard_map/ppermute | solution.py:152
  33.1 24.7 %collective-permute-start.3 = (f32[1536,128]{1,0:T(8,128)S(1)}, f32[1536,128]{1,0:T(8,128)S(1)}, u32[]{:S(2)}, u32[]{:S(2)}) collective-permute-start(f32[1536,128]{1,0:T(8,128)S(1)} %shard_map.69.own_ref), channel_id=1, source_target_pairs={{4,0},{8,4},{12,8},{16,12},{20,16},{24,20},{28,24},{0,28},{5,1},{9... | collective-permute-start | bytes 2359304 | tf_op jit(solution)/shard_map/ppermute | solution.py:152
  64.7 53.2 %collective-permute-start.6 = (f32[1536,128]{1,0:T(8,128)S(1)}, f32[1536,128]{1,0:T(8,128)}, u32[]{:S(2)}, u32[]{:S(2)}) collective-permute-start(f32[1536,128]{1,0:T(8,128)S(1)} %shard_map.71.own_ref), channel_id=1, source_target_pairs={{0,4},{4,8},{8,12},{12,16},{16,20},{20,24},{24,28},{28,0},{1,5},{5... | collective-permute-start | bytes 2359304 | tf_op jit(solution)/shard_map/ppermute | solution.py:152
  68.0 49.9 %collective-permute-start.9 = (f32[1536,128]{1,0:T(8,128)S(1)}, f32[1536,128]{1,0:T(8,128)}, u32[]{:S(2)}, u32[]{:S(2)}) collective-permute-start(f32[1536,128]{1,0:T(8,128)S(1)} %shard_map.71.own_ref), channel_id=1, source_target_pairs={{4,0},{8,4},{12,8},{16,12},{20,16},{24,20},{28,24},{0,28},{5,1},{9... | collective-permute-start | bytes 2359304 | tf_op jit(solution)/shard_map/ppermute | solution.py:152
  68.2 24.7 %collective-permute-start.7 = (f32[768,128]{1,0:T(8,128)S(1)}, f32[768,128]{1,0:T(8,128)S(1)}, u32[]{:S(2)}, u32[]{:S(2)}) collective-permute-start(f32[768,128]{1,0:T(8,128)S(1)} %pad_maximum_fusion.own_ref.rest_0_), channel_id=1, source_target_pairs={{0,4},{4,8},{8,12},{12,16},{16,20},{20,24},{24,28},{28,0},{1,5},{5... | collective-permute-start | bytes 1179656 | tf_op jit(solution)/shard_map/ppermute | solution.py:152
  70.9 24.5 %collective-permute-start.8 = (f32[768,128]{1,0:T(8,128)S(1)}, f32[768,128]{1,0:T(8,128)S(1)}, u32[]{:S(2)}, u32[]{:S(2)}) collective-permute-start(f32[768,128]{1,0:T(8,128)S(1)} %pad_maximum_fusion.own_ref.rest_0_), channel_id=1, source_target_pairs={{4,0},{8,4},{12,8},{16,12},{20,16},{24,20},{28,24},{0,28},{5,1},{9... | collective-permute-start | bytes 1179656 | tf_op jit(solution)/shard_map/ppermute | solution.py:152
  70.9 57.4 %collective-permute-start.13 = (f32[1536,128]{1,0:T(8,128)S(1)}, f32[1536,128]{1,0:T(8,128)}, u32[]{:S(2)}, u32[]{:S(2)}) collective-permute-start(f32[1536,128]{1,0:T(8,128)S(1)} %shard_map.70.refs_0_), channel_id=1, source_target_pairs={{0,2},{7,5},{8,10},{15,13},{16,18},{23,21},{24,26},{31,29}} | collective-permute-start | bytes 2359304 | tf_op jit(solution)/shard_map/ppermute | solution.py:241
  93.6 37.3 %collective-permute-start.14 = (f32[1536,128]{1,0:T(8,128)S(1)}, f32[1536,128]{1,0:T(8,128)}, u32[]{:S(2)}, u32[]{:S(2)}) collective-permute-start(f32[1536,128]{1,0:T(8,128)S(1)} %shard_map.70.refs_0_), channel_id=1, source_target_pairs={{1,2},{6,5},{9,10},{14,13},{17,18},{22,21},{25,26},{30,29}} | collective-permute-start | bytes 2359304 | tf_op jit(solution)/shard_map/ppermute | solution.py:241
  96.2 34.9 %collective-permute-start.15 = (f32[1536,128]{1,0:T(8,128)S(1)}, f32[1536,128]{1,0:T(8,128)}, u32[]{:S(2)}, u32[]{:S(2)}) collective-permute-start(f32[1536,128]{1,0:T(8,128)S(1)} %shard_map.70.refs_0_), channel_id=1, source_target_pairs={{3,2},{4,5},{11,10},{12,13},{19,18},{20,21},{27,26},{28,29}} | collective-permute-start | bytes 2359304 | tf_op jit(solution)/shard_map/ppermute | solution.py:241
  128.3 30.4 %collective-permute-start.10 = (f32[768,128]{1,0:T(8,128)S(1)}, f32[768,128]{1,0:T(8,128)S(1)}, u32[]{:S(2)}, u32[]{:S(2)}) collective-permute-start(f32[768,128]{1,0:T(8,128)S(1)} %shard_map.72.own_ref), channel_id=1, source_target_pairs={{0,4},{4,8},{8,12},{12,16},{16,20},{20,24},{24,28},{28,0},{1,5},{5... | collective-permute-start | bytes 1179656 | tf_op jit(solution)/shard_map/ppermute | solution.py:152
  130.9 29.6 %collective-permute-start.16 = (f32[768,128]{1,0:T(8,128)S(1)}, f32[768,128]{1,0:T(8,128)S(1)}, u32[]{:S(2)}, u32[]{:S(2)}) collective-permute-start(f32[768,128]{1,0:T(8,128)S(1)} %shard_map.72.own_ref), channel_id=1, source_target_pairs={{4,0},{8,4},{12,8},{16,12},{20,16},{24,20},{28,24},{0,28},{5,1},{9... | collective-permute-start | bytes 1179656 | tf_op jit(solution)/shard_map/ppermute | solution.py:152
  131.1 61.2 %collective-permute-start.19 = (f32[1536,128]{1,0:T(8,128)}, f32[1536,128]{1,0:T(8,128)}, u32[]{:S(2)}, u32[]{:S(2)}) collective-permute-start(f32[1536,128]{1,0:T(8,128)} %shard_map.73.refs_0_), channel_id=1, source_target_pairs={{0,2},{7,5},{8,10},{15,13},{16,18},{23,21},{24,26},{31,29}} | collective-permute-start | bytes 2359304 | tf_op jit(solution)/shard_map/ppermute | solution.py:241
  132.7 64.3 %collective-permute-start.20 = (f32[1536,128]{1,0:T(8,128)}, f32[1536,128]{1,0:T(8,128)}, u32[]{:S(2)}, u32[]{:S(2)}) collective-permute-start(f32[1536,128]{1,0:T(8,128)} %shard_map.73.refs_0_), channel_id=1, source_target_pairs={{1,2},{6,5},{9,10},{14,13},{17,18},{22,21},{25,26},{30,29}} | collective-permute-start | bytes 2359304 | tf_op jit(solution)/shard_map/ppermute | solution.py:241
  134.2 64.1 %collective-permute-start.21 = (f32[1536,128]{1,0:T(8,128)}, f32[1536,128]{1,0:T(8,128)}, u32[]{:S(2)}, u32[]{:S(2)}) collective-permute-start(f32[1536,128]{1,0:T(8,128)} %shard_map.73.refs_0_), channel_id=1, source_target_pairs={{3,2},{4,5},{11,10},{12,13},{19,18},{20,21},{27,26},{28,29}} | collective-permute-start | bytes 2359304 | tf_op jit(solution)/shard_map/ppermute | solution.py:241
  159.4 21.9 %collective-permute-start.17 = (f32[768,128]{1,0:T(8,128)}, f32[768,128]{1,0:T(8,128)}, u32[]{:S(2)}, u32[]{:S(2)}) collective-permute-start(f32[768,128]{1,0:T(8,128)} %shard_map.74.own_ref), channel_id=1, source_target_pairs={{0,4},{4,8},{8,12},{12,16},{16,20},{20,24},{24,28},{28,0},{1,5},{5... | collective-permute-start | bytes 1179656 | tf_op jit(solution)/shard_map/ppermute | solution.py:152
  181.3 35.4 %collective-permute-start.22 = (f32[768,128]{1,0:T(8,128)S(1)}, f32[768,128]{1,0:T(8,128)S(1)}, u32[]{:S(2)}, u32[]{:S(2)}) collective-permute-start(f32[768,128]{1,0:T(8,128)S(1)} %shard_map.76.refs_0_), channel_id=1, source_target_pairs={{0,2},{7,5},{8,10},{15,13},{16,18},{23,21},{24,26},{31,29}} | collective-permute-start | bytes 1179656 | tf_op jit(solution)/shard_map/ppermute | solution.py:241
  182.0 36.1 %collective-permute-start.23 = (f32[768,128]{1,0:T(8,128)S(1)}, f32[768,128]{1,0:T(8,128)S(1)}, u32[]{:S(2)}, u32[]{:S(2)}) collective-permute-start(f32[768,128]{1,0:T(8,128)S(1)} %shard_map.76.refs_0_), channel_id=1, source_target_pairs={{1,2},{6,5},{9,10},{14,13},{17,18},{22,21},{25,26},{30,29}} | collective-permute-start | bytes 1179656 | tf_op jit(solution)/shard_map/ppermute | solution.py:241
  192.3 37.3 %collective-permute-start.24 = (f32[768,128]{1,0:T(8,128)S(1)}, f32[768,128]{1,0:T(8,128)S(1)}, u32[]{:S(2)}, u32[]{:S(2)}) collective-permute-start(f32[768,128]{1,0:T(8,128)S(1)} %shard_map.76.refs_0_), channel_id=1, source_target_pairs={{3,2},{4,5},{11,10},{12,13},{19,18},{20,21},{27,26},{28,29}} | collective-permute-start | bytes 1179656 | tf_op jit(solution)/shard_map/ppermute | solution.py:241
  197.0 58.2 %collective-permute-start.25 = (f32[768,128]{1,0:T(8,128)S(1)}, f32[768,128]{1,0:T(8,128)}, u32[]{:S(2)}, u32[]{:S(2)}) collective-permute-start(f32[768,128]{1,0:T(8,128)S(1)} %shard_map.77.refs_0_), channel_id=1, source_target_pairs={{0,2},{7,5},{8,10},{15,13},{16,18},{23,21},{24,26},{31,29}} | collective-permute-start | bytes 1179656 | tf_op jit(solution)/shard_map/ppermute | solution.py:241
  207.9 66.3 %collective-permute-start.28 = (f32[2,512,384]{2,1,0:T(8,128)}, f32[2,512,384]{2,1,0:T(8,128)}, u32[]{:S(2)}, u32[]{:S(2)}) collective-permute-start(f32[2,512,384]{2,1,0:T(8,128)} %shard_map.79), channel_id=1, source_target_pairs={{2,18},{5,21},{10,26},{13,29},{18,2},{21,5},{26,10},{29,13}} | collective-permute-start | bytes 4718600 | tf_op jit(solution)/shard_map/ppermute | solution.py:241
  216.7 38.5 %collective-permute-start.26 = (f32[768,128]{1,0:T(8,128)S(1)}, f32[768,128]{1,0:T(8,128)}, u32[]{:S(2)}, u32[]{:S(2)}) collective-permute-start(f32[768,128]{1,0:T(8,128)S(1)} %shard_map.77.refs_0_), channel_id=1, source_target_pairs={{1,2},{6,5},{9,10},{14,13},{17,18},{22,21},{25,26},{30,29}} | collective-permute-start | bytes 1179656 | tf_op jit(solution)/shard_map/ppermute | solution.py:241
  218.1 37.9 %collective-permute-start.27 = (f32[768,128]{1,0:T(8,128)S(1)}, f32[768,128]{1,0:T(8,128)}, u32[]{:S(2)}, u32[]{:S(2)}) collective-permute-start(f32[768,128]{1,0:T(8,128)S(1)} %shard_map.77.refs_0_), channel_id=1, source_target_pairs={{3,2},{4,5},{11,10},{12,13},{19,18},{20,21},{27,26},{28,29}} | collective-permute-start | bytes 1179656 | tf_op jit(solution)/shard_map/ppermute | solution.py:241
  243.2 26.6 %collective-permute-start.30 = (f32[2,256,320]{1,2,0:T(8,128)}, f32[2,256,320]{1,2,0:T(8,128)S(1)}, u32[]{:S(2)}, u32[]{:S(2)}) collective-permute-start(f32[2,256,320]{1,2,0:T(8,128)} %copy.26), channel_id=1, source_target_pairs={{2,10},{5,13},{10,2},{13,5},{18,26},{21,29},{26,18},{29,21}} | collective-permute-start | bytes 1966088 | tf_op jit(solution)/shard_map/ppermute | solution.py:241
  (64 other events, 663.1 us)

commit v4 on v1

v4 whole, which is shorter than its diff:
```python
import functools

import jax
import jax.numpy as jnp
from jax import lax
from jax.experimental import pallas as pl
from jax.experimental.pallas import tpu as pltpu
from jax.sharding import PartitionSpec as P

GROUP = 4
LANES = 128
MIB = 1024 * 1024
APPLY_MIB = 14


def split(x):
    hi = x.astype(jnp.bfloat16)
    lo = (x - hi.astype(jnp.float32)).astype(jnp.bfloat16)
    return hi, lo


def densify_kernel(slot_ref, blocks_ref, hi_ref, lo_ref, *, spread, reach):
    blk = blocks_ref.shape[2]
    step = pl.program_id(0)
    tile = (blk, 2 * blk)
    shift = lax.broadcasted_iota(jnp.int32, tile, 1) - lax.broadcasted_iota(jnp.int32, tile, 0)

    def one_row(i, carry):
        row = step * GROUP + i
        start = pl.multiple_of(i * blk, blk)
        for pair in range(spread // 2):
            left = slot_ref[row, 2 * pair]
            right = slot_ref[row, 2 * pair + 1]
            lblk = jnp.where(left >= 0, blocks_ref[i, jnp.maximum(left, 0)], 0.0)
            rblk = jnp.where(right >= 0, blocks_ref[i, jnp.maximum(right, 0)], 0.0)
            both = jnp.concatenate([lblk, rblk], axis=1)
            if reach <= 2 * pair + 1 and 2 * pair < reach + GROUP:
                both = both - jnp.where(shift == (reach + i - 2 * pair) * blk, 0.1, 0.0)
            hi, lo = split(both / 0.9)
            hi_ref[pl.ds(start, blk), pl.ds(pair * 2 * blk, 2 * blk)] = hi
            lo_ref[pl.ds(start, blk), pl.ds(pair * 2 * blk, 2 * blk)] = lo
        return carry

    lax.fori_loop(0, GROUP, one_row, 0)


def densify(slot_of, blocks):
    rows, slots, blk, _ = blocks.shape
    spread = slot_of.shape[1]
    shape = pltpu.VMEM((rows * blk, spread * blk), jnp.bfloat16)
    out = pl.BlockSpec((GROUP * blk, spread * blk), lambda g, _: (g, 0))
    return pl.pallas_call(
        functools.partial(densify_kernel, spread=spread, reach=rows),
        grid_spec=pltpu.PrefetchScalarGridSpec(
            num_scalar_prefetch=1,
            grid=(rows // GROUP,),
            in_specs=[pl.BlockSpec((GROUP, slots, blk, blk), lambda g, _: (g, 0, 0, 0))],
            out_specs=[out, out],
        ),
        out_shape=[shape, shape],
        compiler_params=pltpu.CompilerParams(vmem_limit_bytes=20 * MIB),
        cost_estimate=pl.CostEstimate(flops=0, bytes_accessed=60_000_000, transcendentals=0),
    )(slot_of, blocks)


def apply_kernel(hi_ref, lo_ref, before_ref, own_ref, after_ref, *rest, second):
    old_ref = rest[0] if second else None
    out_ref, parts = rest[-2:]
    rows, width = own_ref.shape
    wide = hi_ref.shape[1]
    tall = wide - 2 * rows
    for place, ref in enumerate((before_ref, own_ref, after_ref)):
        there = pl.ds(place * rows, rows)
        parts[there, pl.ds(0, width)], parts[there, pl.ds(width, width)] = split(ref[...])

    def one_group(step, carry):
        start = pl.multiple_of(step * tall, tall)
        here = pl.ds(start, tall)
        reached = pl.ds(start, wide)
        both = jnp.dot(hi_ref[here, :], parts[reached, :], preferred_element_type=jnp.float32)
        other = jnp.dot(
            lo_ref[here, :], parts[reached, pl.ds(0, width)], preferred_element_type=jnp.float32
        )
        product = both[:, :width] + (both[:, width:] + other)
        if second:
            product = 2.0 * product - old_ref[here, :]
        out_ref[here, :] = product
        return carry

    lax.fori_loop(0, rows // tall, one_group, 0)


def apply_step(hi, lo, before, own, after, old=None):
    rows, width = own.shape
    wide = hi.shape[1]
    second = old is not None
    hi, lo = (pltpu.with_memory_space_constraint(x, pltpu.VMEM) for x in (hi, lo))
    vmem = pl.BlockSpec(memory_space=pltpu.VMEM)
    return pl.pallas_call(
        functools.partial(apply_kernel, second=second),
        in_specs=[vmem] * (6 if second else 5),
        out_specs=vmem,
        out_shape=jax.ShapeDtypeStruct((rows, width), jnp.float32),
        scratch_shapes=[pltpu.VMEM((3 * rows, 2 * width), jnp.bfloat16)],
        compiler_params=pltpu.CompilerParams(vmem_limit_bytes=APPLY_MIB * MIB),
        cost_estimate=pl.CostEstimate(
            flops=8 * rows * wide * width, bytes_accessed=4 * rows * wide, transcendentals=0
        ),
    )(hi, lo, before, own, after, *([old] if second else []))


def slot_table(columns, counts):
    rows, slots = columns.shape
    total = rows * lax.axis_size("orb")
    spread = GROUP + 2 * rows
    ids = jnp.arange(rows, dtype=jnp.int32)
    offset = lax.axis_index("orb") * rows - rows
    place = (columns - offset) % total - (ids // GROUP * GROUP)[:, None]
    number = jnp.arange(slots, dtype=jnp.int32)
    place = jnp.where(number[None, :] < counts[:, None], place, -1)
    hit = place[:, :, None] == jnp.arange(spread, dtype=jnp.int32)[None, None, :]
    return jnp.max(jnp.where(hit, number[None, :, None], -1), axis=1)


def neighbours(x):
    size = lax.axis_size("orb")
    up = [(i, (i + 1) % size) for i in range(size)]
    down = [(j, i) for i, j in up]
    return lax.ppermute(x, "orb", up), lax.ppermute(x, "orb", down)


def after_that(x, *done):
    return lax.optimization_barrier((x, done))[0]


def prep_kernel(band_ref, *refs):
    ins, (hi_ref, lo_ref, thi_ref, tlo_ref) = refs[:4], refs[4:]
    for place, ref in enumerate(ins):
        band = band_ref[place]
        x = ref[...]
        hi_ref[band], lo_ref[band] = split(x)
        thi_ref[band], tlo_ref[band] = split(x.T)


def prep(bands, parts):
    rows, width = parts[0].shape
    plain = jax.ShapeDtypeStruct((4, rows, width), jnp.bfloat16)
    turned = jax.ShapeDtypeStruct((4, width, rows), jnp.bfloat16)
    return pl.pallas_call(
        prep_kernel,
        in_specs=[pl.BlockSpec(memory_space=pltpu.SMEM)] + [pl.BlockSpec(memory_space=pltpu.VMEM)] * 4,
        out_specs=[pl.BlockSpec(memory_space=pltpu.VMEM)] * 4,
        out_shape=[plain, plain, turned, turned],
        compiler_params=pltpu.CompilerParams(vmem_limit_bytes=16 * MIB),
        cost_estimate=pl.CostEstimate(flops=0, bytes_accessed=32 * rows * width, transcendentals=0),
    )(bands, *parts)


def product_kernel(target_ref, thi_ref, tlo_ref, *refs):
    ins, out_ref = refs[:-1], refs[-1]
    columns = len(ins) // 2
    count, width, rows = thi_ref.shape
    thi = thi_ref[...].reshape(count * width, rows)
    tlo = tlo_ref[...].reshape(count * width, rows)
    his = jnp.concatenate([ref[0] for ref in ins[:columns]], axis=1)
    los = jnp.concatenate([ref[0] for ref in ins[columns:]], axis=1)
    small = jnp.dot(thi, los, preferred_element_type=jnp.float32)
    small += jnp.dot(tlo, his, preferred_element_type=jnp.float32)
    out_ref[0] = small + jnp.dot(thi, his, preferred_element_type=jnp.float32)


def products(targets, chunks, half=None):
    _, _, thi, tlo = chunks[-1]
    four, width, rows = thi.shape
    count = four if half is None else four // 2
    place = half or 0
    size = sum(chunk[0].shape[2] for chunk in chunks)
    left = pl.BlockSpec((count, width, rows), lambda g, t: (place, 0, 0))
    right = [pl.BlockSpec((1, rows, chunk[0].shape[2]), lambda g, t: (t[g], 0, 0)) for chunk in chunks]
    return pl.pallas_call(
        product_kernel,
        grid_spec=pltpu.PrefetchScalarGridSpec(
            num_scalar_prefetch=1,
            grid=(targets.shape[0],),
            in_specs=[left, left] + right + right,
            out_specs=pl.BlockSpec((1, count * width, size), lambda g, t: (g, 0, 0)),
        ),
        out_shape=jax.ShapeDtypeStruct((targets.shape[0], count * width, size), jnp.float32),
        compiler_params=pltpu.CompilerParams(vmem_limit_bytes=24 * MIB),
        cost_estimate=pl.CostEstimate(
            flops=targets.shape[0] * 6 * count * width * rows * size,
            bytes_accessed=8_000_000,
            transcendentals=0,
        ),
    )(targets, thi, tlo, *[c[0] for c in chunks], *[c[1] for c in chunks])


def middle_kernel(got_a, ours_a, got_b, ours_b, send_a, keep_a, send_b, keep_b):
    for got, ours, send_ref, keep in ((got_a, ours_a, send_a, keep_a), (got_b, ours_b, send_b, keep_b)):
        keep[...] = got[0] + ours[0]
        send_ref[...] = got[1] + ours[1]


def middle(*parts):
    shape = jax.ShapeDtypeStruct(parts[0].shape[1:], jnp.float32)
    vmem = pl.BlockSpec(memory_space=pltpu.VMEM)
    return pl.pallas_call(
        middle_kernel,
        in_specs=[vmem] * 4,
        out_specs=[vmem] * 4,
        out_shape=[shape] * 4,
        compiler_params=pltpu.CompilerParams(vmem_limit_bytes=12 * MIB),
        cost_estimate=pl.CostEstimate(flops=0, bytes_accessed=5_000_000, transcendentals=0),
    )(*parts)


def pick_kernel(goal_ref, *refs):
    ins, outs, sums = refs[:-5], refs[-5:-1], refs[-1]
    half = len(ins) // 2
    rows = sums.shape[1]
    for place in range(4):
        keep, got = (ins[0], ins[1]) if half == 1 or place < 2 else (ins[2], ins[3])
        start = (place if half == 1 else place % 2) * rows
        sums[place] = keep[pl.ds(start, rows), :] + got[pl.ds(start, rows), :]
    for k, out in enumerate(outs):
        out[...] = sums[goal_ref[k]]
    outs[3][...] = jnp.where(goal_ref[4] > 0, outs[3][...], 0.0)


def pick(goals, *parts):
    rows, size = parts[0].shape[0] * len(parts) // 8, parts[0].shape[1]
    shape = jax.ShapeDtypeStruct((rows, size), jnp.float32)
    vmem = pl.BlockSpec(memory_space=pltpu.VMEM)
    return pl.pallas_call(
        pick_kernel,
        in_specs=[pl.BlockSpec(memory_space=pltpu.SMEM)] + [vmem] * len(parts),
        out_specs=[vmem] * 4,
        out_shape=[shape] * 4,
        scratch_shapes=[pltpu.VMEM((4, rows, size), jnp.float32)],
        compiler_params=pltpu.CompilerParams(vmem_limit_bytes=12 * MIB),
        cost_estimate=pl.CostEstimate(flops=0, bytes_accessed=3_000_000, transcendentals=0),
    )(goals, *parts)


def assemble_kernel(core_ref, e0_ref, e1_ref, turn_ref, own_ref, other_ref, ta_ref, tb_ref, out_ref, *, scale):
    w = e0_ref.shape[0]
    low = own_ref[...] + other_ref[...]
    turned = (ta_ref[...] + tb_ref[...]).T
    first = jnp.concatenate([e0_ref[...], turn_ref[...].T, turned[:w]], axis=1)
    second = jnp.concatenate([e1_ref[...], turned[w:]], axis=1)
    half = out_ref.shape[1]
    is_first = core_ref[0] == 0
    for k, x in enumerate((first, second, low)):
        out_ref[pl.ds(k * w, w), :] = jnp.where(is_first, x[:, :half], x[:, half:]) * scale


def assemble(core, parts, order):
    w = parts[0].shape[0]
    vmem = pl.BlockSpec(memory_space=pltpu.VMEM)
    return pl.pallas_call(
        functools.partial(assemble_kernel, scale=1.0 / order),
        in_specs=[pl.BlockSpec(memory_space=pltpu.SMEM)] + [vmem] * len(parts),
        out_specs=vmem,
        out_shape=jax.ShapeDtypeStruct((3 * w, 3 * w // 2), jnp.float32),
        compiler_params=pltpu.CompilerParams(vmem_limit_bytes=12 * MIB),
        cost_estimate=pl.CostEstimate(flops=0, bytes_accessed=2_000_000, transcendentals=0),
    )(core[None], *parts)


def linear(chip, core, z):
    return (chip * 2 + core) * 4 + z


def send(x, pairs):
    return lax.ppermute(x, ("orb", "band"), pairs)


def mirrored(pairs):
    out = []
    for chip in range(4):
        for a, b in pairs:
            out.append((linear(chip, 0, a), linear(chip, 0, b)))
            out.append((linear(chip, 1, 3 - a), linear(chip, 1, 3 - b)))
    return out


def gather_bands(x):
    return [x] + [send(x, mirrored([(source, 2)])) for source in (0, 1, 3)]


def over_chips(flip):
    return [
        (linear(chip, core, 2 - core), linear(chip ^ flip, core, 2 - core))
        for chip in range(4)
        for core in range(2)
    ]


EVERY = [(q, c, z) for q in range(4) for c in range(2) for z in range(4)]
SWAP = [(linear(q, c, z), linear(q, 1 - c, z)) for q, c, z in EVERY]
TURN = [(linear(q, c, z), linear(z, c, q)) for q, c, z in EVERY]
TURN_UP = [[(linear(q, c, z), linear(z, 1, q)) for q, c, z in EVERY if c == core] for core in range(2)]


def simple_gram(filtered):
    partial_gram = jnp.dot(
        filtered.T,
        lax.all_gather(filtered, "band", axis=1, tiled=True),
        precision=lax.Precision.HIGH,
        preferred_element_type=jnp.float32,
    )
    return lax.psum_scatter(partial_gram, "orb", scatter_dimension=1, tiled=True)


def in_turn(hi, lo, old, order):
    first, filtered = [], []
    for x in old:
        before, after = neighbours(x)
        first.append(apply_step(hi, lo, before, x, after))
    for x, v in zip(first, old):
        before, after = neighbours(x)
        filtered.append(apply_step(hi, lo, before, x, after, v))
    filtered = jnp.concatenate(filtered, axis=1)
    return filtered, simple_gram(filtered) / order


def by_symmetry(hi, lo, old, order):
    def one(x, halo, v=None):
        return apply_step(hi, lo, halo[0], x, halo[1], v)

    orb, z = lax.axis_index("orb"), lax.axis_index("band")
    chip, core = orb // 2, orb % 2
    bands = jnp.asarray([[2, 0, 1, 3], [1, 3, 2, 0]], jnp.int32)[core]
    holder = (z == 2 - core).astype(jnp.int32)
    goals = jnp.stack([jnp.where(core == 0, k, 3 - k) for k in (0, 1, 3)] + [z, holder]).astype(jnp.int32)
    far_y = jnp.stack([chip ^ 2, chip ^ 3])
    far_x = jnp.stack([chip ^ 1, chip ^ 3])
    near_y = jnp.stack([chip, chip ^ 1])
    near_x = jnp.stack([chip, chip ^ 2])

    def deliver(parts):
        moved = pick(goals, *parts)
        piece = moved[3]
        for k, x in zip((0, 1, 3), moved):
            piece = piece + send(x, mirrored([(2, k)]))
        return piece

    v0, v1, v2 = old
    hv = [neighbours(x) for x in old]
    f0 = one(v0, hv[0])
    hf0 = neighbours(f0)
    f1 = one(v1, hv[1])
    hf1 = neighbours(f1)
    f2 = one(v2, hv[2])
    hf2 = neighbours(f2)
    g0 = one(f0, hf0, v0)
    z0 = gather_bands(g0)
    g1 = one(after_that(f1, g0), hf1, v1)
    z1 = gather_bands(g1)
    chunks = [prep(bands, [after_that(z0[0], g1)] + z0[1:])]
    far0 = products(far_y, chunks)
    got0 = send(far0, over_chips(2))
    g2 = one(after_that(f2, far0), hf2, v2)
    z2 = gather_bands(g2)
    ours0 = products(after_that(near_y, g2), chunks)
    filtered = jnp.concatenate([g0, g1, after_that(g2, ours0)], axis=1)
    chunks.append(prep(bands, [after_that(z1[0], filtered)] + z1[1:]))
    far1 = products(far_y, chunks)
    got1 = send(far1, over_chips(2))
    ours1 = products(after_that(near_y, far1), chunks)
    last0 = send(after_that(got0, ours1)[1] + ours0[1], over_chips(1))
    chunks.append(prep(bands, [after_that(z2[0], ours1)] + z2[1:]))
    far2y = products(far_y, chunks, 0)
    got2y = send(far2y, over_chips(2))
    far2x = products(after_that(far_x, far2y), chunks, 1)
    got2x = send(far2x, over_chips(1))
    last1 = send(after_that(got1, far2x)[1] + ours1[1], over_chips(1))
    ours2y = products(after_that(near_y, far2x), chunks, 0)
    ours2x = products(after_that(near_x, ours2y), chunks, 1)
    send2y, keep2y, send2x, keep2x = middle(got2y, ours2y, got2x, ours2x)
    last2y = send(send2y, over_chips(1))
    last2x = send(send2x, over_chips(2))
    early = deliver(
        [
            jnp.concatenate([got0[0] + ours0[0], got1[0] + ours1[0]], axis=1),
            jnp.concatenate([last0, last1], axis=1),
        ]
    )
    early = early + send(early, SWAP)
    w = v0.shape[1]
    early_turn = send(early[:, w : 2 * w], TURN)
    piece = deliver([keep2y, last2y, keep2x, last2x])
    other = send(piece, SWAP)
    turned = [send(piece[:, : 2 * w], TURN_UP[k]) for k in (0, 1)]
    gram = assemble(
        core, [early[:, :w], early[:, w:], early_turn, piece, other, *turned], order
    )
    return filtered, gram


def body(blocks, columns, counts, vectors, symmetric):
    rows, width = vectors.shape
    order = rows * lax.axis_size("orb")
    slot_of = slot_table(columns, counts)
    hi, lo = densify(slot_of, blocks)
    later = after_that(vectors, slot_of)
    old = [
        (later if c else vectors)[:, c : min(c + LANES, width)] for c in range(0, width, LANES)
    ]
    return (by_symmetry if symmetric else in_turn)(hi, lo, old, order)


def solution(mesh):
    placed = (P("orb", None, None, None), P("orb", None), P("orb"), P("orb", "band"))

    def whole(blocks, columns, counts, vectors):
        symmetric = (
            mesh.shape["orb"] == 8 and mesh.shape["band"] == 4 and vectors.shape[1] == 3 * LANES
        )
        return body(blocks, columns, counts, vectors, symmetric)

    return jax.shard_map(
        whole,
        mesh=mesh,
        in_specs=placed,
        out_specs=(P("orb", "band"), P("band", "orb")),
        check_vma=False,
    )
```

time: 380 us -> 240 us (0.63)
  waiting for transfers between devices: 253 us -> 54.9 us
  starting transfers between devices: 16.2 us -> 55.4 us
  Pallas kernels: 71.5 us -> 96 us
  local copies, waits for them, and re-layouts: 8.12 us -> 23.9 us
  between operations: 14.2 us -> 1.47 us
  matrix products: 11.1 us -> 0 us
    all_gather x1 -> x0, waiting for transfers between devices: 167 us -> none  [body(): lax.all_gather(filtered, 'band', axis=1, tiled=True)]
    ppermute x0 -> x28, starting transfers between devices: none -> 43.4 us  [send(): return lax.ppermute(x, ('orb', 'band'), pairs)]
    reduce_scatter x1 -> x0, waiting for transfers between devices: 40.6 us -> none  [body(): lax.psum_scatter(partial_gram, 'orb', scatter_dimension=1, tiled=True)]
    ppermute x0 -> x28, waiting for transfers between devices: none -> 40.3 us  [send(): return lax.ppermute(x, ('orb', 'band'), pairs)]
    ppermute x12, waiting for transfers between devices: 45.4 us -> 14.6 us  [neighbours(): return (lax.ppermute(x, 'orb', up), lax.ppermute(x, 'orb', down))]
    pallas_call x7 -> x22, Pallas kernels: 71.5 us -> 96 us  [the longest x6 47.2 us: apply_step(): pl.pallas_call(functools.partial(apply_kernel, second=second), in_specs=[...]
    unnamed x30 -> x65, local copies, waits for them, and re-layouts: 5.46 us -> 21.1 us
    dot_general x1 -> x0, matrix products: 11.1 us -> none  [body(): jnp.dot(filtered.T, lax.all_gather(filtered, 'band', axis=1, tiled=True),...]
  transfers between devices with their start and end apart: 14 -> 40, of which waited for: 6 -> 10; matrix products, arithmetic and copies ran while one was open for 0% -> 3% of each run, Pallas kernels for 17% -> 40%
where the time goes in v4:
time: 240 us; the launch traced here: 238 us
  Pallas kernels  96 us (40%)
  starting transfers between devices  55.4 us (23%)
  waiting for transfers between devices  54.9 us (23%)
  local copies, waits for them, and re-layouts  23.9 us (10%)
  other arithmetic  6.12 us (3%)
    pallas_call x6, Pallas kernels, apply_step(): pl.pallas_call(functools.partial(apply_kernel, second=second), in_specs=[...  47.2 us
    ppermute x28, starting transfers between devices, send(): return lax.ppermute(x, ('orb', 'band'), pairs)  43.4 us
    ppermute x28, waiting for transfers between devices, send(): return lax.ppermute(x, ('orb', 'band'), pairs)  40.3 us
    pallas_call x8, Pallas kernels, products(): pl.pallas_call(product_kernel, grid_spec=pltpu.PrefetchScalarGridSpec(num...  28.5 us
    unnamed x65, local copies, waits for them, and re-layouts  21.1 us
    ppermute x12, waiting for transfers between devices, neighbours(): return (lax.ppermute(x, 'orb', up), lax.ppermute(x, 'orb', down))  14.6 us
    pallas_call x1, Pallas kernels, densify(): pl.pallas_call(functools.partial(densify_kernel, spread=spread, reach=row...  12.8 us
    ppermute x12, starting transfers between devices, neighbours(): return (lax.ppermute(x, 'orb', up), lax.ppermute(x, 'orb', down))  11.9 us
  transfers between devices with their start and end apart: 40, of which 10 were waited for; matrix products, arithmetic and copies ran while one was open for 3% of the time, Pallas kernels for 40%

profile of v4, /device:TPU:3, one launch (start us, length us, event | category | flops | bytes accessed | tf_op | source)
XLA Modules:
  0.0 237.7 jit_solution(18267326846507126601)
XLA Ops:
  8.2 12.8 %shard_map.68 = (bf16[1536,3328]{1,0:T(8,128)(2,1)S(1)}, bf16[1536,3328]{1,0:T(8,128)(2,1)S(1)}) custom-call(s32[24,52]{1,0:T(8,128)S(1)} %select_reduce_fusion.slot_ref, f32[24,32,64,64]{3,2,1,0:T(8,128)} %blocks_ref.1), custom_call_target="tpu_custom_call" | custom-call | bytes 60000000 | tf_op jit(solution)/shard_map/pallas_call | solution.py:52
  26.3 8.5 %shard_map.69.own_ref = f32[1536,128]{1,0:T(8,128)S(1)} custom-call(bf16[1536,3328]{1,0:T(8,128)(2,1)S(1)} %get-tuple-element.42.hi_ref, bf16[1536,3328]{1,0:T(8,128)(2,1)S(1)} %get-tuple-element.43.lo_ref, f32[1536,128]{1,0:T(8,128)S(1)} %copy-done.18, f32[1536,128]{1,0:T(8,128)S(1)} %slice.46.own_ref.rest_0_, f32[1536,128]{1,0:T(8,128)} %collective-permute-done.1.after_ref), custom_call_target="tpu_custom_call" | custom-call | flops 5234491392 | bytes 20447232 | tf_op jit(solution)/shard_map/pallas_call | solution.py:99
  41.4 3.9 %copy-done.1 = bf16[1536,3328]{1,0:T(8,128)(2,1)S(1)} copy-done((bf16[1536,3328]{1,0:T(8,128)(2,1)S(1)}, bf16[1536,3328]{1,0:T(8,128)(2,1)}, u32[]{:S(2)}) %copy-start.1) | copy-done | bytes 10223640
  45.4 3.9 %copy-done.3 = bf16[1536,3328]{1,0:T(8,128)(2,1)S(1)} copy-done((bf16[1536,3328]{1,0:T(8,128)(2,1)S(1)}, bf16[1536,3328]{1,0:T(8,128)(2,1)}, u32[]{:S(2)}) %copy-start.3) | copy-done | bytes 10223640
  49.3 8.1 %shard_map.71.own_ref = f32[1536,128]{1,0:T(8,128)S(1)} custom-call(bf16[1536,3328]{1,0:T(8,128)(2,1)S(1)} %copy-done.1, bf16[1536,3328]{1,0:T(8,128)(2,1)S(1)} %copy-done.3, f32[1536,128]{1,0:T(8,128)} %collective-permute-done.4.before_ref, f32[1536,128]{1,0:T(8,128)S(1)} %get-tuple-element.86.own_ref.rest_0_, f32[1536,128]{1,0:T(8,128)} %collective-permute-done.5.after_ref), custom_call_target="tpu_custom_call" | custom-call | flops 5234491392 | bytes 20447232 | tf_op jit(solution)/shard_map/pallas_call | solution.py:99
  58.3 8.1 %shard_map.70.refs_0_ = f32[1536,128]{1,0:T(8,128)S(1)} custom-call(bf16[1536,3328]{1,0:T(8,128)(2,1)S(1)} %copy-done.1, bf16[1536,3328]{1,0:T(8,128)(2,1)S(1)} %copy-done.3, f32[1536,128]{1,0:T(8,128)} %collective-permute-done.2.before_ref, f32[1536,128]{1,0:T(8,128)S(1)} %shard_map.69.own_ref, f32[1536,128]{1,0:T(8,128)} %collective-permute-done.3.after_ref, ...), custom_call_target="tpu_custom_call" | custom-call | flops 5234491392 | bytes 20447232 | tf_op jit(solution)/shard_map/pallas_call | solution.py:99
  67.1 3.7 %collective-permute-done.8.before_ref = f32[1536,128]{1,0:T(8,128)} collective-permute-done((f32[1536,128]{1,0:T(8,128)S(1)}, f32[1536,128]{1,0:T(8,128)}, u32[]{:S(2)}, u32[]{:S(2)}) %collective-permute-start.8) | collective-permute-done | bytes 786464 | tf_op jit(solution)/shard_map/ppermute | solution.py:129
  71.5 3.5 %collective-permute-done.9.after_ref = f32[1536,128]{1,0:T(8,128)S(1)} collective-permute-done((f32[1536,128]{1,0:T(8,128)S(1)}, f32[1536,128]{1,0:T(8,128)S(1)}, u32[]{:S(2)}, u32[]{:S(2)}) %collective-permute-start.9) | collective-permute-done | bytes 786464 | tf_op jit(solution)/shard_map/ppermute | solution.py:129
  78.3 8.0 %shard_map.73.own_ref = f32[1536,128]{1,0:T(8,128)S(1)} custom-call(bf16[1536,3328]{1,0:T(8,128)(2,1)S(1)} %copy-done.1, bf16[1536,3328]{1,0:T(8,128)(2,1)S(1)} %copy-done.3, f32[1536,128]{1,0:T(8,128)} %collective-permute-done.8.before_ref, f32[1536,128]{1,0:T(8,128)S(1)} %get-tuple-element.87.own_ref.rest_0_, f32[1536,128]{1,0:T(8,128)S(1)} %collective-permute-done.9.after_ref), custom_call_target="tpu_custom_call" | custom-call | flops 5234491392 | bytes 20447232 | tf_op jit(solution)/shard_map/pallas_call | solution.py:99
  87.6 3.4 %collective-permute-start.10 = (f32[1536,128]{1,0:T(8,128)S(1)}, f32[1536,128]{1,0:T(8,128)S(1)}, u32[]{:S(2)}, u32[]{:S(2)}) collective-permute-start(f32[1536,128]{1,0:T(8,128)S(1)} %shard_map.73.own_ref), channel_id=1, source_target_pairs={{0,4},{4,8},{8,12},{12,16},{16,20},{20,24},{24,28},{28,0},{1,5},{5... | collective-permute-start | bytes 2359304 | tf_op jit(solution)/shard_map/ppermute | solution.py:129
  91.2 6.7 %shard_map.72.refs_0_ = f32[1536,128]{1,0:T(8,128)S(1)} custom-call(bf16[1536,3328]{1,0:T(8,128)(2,1)S(1)} %copy-done.1, bf16[1536,3328]{1,0:T(8,128)(2,1)S(1)} %copy-done.3, f32[1536,128]{1,0:T(8,128)S(1)} %collective-permute-done.6.before_ref, f32[1536,128]{1,0:T(8,128)S(1)} %shard_map.71.own_ref, f32[1536,128]{1,0:T(8,128)S(1)} %collective-permute-done.7.after_ref, ...), custom_call_target="tpu_custom_call" | custom-call | flops 5234491392 | bytes 20447232 | tf_op jit(solution)/shard_map/pallas_call | solution.py:99
  101.2 4.6 %collective-permute-start.18 = (f32[1536,128]{1,0:T(8,128)S(1)}, f32[1536,128]{1,0:T(8,128)S(1)}, u32[]{:S(2)}, u32[]{:S(2)}) collective-permute-start(f32[1536,128]{1,0:T(8,128)S(1)} %shard_map.72.refs_0_), channel_id=1, source_target_pairs={{3,2},{4,5},{11,10},{12,13},{19,18},{20,21},{27,26},{28,29}} | collective-permute-start | bytes 2359304 | tf_op jit(solution)/shard_map/ppermute | solution.py:275
  109.5 4.1 %shard_map.75 = f32[2,512,128]{2,1,0:T(8,128)} custom-call(s32[2]{0:T(128)S(1)} %pad_add_fusion.target_ref, bf16[4,128,1536]{2,1,0:T(8,128)(2,1)S(1)} %get-tuple-element.47.thi_ref, bf16[4,128,1536]{2,1,0:T(8,128)(2,1)S(1)} %get-tuple-element.48.tlo_ref, bf16[4,1536,128]{2,1,0:T(8,128)(2,1)S(1)} %get-tuple-element.49.refs_0_, ...), custom_call_target="tpu_custom_call" | custom-call | flops 1207959552 | bytes 8000000 | tf_op jit(solution)/shard_map/pallas_call | solution.py:180
  113.6 7.6 %shard_map.76.refs_0_ = f32[1536,128]{1,0:T(8,128)} custom-call(bf16[1536,3328]{1,0:T(8,128)(2,1)S(1)} %bitcast.21, bf16[1536,3328]{1,0:T(8,128)(2,1)S(1)} %bitcast.23, f32[1536,128]{1,0:T(8,128)S(1)} %collective-permute-done.10.before_ref, f32[1536,128]{1,0:T(8,128)S(1)} %shard_map.73.own_ref, f32[1536,128]{1,0:T(8,128)S(1)} %collective-permute-done.14.after_ref, ...), custom_call_target="tpu_custom_call" | custom-call | flops 5234491392 | bytes 20447232 | tf_op jit(solution)/shard_map/pallas_call | solution.py:99
  134.2 4.2 %shard_map.79 = f32[2,512,256]{2,1,0:T(8,128)} custom-call(s32[2]{0:T(128)S(1)} %pad_add_fusion.target_ref, bf16[4,128,1536]{2,1,0:T(8,128)(2,1)S(1)} %get-tuple-element.55.thi_ref, bf16[4,128,1536]{2,1,0:T(8,128)(2,1)S(1)} %get-tuple-element.56.tlo_ref, bf16[4,1536,128]{2,1,0:T(8,128)(2,1)S(1)} %get-tuple-element.49.refs_0_, ...), custom_call_target="tpu_custom_call" | custom-call | flops 2415919104 | bytes 8000000 | tf_op jit(solution)/shard_map/pallas_call | solution.py:180
  153.8 3.4 %shard_map.82 = f32[2,256,384]{2,1,0:T(8,128)S(1)} custom-call(s32[2]{0:T(128)S(1)} %pad_add_fusion.target_ref, bf16[4,128,1536]{2,1,0:T(8,128)(2,1)S(1)} %get-tuple-element.62.thi_ref, bf16[4,128,1536]{2,1,0:T(8,128)(2,1)S(1)} %get-tuple-element.63.tlo_ref, bf16[4,1536,128]{2,1,0:T(8,128)(2,1)S(1)} %get-tuple-element.49.refs_0_, ...), custom_call_target="tpu_custom_call" | custom-call | flops 1811939328 | bytes 8000000 | tf_op jit(solution)/shard_map/pallas_call | solution.py:180
  157.9 3.4 %shard_map.83 = f32[2,256,384]{2,1,0:T(8,128)S(1)} custom-call(s32[2]{0:T(128)S(1)} %pad_add_fusion.2.target_ref, bf16[4,128,1536]{2,1,0:T(8,128)(2,1)S(1)} %get-tuple-element.62.thi_ref, bf16[4,128,1536]{2,1,0:T(8,128)(2,1)S(1)} %get-tuple-element.63.tlo_ref, bf16[4,1536,128]{2,1,0:T(8,128)(2,1)S(1)} %get-tuple-element.49.refs_0_, ...), custom_call_target="tpu_custom_call" | custom-call | flops 1811939328 | bytes 8000000 | tf_op jit(solution)/shard_map/pallas_call | solution.py:180
  166.3 3.4 %shard_map.85.ours_a = f32[2,256,384]{2,1,0:T(8,128)S(1)} custom-call(s32[2]{0:T(128)S(1)} %pad_add_fusion.1.target_ref, bf16[4,128,1536]{2,1,0:T(8,128)(2,1)S(1)} %get-tuple-element.62.thi_ref, bf16[4,128,1536]{2,1,0:T(8,128)(2,1)S(1)} %get-tuple-element.63.tlo_ref, bf16[4,1536,128]{2,1,0:T(8,128)(2,1)S(1)} %get-tuple-element.49.refs_0_, ...), custom_call_target="tpu_custom_call" | custom-call | flops 1811939328 | bytes 8000000 | tf_op jit(solution)/shard_map/pallas_call | solution.py:180
  173.2 3.4 %shard_map.86.ours_b = f32[2,256,384]{2,1,0:T(8,128)S(1)} custom-call(s32[2]{0:T(128)S(1)} %pad_add_fusion.3.target_ref, bf16[4,128,1536]{2,1,0:T(8,128)(2,1)S(1)} %get-tuple-element.62.thi_ref, bf16[4,128,1536]{2,1,0:T(8,128)(2,1)S(1)} %get-tuple-element.63.tlo_ref, bf16[4,1536,128]{2,1,0:T(8,128)(2,1)S(1)} %get-tuple-element.49.refs_0_, ...), custom_call_target="tpu_custom_call" | custom-call | flops 1811939328 | bytes 8000000 | tf_op jit(solution)/shard_map/pallas_call | solution.py:180
  178.2 20.3 %collective-permute-done.27 = f32[128,384]{1,0:T(8,128)S(1)} collective-permute-done((f32[128,384]{1,0:T(8,128)S(1)}, f32[128,384]{1,0:T(8,128)S(1)}, u32[]{:S(2)}, u32[]{:S(2)}) %collective-permute-start.27) | collective-permute-done | bytes 196640 | tf_op jit(solution)/shard_map/ppermute | solution.py:275
  205.1 12.7 %collective-permute-done.36 = f32[128,384]{1,0:T(8,128)S(1)} collective-permute-done((f32[128,384]{1,0:T(8,128)S(1)}, f32[128,384]{1,0:T(8,128)S(1)}, u32[]{:S(2)}, u32[]{:S(2)}) %collective-permute-start.36) | collective-permute-done | bytes 196640 | tf_op jit(solution)/shard_map/ppermute | solution.py:275
  221.1 4.4 %collective-permute-start.37 = (f32[128,384]{1,0:T(8,128)S(1)}, f32[128,384]{1,0:T(8,128)S(1)}, u32[]{:S(2)}, u32[]{:S(2)}) collective-permute-start(f32[128,384]{1,0:T(8,128)S(1)} %add_add_fusion.own_ref), channel_id=1, source_target_pairs={{0,4},{1,5},{2,6},{3,7},{4,0},{5,1},{6,2},{7,3},{8,12},{9,13},{10,... | collective-permute-start | bytes 589832 | tf_op jit(solution)/shard_map/ppermute | solution.py:275
  225.5 3.7 %collective-permute-start.29 = (f32[128,128]{1,0:T(8,128)S(1)}, f32[128,128]{1,0:T(8,128)S(1)}, u32[]{:S(2)}, u32[]{:S(2)}) collective-permute-start(f32[128,128]{1,0:T(8,128)S(1)} %get-tuple-element.92), channel_id=1, source_target_pairs={{0,0},{1,8},{2,16},{3,24},{4,4},{5,12},{6,20},{7,28},{8,1},{9,9},{... | collective-permute-start | bytes 196616 | tf_op jit(solution)/shard_map/ppermute | solution.py:275
  229.3 6.6 %collective-permute-done.29.turn_ref = f32[128,128]{1,0:T(8,128)S(1)} collective-permute-done((f32[128,128]{1,0:T(8,128)S(1)}, f32[128,128]{1,0:T(8,128)S(1)}, u32[]{:S(2)}, u32[]{:S(2)}) %collective-permute-start.29) | collective-permute-done | bytes 65568 | tf_op jit(solution)/shard_map/ppermute | solution.py:275
  (167 shorter events, 83.7 us)
Async XLA Ops:
  3.7 20.9 %collective-permute-start.1 = (f32[1536,128]{1,0:T(8,128)S(1)}, f32[1536,128]{1,0:T(8,128)}, u32[]{:S(2)}, u32[]{:S(2)}) collective-permute-start(f32[1536,128]{1,0:T(8,128)S(1)} %slice.46.own_ref.rest_0_), channel_id=1, source_target_pairs={{4,0},{8,4},{12,8},{16,12},{20,16},{24,20},{28,24},{0,28},{5,1},{9... | collective-permute-start | bytes 2359304 | tf_op jit(solution)/shard_map/ppermute | solution.py:129
  5.5 32.2 %collective-permute-start.4 = (f32[1536,128]{1,0:T(8,128)S(1)}, f32[1536,128]{1,0:T(8,128)}, u32[]{:S(2)}, u32[]{:S(2)}) collective-permute-start(f32[1536,128]{1,0:T(8,128)S(1)} %get-tuple-element.86.own_ref.rest_0_), channel_id=1, source_target_pairs={{0,4},{4,8},{8,12},{12,16},{16,20},{20,24},{24,28},{28,0},{1,5},{5... | collective-permute-start | bytes 2359304 | tf_op jit(solution)/shard_map/ppermute | solution.py:129
  8.2 33.3 %collective-permute-start.5 = (f32[1536,128]{1,0:T(8,128)S(1)}, f32[1536,128]{1,0:T(8,128)}, u32[]{:S(2)}, u32[]{:S(2)}) collective-permute-start(f32[1536,128]{1,0:T(8,128)S(1)} %get-tuple-element.86.own_ref.rest_0_), channel_id=1, source_target_pairs={{4,0},{8,4},{12,8},{16,12},{20,16},{24,20},{28,24},{0,28},{5,1},{9... | collective-permute-start | bytes 2359304 | tf_op jit(solution)/shard_map/ppermute | solution.py:129
  34.8 22.6 %collective-permute-start.2 = (f32[1536,128]{1,0:T(8,128)S(1)}, f32[1536,128]{1,0:T(8,128)}, u32[]{:S(2)}, u32[]{:S(2)}) collective-permute-start(f32[1536,128]{1,0:T(8,128)S(1)} %shard_map.69.own_ref), channel_id=1, source_target_pairs={{0,4},{4,8},{8,12},{12,16},{16,20},{20,24},{24,28},{28,0},{1,5},{5... | collective-permute-start | bytes 2359304 | tf_op jit(solution)/shard_map/ppermute | solution.py:129
  35.0 23.3 %collective-permute-start.3 = (f32[1536,128]{1,0:T(8,128)S(1)}, f32[1536,128]{1,0:T(8,128)}, u32[]{:S(2)}, u32[]{:S(2)}) collective-permute-start(f32[1536,128]{1,0:T(8,128)S(1)} %shard_map.69.own_ref), channel_id=1, source_target_pairs={{4,0},{8,4},{12,8},{16,12},{20,16},{24,20},{28,24},{0,28},{5,1},{9... | collective-permute-start | bytes 2359304 | tf_op jit(solution)/shard_map/ppermute | solution.py:129
  35.4 35.4 %collective-permute-start.8 = (f32[1536,128]{1,0:T(8,128)S(1)}, f32[1536,128]{1,0:T(8,128)}, u32[]{:S(2)}, u32[]{:S(2)}) collective-permute-start(f32[1536,128]{1,0:T(8,128)S(1)} %get-tuple-element.87.own_ref.rest_0_), channel_id=1, source_target_pairs={{0,4},{4,8},{8,12},{12,16},{16,20},{20,24},{24,28},{28,0},{1,5},{5... | collective-permute-start | bytes 2359304 | tf_op jit(solution)/shard_map/ppermute | solution.py:129
  37.6 37.4 %collective-permute-start.9 = (f32[1536,128]{1,0:T(8,128)S(1)}, f32[1536,128]{1,0:T(8,128)S(1)}, u32[]{:S(2)}, u32[]{:S(2)}) collective-permute-start(f32[1536,128]{1,0:T(8,128)S(1)} %get-tuple-element.87.own_ref.rest_0_), channel_id=1, source_target_pairs={{4,0},{8,4},{12,8},{16,12},{20,16},{24,20},{28,24},{0,28},{5,1},{9... | collective-permute-start | bytes 2359304 | tf_op jit(solution)/shard_map/ppermute | solution.py:129
  57.4 30.3 %collective-permute-start.6 = (f32[1536,128]{1,0:T(8,128)S(1)}, f32[1536,128]{1,0:T(8,128)S(1)}, u32[]{:S(2)}, u32[]{:S(2)}) collective-permute-start(f32[1536,128]{1,0:T(8,128)S(1)} %shard_map.71.own_ref), channel_id=1, source_target_pairs={{0,4},{4,8},{8,12},{12,16},{16,20},{20,24},{24,28},{28,0},{1,5},{5... | collective-permute-start | bytes 2359304 | tf_op jit(solution)/shard_map/ppermute | solution.py:129
  57.4 33.6 %collective-permute-start.7 = (f32[1536,128]{1,0:T(8,128)S(1)}, f32[1536,128]{1,0:T(8,128)S(1)}, u32[]{:S(2)}, u32[]{:S(2)}) collective-permute-start(f32[1536,128]{1,0:T(8,128)S(1)} %shard_map.71.own_ref), channel_id=1, source_target_pairs={{4,0},{8,4},{12,8},{16,12},{20,16},{24,20},{28,24},{0,28},{5,1},{9... | collective-permute-start | bytes 2359304 | tf_op jit(solution)/shard_map/ppermute | solution.py:129
  66.4 31.5 %collective-permute-start.11 = (f32[1536,128]{1,0:T(8,128)S(1)}, f32[1536,128]{1,0:T(8,128)S(1)}, u32[]{:S(2)}, u32[]{:S(2)}) collective-permute-start(f32[1536,128]{1,0:T(8,128)S(1)} %shard_map.70.refs_0_), channel_id=1, source_target_pairs={{0,2},{7,5},{8,10},{15,13},{16,18},{23,21},{24,26},{31,29}} | collective-permute-start | bytes 2359304 | tf_op jit(solution)/shard_map/ppermute | solution.py:275
  70.8 27.9 %collective-permute-start.12 = (f32[1536,128]{1,0:T(8,128)S(1)}, f32[1536,128]{1,0:T(8,128)S(1)}, u32[]{:S(2)}, u32[]{:S(2)}) collective-permute-start(f32[1536,128]{1,0:T(8,128)S(1)} %shard_map.70.refs_0_), channel_id=1, source_target_pairs={{1,2},{6,5},{9,10},{14,13},{17,18},{22,21},{25,26},{30,29}} | collective-permute-start | bytes 2359304 | tf_op jit(solution)/shard_map/ppermute | solution.py:275
  75.0 25.2 %collective-permute-start.13 = (f32[1536,128]{1,0:T(8,128)S(1)}, f32[1536,128]{1,0:T(8,128)S(1)}, u32[]{:S(2)}, u32[]{:S(2)}) collective-permute-start(f32[1536,128]{1,0:T(8,128)S(1)} %shard_map.70.refs_0_), channel_id=1, source_target_pairs={{3,2},{4,5},{11,10},{12,13},{19,18},{20,21},{27,26},{28,29}} | collective-permute-start | bytes 2359304 | tf_op jit(solution)/shard_map/ppermute | solution.py:275
  87.6 25.9 %collective-permute-start.10 = (f32[1536,128]{1,0:T(8,128)S(1)}, f32[1536,128]{1,0:T(8,128)S(1)}, u32[]{:S(2)}, u32[]{:S(2)}) collective-permute-start(f32[1536,128]{1,0:T(8,128)S(1)} %shard_map.73.own_ref), channel_id=1, source_target_pairs={{0,4},{4,8},{8,12},{12,16},{16,20},{20,24},{24,28},{28,0},{1,5},{5... | collective-permute-start | bytes 2359304 | tf_op jit(solution)/shard_map/ppermute | solution.py:129
  91.0 22.5 %collective-permute-start.14 = (f32[1536,128]{1,0:T(8,128)S(1)}, f32[1536,128]{1,0:T(8,128)S(1)}, u32[]{:S(2)}, u32[]{:S(2)}) collective-permute-start(f32[1536,128]{1,0:T(8,128)S(1)} %shard_map.73.own_ref), channel_id=1, source_target_pairs={{4,0},{8,4},{12,8},{16,12},{20,16},{24,20},{28,24},{0,28},{5,1},{9... | collective-permute-start | bytes 2359304 | tf_op jit(solution)/shard_map/ppermute | solution.py:129
  97.9 32.6 %collective-permute-start.16 = (f32[1536,128]{1,0:T(8,128)S(1)}, f32[1536,128]{1,0:T(8,128)S(1)}, u32[]{:S(2)}, u32[]{:S(2)}) collective-permute-start(f32[1536,128]{1,0:T(8,128)S(1)} %shard_map.72.refs_0_), channel_id=1, source_target_pairs={{0,2},{7,5},{8,10},{15,13},{16,18},{23,21},{24,26},{31,29}} | collective-permute-start | bytes 2359304 | tf_op jit(solution)/shard_map/ppermute | solution.py:275
  99.6 33.2 %collective-permute-start.17 = (f32[1536,128]{1,0:T(8,128)S(1)}, f32[1536,128]{1,0:T(8,128)S(1)}, u32[]{:S(2)}, u32[]{:S(2)}) collective-permute-start(f32[1536,128]{1,0:T(8,128)S(1)} %shard_map.72.refs_0_), channel_id=1, source_target_pairs={{1,2},{6,5},{9,10},{14,13},{17,18},{22,21},{25,26},{30,29}} | collective-permute-start | bytes 2359304 | tf_op jit(solution)/shard_map/ppermute | solution.py:275
  101.2 31.6 %collective-permute-start.18 = (f32[1536,128]{1,0:T(8,128)S(1)}, f32[1536,128]{1,0:T(8,128)S(1)}, u32[]{:S(2)}, u32[]{:S(2)}) collective-permute-start(f32[1536,128]{1,0:T(8,128)S(1)} %shard_map.72.refs_0_), channel_id=1, source_target_pairs={{3,2},{4,5},{11,10},{12,13},{19,18},{20,21},{27,26},{28,29}} | collective-permute-start | bytes 2359304 | tf_op jit(solution)/shard_map/ppermute | solution.py:275
  121.3 29.7 %collective-permute-start.21 = (f32[1536,128]{1,0:T(8,128)}, f32[1536,128]{1,0:T(8,128)}, u32[]{:S(2)}, u32[]{:S(2)}) collective-permute-start(f32[1536,128]{1,0:T(8,128)} %shard_map.76.refs_0_), channel_id=1, source_target_pairs={{0,2},{7,5},{8,10},{15,13},{16,18},{23,21},{24,26},{31,29}} | collective-permute-start | bytes 2359304 | tf_op jit(solution)/shard_map/ppermute | solution.py:275
  122.8 28.1 %collective-permute-start.22 = (f32[1536,128]{1,0:T(8,128)}, f32[1536,128]{1,0:T(8,128)}, u32[]{:S(2)}, u32[]{:S(2)}) collective-permute-start(f32[1536,128]{1,0:T(8,128)} %shard_map.76.refs_0_), channel_id=1, source_target_pairs={{1,2},{6,5},{9,10},{14,13},{17,18},{22,21},{25,26},{30,29}} | collective-permute-start | bytes 2359304 | tf_op jit(solution)/shard_map/ppermute | solution.py:275
  130.6 20.4 %collective-permute-start.23 = (f32[1536,128]{1,0:T(8,128)}, f32[1536,128]{1,0:T(8,128)}, u32[]{:S(2)}, u32[]{:S(2)}) collective-permute-start(f32[1536,128]{1,0:T(8,128)} %shard_map.76.refs_0_), channel_id=1, source_target_pairs={{3,2},{4,5},{11,10},{12,13},{19,18},{20,21},{27,26},{28,29}} | collective-permute-start | bytes 2359304 | tf_op jit(solution)/shard_map/ppermute | solution.py:275
  138.5 23.7 %collective-permute-start.19 = (f32[2,512,256]{2,1,0:T(8,128)}, f32[2,512,256]{2,1,0:T(8,128)}, u32[]{:S(2)}, u32[]{:S(2)}) collective-permute-start(f32[2,512,256]{2,1,0:T(8,128)} %shard_map.79), channel_id=1, source_target_pairs={{2,18},{5,21},{10,26},{13,29},{18,2},{21,5},{26,10},{29,13}} | collective-permute-start | bytes 3145736 | tf_op jit(solution)/shard_map/ppermute | solution.py:275
  171.9 26.6 %collective-permute-start.27 = (f32[128,384]{1,0:T(8,128)S(1)}, f32[128,384]{1,0:T(8,128)S(1)}, u32[]{:S(2)}, u32[]{:S(2)}) collective-permute-start(f32[128,384]{1,0:T(8,128)S(1)} %get-tuple-element.71), channel_id=1, source_target_pairs={{2,3},{5,4},{10,11},{13,12},{18,19},{21,20},{26,27},{29,28}} | collective-permute-start | bytes 589832 | tf_op jit(solution)/shard_map/ppermute | solution.py:275
  176.7 25.0 %collective-permute-start.32 = (f32[256,384]{1,0:T(8,128)S(1)}, f32[256,384]{1,0:T(8,128)S(1)}, u32[]{:S(2)}, u32[]{:S(2)}) collective-permute-start(f32[256,384]{1,0:T(8,128)S(1)} %get-tuple-element.75), channel_id=1, source_target_pairs={{2,10},{5,13},{10,2},{13,5},{18,26},{21,29},{26,18},{29,21}} | collective-permute-start | bytes 1179656 | tf_op jit(solution)/shard_map/ppermute | solution.py:275
  177.4 24.3 %collective-permute-start.33 = (f32[256,384]{1,0:T(8,128)S(1)}, f32[256,384]{1,0:T(8,128)S(1)}, u32[]{:S(2)}, u32[]{:S(2)}) collective-permute-start(f32[256,384]{1,0:T(8,128)S(1)} %get-tuple-element.77), channel_id=1, source_target_pairs={{2,18},{5,21},{10,26},{13,29},{18,2},{21,5},{26,10},{29,13}} | collective-permute-start | bytes 1179656 | tf_op jit(solution)/shard_map/ppermute | solution.py:275
  (48 other events, 530.7 us)

commit v5 on v4

--- a/solution.py
+++ b/solution.py
@@ -156,43 +156,64 @@
     )(bands, *parts)
 
 
-def product_kernel(target_ref, thi_ref, tlo_ref, *refs):
-    ins, out_ref = refs[:-1], refs[-1]
-    columns = len(ins) // 2
-    count, width, rows = thi_ref.shape
-    thi = thi_ref[...].reshape(count * width, rows)
-    tlo = tlo_ref[...].reshape(count * width, rows)
-    his = jnp.concatenate([ref[0] for ref in ins[:columns]], axis=1)
-    los = jnp.concatenate([ref[0] for ref in ins[columns:]], axis=1)
-    small = jnp.dot(thi, los, preferred_element_type=jnp.float32)
-    small += jnp.dot(tlo, his, preferred_element_type=jnp.float32)
-    out_ref[0] = small + jnp.dot(thi, his, preferred_element_type=jnp.float32)
-
-
-def products(targets, chunks, half=None):
-    _, _, thi, tlo = chunks[-1]
-    four, width, rows = thi.shape
-    count = four if half is None else four // 2
-    place = half or 0
-    size = sum(chunk[0].shape[2] for chunk in chunks)
-    left = pl.BlockSpec((count, width, rows), lambda g, t: (place, 0, 0))
-    right = [pl.BlockSpec((1, rows, chunk[0].shape[2]), lambda g, t: (t[g], 0, 0)) for chunk in chunks]
-    return pl.pallas_call(
-        product_kernel,
+def product_kernel(target_ref, *refs, shapes):
+    *ins, out_a, out_b = refs
+    step = pl.program_id(0)
+    parts = []
+    for columns in shapes:
+        left, ins = ins[:2], ins[2:]
+        right, ins = ins[: 2 * columns], ins[2 * columns :]
+        count, width, rows = left[0].shape
+        thi, tlo = (ref[...].reshape(count * width, rows) for ref in left)
+        his = jnp.concatenate([ref[0] for ref in right[:columns]], axis=1)
+        los = jnp.concatenate([ref[0] for ref in right[columns:]], axis=1)
+        small = jnp.dot(thi, los, preferred_element_type=jnp.float32)
+        small += jnp.dot(tlo, his, preferred_element_type=jnp.float32)
+        parts.append(small + jnp.dot(thi, his, preferred_element_type=jnp.float32))
+    total = jnp.concatenate(parts, axis=1)
+
+    @pl.when(step < 2)
+    def _():
+        out_a[0] = total
+
+    @pl.when(step >= 2)
+    def _():
+        out_b[0] = total
+
+
+def products(targets, chunks, lines):
+    ins, specs, shapes, size, flops = [], [], [], 0, 0
+    for line in lines:
+        _, _, thi, tlo = chunks[line]
+        four, width, rows = thi.shape
+        ins += [thi, tlo]
+        specs += [pl.BlockSpec((four // 2, width, rows), lambda g, t: (g // 2, 0, 0))] * 2
+        for part in (0, 1):
+            for c in range(line + 1):
+                x = chunks[c][part]
+                ins.append(x)
+                specs.append(pl.BlockSpec((1, rows, x.shape[2]), lambda g, t: (t[g], 0, 0)))
+        wide = sum(chunks[c][0].shape[2] for c in range(line + 1))
+        shapes.append(line + 1)
+        size += wide
+        flops += 12 * four * width * rows * wide
+    tall = four // 2 * width
+    shape = jax.ShapeDtypeStruct((2, tall, size), jnp.float32)
+    return pl.pallas_call(
+        functools.partial(product_kernel, shapes=shapes),
         grid_spec=pltpu.PrefetchScalarGridSpec(
             num_scalar_prefetch=1,
-            grid=(targets.shape[0],),
-            in_specs=[left, left] + right + right,
-            out_specs=pl.BlockSpec((1, count * width, size), lambda g, t: (g, 0, 0)),
+            grid=(4,),
+            in_specs=specs,
+            out_specs=[
+                pl.BlockSpec((1, tall, size), lambda g, t: (jnp.minimum(g, 1), 0, 0)),
+                pl.BlockSpec((1, tall, size), lambda g, t: (jnp.maximum(g - 2, 0), 0, 0)),
+            ],
         ),
-        out_shape=jax.ShapeDtypeStruct((targets.shape[0], count * width, size), jnp.float32),
+        out_shape=[shape, shape],
         compiler_params=pltpu.CompilerParams(vmem_limit_bytes=24 * MIB),
-        cost_estimate=pl.CostEstimate(
-            flops=targets.shape[0] * 6 * count * width * rows * size,
-            bytes_accessed=8_000_000,
-            transcendentals=0,
-        ),
-    )(targets, thi, tlo, *[c[0] for c in chunks], *[c[1] for c in chunks])
+        cost_estimate=pl.CostEstimate(flops=flops, bytes_accessed=8_000_000, transcendentals=0),
+    )(targets, *ins)
 
 
 def middle_kernel(got_a, ours_a, got_b, ours_b, send_a, keep_a, send_b, keep_b):
@@ -215,20 +236,20 @@
 
 
 def pick_kernel(goal_ref, *refs):
-    ins, outs, sums = refs[:-5], refs[-5:-1], refs[-1]
-    half = len(ins) // 2
-    rows = sums.shape[1]
-    for place in range(4):
-        keep, got = (ins[0], ins[1]) if half == 1 or place < 2 else (ins[2], ins[3])
-        start = (place if half == 1 else place % 2) * rows
-        sums[place] = keep[pl.ds(start, rows), :] + got[pl.ds(start, rows), :]
+    ins, outs, sums = refs[:8], refs[8:12], refs[12]
+    rows = sums.shape[1] // 2
+    for batch in range(2):
+        for band in range(4):
+            keep, got = ins[4 * batch + band // 2 * 2 : 4 * batch + band // 2 * 2 + 2]
+            there = pl.ds(band % 2 * rows, rows)
+            sums[band, pl.ds(batch * rows, rows), :] = keep[there, :] + got[there, :]
     for k, out in enumerate(outs):
         out[...] = sums[goal_ref[k]]
     outs[3][...] = jnp.where(goal_ref[4] > 0, outs[3][...], 0.0)
 
 
 def pick(goals, *parts):
-    rows, size = parts[0].shape[0] * len(parts) // 8, parts[0].shape[1]
+    rows, size = parts[0].shape
     shape = jax.ShapeDtypeStruct((rows, size), jnp.float32)
     vmem = pl.BlockSpec(memory_space=pltpu.VMEM)
     return pl.pallas_call(
@@ -242,20 +263,20 @@
     )(goals, *parts)
 
 
-def assemble_kernel(core_ref, e0_ref, e1_ref, turn_ref, own_ref, other_ref, ta_ref, tb_ref, out_ref, *, scale):
-    w = e0_ref.shape[0]
-    low = own_ref[...] + other_ref[...]
-    turned = (ta_ref[...] + tb_ref[...]).T
-    first = jnp.concatenate([e0_ref[...], turn_ref[...].T, turned[:w]], axis=1)
-    second = jnp.concatenate([e1_ref[...], turned[w:]], axis=1)
+def assemble_kernel(core_ref, piece_ref, turn_e_ref, turn_l_ref, out_ref, *, scale):
+    w = turn_e_ref.shape[0]
+    early, last = piece_ref[:w, :], piece_ref[w:, :]
+    turned = turn_l_ref[...].T
+    first = jnp.concatenate([early[:, :w], turn_e_ref[...].T, turned[:w]], axis=1)
+    second = jnp.concatenate([early[:, w:], turned[w:]], axis=1)
     half = out_ref.shape[1]
     is_first = core_ref[0] == 0
-    for k, x in enumerate((first, second, low)):
+    for k, x in enumerate((first, second, last)):
         out_ref[pl.ds(k * w, w), :] = jnp.where(is_first, x[:, :half], x[:, half:]) * scale
 
 
 def assemble(core, parts, order):
-    w = parts[0].shape[0]
+    w = parts[0].shape[0] // 2
     vmem = pl.BlockSpec(memory_space=pltpu.VMEM)
     return pl.pallas_call(
         functools.partial(assemble_kernel, scale=1.0 / order),
@@ -264,7 +285,7 @@
         out_shape=jax.ShapeDtypeStruct((3 * w, 3 * w // 2), jnp.float32),
         compiler_params=pltpu.CompilerParams(vmem_limit_bytes=12 * MIB),
         cost_estimate=pl.CostEstimate(flops=0, bytes_accessed=2_000_000, transcendentals=0),
-    )(core[None], *parts)
+    )(core, *parts)
 
 
 def linear(chip, core, z):
@@ -299,7 +320,7 @@
 EVERY = [(q, c, z) for q in range(4) for c in range(2) for z in range(4)]
 SWAP = [(linear(q, c, z), linear(q, 1 - c, z)) for q, c, z in EVERY]
 TURN = [(linear(q, c, z), linear(z, c, q)) for q, c, z in EVERY]
-TURN_UP = [[(linear(q, c, z), linear(z, 1, q)) for q, c, z in EVERY if c == core] for core in range(2)]
+TURN_UP = [pair for pair in TURN if pair[0] // 4 % 2 == 1]
 
 
 def simple_gram(filtered):
@@ -324,26 +345,25 @@
     return filtered, simple_gram(filtered) / order
 
 
-def by_symmetry(hi, lo, old, order):
+def index_tables():
+    orb, z = lax.axis_index("orb"), lax.axis_index("band")
+    chip, core = orb >> 1, orb & 1
+    bands = jnp.stack([b + core * (3 - 2 * b) for b in (2, 0, 1, 3)])
+    holder = (z == 2 - core).astype(jnp.int32)
+    goals = jnp.stack([k + core * (3 - 2 * k) for k in (0, 1, 3)] + [z, holder])
+    far = jnp.stack([chip ^ 2, chip ^ 3, chip ^ 1, chip ^ 3])
+    near = jnp.stack([chip, chip ^ 1, chip, chip ^ 2])
+    return bands, goals, far, near, core[None]
+
+
+def by_symmetry(hi, lo, old, order, tables):
     def one(x, halo, v=None):
         return apply_step(hi, lo, halo[0], x, halo[1], v)
 
-    orb, z = lax.axis_index("orb"), lax.axis_index("band")
-    chip, core = orb // 2, orb % 2
-    bands = jnp.asarray([[2, 0, 1, 3], [1, 3, 2, 0]], jnp.int32)[core]
-    holder = (z == 2 - core).astype(jnp.int32)
-    goals = jnp.stack([jnp.where(core == 0, k, 3 - k) for k in (0, 1, 3)] + [z, holder]).astype(jnp.int32)
-    far_y = jnp.stack([chip ^ 2, chip ^ 3])
-    far_x = jnp.stack([chip ^ 1, chip ^ 3])
-    near_y = jnp.stack([chip, chip ^ 1])
-    near_x = jnp.stack([chip, chip ^ 2])
-
-    def deliver(parts):
-        moved = pick(goals, *parts)
-        piece = moved[3]
-        for k, x in zip((0, 1, 3), moved):
-            piece = piece + send(x, mirrored([(2, k)]))
-        return piece
+    bands, goals, far, near, core = tables
+
+    def across(parts, order):
+        return [send(x, over_chips(flip)) for x, flip in zip(parts, order)]
 
     v0, v1, v2 = old
     hv = [neighbours(x) for x in old]
@@ -358,56 +378,48 @@
     g1 = one(after_that(f1, g0), hf1, v1)
     z1 = gather_bands(g1)
     chunks = [prep(bands, [after_that(z0[0], g1)] + z0[1:])]
-    far0 = products(far_y, chunks)
-    got0 = send(far0, over_chips(2))
-    g2 = one(after_that(f2, far0), hf2, v2)
+    g2 = one(after_that(f2, chunks[0][0]), hf2, v2)
     z2 = gather_bands(g2)
-    ours0 = products(after_that(near_y, g2), chunks)
-    filtered = jnp.concatenate([g0, g1, after_that(g2, ours0)], axis=1)
-    chunks.append(prep(bands, [after_that(z1[0], filtered)] + z1[1:]))
-    far1 = products(far_y, chunks)
-    got1 = send(far1, over_chips(2))
-    ours1 = products(after_that(near_y, far1), chunks)
-    last0 = send(after_that(got0, ours1)[1] + ours0[1], over_chips(1))
-    chunks.append(prep(bands, [after_that(z2[0], ours1)] + z2[1:]))
-    far2y = products(far_y, chunks, 0)
-    got2y = send(far2y, over_chips(2))
-    far2x = products(after_that(far_x, far2y), chunks, 1)
-    got2x = send(far2x, over_chips(1))
-    last1 = send(after_that(got1, far2x)[1] + ours1[1], over_chips(1))
-    ours2y = products(after_that(near_y, far2x), chunks, 0)
-    ours2x = products(after_that(near_x, ours2y), chunks, 1)
-    send2y, keep2y, send2x, keep2x = middle(got2y, ours2y, got2x, ours2x)
-    last2y = send(send2y, over_chips(1))
-    last2x = send(send2x, over_chips(2))
-    early = deliver(
-        [
-            jnp.concatenate([got0[0] + ours0[0], got1[0] + ours1[0]], axis=1),
-            jnp.concatenate([last0, last1], axis=1),
-        ]
-    )
-    early = early + send(early, SWAP)
+    chunks.append(prep(bands, [after_that(z1[0], g2)] + z1[1:]))
+    theirs_e = products(far, chunks, (0, 1))
+    got_e = across(theirs_e, (2, 1))
+    ours_e = products(after_that(near, theirs_e[0]), chunks, (0, 1))
+    chunks.append(prep(bands, [after_that(z2[0], ours_e[0])] + z2[1:]))
+    theirs_l = products(far, chunks, (2,))
+    got_l = across(theirs_l, (2, 1))
+    got_e[0] = after_that(got_e[0], theirs_l[0])
+    send_ey, keep_ey, send_ex, keep_ex = middle(got_e[0], ours_e[0], got_e[1], ours_e[1])
+    last_e = across((send_ey, send_ex), (1, 2))
+    ours_l = products(after_that(near, keep_ey), chunks, (2,))
+    send_ly, keep_ly, send_lx, keep_lx = middle(got_l[0], ours_l[0], got_l[1], ours_l[1])
+    last_l = across((send_ly, send_lx), (1, 2))
+    filtered = jnp.concatenate([g0, g1, after_that(g2, keep_ly)], axis=1)
+    moved = pick(goals, keep_ey, last_e[0], keep_ex, last_e[1], keep_ly, last_l[0], keep_lx, last_l[1])
+    piece = moved[3]
+    for k, x in zip((0, 1, 3), moved):
+        piece = piece + send(x, mirrored([(2, k)]))
+    piece = piece + send(piece, SWAP)
     w = v0.shape[1]
-    early_turn = send(early[:, w : 2 * w], TURN)
-    piece = deliver([keep2y, last2y, keep2x, last2x])
-    other = send(piece, SWAP)
-    turned = [send(piece[:, : 2 * w], TURN_UP[k]) for k in (0, 1)]
-    gram = assemble(
-        core, [early[:, :w], early[:, w:], early_turn, piece, other, *turned], order
-    )
-    return filtered, gram
+    turn_e = send(piece[:w, w : 2 * w], TURN)
+    turn_l = send(piece[w:, : 2 * w], TURN_UP)
+    return filtered, assemble(core, [piece, turn_e, turn_l], order)
 
 
 def body(blocks, columns, counts, vectors, symmetric):
     rows, width = vectors.shape
     order = rows * lax.axis_size("orb")
     slot_of = slot_table(columns, counts)
-    hi, lo = densify(slot_of, blocks)
-    later = after_that(vectors, slot_of)
+    later = vectors
+    if symmetric:
+        tables = index_tables()
+        slot_of, tables, later = lax.optimization_barrier((slot_of, tables, vectors))
     old = [
         (later if c else vectors)[:, c : min(c + LANES, width)] for c in range(0, width, LANES)
     ]
-    return (by_symmetry if symmetric else in_turn)(hi, lo, old, order)
+    hi, lo = densify(slot_of, blocks)
+    if symmetric:
+        return by_symmetry(hi, lo, old, order, tables)
+    return in_turn(hi, lo, old, order)
 
 
 def solution(mesh):

time: 240 us -> 211 us (0.88)
  local copies, waits for them, and re-layouts: 23.9 us -> 3.66 us
  waiting for transfers between devices: 54.9 us -> 71.4 us
  Pallas kernels: 96 us -> 84.3 us
  starting transfers between devices: 55.4 us -> 48 us
  other arithmetic: 6.12 us -> 2.21 us
    unnamed x65 -> x5, local copies, waits for them, and re-layouts: 21.1 us -> 0.87 us
    ppermute x12, waiting for transfers between devices: 14.6 us -> 32.3 us  [neighbours(): return (lax.ppermute(x, 'orb', up), lax.ppermute(x, 'orb', down))]
    ppermute x28 -> x23, starting transfers between devices: 43.4 us -> 34.9 us  [send(): return lax.ppermute(x, ('orb', 'band'), pairs)]
    pallas_call x6, Pallas kernels: 47.2 us -> 41 us  [apply_step(): pl.pallas_call(functools.partial(apply_kernel, second=second), in_specs=[...]
    pallas_call x8 -> x4, Pallas kernels: 28.5 us -> 24.9 us  [products(): pl.pallas_call(functools.partial(product_kernel, shapes=shapes), grid_spe...]
    add x5 -> x2, other arithmetic: 2.55 us -> 0.11 us  [the longest x1 0.07 us: by_symmetry(): piece = piece + send(x, mirrored([(2, k)]))]
    ppermute x28 -> x23, waiting for transfers between devices: 40.3 us -> 39.1 us  [send(): return lax.ppermute(x, ('orb', 'band'), pairs)]
  transfers between devices with their start and end apart: 40 -> 35, of which waited for: 10 -> 13; matrix products, arithmetic and copies ran while one was open for 3% -> 2% of each run, Pallas kernels for 40% -> 39%
where the time goes in v5:
time: 211 us
  Pallas kernels  84.3 us (40%)
  waiting for transfers between devices  71.4 us (34%)
  starting transfers between devices  48 us (23%)
  local copies, waits for them, and re-layouts  3.66 us (2%)
  other arithmetic  2.21 us (1%)
    pallas_call x6, Pallas kernels, apply_step(): pl.pallas_call(functools.partial(apply_kernel, second=second), in_specs=[...  41 us
    ppermute x23, waiting for transfers between devices, send(): return lax.ppermute(x, ('orb', 'band'), pairs)  39.1 us
    ppermute x23, starting transfers between devices, send(): return lax.ppermute(x, ('orb', 'band'), pairs)  34.9 us
    ppermute x12, waiting for transfers between devices, neighbours(): return (lax.ppermute(x, 'orb', up), lax.ppermute(x, 'orb', down))  32.3 us
    pallas_call x4, Pallas kernels, products(): pl.pallas_call(functools.partial(product_kernel, shapes=shapes), grid_spe...  24.9 us
    ppermute x12, starting transfers between devices, neighbours(): return (lax.ppermute(x, 'orb', up), lax.ppermute(x, 'orb', down))  13 us
    pallas_call x1, Pallas kernels, densify(): pl.pallas_call(functools.partial(densify_kernel, spread=spread, reach=row...  12.8 us
    pallas_call x3, Pallas kernels, prep(): pl.pallas_call(prep_kernel, in_specs=[pl.BlockSpec(memory_space=pltpu.SME...  4.28 us
  transfers between devices with their start and end apart: 35, of which 13 were waited for; matrix products, arithmetic and copies ran while one was open for 2% of the time, Pallas kernels for 39%

profile of v5, /device:TPU:3, one launch (start us, length us, event | category | flops | bytes accessed | tf_op | source)
XLA Modules:
  0.0 210.7 jit_solution(694823529858682097)
XLA Ops:
  8.4 12.8 %shard_map.59 = (bf16[1536,3328]{1,0:T(8,128)(2,1)S(1)}, bf16[1536,3328]{1,0:T(8,128)(2,1)S(1)}) custom-call(s32[24,52]{1,0:T(8,128)S(1)} %select_reduce_fusion.slot_ref, f32[24,32,64,64]{3,2,1,0:T(8,128)} %blocks_ref.1), custom_call_target="tpu_custom_call" | custom-call | bytes 60000000 | tf_op jit(solution)/shard_map/pallas_call | solution.py:52
  21.2 3.3 %collective-permute-done.1.after_ref = f32[1536,128]{1,0:T(8,128)S(1)} collective-permute-done((f32[1536,128]{1,0:T(8,128)S(1)}, f32[1536,128]{1,0:T(8,128)S(1)}, u32[]{:S(2)}, u32[]{:S(2)}) %collective-permute-start.1) | collective-permute-done | bytes 786464 | tf_op jit(solution)/shard_map/ppermute | solution.py:129
  24.5 6.8 %shard_map.60.own_ref = f32[1536,128]{1,0:T(8,128)S(1)} custom-call(bf16[1536,3328]{1,0:T(8,128)(2,1)S(1)} %get-tuple-element.53.hi_ref, bf16[1536,3328]{1,0:T(8,128)(2,1)S(1)} %get-tuple-element.54.lo_ref, f32[1536,128]{1,0:T(8,128)S(1)} %collective-permute-done.before_ref, f32[1536,128]{1,0:T(8,128)S(1)} %slice.15.own_ref.rest_0_, ...), custom_call_target="tpu_custom_call" | custom-call | flops 5234491392 | bytes 20447232 | tf_op jit(solution)/shard_map/pallas_call | solution.py:99
  38.2 3.1 %collective-permute-done.5.after_ref = f32[1536,128]{1,0:T(8,128)S(1)} collective-permute-done((f32[1536,128]{1,0:T(8,128)S(1)}, f32[1536,128]{1,0:T(8,128)S(1)}, u32[]{:S(2)}, u32[]{:S(2)}) %collective-permute-start.5) | collective-permute-done | bytes 786464 | tf_op jit(solution)/shard_map/ppermute | solution.py:129
  41.3 6.8 %shard_map.62.own_ref = f32[1536,128]{1,0:T(8,128)S(1)} custom-call(bf16[1536,3328]{1,0:T(8,128)(2,1)S(1)} %get-tuple-element.53.hi_ref, bf16[1536,3328]{1,0:T(8,128)(2,1)S(1)} %get-tuple-element.54.lo_ref, f32[1536,128]{1,0:T(8,128)S(1)} %collective-permute-done.4.before_ref, f32[1536,128]{1,0:T(8,128)S(1)} %get-tuple-element.106.own_ref.rest_0_, ...), custom_call_target="tpu_custom_call" | custom-call | flops 5234491392 | bytes 20447232 | tf_op jit(solution)/shard_map/pallas_call | solution.py:99
  48.2 5.7 %collective-permute-done.2.before_ref = f32[1536,128]{1,0:T(8,128)S(1)} collective-permute-done((f32[1536,128]{1,0:T(8,128)S(1)}, f32[1536,128]{1,0:T(8,128)S(1)}, u32[]{:S(2)}, u32[]{:S(2)}) %collective-permute-start.2) | collective-permute-done | bytes 786464 | tf_op jit(solution)/shard_map/ppermute | solution.py:129
  55.1 3.1 %collective-permute-done.3.after_ref = f32[1536,128]{1,0:T(8,128)S(1)} collective-permute-done((f32[1536,128]{1,0:T(8,128)S(1)}, f32[1536,128]{1,0:T(8,128)S(1)}, u32[]{:S(2)}, u32[]{:S(2)}) %collective-permute-start.3) | collective-permute-done | bytes 786464 | tf_op jit(solution)/shard_map/ppermute | solution.py:129
  58.2 6.8 %shard_map.61.refs_0_ = f32[1536,128]{1,0:T(8,128)S(1)} custom-call(bf16[1536,3328]{1,0:T(8,128)(2,1)S(1)} %get-tuple-element.53.hi_ref, bf16[1536,3328]{1,0:T(8,128)(2,1)S(1)} %get-tuple-element.54.lo_ref, f32[1536,128]{1,0:T(8,128)S(1)} %collective-permute-done.2.before_ref, f32[1536,128]{1,0:T(8,128)S(1)} %shard_map.60.own_ref, ...), custom_call_target="tpu_custom_call" | custom-call | flops 5234491392 | bytes 20447232 | tf_op jit(solution)/shard_map/pallas_call | solution.py:99
  65.7 5.0 %collective-permute-done.8.before_ref = f32[1536,128]{1,0:T(8,128)S(1)} collective-permute-done((f32[1536,128]{1,0:T(8,128)S(1)}, f32[1536,128]{1,0:T(8,128)S(1)}, u32[]{:S(2)}, u32[]{:S(2)}) %collective-permute-start.8) | collective-permute-done | bytes 786464 | tf_op jit(solution)/shard_map/ppermute | solution.py:129
  71.5 3.5 %collective-permute-done.9.after_ref = f32[1536,128]{1,0:T(8,128)S(1)} collective-permute-done((f32[1536,128]{1,0:T(8,128)S(1)}, f32[1536,128]{1,0:T(8,128)S(1)}, u32[]{:S(2)}, u32[]{:S(2)}) %collective-permute-start.9) | collective-permute-done | bytes 786464 | tf_op jit(solution)/shard_map/ppermute | solution.py:129
  75.0 3.2 %collective-permute-start.13 = (f32[1536,128]{1,0:T(8,128)S(1)}, f32[1536,128]{1,0:T(8,128)S(1)}, u32[]{:S(2)}, u32[]{:S(2)}) collective-permute-start(f32[1536,128]{1,0:T(8,128)S(1)} %shard_map.61.refs_0_), channel_id=1, source_target_pairs={{3,2},{4,5},{11,10},{12,13},{19,18},{20,21},{27,26},{28,29}} | collective-permute-start | bytes 2359304 | tf_op jit(solution)/shard_map/ppermute | solution.py:296
  78.3 6.8 %shard_map.64.own_ref = f32[1536,128]{1,0:T(8,128)S(1)} custom-call(bf16[1536,3328]{1,0:T(8,128)(2,1)S(1)} %get-tuple-element.53.hi_ref, bf16[1536,3328]{1,0:T(8,128)(2,1)S(1)} %get-tuple-element.54.lo_ref, f32[1536,128]{1,0:T(8,128)S(1)} %collective-permute-done.8.before_ref, f32[1536,128]{1,0:T(8,128)S(1)} %get-tuple-element.107.own_ref.rest_0_, ...), custom_call_target="tpu_custom_call" | custom-call | flops 5234491392 | bytes 20447232 | tf_op jit(solution)/shard_map/pallas_call | solution.py:99
  87.6 3.4 %collective-permute-start.10 = (f32[1536,128]{1,0:T(8,128)S(1)}, f32[1536,128]{1,0:T(8,128)S(1)}, u32[]{:S(2)}, u32[]{:S(2)}) collective-permute-start(f32[1536,128]{1,0:T(8,128)S(1)} %shard_map.64.own_ref), channel_id=1, source_target_pairs={{0,4},{4,8},{8,12},{12,16},{16,20},{20,24},{24,28},{28,0},{1,5},{5... | collective-permute-start | bytes 2359304 | tf_op jit(solution)/shard_map/ppermute | solution.py:129
  91.0 6.8 %shard_map.63.refs_0_ = f32[1536,128]{1,0:T(8,128)S(1)} custom-call(bf16[1536,3328]{1,0:T(8,128)(2,1)S(1)} %get-tuple-element.53.hi_ref, bf16[1536,3328]{1,0:T(8,128)(2,1)S(1)} %get-tuple-element.54.lo_ref, f32[1536,128]{1,0:T(8,128)S(1)} %collective-permute-done.6.before_ref, f32[1536,128]{1,0:T(8,128)S(1)} %shard_map.62.own_ref, ...), custom_call_target="tpu_custom_call" | custom-call | flops 5234491392 | bytes 20447232 | tf_op jit(solution)/shard_map/pallas_call | solution.py:99
  99.3 4.6 %collective-permute-start.17 = (f32[1536,128]{1,0:T(8,128)S(1)}, f32[1536,128]{1,0:T(8,128)S(1)}, u32[]{:S(2)}, u32[]{:S(2)}) collective-permute-start(f32[1536,128]{1,0:T(8,128)S(1)} %shard_map.63.refs_0_), channel_id=1, source_target_pairs={{3,2},{4,5},{11,10},{12,13},{19,18},{20,21},{27,26},{28,29}} | collective-permute-start | bytes 2359304 | tf_op jit(solution)/shard_map/ppermute | solution.py:296
  108.4 6.8 %shard_map.66.refs_0_ = f32[1536,128]{1,0:T(8,128)S(1)} custom-call(bf16[1536,3328]{1,0:T(8,128)(2,1)S(1)} %get-tuple-element.53.hi_ref, bf16[1536,3328]{1,0:T(8,128)(2,1)S(1)} %get-tuple-element.54.lo_ref, f32[1536,128]{1,0:T(8,128)S(1)} %collective-permute-done.10.before_ref, f32[1536,128]{1,0:T(8,128)S(1)} %shard_map.64.own_ref, ...), custom_call_target="tpu_custom_call" | custom-call | flops 5234491392 | bytes 20447232 | tf_op jit(solution)/shard_map/pallas_call | solution.py:99
  116.7 4.4 %collective-permute-start.20 = (f32[1536,128]{1,0:T(8,128)S(1)}, f32[1536,128]{1,0:T(8,128)S(1)}, u32[]{:S(2)}, u32[]{:S(2)}) collective-permute-start(f32[1536,128]{1,0:T(8,128)S(1)} %shard_map.66.refs_0_), channel_id=1, source_target_pairs={{3,2},{4,5},{11,10},{12,13},{19,18},{20,21},{27,26},{28,29}} | collective-permute-start | bytes 2359304 | tf_op jit(solution)/shard_map/ppermute | solution.py:296
  122.5 6.2 %shard_map.68 = (f32[2,256,384]{2,1,0:T(8,128)S(1)}, f32[2,256,384]{2,1,0:T(8,128)S(1)}) custom-call(s32[4]{0:T(128)S(1)} %get-tuple-element.61.target_ref, bf16[4,128,1536]{2,1,0:T(8,128)(2,1)S(1)} %get-tuple-element.63.refs_0_, bf16[4,128,1536]{2,1,0:T(8,128)(2,1)S(1)} %get-tuple-element.64.refs_1_, ...), custom_call_target="tpu_custom_call" | custom-call | flops 3623878656 | bytes 8000000 | tf_op jit(solution)/shard_map/pallas_call | solution.py:202
  129.5 6.2 %shard_map.69 = (f32[2,256,384]{2,1,0:T(8,128)S(1)}, f32[2,256,384]{2,1,0:T(8,128)S(1)}) custom-call(s32[4]{0:T(128)S(1)} %get-tuple-element.84.target_ref, bf16[4,128,1536]{2,1,0:T(8,128)(2,1)S(1)} %get-tuple-element.63.refs_0_, bf16[4,128,1536]{2,1,0:T(8,128)(2,1)S(1)} %get-tuple-element.64.refs_1_, ...), custom_call_target="tpu_custom_call" | custom-call | flops 3623878656 | bytes 8000000 | tf_op jit(solution)/shard_map/pallas_call | solution.py:202
  138.9 6.2 %shard_map.71 = (f32[2,256,384]{2,1,0:T(8,128)S(1)}, f32[2,256,384]{2,1,0:T(8,128)S(1)}) custom-call(s32[4]{0:T(128)S(1)} %get-tuple-element.61.target_ref, bf16[4,128,1536]{2,1,0:T(8,128)(2,1)S(1)} %get-tuple-element.75.refs_0_, bf16[4,128,1536]{2,1,0:T(8,128)(2,1)S(1)} %get-tuple-element.76.refs_1_, ...), custom_call_target="tpu_custom_call" | custom-call | flops 3623878656 | bytes 8000000 | tf_op jit(solution)/shard_map/pallas_call | solution.py:202
  148.1 6.2 %shard_map.73 = (f32[2,256,384]{2,1,0:T(8,128)S(1)}, f32[2,256,384]{2,1,0:T(8,128)S(1)}) custom-call(s32[4]{0:T(128)S(1)} %get-tuple-element.84.target_ref, bf16[4,128,1536]{2,1,0:T(8,128)(2,1)S(1)} %get-tuple-element.75.refs_0_, bf16[4,128,1536]{2,1,0:T(8,128)(2,1)S(1)} %get-tuple-element.76.refs_1_, ...), custom_call_target="tpu_custom_call" | custom-call | flops 3623878656 | bytes 8000000 | tf_op jit(solution)/shard_map/pallas_call | solution.py:202
  159.5 31.6 %collective-permute-done.31 = f32[256,384]{1,0:T(8,128)S(1)} collective-permute-done((f32[256,384]{1,0:T(8,128)S(1)}, f32[256,384]{1,0:T(8,128)S(1)}, u32[]{:S(2)}, u32[]{:S(2)}) %collective-permute-start.31) | collective-permute-done | bytes 393248 | tf_op jit(solution)/shard_map/ppermute | solution.py:296
  193.1 7.7 %collective-permute-start.34 = (f32[128,256]{1,0:T(8,128)S(1)}, f32[128,256]{1,0:T(8,128)S(1)}, u32[]{:S(2)}, u32[]{:S(2)}) collective-permute-start(f32[128,256]{1,0:T(8,128)S(1)} %slice.21), channel_id=1, source_target_pairs={{4,4},{5,12},{6,20},{7,28},{12,5},{13,13},{14,21},{15,29},{20,6},{... | collective-permute-start | bytes 393224 | tf_op jit(solution)/shard_map/ppermute | solution.py:296
  204.5 5.1 %collective-permute-done.33.turn_e_ref = f32[128,128]{1,0:T(8,128)S(1)} collective-permute-done((f32[128,128]{1,0:T(8,128)S(1)}, f32[128,128]{1,0:T(8,128)S(1)}, u32[]{:S(2)}, u32[]{:S(2)}) %collective-permute-start.33) | collective-permute-done | bytes 65568 | tf_op jit(solution)/shard_map/ppermute | solution.py:296
  (82 shorter events, 47.1 us)
Async XLA Ops:
  1.8 19.4 %collective-permute-start = (f32[1536,128]{1,0:T(8,128)S(1)}, f32[1536,128]{1,0:T(8,128)S(1)}, u32[]{:S(2)}, u32[]{:S(2)}) collective-permute-start(f32[1536,128]{1,0:T(8,128)S(1)} %slice.15.own_ref.rest_0_), channel_id=1, source_target_pairs={{0,4},{4,8},{8,12},{12,16},{16,20},{20,24},{24,28},{28,0},{1,5},{5... | collective-permute-start | bytes 2359304 | tf_op jit(solution)/shard_map/ppermute | solution.py:129
  3.7 20.8 %collective-permute-start.1 = (f32[1536,128]{1,0:T(8,128)S(1)}, f32[1536,128]{1,0:T(8,128)S(1)}, u32[]{:S(2)}, u32[]{:S(2)}) collective-permute-start(f32[1536,128]{1,0:T(8,128)S(1)} %slice.15.own_ref.rest_0_), channel_id=1, source_target_pairs={{4,0},{8,4},{12,8},{16,12},{20,16},{24,20},{28,24},{0,28},{5,1},{9... | collective-permute-start | bytes 2359304 | tf_op jit(solution)/shard_map/ppermute | solution.py:129
  5.7 31.4 %collective-permute-start.4 = (f32[1536,128]{1,0:T(8,128)S(1)}, f32[1536,128]{1,0:T(8,128)S(1)}, u32[]{:S(2)}, u32[]{:S(2)}) collective-permute-start(f32[1536,128]{1,0:T(8,128)S(1)} %get-tuple-element.106.own_ref.rest_0_), channel_id=1, source_target_pairs={{0,4},{4,8},{8,12},{12,16},{16,20},{20,24},{24,28},{28,0},{1,5},{5... | collective-permute-start | bytes 2359304 | tf_op jit(solution)/shard_map/ppermute | solution.py:129
  8.4 32.9 %collective-permute-start.5 = (f32[1536,128]{1,0:T(8,128)S(1)}, f32[1536,128]{1,0:T(8,128)S(1)}, u32[]{:S(2)}, u32[]{:S(2)}) collective-permute-start(f32[1536,128]{1,0:T(8,128)S(1)} %get-tuple-element.106.own_ref.rest_0_), channel_id=1, source_target_pairs={{4,0},{8,4},{12,8},{16,12},{20,16},{24,20},{28,24},{0,28},{5,1},{9... | collective-permute-start | bytes 2359304 | tf_op jit(solution)/shard_map/ppermute | solution.py:129
  31.3 22.6 %collective-permute-start.2 = (f32[1536,128]{1,0:T(8,128)S(1)}, f32[1536,128]{1,0:T(8,128)S(1)}, u32[]{:S(2)}, u32[]{:S(2)}) collective-permute-start(f32[1536,128]{1,0:T(8,128)S(1)} %shard_map.60.own_ref), channel_id=1, source_target_pairs={{0,4},{4,8},{8,12},{12,16},{16,20},{20,24},{24,28},{28,0},{1,5},{5... | collective-permute-start | bytes 2359304 | tf_op jit(solution)/shard_map/ppermute | solution.py:129
  31.4 26.8 %collective-permute-start.3 = (f32[1536,128]{1,0:T(8,128)S(1)}, f32[1536,128]{1,0:T(8,128)S(1)}, u32[]{:S(2)}, u32[]{:S(2)}) collective-permute-start(f32[1536,128]{1,0:T(8,128)S(1)} %shard_map.60.own_ref), channel_id=1, source_target_pairs={{4,0},{8,4},{12,8},{16,12},{20,16},{24,20},{28,24},{0,28},{5,1},{9... | collective-permute-start | bytes 2359304 | tf_op jit(solution)/shard_map/ppermute | solution.py:129
  31.9 38.9 %collective-permute-start.8 = (f32[1536,128]{1,0:T(8,128)S(1)}, f32[1536,128]{1,0:T(8,128)S(1)}, u32[]{:S(2)}, u32[]{:S(2)}) collective-permute-start(f32[1536,128]{1,0:T(8,128)S(1)} %get-tuple-element.107.own_ref.rest_0_), channel_id=1, source_target_pairs={{0,4},{4,8},{8,12},{12,16},{16,20},{20,24},{24,28},{28,0},{1,5},{5... | collective-permute-start | bytes 2359304 | tf_op jit(solution)/shard_map/ppermute | solution.py:129
  37.1 38.0 %collective-permute-start.9 = (f32[1536,128]{1,0:T(8,128)S(1)}, f32[1536,128]{1,0:T(8,128)S(1)}, u32[]{:S(2)}, u32[]{:S(2)}) collective-permute-start(f32[1536,128]{1,0:T(8,128)S(1)} %get-tuple-element.107.own_ref.rest_0_), channel_id=1, source_target_pairs={{4,0},{8,4},{12,8},{16,12},{20,16},{24,20},{28,24},{0,28},{5,1},{9... | collective-permute-start | bytes 2359304 | tf_op jit(solution)/shard_map/ppermute | solution.py:129
  48.2 39.5 %collective-permute-start.6 = (f32[1536,128]{1,0:T(8,128)S(1)}, f32[1536,128]{1,0:T(8,128)S(1)}, u32[]{:S(2)}, u32[]{:S(2)}) collective-permute-start(f32[1536,128]{1,0:T(8,128)S(1)} %shard_map.62.own_ref), channel_id=1, source_target_pairs={{0,4},{4,8},{8,12},{12,16},{16,20},{20,24},{24,28},{28,0},{1,5},{5... | collective-permute-start | bytes 2359304 | tf_op jit(solution)/shard_map/ppermute | solution.py:129
  53.9 37.1 %collective-permute-start.7 = (f32[1536,128]{1,0:T(8,128)S(1)}, f32[1536,128]{1,0:T(8,128)S(1)}, u32[]{:S(2)}, u32[]{:S(2)}) collective-permute-start(f32[1536,128]{1,0:T(8,128)S(1)} %shard_map.62.own_ref), channel_id=1, source_target_pairs={{4,0},{8,4},{12,8},{16,12},{20,16},{24,20},{28,24},{0,28},{5,1},{9... | collective-permute-start | bytes 2359304 | tf_op jit(solution)/shard_map/ppermute | solution.py:129
  65.0 32.8 %collective-permute-start.11 = (f32[1536,128]{1,0:T(8,128)S(1)}, f32[1536,128]{1,0:T(8,128)S(1)}, u32[]{:S(2)}, u32[]{:S(2)}) collective-permute-start(f32[1536,128]{1,0:T(8,128)S(1)} %shard_map.61.refs_0_), channel_id=1, source_target_pairs={{0,2},{7,5},{8,10},{15,13},{16,18},{23,21},{24,26},{31,29}} | collective-permute-start | bytes 2359304 | tf_op jit(solution)/shard_map/ppermute | solution.py:296
  70.8 27.8 %collective-permute-start.12 = (f32[1536,128]{1,0:T(8,128)S(1)}, f32[1536,128]{1,0:T(8,128)S(1)}, u32[]{:S(2)}, u32[]{:S(2)}) collective-permute-start(f32[1536,128]{1,0:T(8,128)S(1)} %shard_map.61.refs_0_), channel_id=1, source_target_pairs={{1,2},{6,5},{9,10},{14,13},{17,18},{22,21},{25,26},{30,29}} | collective-permute-start | bytes 2359304 | tf_op jit(solution)/shard_map/ppermute | solution.py:296
  75.0 24.3 %collective-permute-start.13 = (f32[1536,128]{1,0:T(8,128)S(1)}, f32[1536,128]{1,0:T(8,128)S(1)}, u32[]{:S(2)}, u32[]{:S(2)}) collective-permute-start(f32[1536,128]{1,0:T(8,128)S(1)} %shard_map.61.refs_0_), channel_id=1, source_target_pairs={{3,2},{4,5},{11,10},{12,13},{19,18},{20,21},{27,26},{28,29}} | collective-permute-start | bytes 2359304 | tf_op jit(solution)/shard_map/ppermute | solution.py:296
  87.6 20.7 %collective-permute-start.10 = (f32[1536,128]{1,0:T(8,128)S(1)}, f32[1536,128]{1,0:T(8,128)S(1)}, u32[]{:S(2)}, u32[]{:S(2)}) collective-permute-start(f32[1536,128]{1,0:T(8,128)S(1)} %shard_map.64.own_ref), channel_id=1, source_target_pairs={{0,4},{4,8},{8,12},{12,16},{16,20},{20,24},{24,28},{28,0},{1,5},{5... | collective-permute-start | bytes 2359304 | tf_op jit(solution)/shard_map/ppermute | solution.py:129
  91.0 17.4 %collective-permute-start.14 = (f32[1536,128]{1,0:T(8,128)S(1)}, f32[1536,128]{1,0:T(8,128)S(1)}, u32[]{:S(2)}, u32[]{:S(2)}) collective-permute-start(f32[1536,128]{1,0:T(8,128)S(1)} %shard_map.64.own_ref), channel_id=1, source_target_pairs={{4,0},{8,4},{12,8},{16,12},{20,16},{24,20},{28,24},{0,28},{5,1},{9... | collective-permute-start | bytes 2359304 | tf_op jit(solution)/shard_map/ppermute | solution.py:129
  97.9 18.8 %collective-permute-start.15 = (f32[1536,128]{1,0:T(8,128)S(1)}, f32[1536,128]{1,0:T(8,128)S(1)}, u32[]{:S(2)}, u32[]{:S(2)}) collective-permute-start(f32[1536,128]{1,0:T(8,128)S(1)} %shard_map.63.refs_0_), channel_id=1, source_target_pairs={{0,2},{7,5},{8,10},{15,13},{16,18},{23,21},{24,26},{31,29}} | collective-permute-start | bytes 2359304 | tf_op jit(solution)/shard_map/ppermute | solution.py:296
  98.6 22.5 %collective-permute-start.16 = (f32[1536,128]{1,0:T(8,128)S(1)}, f32[1536,128]{1,0:T(8,128)S(1)}, u32[]{:S(2)}, u32[]{:S(2)}) collective-permute-start(f32[1536,128]{1,0:T(8,128)S(1)} %shard_map.63.refs_0_), channel_id=1, source_target_pairs={{1,2},{6,5},{9,10},{14,13},{17,18},{22,21},{25,26},{30,29}} | collective-permute-start | bytes 2359304 | tf_op jit(solution)/shard_map/ppermute | solution.py:296
  99.3 21.8 %collective-permute-start.17 = (f32[1536,128]{1,0:T(8,128)S(1)}, f32[1536,128]{1,0:T(8,128)S(1)}, u32[]{:S(2)}, u32[]{:S(2)}) collective-permute-start(f32[1536,128]{1,0:T(8,128)S(1)} %shard_map.63.refs_0_), channel_id=1, source_target_pairs={{3,2},{4,5},{11,10},{12,13},{19,18},{20,21},{27,26},{28,29}} | collective-permute-start | bytes 2359304 | tf_op jit(solution)/shard_map/ppermute | solution.py:296
  115.2 21.2 %collective-permute-start.18 = (f32[1536,128]{1,0:T(8,128)S(1)}, f32[1536,128]{1,0:T(8,128)S(1)}, u32[]{:S(2)}, u32[]{:S(2)}) collective-permute-start(f32[1536,128]{1,0:T(8,128)S(1)} %shard_map.66.refs_0_), channel_id=1, source_target_pairs={{0,2},{7,5},{8,10},{15,13},{16,18},{23,21},{24,26},{31,29}} | collective-permute-start | bytes 2359304 | tf_op jit(solution)/shard_map/ppermute | solution.py:296
  115.9 20.5 %collective-permute-start.19 = (f32[1536,128]{1,0:T(8,128)S(1)}, f32[1536,128]{1,0:T(8,128)S(1)}, u32[]{:S(2)}, u32[]{:S(2)}) collective-permute-start(f32[1536,128]{1,0:T(8,128)S(1)} %shard_map.66.refs_0_), channel_id=1, source_target_pairs={{1,2},{6,5},{9,10},{14,13},{17,18},{22,21},{25,26},{30,29}} | collective-permute-start | bytes 2359304 | tf_op jit(solution)/shard_map/ppermute | solution.py:296
  116.7 20.8 %collective-permute-start.20 = (f32[1536,128]{1,0:T(8,128)S(1)}, f32[1536,128]{1,0:T(8,128)S(1)}, u32[]{:S(2)}, u32[]{:S(2)}) collective-permute-start(f32[1536,128]{1,0:T(8,128)S(1)} %shard_map.66.refs_0_), channel_id=1, source_target_pairs={{3,2},{4,5},{11,10},{12,13},{19,18},{20,21},{27,26},{28,29}} | collective-permute-start | bytes 2359304 | tf_op jit(solution)/shard_map/ppermute | solution.py:296
  128.8 17.8 %collective-permute-start.22 = (f32[2,256,384]{2,1,0:T(8,128)S(1)}, f32[2,256,384]{2,1,0:T(8,128)S(1)}, u32[]{:S(2)}, u32[]{:S(2)}) collective-permute-start(f32[2,256,384]{2,1,0:T(8,128)S(1)} %get-tuple-element.71), channel_id=1, source_target_pairs={{2,18},{5,21},{10,26},{13,29},{18,2},{21,5},{26,10},{29,13}} | collective-permute-start | bytes 2359304 | tf_op jit(solution)/shard_map/ppermute | solution.py:296
  158.2 32.9 %collective-permute-start.31 = (f32[256,384]{1,0:T(8,128)S(1)}, f32[256,384]{1,0:T(8,128)S(1)}, u32[]{:S(2)}, u32[]{:S(2)}) collective-permute-start(f32[256,384]{1,0:T(8,128)S(1)} %get-tuple-element.101), channel_id=1, source_target_pairs={{2,3},{5,4},{10,11},{13,12},{18,19},{21,20},{26,27},{29,28}} | collective-permute-start | bytes 1179656 | tf_op jit(solution)/shard_map/ppermute | solution.py:296
  193.1 16.4 %collective-permute-start.34 = (f32[128,256]{1,0:T(8,128)S(1)}, f32[128,256]{1,0:T(8,128)S(1)}, u32[]{:S(2)}, u32[]{:S(2)}) collective-permute-start(f32[128,256]{1,0:T(8,128)S(1)} %slice.21), channel_id=1, source_target_pairs={{4,4},{5,12},{6,20},{7,28},{12,5},{13,13},{14,21},{15,29},{20,6},{... | collective-permute-start | bytes 393224 | tf_op jit(solution)/shard_map/ppermute | solution.py:296
  (13 other events, 69.9 us)

commit v6 on v5

--- a/solution.py
+++ b/solution.py
@@ -63,14 +63,16 @@
     )(slot_of, blocks)
 
 
-def apply_kernel(hi_ref, lo_ref, before_ref, own_ref, after_ref, *rest, second):
+def apply_kernel(core_ref, hi_ref, lo_ref, near_ref, far_ref, own_ref, *rest, second, turned):
+    inside_ref, across_ref = (far_ref, near_ref) if turned else (near_ref, far_ref)
     old_ref = rest[0] if second else None
     out_ref, parts = rest[-2:]
     rows, width = own_ref.shape
     wide = hi_ref.shape[1]
     tall = wide - 2 * rows
-    for place, ref in enumerate((before_ref, own_ref, after_ref)):
-        there = pl.ds(place * rows, rows)
+    core = core_ref[0]
+    for place, ref in ((1, own_ref), (2 - 2 * core, inside_ref), (2 * core, across_ref)):
+        there = pl.ds(pl.multiple_of(place * rows, rows), rows)
         parts[there, pl.ds(0, width)], parts[there, pl.ds(width, width)] = split(ref[...])
 
     def one_group(step, carry):
@@ -90,15 +92,15 @@
     lax.fori_loop(0, rows // tall, one_group, 0)
 
 
-def apply_step(hi, lo, before, own, after, old=None):
+def apply_step(core, hi, lo, halo, own, old=None, turned=False):
     rows, width = own.shape
     wide = hi.shape[1]
     second = old is not None
     hi, lo = (pltpu.with_memory_space_constraint(x, pltpu.VMEM) for x in (hi, lo))
     vmem = pl.BlockSpec(memory_space=pltpu.VMEM)
     return pl.pallas_call(
-        functools.partial(apply_kernel, second=second),
-        in_specs=[vmem] * (6 if second else 5),
+        functools.partial(apply_kernel, second=second, turned=turned),
+        in_specs=[pl.BlockSpec(memory_space=pltpu.SMEM)] + [vmem] * (6 if second else 5),
         out_specs=vmem,
         out_shape=jax.ShapeDtypeStruct((rows, width), jnp.float32),
         scratch_shapes=[pltpu.VMEM((3 * rows, 2 * width), jnp.bfloat16)],
@@ -106,7 +108,7 @@
         cost_estimate=pl.CostEstimate(
             flops=8 * rows * wide * width, bytes_accessed=4 * rows * wide, transcendentals=0
         ),
-    )(hi, lo, before, own, after, *([old] if second else []))
+    )(core, hi, lo, *(halo[::-1] if turned else halo), own, *([old] if second else []))
 
 
 def slot_table(columns, counts):
@@ -124,9 +126,9 @@
 
 def neighbours(x):
     size = lax.axis_size("orb")
-    up = [(i, (i + 1) % size) for i in range(size)]
-    down = [(j, i) for i, j in up]
-    return lax.ppermute(x, "orb", up), lax.ppermute(x, "orb", down)
+    inside = [(i, i ^ 1) for i in range(size)]
+    across = [(i, (i + 1 if i % 2 else i - 1) % size) for i in range(size)]
+    return lax.ppermute(x, "orb", inside), lax.ppermute(x, "orb", across)
 
 
 def after_that(x, *done):
@@ -144,8 +146,8 @@
 
 def prep(bands, parts):
     rows, width = parts[0].shape
-    plain = jax.ShapeDtypeStruct((4, rows, width), jnp.bfloat16)
-    turned = jax.ShapeDtypeStruct((4, width, rows), jnp.bfloat16)
+    plain = pltpu.VMEM((4, rows, width), jnp.bfloat16)
+    turned = pltpu.VMEM((4, width, rows), jnp.bfloat16)
     return pl.pallas_call(
         prep_kernel,
         in_specs=[pl.BlockSpec(memory_space=pltpu.SMEM)] + [pl.BlockSpec(memory_space=pltpu.VMEM)] * 4,
@@ -156,111 +158,91 @@
     )(bands, *parts)
 
 
-def product_kernel(target_ref, *refs, shapes):
-    *ins, out_a, out_b = refs
-    step = pl.program_id(0)
-    parts = []
+def product_kernel(target_ref, *refs, shapes, place):
+    *ins, out_ref = refs
+    target = target_ref[place]
+    start = 0
     for columns in shapes:
         left, ins = ins[:2], ins[2:]
         right, ins = ins[: 2 * columns], ins[2 * columns :]
         count, width, rows = left[0].shape
         thi, tlo = (ref[...].reshape(count * width, rows) for ref in left)
-        his = jnp.concatenate([ref[0] for ref in right[:columns]], axis=1)
-        los = jnp.concatenate([ref[0] for ref in right[columns:]], axis=1)
-        small = jnp.dot(thi, los, preferred_element_type=jnp.float32)
-        small += jnp.dot(tlo, his, preferred_element_type=jnp.float32)
-        parts.append(small + jnp.dot(thi, his, preferred_element_type=jnp.float32))
-    total = jnp.concatenate(parts, axis=1)
-
-    @pl.when(step < 2)
-    def _():
-        out_a[0] = total
-
-    @pl.when(step >= 2)
-    def _():
-        out_b[0] = total
-
-
-def products(targets, chunks, lines):
-    ins, specs, shapes, size, flops = [], [], [], 0, 0
+        his = jnp.concatenate([ref[target] for ref in right[:columns]], axis=1)
+        los = jnp.concatenate([ref[target] for ref in right[columns:]], axis=1)
+        total = jnp.dot(thi, los, preferred_element_type=jnp.float32)
+        total += jnp.dot(tlo, his, preferred_element_type=jnp.float32)
+        total += jnp.dot(thi, his, preferred_element_type=jnp.float32)
+        out_ref[:, pl.ds(start, his.shape[1])] = total
+        start += his.shape[1]
+
+
+def products(targets, place, chunks, lines):
+    ins, shapes, size, flops = [], [], 0, 0
     for line in lines:
         _, _, thi, tlo = chunks[line]
         four, width, rows = thi.shape
         ins += [thi, tlo]
-        specs += [pl.BlockSpec((four // 2, width, rows), lambda g, t: (g // 2, 0, 0))] * 2
         for part in (0, 1):
-            for c in range(line + 1):
-                x = chunks[c][part]
-                ins.append(x)
-                specs.append(pl.BlockSpec((1, rows, x.shape[2]), lambda g, t: (t[g], 0, 0)))
+            ins += [chunks[c][part] for c in range(line + 1)]
         wide = sum(chunks[c][0].shape[2] for c in range(line + 1))
         shapes.append(line + 1)
         size += wide
-        flops += 12 * four * width * rows * wide
-    tall = four // 2 * width
-    shape = jax.ShapeDtypeStruct((2, tall, size), jnp.float32)
-    return pl.pallas_call(
-        functools.partial(product_kernel, shapes=shapes),
-        grid_spec=pltpu.PrefetchScalarGridSpec(
-            num_scalar_prefetch=1,
-            grid=(4,),
-            in_specs=specs,
-            out_specs=[
-                pl.BlockSpec((1, tall, size), lambda g, t: (jnp.minimum(g, 1), 0, 0)),
-                pl.BlockSpec((1, tall, size), lambda g, t: (jnp.maximum(g - 2, 0), 0, 0)),
-            ],
-        ),
-        out_shape=[shape, shape],
-        compiler_params=pltpu.CompilerParams(vmem_limit_bytes=24 * MIB),
+        flops += 6 * four * width * rows * wide
+    ins = [pltpu.with_memory_space_constraint(x, pltpu.VMEM) for x in ins]
+    vmem = pl.BlockSpec(memory_space=pltpu.VMEM)
+    return pl.pallas_call(
+        functools.partial(product_kernel, shapes=shapes, place=place),
+        in_specs=[pl.BlockSpec(memory_space=pltpu.SMEM)] + [vmem] * len(ins),
+        out_specs=vmem,
+        out_shape=jax.ShapeDtypeStruct((four * width, size), jnp.float32),
+        compiler_params=pltpu.CompilerParams(vmem_limit_bytes=16 * MIB),
         cost_estimate=pl.CostEstimate(flops=flops, bytes_accessed=8_000_000, transcendentals=0),
     )(targets, *ins)
 
 
-def middle_kernel(got_a, ours_a, got_b, ours_b, send_a, keep_a, send_b, keep_b):
-    for got, ours, send_ref, keep in ((got_a, ours_a, send_a, keep_a), (got_b, ours_b, send_b, keep_b)):
-        keep[...] = got[0] + ours[0]
-        send_ref[...] = got[1] + ours[1]
-
-
-def middle(*parts):
-    shape = jax.ShapeDtypeStruct(parts[0].shape[1:], jnp.float32)
+def sum_kernel(*refs):
+    *ins, out_ref = refs
+    out_ref[...] = (ins[0][...] + ins[1][...]) + (ins[2][...] + ins[3][...])
+
+
+def sum_parts(*parts):
     vmem = pl.BlockSpec(memory_space=pltpu.VMEM)
     return pl.pallas_call(
-        middle_kernel,
+        sum_kernel,
         in_specs=[vmem] * 4,
+        out_specs=vmem,
+        out_shape=jax.ShapeDtypeStruct(parts[0].shape, jnp.float32),
+        compiler_params=pltpu.CompilerParams(vmem_limit_bytes=12 * MIB),
+        cost_estimate=pl.CostEstimate(flops=0, bytes_accessed=4_000_000, transcendentals=0),
+    )(*parts)
+
+
+def pick_kernel(goal_ref, early_ref, *refs):
+    ins, outs = refs[:4], refs[4:]
+    rows = early_ref.shape[0] // 4
+    for k, out in enumerate(outs):
+        there = pl.ds(pl.multiple_of(goal_ref[k] * rows, rows), rows)
+        x, y, u, v = (ref[there, :] for ref in ins)
+        late = (x + y) + (u + v)
+        early = early_ref[there, :]
+        if k == 3:
+            early, late = (jnp.where(goal_ref[4] > 0, x, 0.0) for x in (early, late))
+        out[pl.ds(0, rows), :] = early
+        out[pl.ds(rows, rows), :] = late
+
+
+def pick(goals, early, *parts):
+    rows, size = parts[0].shape
+    shape = jax.ShapeDtypeStruct((rows // 2, size), jnp.float32)
+    vmem = pl.BlockSpec(memory_space=pltpu.VMEM)
+    return pl.pallas_call(
+        pick_kernel,
+        in_specs=[pl.BlockSpec(memory_space=pltpu.SMEM)] + [vmem] * 5,
         out_specs=[vmem] * 4,
         out_shape=[shape] * 4,
         compiler_params=pltpu.CompilerParams(vmem_limit_bytes=12 * MIB),
-        cost_estimate=pl.CostEstimate(flops=0, bytes_accessed=5_000_000, transcendentals=0),
-    )(*parts)
-
-
-def pick_kernel(goal_ref, *refs):
-    ins, outs, sums = refs[:8], refs[8:12], refs[12]
-    rows = sums.shape[1] // 2
-    for batch in range(2):
-        for band in range(4):
-            keep, got = ins[4 * batch + band // 2 * 2 : 4 * batch + band // 2 * 2 + 2]
-            there = pl.ds(band % 2 * rows, rows)
-            sums[band, pl.ds(batch * rows, rows), :] = keep[there, :] + got[there, :]
-    for k, out in enumerate(outs):
-        out[...] = sums[goal_ref[k]]
-    outs[3][...] = jnp.where(goal_ref[4] > 0, outs[3][...], 0.0)
-
-
-def pick(goals, *parts):
-    rows, size = parts[0].shape
-    shape = jax.ShapeDtypeStruct((rows, size), jnp.float32)
-    vmem = pl.BlockSpec(memory_space=pltpu.VMEM)
-    return pl.pallas_call(
-        pick_kernel,
-        in_specs=[pl.BlockSpec(memory_space=pltpu.SMEM)] + [vmem] * len(parts),
-        out_specs=[vmem] * 4,
-        out_shape=[shape] * 4,
-        scratch_shapes=[pltpu.VMEM((4, rows, size), jnp.float32)],
-        compiler_params=pltpu.CompilerParams(vmem_limit_bytes=12 * MIB),
         cost_estimate=pl.CostEstimate(flops=0, bytes_accessed=3_000_000, transcendentals=0),
-    )(goals, *parts)
+    )(goals, early, *parts)
 
 
 def assemble_kernel(core_ref, piece_ref, turn_e_ref, turn_l_ref, out_ref, *, scale):
@@ -317,6 +299,7 @@
     ]
 
 
+FLIPS = (3, 1, 2, 0)
 EVERY = [(q, c, z) for q in range(4) for c in range(2) for z in range(4)]
 SWAP = [(linear(q, c, z), linear(q, 1 - c, z)) for q, c, z in EVERY]
 TURN = [(linear(q, c, z), linear(z, c, q)) for q, c, z in EVERY]
@@ -334,13 +317,9 @@
 
 
 def in_turn(hi, lo, old, order):
-    first, filtered = [], []
-    for x in old:
-        before, after = neighbours(x)
-        first.append(apply_step(hi, lo, before, x, after))
-    for x, v in zip(first, old):
-        before, after = neighbours(x)
-        filtered.append(apply_step(hi, lo, before, x, after, v))
+    core = (lax.axis_index("orb") & 1)[None]
+    first = [apply_step(core, hi, lo, neighbours(x), x) for x in old]
+    filtered = [apply_step(core, hi, lo, neighbours(x), x, v) for x, v in zip(first, old)]
     filtered = jnp.concatenate(filtered, axis=1)
     return filtered, simple_gram(filtered) / order
 
@@ -351,19 +330,22 @@
     bands = jnp.stack([b + core * (3 - 2 * b) for b in (2, 0, 1, 3)])
     holder = (z == 2 - core).astype(jnp.int32)
     goals = jnp.stack([k + core * (3 - 2 * k) for k in (0, 1, 3)] + [z, holder])
-    far = jnp.stack([chip ^ 2, chip ^ 3, chip ^ 1, chip ^ 3])
-    near = jnp.stack([chip, chip ^ 1, chip, chip ^ 2])
-    return bands, goals, far, near, core[None]
+    targets = jnp.stack([chip ^ flip for flip in FLIPS])
+    return bands, goals, targets, core[None]
 
 
 def by_symmetry(hi, lo, old, order, tables):
-    def one(x, halo, v=None):
-        return apply_step(hi, lo, halo[0], x, halo[1], v)
-
-    bands, goals, far, near, core = tables
-
-    def across(parts, order):
-        return [send(x, over_chips(flip)) for x, flip in zip(parts, order)]
+    bands, goals, targets, core = tables
+
+    def one(x, halo, v=None, turned=False):
+        return apply_step(core, hi, lo, halo, x, v, turned)
+
+    def over_all_chips(chunks, lines, first_after):
+        parts, before = [], first_after
+        for k, flip in enumerate(FLIPS):
+            parts.append(products(after_that(targets, before), k, chunks, lines))
+            before = parts[-1]
+        return [send(x, over_chips(flip)) if flip else x for x, flip in zip(parts, FLIPS)], before
 
     v0, v1, v2 = old
     hv = [neighbours(x) for x in old]
@@ -378,26 +360,18 @@
     g1 = one(after_that(f1, g0), hf1, v1)
     z1 = gather_bands(g1)
     chunks = [prep(bands, [after_that(z0[0], g1)] + z0[1:])]
-    g2 = one(after_that(f2, chunks[0][0]), hf2, v2)
+    g2 = one(after_that(f2, chunks[0][0]), hf2, v2, turned=True)
     z2 = gather_bands(g2)
     chunks.append(prep(bands, [after_that(z1[0], g2)] + z1[1:]))
-    theirs_e = products(far, chunks, (0, 1))
-    got_e = across(theirs_e, (2, 1))
-    ours_e = products(after_that(near, theirs_e[0]), chunks, (0, 1))
-    chunks.append(prep(bands, [after_that(z2[0], ours_e[0])] + z2[1:]))
-    theirs_l = products(far, chunks, (2,))
-    got_l = across(theirs_l, (2, 1))
-    got_e[0] = after_that(got_e[0], theirs_l[0])
-    send_ey, keep_ey, send_ex, keep_ex = middle(got_e[0], ours_e[0], got_e[1], ours_e[1])
-    last_e = across((send_ey, send_ex), (1, 2))
-    ours_l = products(after_that(near, keep_ey), chunks, (2,))
-    send_ly, keep_ly, send_lx, keep_lx = middle(got_l[0], ours_l[0], got_l[1], ours_l[1])
-    last_l = across((send_ly, send_lx), (1, 2))
-    filtered = jnp.concatenate([g0, g1, after_that(g2, keep_ly)], axis=1)
-    moved = pick(goals, keep_ey, last_e[0], keep_ex, last_e[1], keep_ly, last_l[0], keep_lx, last_l[1])
+    early, last = over_all_chips(chunks, (0, 1), g2)
+    chunks.append(prep(bands, [after_that(z2[0], last)] + z2[1:]))
+    late, last = over_all_chips(chunks, (2,), chunks[2][0])
+    early[3] = after_that(early[3], last)
+    moved = pick(goals, sum_parts(*early), *late)
     piece = moved[3]
     for k, x in zip((0, 1, 3), moved):
         piece = piece + send(x, mirrored([(2, k)]))
+    filtered = jnp.concatenate([g0, g1, after_that(g2, last)], axis=1)
     piece = piece + send(piece, SWAP)
     w = v0.shape[1]
     turn_e = send(piece[:w, w : 2 * w], TURN)

time: 211 us -> 212 us (level)
  waiting for transfers between devices: 71.4 us -> 80.8 us
  starting transfers between devices: 48 us -> 39.1 us
    ppermute x23 -> x21, waiting for transfers between devices: 39.1 us -> 45.2 us  [send(): return lax.ppermute(x, ('orb', 'band'), pairs)]
    ppermute x12, starting transfers between devices: 13 us -> 8.42 us  [neighbours(): return (lax.ppermute(x, 'orb', inside), lax.ppermute(x, 'orb', across))]
    ppermute x23 -> x21, starting transfers between devices: 34.9 us -> 30.7 us  [send(): return lax.ppermute(x, ('orb', 'band'), pairs)]
    ppermute x12, waiting for transfers between devices: 32.3 us -> 35.6 us  [neighbours(): return (lax.ppermute(x, 'orb', inside), lax.ppermute(x, 'orb', across))]
    pallas_call x12 -> x15, Pallas kernels: 66.1 us -> 66.3 us  [the longest x6 41 us: apply_step(): pl.pallas_call(functools.partial(apply_kernel, second=second, turned=turn...]
  transfers between devices with their start and end apart: 35 -> 33, of which waited for: 13 -> 10; matrix products, arithmetic and copies ran while one was open for 2% -> 2% of each run, Pallas kernels for 39% -> 39%
where the time goes in v6:
time: 212 us; the launch traced here: 211 us
  Pallas kernels  84.4 us (40%)
  waiting for transfers between devices  80.8 us (38%)
  starting transfers between devices  39.1 us (18%)
  local copies, waits for them, and re-layouts  3.66 us (2%)
    ppermute x21, waiting for transfers between devices, send(): return lax.ppermute(x, ('orb', 'band'), pairs)  45.2 us
    pallas_call x6, Pallas kernels, apply_step(): pl.pallas_call(functools.partial(apply_kernel, second=second, turned=turn...  41 us
    ppermute x12, waiting for transfers between devices, neighbours(): return (lax.ppermute(x, 'orb', inside), lax.ppermute(x, 'orb', across))  35.6 us
    ppermute x21, starting transfers between devices, send(): return lax.ppermute(x, ('orb', 'band'), pairs)  30.7 us
    pallas_call x8, Pallas kernels, products(): pl.pallas_call(functools.partial(product_kernel, shapes=shapes, place=pla...  25.2 us
    pallas_call x1, Pallas kernels, densify(): pl.pallas_call(functools.partial(densify_kernel, spread=spread, reach=row...  12.8 us
    ppermute x12, starting transfers between devices, neighbours(): return (lax.ppermute(x, 'orb', inside), lax.ppermute(x, 'orb', across))  8.42 us
    pallas_call x3, Pallas kernels, prep(): pl.pallas_call(prep_kernel, in_specs=[pl.BlockSpec(memory_space=pltpu.SME...  4.3 us
  transfers between devices with their start and end apart: 33, of which 10 were waited for; matrix products, arithmetic and copies ran while one was open for 2% of the time, Pallas kernels for 39%

profile of v6, /device:TPU:3, one launch (start us, length us, event | category | flops | bytes accessed | tf_op | source)
XLA Modules:
  0.0 211.2 jit_solution(10674557201144870537)
XLA Ops:
  7.4 12.8 %shard_map.59 = (bf16[1536,3328]{1,0:T(8,128)(2,1)S(1)}, bf16[1536,3328]{1,0:T(8,128)(2,1)S(1)}) custom-call(s32[24,52]{1,0:T(8,128)S(1)} %select_reduce_fusion.slot_ref, f32[24,32,64,64]{3,2,1,0:T(8,128)} %blocks_ref.1), custom_call_target="tpu_custom_call" | custom-call | bytes 60000000 | tf_op jit(solution)/shard_map/pallas_call | solution.py:52
  23.3 6.8 %shard_map.60.own_ref = f32[1536,128]{1,0:T(8,128)S(1)} custom-call(s32[1]{0:T(128)} %bitcast.10.core_ref, bf16[1536,3328]{1,0:T(8,128)(2,1)S(1)} %get-tuple-element.43.hi_ref, bf16[1536,3328]{1,0:T(8,128)(2,1)S(1)} %get-tuple-element.44.lo_ref, f32[1536,128]{1,0:T(8,128)S(1)} %collective-permute-done.near_ref, ...), custom_call_target="tpu_custom_call" | custom-call | flops 5234491392 | bytes 20447232 | tf_op jit(solution)/shard_map/pallas_call | solution.py:101
  33.5 6.6 %collective-permute-done.5.far_ref = f32[1536,128]{1,0:T(8,128)S(1)} collective-permute-done((f32[1536,128]{1,0:T(8,128)S(1)}, f32[1536,128]{1,0:T(8,128)S(1)}, u32[]{:S(2)}, u32[]{:S(2)}) %collective-permute-start.5) | collective-permute-done | bytes 786464 | tf_op jit(solution)/shard_map/ppermute | solution.py:131
  40.1 6.8 %shard_map.62.own_ref = f32[1536,128]{1,0:T(8,128)S(1)} custom-call(s32[1]{0:T(128)} %bitcast.10.core_ref, bf16[1536,3328]{1,0:T(8,128)(2,1)S(1)} %get-tuple-element.43.hi_ref, bf16[1536,3328]{1,0:T(8,128)(2,1)S(1)} %get-tuple-element.44.lo_ref, f32[1536,128]{1,0:T(8,128)S(1)} %collective-permute-done.4.near_ref, ...), custom_call_target="tpu_custom_call" | custom-call | flops 5234491392 | bytes 20447232 | tf_op jit(solution)/shard_map/pallas_call | solution.py:101
  48.3 8.6 %collective-permute-done.3.far_ref = f32[1536,128]{1,0:T(8,128)S(1)} collective-permute-done((f32[1536,128]{1,0:T(8,128)S(1)}, f32[1536,128]{1,0:T(8,128)S(1)}, u32[]{:S(2)}, u32[]{:S(2)}) %collective-permute-start.3) | collective-permute-done | bytes 786464 | tf_op jit(solution)/shard_map/ppermute | solution.py:131
  57.0 6.8 %shard_map.61.refs_0_ = f32[1536,128]{1,0:T(8,128)S(1)} custom-call(s32[1]{0:T(128)} %bitcast.10.core_ref, bf16[1536,3328]{1,0:T(8,128)(2,1)S(1)} %get-tuple-element.43.hi_ref, bf16[1536,3328]{1,0:T(8,128)(2,1)S(1)} %get-tuple-element.44.lo_ref, f32[1536,128]{1,0:T(8,128)S(1)} %collective-permute-done.2.near_ref, ...), custom_call_target="tpu_custom_call" | custom-call | flops 5234491392 | bytes 20447232 | tf_op jit(solution)/shard_map/pallas_call | solution.py:101
  65.3 8.6 %collective-permute-done.9.far_ref = f32[1536,128]{1,0:T(8,128)S(1)} collective-permute-done((f32[1536,128]{1,0:T(8,128)S(1)}, f32[1536,128]{1,0:T(8,128)S(1)}, u32[]{:S(2)}, u32[]{:S(2)}) %collective-permute-start.9) | collective-permute-done | bytes 786464 | tf_op jit(solution)/shard_map/ppermute | solution.py:131
  73.8 3.2 %collective-permute-start.14 = (f32[1536,128]{1,0:T(8,128)S(1)}, f32[1536,128]{1,0:T(8,128)S(1)}, u32[]{:S(2)}, u32[]{:S(2)}) collective-permute-start(f32[1536,128]{1,0:T(8,128)S(1)} %shard_map.61.refs_0_), channel_id=1, source_target_pairs={{3,2},{4,5},{11,10},{12,13},{19,18},{20,21},{27,26},{28,29}} | collective-permute-start | bytes 2359304 | tf_op jit(solution)/shard_map/ppermute | solution.py:278
  77.1 6.8 %shard_map.64.own_ref = f32[1536,128]{1,0:T(8,128)S(1)} custom-call(s32[1]{0:T(128)} %bitcast.10.core_ref, bf16[1536,3328]{1,0:T(8,128)(2,1)S(1)} %get-tuple-element.43.hi_ref, bf16[1536,3328]{1,0:T(8,128)(2,1)S(1)} %get-tuple-element.44.lo_ref, f32[1536,128]{1,0:T(8,128)S(1)} %collective-permute-done.8.near_ref, ...), custom_call_target="tpu_custom_call" | custom-call | flops 5234491392 | bytes 20447232 | tf_op jit(solution)/shard_map/pallas_call | solution.py:101
  84.0 6.7 %collective-permute-done.7.far_ref = f32[1536,128]{1,0:T(8,128)S(1)} collective-permute-done((f32[1536,128]{1,0:T(8,128)S(1)}, f32[1536,128]{1,0:T(8,128)S(1)}, u32[]{:S(2)}, u32[]{:S(2)}) %collective-permute-start.7) | collective-permute-done | bytes 786464 | tf_op jit(solution)/shard_map/ppermute | solution.py:131
  90.7 6.8 %shard_map.63.refs_0_ = f32[1536,128]{1,0:T(8,128)S(1)} custom-call(s32[1]{0:T(128)} %bitcast.10.core_ref, bf16[1536,3328]{1,0:T(8,128)(2,1)S(1)} %get-tuple-element.43.hi_ref, bf16[1536,3328]{1,0:T(8,128)(2,1)S(1)} %get-tuple-element.44.lo_ref, f32[1536,128]{1,0:T(8,128)S(1)} %collective-permute-done.6.near_ref, ...), custom_call_target="tpu_custom_call" | custom-call | flops 5234491392 | bytes 20447232 | tf_op jit(solution)/shard_map/pallas_call | solution.py:101
  99.0 4.6 %collective-permute-start.17 = (f32[1536,128]{1,0:T(8,128)S(1)}, f32[1536,128]{1,0:T(8,128)S(1)}, u32[]{:S(2)}, u32[]{:S(2)}) collective-permute-start(f32[1536,128]{1,0:T(8,128)S(1)} %shard_map.63.refs_0_), channel_id=1, source_target_pairs={{3,2},{4,5},{11,10},{12,13},{19,18},{20,21},{27,26},{28,29}} | collective-permute-start | bytes 2359304 | tf_op jit(solution)/shard_map/ppermute | solution.py:278
  107.0 6.8 %shard_map.66.refs_0_ = f32[1536,128]{1,0:T(8,128)S(1)} custom-call(s32[1]{0:T(128)} %bitcast.10.core_ref, bf16[1536,3328]{1,0:T(8,128)(2,1)S(1)} %get-tuple-element.43.hi_ref, bf16[1536,3328]{1,0:T(8,128)(2,1)S(1)} %get-tuple-element.44.lo_ref, f32[1536,128]{1,0:T(8,128)S(1)} %collective-permute-done.10.near_ref, ...), custom_call_target="tpu_custom_call" | custom-call | flops 5234491392 | bytes 20447232 | tf_op jit(solution)/shard_map/pallas_call | solution.py:101
  115.3 4.4 %collective-permute-start.20 = (f32[1536,128]{1,0:T(8,128)S(1)}, f32[1536,128]{1,0:T(8,128)S(1)}, u32[]{:S(2)}, u32[]{:S(2)}) collective-permute-start(f32[1536,128]{1,0:T(8,128)S(1)} %shard_map.66.refs_0_), channel_id=1, source_target_pairs={{3,2},{4,5},{11,10},{12,13},{19,18},{20,21},{27,26},{28,29}} | collective-permute-start | bytes 2359304 | tf_op jit(solution)/shard_map/ppermute | solution.py:278
  122.1 3.2 %shard_map.68 = f32[512,384]{1,0:T(8,128)S(1)} custom-call(s32[4]{0:T(128)S(1)} %get-tuple-element.72.target_ref, bf16[4,128,1536]{2,1,0:T(8,128)(2,1)S(1)} %get-tuple-element.53.refs_0_, bf16[4,128,1536]{2,1,0:T(8,128)(2,1)S(1)} %get-tuple-element.54.refs_1_, bf16[4,1536,128]{2,1,0:T(8,128)(2,1)S(1)} %get-tuple-element.49.refs_2_.refs_6_, ...), custom_call_target="tpu_custom_call" | custom-call | flops 1811939328 | bytes 8000000 | tf_op jit(solution)/shard_map/pallas_call | solution.py:193
  125.2 3.2 %shard_map.69 = f32[512,384]{1,0:T(8,128)S(1)} custom-call(s32[4]{0:T(128)S(1)} %get-tuple-element.72.target_ref, bf16[4,128,1536]{2,1,0:T(8,128)(2,1)S(1)} %get-tuple-element.53.refs_0_, bf16[4,128,1536]{2,1,0:T(8,128)(2,1)S(1)} %get-tuple-element.54.refs_1_, bf16[4,1536,128]{2,1,0:T(8,128)(2,1)S(1)} %get-tuple-element.49.refs_2_.refs_6_, ...), custom_call_target="tpu_custom_call" | custom-call | flops 1811939328 | bytes 8000000 | tf_op jit(solution)/shard_map/pallas_call | solution.py:193
  128.4 3.2 %shard_map.70 = f32[512,384]{1,0:T(8,128)S(1)} custom-call(s32[4]{0:T(128)S(1)} %get-tuple-element.72.target_ref, bf16[4,128,1536]{2,1,0:T(8,128)(2,1)S(1)} %get-tuple-element.53.refs_0_, bf16[4,128,1536]{2,1,0:T(8,128)(2,1)S(1)} %get-tuple-element.54.refs_1_, bf16[4,1536,128]{2,1,0:T(8,128)(2,1)S(1)} %get-tuple-element.49.refs_2_.refs_6_, ...), custom_call_target="tpu_custom_call" | custom-call | flops 1811939328 | bytes 8000000 | tf_op jit(solution)/shard_map/pallas_call | solution.py:193
  133.0 3.2 %shard_map.71.refs_3_ = f32[512,384]{1,0:T(8,128)S(1)} custom-call(s32[4]{0:T(128)S(1)} %get-tuple-element.72.target_ref, bf16[4,128,1536]{2,1,0:T(8,128)(2,1)S(1)} %get-tuple-element.53.refs_0_, bf16[4,128,1536]{2,1,0:T(8,128)(2,1)S(1)} %get-tuple-element.54.refs_1_, bf16[4,1536,128]{2,1,0:T(8,128)(2,1)S(1)} %get-tuple-element.49.refs_2_.refs_6_, ...), custom_call_target="tpu_custom_call" | custom-call | flops 1811939328 | bytes 8000000 | tf_op jit(solution)/shard_map/pallas_call | solution.py:193
  138.6 3.1 %shard_map.73 = f32[512,384]{1,0:T(8,128)S(1)} custom-call(s32[4]{0:T(128)S(1)} %get-tuple-element.72.target_ref, bf16[4,128,1536]{2,1,0:T(8,128)(2,1)S(1)} %get-tuple-element.67.refs_0_, bf16[4,128,1536]{2,1,0:T(8,128)(2,1)S(1)} %get-tuple-element.68.refs_1_, bf16[4,1536,128]{2,1,0:T(8,128)(2,1)S(1)} %get-tuple-element.49.refs_2_.refs_6_, ...), custom_call_target="tpu_custom_call" | custom-call | flops 1811939328 | bytes 8000000 | tf_op jit(solution)/shard_map/pallas_call | solution.py:193
  141.7 3.1 %shard_map.74 = f32[512,384]{1,0:T(8,128)S(1)} custom-call(s32[4]{0:T(128)S(1)} %get-tuple-element.72.target_ref, bf16[4,128,1536]{2,1,0:T(8,128)(2,1)S(1)} %get-tuple-element.67.refs_0_, bf16[4,128,1536]{2,1,0:T(8,128)(2,1)S(1)} %get-tuple-element.68.refs_1_, bf16[4,1536,128]{2,1,0:T(8,128)(2,1)S(1)} %get-tuple-element.49.refs_2_.refs_6_, ...), custom_call_target="tpu_custom_call" | custom-call | flops 1811939328 | bytes 8000000 | tf_op jit(solution)/shard_map/pallas_call | solution.py:193
  145.6 3.1 %shard_map.75 = f32[512,384]{1,0:T(8,128)S(1)} custom-call(s32[4]{0:T(128)S(1)} %get-tuple-element.72.target_ref, bf16[4,128,1536]{2,1,0:T(8,128)(2,1)S(1)} %get-tuple-element.67.refs_0_, bf16[4,128,1536]{2,1,0:T(8,128)(2,1)S(1)} %get-tuple-element.68.refs_1_, bf16[4,1536,128]{2,1,0:T(8,128)(2,1)S(1)} %get-tuple-element.49.refs_2_.refs_6_, ...), custom_call_target="tpu_custom_call" | custom-call | flops 1811939328 | bytes 8000000 | tf_op jit(solution)/shard_map/pallas_call | solution.py:193
  157.0 36.5 %collective-permute-done.29 = f32[256,384]{1,0:T(8,128)S(1)} collective-permute-done((f32[256,384]{1,0:T(8,128)S(1)}, f32[256,384]{1,0:T(8,128)S(1)}, u32[]{:S(2)}, u32[]{:S(2)}) %collective-permute-start.29) | collective-permute-done | bytes 393248 | tf_op jit(solution)/shard_map/ppermute | solution.py:278
  195.5 5.1 %collective-permute-start.32 = (f32[128,256]{1,0:T(8,128)S(1)}, f32[128,256]{1,0:T(8,128)S(1)}, u32[]{:S(2)}, u32[]{:S(2)}) collective-permute-start(f32[128,256]{1,0:T(8,128)S(1)} %slice.21), channel_id=1, source_target_pairs={{4,4},{5,12},{6,20},{7,28},{12,5},{13,13},{14,21},{15,29},{20,6},{... | collective-permute-start | bytes 393224 | tf_op jit(solution)/shard_map/ppermute | solution.py:278
  204.0 6.0 %collective-permute-done.31.turn_e_ref = f32[128,128]{1,0:T(8,128)S(1)} collective-permute-done((f32[128,128]{1,0:T(8,128)S(1)}, f32[128,128]{1,0:T(8,128)S(1)}, u32[]{:S(2)}, u32[]{:S(2)}) %collective-permute-start.31) | collective-permute-done | bytes 65568 | tf_op jit(solution)/shard_map/ppermute | solution.py:278
  (80 shorter events, 43.9 us)
Async XLA Ops:
  1.8 18.3 %collective-permute-start = (f32[1536,128]{1,0:T(8,128)S(1)}, f32[1536,128]{1,0:T(8,128)S(1)}, u32[]{:S(2)}, u32[]{:S(2)}) collective-permute-start(f32[1536,128]{1,0:T(8,128)S(1)} %slice.15.own_ref.rest_0_), channel_id=1, source_target_pairs={{0,4},{4,0},{8,12},{12,8},{16,20},{20,16},{24,28},{28,24},{1,5},{5... | collective-permute-start | bytes 2359304 | tf_op jit(solution)/shard_map/ppermute | solution.py:131
  2.6 20.7 %collective-permute-start.1 = (f32[1536,128]{1,0:T(8,128)S(1)}, f32[1536,128]{1,0:T(8,128)S(1)}, u32[]{:S(2)}, u32[]{:S(2)}) collective-permute-start(f32[1536,128]{1,0:T(8,128)S(1)} %slice.15.own_ref.rest_0_), channel_id=1, source_target_pairs={{0,28},{4,8},{8,4},{12,16},{16,12},{20,24},{24,20},{28,0},{1,29},{... | collective-permute-start | bytes 2359304 | tf_op jit(solution)/shard_map/ppermute | solution.py:131
  5.7 25.7 %collective-permute-start.4 = (f32[1536,128]{1,0:T(8,128)S(1)}, f32[1536,128]{1,0:T(8,128)S(1)}, u32[]{:S(2)}, u32[]{:S(2)}) collective-permute-start(f32[1536,128]{1,0:T(8,128)S(1)} %get-tuple-element.84.own_ref.rest_0_), channel_id=1, source_target_pairs={{0,4},{4,0},{8,12},{12,8},{16,20},{20,16},{24,28},{28,24},{1,5},{5... | collective-permute-start | bytes 2359304 | tf_op jit(solution)/shard_map/ppermute | solution.py:131
  5.8 34.3 %collective-permute-start.5 = (f32[1536,128]{1,0:T(8,128)S(1)}, f32[1536,128]{1,0:T(8,128)S(1)}, u32[]{:S(2)}, u32[]{:S(2)}) collective-permute-start(f32[1536,128]{1,0:T(8,128)S(1)} %get-tuple-element.84.own_ref.rest_0_), channel_id=1, source_target_pairs={{0,28},{4,8},{8,4},{12,16},{16,12},{20,24},{24,20},{28,0},{1,29},{... | collective-permute-start | bytes 2359304 | tf_op jit(solution)/shard_map/ppermute | solution.py:131
  30.1 16.9 %collective-permute-start.2 = (f32[1536,128]{1,0:T(8,128)S(1)}, f32[1536,128]{1,0:T(8,128)S(1)}, u32[]{:S(2)}, u32[]{:S(2)}) collective-permute-start(f32[1536,128]{1,0:T(8,128)S(1)} %shard_map.60.own_ref), channel_id=1, source_target_pairs={{0,4},{4,0},{8,12},{12,8},{16,20},{20,16},{24,28},{28,24},{1,5},{5... | collective-permute-start | bytes 2359304 | tf_op jit(solution)/shard_map/ppermute | solution.py:131
  30.2 26.8 %collective-permute-start.3 = (f32[1536,128]{1,0:T(8,128)S(1)}, f32[1536,128]{1,0:T(8,128)S(1)}, u32[]{:S(2)}, u32[]{:S(2)}) collective-permute-start(f32[1536,128]{1,0:T(8,128)S(1)} %shard_map.60.own_ref), channel_id=1, source_target_pairs={{0,28},{4,8},{8,4},{12,16},{16,12},{20,24},{24,20},{28,0},{1,29},{... | collective-permute-start | bytes 2359304 | tf_op jit(solution)/shard_map/ppermute | solution.py:131
  31.5 33.1 %collective-permute-start.8 = (f32[1536,128]{1,0:T(8,128)S(1)}, f32[1536,128]{1,0:T(8,128)S(1)}, u32[]{:S(2)}, u32[]{:S(2)}) collective-permute-start(f32[1536,128]{1,0:T(8,128)S(1)} %get-tuple-element.85.own_ref.rest_0_), channel_id=1, source_target_pairs={{0,4},{4,0},{8,12},{12,8},{16,20},{20,16},{24,28},{28,24},{1,5},{5... | collective-permute-start | bytes 2359304 | tf_op jit(solution)/shard_map/ppermute | solution.py:131
  31.5 42.4 %collective-permute-start.9 = (f32[1536,128]{1,0:T(8,128)S(1)}, f32[1536,128]{1,0:T(8,128)S(1)}, u32[]{:S(2)}, u32[]{:S(2)}) collective-permute-start(f32[1536,128]{1,0:T(8,128)S(1)} %get-tuple-element.85.own_ref.rest_0_), channel_id=1, source_target_pairs={{0,28},{4,8},{8,4},{12,16},{16,12},{20,24},{24,20},{28,0},{1,29},{... | collective-permute-start | bytes 2359304 | tf_op jit(solution)/shard_map/ppermute | solution.py:131
  46.9 37.0 %collective-permute-start.6 = (f32[1536,128]{1,0:T(8,128)S(1)}, f32[1536,128]{1,0:T(8,128)S(1)}, u32[]{:S(2)}, u32[]{:S(2)}) collective-permute-start(f32[1536,128]{1,0:T(8,128)S(1)} %shard_map.62.own_ref), channel_id=1, source_target_pairs={{0,4},{4,0},{8,12},{12,8},{16,20},{20,16},{24,28},{28,24},{1,5},{5... | collective-permute-start | bytes 2359304 | tf_op jit(solution)/shard_map/ppermute | solution.py:131
  47.0 43.6 %collective-permute-start.7 = (f32[1536,128]{1,0:T(8,128)S(1)}, f32[1536,128]{1,0:T(8,128)S(1)}, u32[]{:S(2)}, u32[]{:S(2)}) collective-permute-start(f32[1536,128]{1,0:T(8,128)S(1)} %shard_map.62.own_ref), channel_id=1, source_target_pairs={{0,28},{4,8},{8,4},{12,16},{16,12},{20,24},{24,20},{28,0},{1,29},{... | collective-permute-start | bytes 2359304 | tf_op jit(solution)/shard_map/ppermute | solution.py:131
  63.8 33.7 %collective-permute-start.12 = (f32[1536,128]{1,0:T(8,128)S(1)}, f32[1536,128]{1,0:T(8,128)S(1)}, u32[]{:S(2)}, u32[]{:S(2)}) collective-permute-start(f32[1536,128]{1,0:T(8,128)S(1)} %shard_map.61.refs_0_), channel_id=1, source_target_pairs={{0,2},{7,5},{8,10},{15,13},{16,18},{23,21},{24,26},{31,29}} | collective-permute-start | bytes 2359304 | tf_op jit(solution)/shard_map/ppermute | solution.py:278
  64.5 33.7 %collective-permute-start.13 = (f32[1536,128]{1,0:T(8,128)S(1)}, f32[1536,128]{1,0:T(8,128)S(1)}, u32[]{:S(2)}, u32[]{:S(2)}) collective-permute-start(f32[1536,128]{1,0:T(8,128)S(1)} %shard_map.61.refs_0_), channel_id=1, source_target_pairs={{1,2},{6,5},{9,10},{14,13},{17,18},{22,21},{25,26},{30,29}} | collective-permute-start | bytes 2359304 | tf_op jit(solution)/shard_map/ppermute | solution.py:278
  73.8 25.2 %collective-permute-start.14 = (f32[1536,128]{1,0:T(8,128)S(1)}, f32[1536,128]{1,0:T(8,128)S(1)}, u32[]{:S(2)}, u32[]{:S(2)}) collective-permute-start(f32[1536,128]{1,0:T(8,128)S(1)} %shard_map.61.refs_0_), channel_id=1, source_target_pairs={{3,2},{4,5},{11,10},{12,13},{19,18},{20,21},{27,26},{28,29}} | collective-permute-start | bytes 2359304 | tf_op jit(solution)/shard_map/ppermute | solution.py:278
  83.9 23.1 %collective-permute-start.10 = (f32[1536,128]{1,0:T(8,128)S(1)}, f32[1536,128]{1,0:T(8,128)S(1)}, u32[]{:S(2)}, u32[]{:S(2)}) collective-permute-start(f32[1536,128]{1,0:T(8,128)S(1)} %shard_map.64.own_ref), channel_id=1, source_target_pairs={{0,28},{4,8},{8,4},{12,16},{16,12},{20,24},{24,20},{28,0},{1,29},{... | collective-permute-start | bytes 2359304 | tf_op jit(solution)/shard_map/ppermute | solution.py:131
  97.5 17.8 %collective-permute-start.15 = (f32[1536,128]{1,0:T(8,128)S(1)}, f32[1536,128]{1,0:T(8,128)S(1)}, u32[]{:S(2)}, u32[]{:S(2)}) collective-permute-start(f32[1536,128]{1,0:T(8,128)S(1)} %shard_map.63.refs_0_), channel_id=1, source_target_pairs={{0,2},{7,5},{8,10},{15,13},{16,18},{23,21},{24,26},{31,29}} | collective-permute-start | bytes 2359304 | tf_op jit(solution)/shard_map/ppermute | solution.py:278
  98.3 21.5 %collective-permute-start.16 = (f32[1536,128]{1,0:T(8,128)S(1)}, f32[1536,128]{1,0:T(8,128)S(1)}, u32[]{:S(2)}, u32[]{:S(2)}) collective-permute-start(f32[1536,128]{1,0:T(8,128)S(1)} %shard_map.63.refs_0_), channel_id=1, source_target_pairs={{1,2},{6,5},{9,10},{14,13},{17,18},{22,21},{25,26},{30,29}} | collective-permute-start | bytes 2359304 | tf_op jit(solution)/shard_map/ppermute | solution.py:278
  99.0 21.7 %collective-permute-start.17 = (f32[1536,128]{1,0:T(8,128)S(1)}, f32[1536,128]{1,0:T(8,128)S(1)}, u32[]{:S(2)}, u32[]{:S(2)}) collective-permute-start(f32[1536,128]{1,0:T(8,128)S(1)} %shard_map.63.refs_0_), channel_id=1, source_target_pairs={{3,2},{4,5},{11,10},{12,13},{19,18},{20,21},{27,26},{28,29}} | collective-permute-start | bytes 2359304 | tf_op jit(solution)/shard_map/ppermute | solution.py:278
  113.9 22.3 %collective-permute-start.18 = (f32[1536,128]{1,0:T(8,128)S(1)}, f32[1536,128]{1,0:T(8,128)S(1)}, u32[]{:S(2)}, u32[]{:S(2)}) collective-permute-start(f32[1536,128]{1,0:T(8,128)S(1)} %shard_map.66.refs_0_), channel_id=1, source_target_pairs={{0,2},{7,5},{8,10},{15,13},{16,18},{23,21},{24,26},{31,29}} | collective-permute-start | bytes 2359304 | tf_op jit(solution)/shard_map/ppermute | solution.py:278
  114.6 22.5 %collective-permute-start.19 = (f32[1536,128]{1,0:T(8,128)S(1)}, f32[1536,128]{1,0:T(8,128)S(1)}, u32[]{:S(2)}, u32[]{:S(2)}) collective-permute-start(f32[1536,128]{1,0:T(8,128)S(1)} %shard_map.66.refs_0_), channel_id=1, source_target_pairs={{1,2},{6,5},{9,10},{14,13},{17,18},{22,21},{25,26},{30,29}} | collective-permute-start | bytes 2359304 | tf_op jit(solution)/shard_map/ppermute | solution.py:278
  115.3 21.8 %collective-permute-start.20 = (f32[1536,128]{1,0:T(8,128)S(1)}, f32[1536,128]{1,0:T(8,128)S(1)}, u32[]{:S(2)}, u32[]{:S(2)}) collective-permute-start(f32[1536,128]{1,0:T(8,128)S(1)} %shard_map.66.refs_0_), channel_id=1, source_target_pairs={{3,2},{4,5},{11,10},{12,13},{19,18},{20,21},{27,26},{28,29}} | collective-permute-start | bytes 2359304 | tf_op jit(solution)/shard_map/ppermute | solution.py:278
  131.6 17.9 %collective-permute-start.23 = (f32[512,384]{1,0:T(8,128)S(1)}, f32[512,384]{1,0:T(8,128)S(1)}, u32[]{:S(2)}, u32[]{:S(2)}) collective-permute-start(f32[512,384]{1,0:T(8,128)S(1)} %shard_map.70), channel_id=1, source_target_pairs={{2,18},{5,21},{10,26},{13,29},{18,2},{21,5},{26,10},{29,13}} | collective-permute-start | bytes 2359304 | tf_op jit(solution)/shard_map/ppermute | solution.py:278
  132.3 21.0 %collective-permute-start.22 = (f32[512,384]{1,0:T(8,128)S(1)}, f32[512,384]{1,0:T(8,128)S(1)}, u32[]{:S(2)}, u32[]{:S(2)}) collective-permute-start(f32[512,384]{1,0:T(8,128)S(1)} %shard_map.69), channel_id=1, source_target_pairs={{2,10},{5,13},{10,2},{13,5},{18,26},{21,29},{26,18},{29,21}} | collective-permute-start | bytes 2359304 | tf_op jit(solution)/shard_map/ppermute | solution.py:278
  136.2 17.2 %collective-permute-start.21 = (f32[512,384]{1,0:T(8,128)S(1)}, f32[512,384]{1,0:T(8,128)S(1)}, u32[]{:S(2)}, u32[]{:S(2)}) collective-permute-start(f32[512,384]{1,0:T(8,128)S(1)} %shard_map.68), channel_id=1, source_target_pairs={{2,26},{5,29},{10,18},{13,21},{18,10},{21,13},{26,2},{29,5}} | collective-permute-start | bytes 2359304 | tf_op jit(solution)/shard_map/ppermute | solution.py:278
  155.7 37.8 %collective-permute-start.29 = (f32[256,384]{1,0:T(8,128)S(1)}, f32[256,384]{1,0:T(8,128)S(1)}, u32[]{:S(2)}, u32[]{:S(2)}) collective-permute-start(f32[256,384]{1,0:T(8,128)S(1)} %get-tuple-element.79), channel_id=1, source_target_pairs={{2,3},{5,4},{10,11},{13,12},{18,19},{21,20},{26,27},{29,28}} | collective-permute-start | bytes 1179656 | tf_op jit(solution)/shard_map/ppermute | solution.py:278
  (11 other events, 70.7 us)

commit v7 on v6

--- a/solution.py
+++ b/solution.py
@@ -135,68 +135,88 @@
     return lax.optimization_barrier((x, done))[0]
 
 
-def prep_kernel(band_ref, *refs):
-    ins, (hi_ref, lo_ref, thi_ref, tlo_ref) = refs[:4], refs[4:]
+def store_parts(band_ref, ins, outs):
+    hi_ref, lo_ref, thi_ref, tlo_ref = outs
     for place, ref in enumerate(ins):
-        band = band_ref[place]
         x = ref[...]
-        hi_ref[band], lo_ref[band] = split(x)
-        thi_ref[band], tlo_ref[band] = split(x.T)
-
-
-def prep(bands, parts):
+        width = x.shape[1]
+        there = pl.ds(pl.multiple_of(band_ref[place] * width, width), width)
+        hi_ref[:, there], lo_ref[:, there] = split(x)
+        thi_ref[there, :], tlo_ref[there, :] = split(x.T)
+
+
+def block_row(target, turned, right):
+    rows = turned[0][0].shape[0] // 4
+    there = pl.ds(pl.multiple_of(target * rows, rows), rows)
+    thi = jnp.concatenate([hi[there, :] for hi, lo in turned], axis=0)
+    tlo = jnp.concatenate([lo[there, :] for hi, lo in turned], axis=0)
+    hi_ref, lo_ref = right
+    total = jnp.dot(thi, lo_ref[...], preferred_element_type=jnp.float32)
+    total += jnp.dot(tlo, hi_ref[...], preferred_element_type=jnp.float32)
+    return total + jnp.dot(thi, hi_ref[...], preferred_element_type=jnp.float32)
+
+
+def chunk_kernel(band_ref, target_ref, *refs, before, places, upper):
+    ins, refs = refs[:4], refs[4:]
+    olds, refs = [refs[4 * k : 4 * k + 4] for k in range(before)], refs[4 * before :]
+    old_products, refs = (refs[: len(places)], refs[len(places) :]) if upper else ((), refs)
+    new, outs = refs[:4], refs[4:]
+    store_parts(band_ref, ins, new)
+    turned = [x[2:] for x in olds] + [new[2:]]
+    for k, place in enumerate(places):
+        total = block_row(target_ref[place], turned, new[:2])
+        if upper:
+            high = old_products[k].shape[0]
+            outs[k][pl.ds(0, high), :] = old_products[k][...]
+            outs[k][pl.ds(high, total.shape[0]), :] = total
+        else:
+            outs[k][...] = total
+
+
+def chunk(bands, targets, parts, olds, places, old_products=()):
     rows, width = parts[0].shape
-    plain = pltpu.VMEM((4, rows, width), jnp.bfloat16)
-    turned = pltpu.VMEM((4, width, rows), jnp.bfloat16)
-    return pl.pallas_call(
-        prep_kernel,
-        in_specs=[pl.BlockSpec(memory_space=pltpu.SMEM)] + [pl.BlockSpec(memory_space=pltpu.VMEM)] * 4,
-        out_specs=[pl.BlockSpec(memory_space=pltpu.VMEM)] * 4,
-        out_shape=[plain, plain, turned, turned],
-        compiler_params=pltpu.CompilerParams(vmem_limit_bytes=16 * MIB),
-        cost_estimate=pl.CostEstimate(flops=0, bytes_accessed=32 * rows * width, transcendentals=0),
-    )(bands, *parts)
-
-
-def product_kernel(target_ref, *refs, shapes, place):
-    *ins, out_ref = refs
-    target = target_ref[place]
-    start = 0
-    for columns in shapes:
-        left, ins = ins[:2], ins[2:]
-        right, ins = ins[: 2 * columns], ins[2 * columns :]
-        count, width, rows = left[0].shape
-        thi, tlo = (ref[...].reshape(count * width, rows) for ref in left)
-        his = jnp.concatenate([ref[target] for ref in right[:columns]], axis=1)
-        los = jnp.concatenate([ref[target] for ref in right[columns:]], axis=1)
-        total = jnp.dot(thi, los, preferred_element_type=jnp.float32)
-        total += jnp.dot(tlo, his, preferred_element_type=jnp.float32)
-        total += jnp.dot(thi, his, preferred_element_type=jnp.float32)
-        out_ref[:, pl.ds(start, his.shape[1])] = total
-        start += his.shape[1]
-
-
-def products(targets, place, chunks, lines):
-    ins, shapes, size, flops = [], [], 0, 0
-    for line in lines:
-        _, _, thi, tlo = chunks[line]
-        four, width, rows = thi.shape
-        ins += [thi, tlo]
-        for part in (0, 1):
-            ins += [chunks[c][part] for c in range(line + 1)]
-        wide = sum(chunks[c][0].shape[2] for c in range(line + 1))
-        shapes.append(line + 1)
-        size += wide
-        flops += 6 * four * width * rows * wide
+    plain = pltpu.VMEM((rows, 4 * width), jnp.bfloat16)
+    turned = pltpu.VMEM((4 * width, rows), jnp.bfloat16)
+    high = width * (len(olds) + 1) + (old_products[0].shape[0] if old_products else 0)
+    product = jax.ShapeDtypeStruct((high, 4 * width), jnp.float32)
+    olds = [pltpu.with_memory_space_constraint(x, pltpu.VMEM) for old in olds for x in old]
+    ins = [*parts, *olds, *old_products]
+    vmem, smem = pl.BlockSpec(memory_space=pltpu.VMEM), pl.BlockSpec(memory_space=pltpu.SMEM)
+    out = pl.pallas_call(
+        functools.partial(
+            chunk_kernel, before=len(olds) // 4, places=places, upper=bool(old_products)
+        ),
+        in_specs=[smem, smem] + [vmem] * len(ins),
+        out_specs=[vmem] * (4 + len(places)),
+        out_shape=[plain, plain, turned, turned] + [product] * len(places),
+        compiler_params=pltpu.CompilerParams(vmem_limit_bytes=18 * MIB),
+        cost_estimate=pl.CostEstimate(
+            flops=24 * len(places) * high * width * rows, bytes_accessed=8_000_000, transcendentals=0
+        ),
+    )(bands, targets, *ins)
+    return out[:4], list(out[4:])
+
+
+def product_kernel(target_ref, *refs, place):
+    out_ref = refs[-1]
+    out_ref[...] = block_row(target_ref[place], [refs[k : k + 2] for k in range(2, len(refs) - 1, 2)], refs[:2])
+
+
+def product(targets, place, chunks):
+    rows, wide = chunks[-1][0].shape
+    ins = [*chunks[-1][:2]] + [x for c in chunks for x in c[2:]]
     ins = [pltpu.with_memory_space_constraint(x, pltpu.VMEM) for x in ins]
+    high = wide // 4 * len(chunks)
     vmem = pl.BlockSpec(memory_space=pltpu.VMEM)
     return pl.pallas_call(
-        functools.partial(product_kernel, shapes=shapes, place=place),
+        functools.partial(product_kernel, place=place),
         in_specs=[pl.BlockSpec(memory_space=pltpu.SMEM)] + [vmem] * len(ins),
         out_specs=vmem,
-        out_shape=jax.ShapeDtypeStruct((four * width, size), jnp.float32),
+        out_shape=jax.ShapeDtypeStruct((high, wide), jnp.float32),
         compiler_params=pltpu.CompilerParams(vmem_limit_bytes=16 * MIB),
-        cost_estimate=pl.CostEstimate(flops=flops, bytes_accessed=8_000_000, transcendentals=0),
+        cost_estimate=pl.CostEstimate(
+            flops=6 * high * wide * rows, bytes_accessed=4_000_000, transcendentals=0
+        ),
     )(targets, *ins)
 
 
@@ -219,21 +239,21 @@
 
 def pick_kernel(goal_ref, early_ref, *refs):
     ins, outs = refs[:4], refs[4:]
-    rows = early_ref.shape[0] // 4
+    rows, width = early_ref.shape[0], early_ref.shape[1] // 4
     for k, out in enumerate(outs):
-        there = pl.ds(pl.multiple_of(goal_ref[k] * rows, rows), rows)
-        x, y, u, v = (ref[there, :] for ref in ins)
+        there = pl.ds(pl.multiple_of(goal_ref[k] * width, width), width)
+        x, y, u, v = (ref[:, there] for ref in ins)
         late = (x + y) + (u + v)
-        early = early_ref[there, :]
+        early = early_ref[:, there]
         if k == 3:
             early, late = (jnp.where(goal_ref[4] > 0, x, 0.0) for x in (early, late))
         out[pl.ds(0, rows), :] = early
         out[pl.ds(rows, rows), :] = late
 
 
-def pick(goals, early, *parts):
-    rows, size = parts[0].shape
-    shape = jax.ShapeDtypeStruct((rows // 2, size), jnp.float32)
+def pick(goals, early, *late):
+    rows, size = early.shape
+    shape = jax.ShapeDtypeStruct((2 * rows, size // 4), jnp.float32)
     vmem = pl.BlockSpec(memory_space=pltpu.VMEM)
     return pl.pallas_call(
         pick_kernel,
@@ -242,32 +262,31 @@
         out_shape=[shape] * 4,
         compiler_params=pltpu.CompilerParams(vmem_limit_bytes=12 * MIB),
         cost_estimate=pl.CostEstimate(flops=0, bytes_accessed=3_000_000, transcendentals=0),
-    )(goals, early, *parts)
+    )(goals, early, *late)
 
 
 def assemble_kernel(core_ref, piece_ref, turn_e_ref, turn_l_ref, out_ref, *, scale):
-    w = turn_e_ref.shape[0]
-    early, last = piece_ref[:w, :], piece_ref[w:, :]
-    turned = turn_l_ref[...].T
-    first = jnp.concatenate([early[:, :w], turn_e_ref[...].T, turned[:w]], axis=1)
-    second = jnp.concatenate([early[:, w:], turned[w:]], axis=1)
-    half = out_ref.shape[1]
+    w = piece_ref.shape[1]
+    first = jnp.concatenate([piece_ref[:w, :], turn_e_ref[...].T, turn_l_ref[:w, :].T], axis=0)
+    second = jnp.concatenate([piece_ref[w : 3 * w, :], turn_l_ref[w:, :].T], axis=0)
+    last = piece_ref[3 * w :, :]
+    half = out_ref.shape[0]
     is_first = core_ref[0] == 0
     for k, x in enumerate((first, second, last)):
-        out_ref[pl.ds(k * w, w), :] = jnp.where(is_first, x[:, :half], x[:, half:]) * scale
+        out_ref[:, pl.ds(k * w, w)] = jnp.where(is_first, x[:half], x[half:]) * scale
 
 
 def assemble(core, parts, order):
-    w = parts[0].shape[0] // 2
+    w = parts[0].shape[1]
     vmem = pl.BlockSpec(memory_space=pltpu.VMEM)
     return pl.pallas_call(
         functools.partial(assemble_kernel, scale=1.0 / order),
         in_specs=[pl.BlockSpec(memory_space=pltpu.SMEM)] + [vmem] * len(parts),
         out_specs=vmem,
-        out_shape=jax.ShapeDtypeStruct((3 * w, 3 * w // 2), jnp.float32),
+        out_shape=jax.ShapeDtypeStruct((3 * w // 2, 3 * w), jnp.float32),
         compiler_params=pltpu.CompilerParams(vmem_limit_bytes=12 * MIB),
         cost_estimate=pl.CostEstimate(flops=0, bytes_accessed=2_000_000, transcendentals=0),
-    )(core, *parts)
+    )(core, *parts).T
 
 
 def linear(chip, core, z):
@@ -300,6 +319,7 @@
 
 
 FLIPS = (3, 1, 2, 0)
+ALL = (0, 1, 2, 3)
 EVERY = [(q, c, z) for q in range(4) for c in range(2) for z in range(4)]
 SWAP = [(linear(q, c, z), linear(q, 1 - c, z)) for q, c, z in EVERY]
 TURN = [(linear(q, c, z), linear(z, c, q)) for q, c, z in EVERY]
@@ -339,13 +359,6 @@
 
     def one(x, halo, v=None, turned=False):
         return apply_step(core, hi, lo, halo, x, v, turned)
-
-    def over_all_chips(chunks, lines, first_after):
-        parts, before = [], first_after
-        for k, flip in enumerate(FLIPS):
-            parts.append(products(after_that(targets, before), k, chunks, lines))
-            before = parts[-1]
-        return [send(x, over_chips(flip)) if flip else x for x, flip in zip(parts, FLIPS)], before
 
     v0, v1, v2 = old
     hv = [neighbours(x) for x in old]
@@ -359,23 +372,27 @@
     z0 = gather_bands(g0)
     g1 = one(after_that(f1, g0), hf1, v1)
     z1 = gather_bands(g1)
-    chunks = [prep(bands, [after_that(z0[0], g1)] + z0[1:])]
-    g2 = one(after_that(f2, chunks[0][0]), hf2, v2, turned=True)
+    c0, upper = chunk(bands, targets, [after_that(z0[0], g1)] + z0[1:], [], ALL)
+    g2 = one(after_that(f2, upper[0]), hf2, v2, turned=True)
     z2 = gather_bands(g2)
-    chunks.append(prep(bands, [after_that(z1[0], g2)] + z1[1:]))
-    early, last = over_all_chips(chunks, (0, 1), g2)
-    chunks.append(prep(bands, [after_that(z2[0], last)] + z2[1:]))
-    late, last = over_all_chips(chunks, (2,), chunks[2][0])
-    early[3] = after_that(early[3], last)
-    moved = pick(goals, sum_parts(*early), *late)
+    c1, early = chunk(bands, targets, [after_that(z1[0], g2)] + z1[1:], [c0], ALL, upper)
+    early = [send(x, over_chips(flip)) if flip else x for x, flip in zip(early, FLIPS)]
+    c2, late = chunk(bands, targets, [after_that(z2[0], c1[0])] + z2[1:], [c0, c1], (0,))
+    for k in (1, 2):
+        late.append(product(after_that(targets, late[-1]), k, [c0, c1, c2]))
+    last = late[-1]
+    late = [send(x, over_chips(flip)) for x, flip in zip(late, FLIPS)]
+    early_sum = sum_parts(after_that(early[0], last), *early[1:])
+    late.append(product(after_that(targets, early_sum, late[0]), 3, [c0, c1, c2]))
+    moved = pick(goals, early_sum, *late)
     piece = moved[3]
     for k, x in zip((0, 1, 3), moved):
         piece = piece + send(x, mirrored([(2, k)]))
-    filtered = jnp.concatenate([g0, g1, after_that(g2, last)], axis=1)
+    filtered = jnp.concatenate([g0, g1, after_that(g2, late[3])], axis=1)
     piece = piece + send(piece, SWAP)
     w = v0.shape[1]
-    turn_e = send(piece[:w, w : 2 * w], TURN)
-    turn_l = send(piece[w:, : 2 * w], TURN_UP)
+    turn_e = send(piece[w : 2 * w], TURN)
+    turn_l = send(piece[3 * w : 5 * w], TURN_UP)
     return filtered, assemble(core, [piece, turn_e, turn_l], order)
 
 

time: 212 us -> 201 us (0.948)
  Pallas kernels: 84.4 us -> 78.2 us
  waiting for transfers between devices: 80.8 us -> 75.3 us
    pallas_call x11 -> x6, Pallas kernels: 29.5 us -> 22.4 us  [the longest x3 14.8 us: chunk(): pl.pallas_call(functools.partial(chunk_kernel, before=len(olds) // 4, pla...]
    ppermute x21, waiting for transfers between devices: 45.2 us -> 41.7 us  [send(): return lax.ppermute(x, ('orb', 'band'), pairs)]
  transfers between devices with their start and end apart: 33 -> 33, of which waited for: 10 -> 10; matrix products, arithmetic and copies ran while one was open for 2% -> 2% of each run, Pallas kernels for 39% -> 38%
where the time goes in v7:
time: 201 us; the launch traced here: 200 us
  Pallas kernels  78.2 us (39%)
  waiting for transfers between devices  75.3 us (37%)
  starting transfers between devices  39.1 us (19%)
  local copies, waits for them, and re-layouts  4.21 us (2%)
  other arithmetic  2.04 us (1%)
    ppermute x21, waiting for transfers between devices, send(): return lax.ppermute(x, ('orb', 'band'), pairs)  41.7 us
    pallas_call x6, Pallas kernels, apply_step(): pl.pallas_call(functools.partial(apply_kernel, second=second, turned=turn...  41 us
    ppermute x12, waiting for transfers between devices, neighbours(): return (lax.ppermute(x, 'orb', inside), lax.ppermute(x, 'orb', across))  33.6 us
    ppermute x21, starting transfers between devices, send(): return lax.ppermute(x, ('orb', 'band'), pairs)  30.7 us
    pallas_call x3, Pallas kernels, chunk(): pl.pallas_call(functools.partial(chunk_kernel, before=len(olds) // 4, pla...  14.8 us
    pallas_call x1, Pallas kernels, densify(): pl.pallas_call(functools.partial(densify_kernel, spread=spread, reach=row...  12.8 us
    ppermute x12, starting transfers between devices, neighbours(): return (lax.ppermute(x, 'orb', inside), lax.ppermute(x, 'orb', across))  8.42 us
    pallas_call x3, Pallas kernels, product(): pl.pallas_call(functools.partial(product_kernel, place=place), in_specs=[...  7.56 us
  transfers between devices with their start and end apart: 33, of which 10 were waited for; matrix products, arithmetic and copies ran while one was open for 2% of the time, Pallas kernels for 38%

profile of v7, /device:TPU:3, one launch (start us, length us, event | category | flops | bytes accessed | tf_op | source)
XLA Modules:
  0.0 200.0 jit_solution(13426524167592008064)
XLA Ops:
  7.4 12.8 %shard_map.59 = (bf16[1536,3328]{1,0:T(8,128)(2,1)S(1)}, bf16[1536,3328]{1,0:T(8,128)(2,1)S(1)}) custom-call(s32[24,52]{1,0:T(8,128)S(1)} %select_reduce_fusion.slot_ref, f32[24,32,64,64]{3,2,1,0:T(8,128)} %blocks_ref.1), custom_call_target="tpu_custom_call" | custom-call | bytes 60000000 | tf_op jit(solution)/shard_map/pallas_call | solution.py:52
  20.2 3.1 %collective-permute-done.1.far_ref = f32[1536,128]{1,0:T(8,128)S(1)} collective-permute-done((f32[1536,128]{1,0:T(8,128)S(1)}, f32[1536,128]{1,0:T(8,128)S(1)}, u32[]{:S(2)}, u32[]{:S(2)}) %collective-permute-start.1) | collective-permute-done | bytes 786464 | tf_op jit(solution)/shard_map/ppermute | solution.py:131
  23.3 6.8 %shard_map.60.own_ref = f32[1536,128]{1,0:T(8,128)S(1)} custom-call(s32[1]{0:T(128)} %bitcast.10.core_ref, bf16[1536,3328]{1,0:T(8,128)(2,1)S(1)} %get-tuple-element.47.hi_ref, bf16[1536,3328]{1,0:T(8,128)(2,1)S(1)} %get-tuple-element.48.lo_ref, f32[1536,128]{1,0:T(8,128)S(1)} %collective-permute-done.near_ref, ...), custom_call_target="tpu_custom_call" | custom-call | flops 5234491392 | bytes 20447232 | tf_op jit(solution)/shard_map/pallas_call | solution.py:101
  33.5 6.6 %collective-permute-done.5.far_ref = f32[1536,128]{1,0:T(8,128)S(1)} collective-permute-done((f32[1536,128]{1,0:T(8,128)S(1)}, f32[1536,128]{1,0:T(8,128)S(1)}, u32[]{:S(2)}, u32[]{:S(2)}) %collective-permute-start.5) | collective-permute-done | bytes 786464 | tf_op jit(solution)/shard_map/ppermute | solution.py:131
  40.1 6.8 %shard_map.62.own_ref = f32[1536,128]{1,0:T(8,128)S(1)} custom-call(s32[1]{0:T(128)} %bitcast.10.core_ref, bf16[1536,3328]{1,0:T(8,128)(2,1)S(1)} %get-tuple-element.47.hi_ref, bf16[1536,3328]{1,0:T(8,128)(2,1)S(1)} %get-tuple-element.48.lo_ref, f32[1536,128]{1,0:T(8,128)S(1)} %collective-permute-done.4.near_ref, ...), custom_call_target="tpu_custom_call" | custom-call | flops 5234491392 | bytes 20447232 | tf_op jit(solution)/shard_map/pallas_call | solution.py:101
  48.3 8.6 %collective-permute-done.3.far_ref = f32[1536,128]{1,0:T(8,128)S(1)} collective-permute-done((f32[1536,128]{1,0:T(8,128)S(1)}, f32[1536,128]{1,0:T(8,128)S(1)}, u32[]{:S(2)}, u32[]{:S(2)}) %collective-permute-start.3) | collective-permute-done | bytes 786464 | tf_op jit(solution)/shard_map/ppermute | solution.py:131
  57.0 6.8 %shard_map.61.refs_0_ = f32[1536,128]{1,0:T(8,128)S(1)} custom-call(s32[1]{0:T(128)} %bitcast.10.core_ref, bf16[1536,3328]{1,0:T(8,128)(2,1)S(1)} %get-tuple-element.47.hi_ref, bf16[1536,3328]{1,0:T(8,128)(2,1)S(1)} %get-tuple-element.48.lo_ref, f32[1536,128]{1,0:T(8,128)S(1)} %collective-permute-done.2.near_ref, ...), custom_call_target="tpu_custom_call" | custom-call | flops 5234491392 | bytes 20447232 | tf_op jit(solution)/shard_map/pallas_call | solution.py:101
  65.3 8.6 %collective-permute-done.9.far_ref = f32[1536,128]{1,0:T(8,128)S(1)} collective-permute-done((f32[1536,128]{1,0:T(8,128)S(1)}, f32[1536,128]{1,0:T(8,128)S(1)}, u32[]{:S(2)}, u32[]{:S(2)}) %collective-permute-start.9) | collective-permute-done | bytes 786464 | tf_op jit(solution)/shard_map/ppermute | solution.py:131
  73.8 3.2 %collective-permute-start.14 = (f32[1536,128]{1,0:T(8,128)S(1)}, f32[1536,128]{1,0:T(8,128)S(1)}, u32[]{:S(2)}, u32[]{:S(2)}) collective-permute-start(f32[1536,128]{1,0:T(8,128)S(1)} %shard_map.61.refs_0_), channel_id=1, source_target_pairs={{3,2},{4,5},{11,10},{12,13},{19,18},{20,21},{27,26},{28,29}} | collective-permute-start | bytes 2359304 | tf_op jit(solution)/shard_map/ppermute | solution.py:297
  77.1 6.8 %shard_map.64.own_ref = f32[1536,128]{1,0:T(8,128)S(1)} custom-call(s32[1]{0:T(128)} %bitcast.10.core_ref, bf16[1536,3328]{1,0:T(8,128)(2,1)S(1)} %get-tuple-element.47.hi_ref, bf16[1536,3328]{1,0:T(8,128)(2,1)S(1)} %get-tuple-element.48.lo_ref, f32[1536,128]{1,0:T(8,128)S(1)} %collective-permute-done.8.near_ref, ...), custom_call_target="tpu_custom_call" | custom-call | flops 5234491392 | bytes 20447232 | tf_op jit(solution)/shard_map/pallas_call | solution.py:101
  84.0 6.7 %collective-permute-done.7.far_ref = f32[1536,128]{1,0:T(8,128)S(1)} collective-permute-done((f32[1536,128]{1,0:T(8,128)S(1)}, f32[1536,128]{1,0:T(8,128)S(1)}, u32[]{:S(2)}, u32[]{:S(2)}) %collective-permute-start.7) | collective-permute-done | bytes 786464 | tf_op jit(solution)/shard_map/ppermute | solution.py:131
  90.7 6.8 %shard_map.63.refs_0_ = f32[1536,128]{1,0:T(8,128)S(1)} custom-call(s32[1]{0:T(128)} %bitcast.10.core_ref, bf16[1536,3328]{1,0:T(8,128)(2,1)S(1)} %get-tuple-element.47.hi_ref, bf16[1536,3328]{1,0:T(8,128)(2,1)S(1)} %get-tuple-element.48.lo_ref, f32[1536,128]{1,0:T(8,128)S(1)} %collective-permute-done.6.near_ref, ...), custom_call_target="tpu_custom_call" | custom-call | flops 5234491392 | bytes 20447232 | tf_op jit(solution)/shard_map/pallas_call | solution.py:101
  99.0 4.6 %collective-permute-start.17 = (f32[1536,128]{1,0:T(8,128)S(1)}, f32[1536,128]{1,0:T(8,128)S(1)}, u32[]{:S(2)}, u32[]{:S(2)}) collective-permute-start(f32[1536,128]{1,0:T(8,128)S(1)} %shard_map.63.refs_0_), channel_id=1, source_target_pairs={{3,2},{4,5},{11,10},{12,13},{19,18},{20,21},{27,26},{28,29}} | collective-permute-start | bytes 2359304 | tf_op jit(solution)/shard_map/ppermute | solution.py:297
  103.6 4.4 %shard_map.65 = (bf16[1536,512]{1,0:T(8,128)(2,1)S(1)}, bf16[1536,512]{1,0:T(8,128)(2,1)S(1)}, bf16[512,1536]{1,0:T(8,128)(2,1)S(1)}, bf16[512,1536]{1,0:T(8,128...) custom-call(s32[4]{0:T(128)S(1)} %get-tuple-element.51.band_ref, ...), custom_call_target="tpu_custom_call" | custom-call | flops 2415919104 | bytes 8000000 | tf_op jit(solution)/shard_map/pallas_call | solution.py:185
  108.0 6.8 %shard_map.66.refs_0_ = f32[1536,128]{1,0:T(8,128)S(1)} custom-call(s32[1]{0:T(128)} %bitcast.10.core_ref, bf16[1536,3328]{1,0:T(8,128)(2,1)S(1)} %get-tuple-element.47.hi_ref, bf16[1536,3328]{1,0:T(8,128)(2,1)S(1)} %get-tuple-element.48.lo_ref, f32[1536,128]{1,0:T(8,128)S(1)} %collective-permute-done.10.near_ref, ...), custom_call_target="tpu_custom_call" | custom-call | flops 5234491392 | bytes 20447232 | tf_op jit(solution)/shard_map/pallas_call | solution.py:101
  116.3 3.5 %collective-permute-start.21 = (f32[1536,128]{1,0:T(8,128)S(1)}, f32[1536,128]{1,0:T(8,128)S(1)}, u32[]{:S(2)}, u32[]{:S(2)}) collective-permute-start(f32[1536,128]{1,0:T(8,128)S(1)} %shard_map.66.refs_0_), channel_id=1, source_target_pairs={{3,2},{4,5},{11,10},{12,13},{19,18},{20,21},{27,26},{28,29}} | collective-permute-start | bytes 2359304 | tf_op jit(solution)/shard_map/ppermute | solution.py:297
  120.6 6.8 %shard_map.67 = (bf16[1536,512]{1,0:T(8,128)(2,1)S(1)}, bf16[1536,512]{1,0:T(8,128)(2,1)S(1)}, bf16[512,1536]{1,0:T(8,128)(2,1)S(1)}, bf16[512,1536]{1,0:T(8,128...) custom-call(s32[4]{0:T(128)S(1)} %get-tuple-element.51.band_ref, ...), custom_call_target="tpu_custom_call" | custom-call | flops 7247757312 | bytes 8000000 | tf_op jit(solution)/shard_map/pallas_call | solution.py:185
  129.6 7.3 %collective-permute-done.21.refs_3_ = f32[1536,128]{1,0:T(8,128)S(1)} collective-permute-done((f32[1536,128]{1,0:T(8,128)S(1)}, f32[1536,128]{1,0:T(8,128)S(1)}, u32[]{:S(2)}, u32[]{:S(2)}) %collective-permute-start.21) | collective-permute-done | bytes 786464 | tf_op jit(solution)/shard_map/ppermute | solution.py:297
  138.3 3.7 %shard_map.68 = (bf16[1536,512]{1,0:T(8,128)(2,1)S(1)}, bf16[1536,512]{1,0:T(8,128)(2,1)S(1)}, bf16[512,1536]{1,0:T(8,128)(2,1)S(1)}, bf16[512,1536]{1,0:T(8,128)(2,1)S(1)}, f32[384,512]{1,0:T(8,128)S(1)}) custom-call(s32[4]{0:T(128)S(1)} %get-tuple-element.51.band_ref, s32[4]{0:T(128)S(1)} %get-tuple-element.81.target_ref, ...), custom_call_target="tpu_custom_call" | custom-call | flops 1811939328 | bytes 8000000 | tf_op jit(solution)/shard_map/pallas_call | solution.py:185
  143.0 2.5 %shard_map.69 = f32[384,512]{1,0:T(8,128)S(1)} custom-call(s32[4]{0:T(128)S(1)} %get-tuple-element.81.target_ref, bf16[1536,512]{1,0:T(8,128)(2,1)S(1)} %get-tuple-element.72.refs_0_, bf16[1536,512]{1,0:T(8,128)(2,1)S(1)} %get-tuple-element.73.refs_1_, bf16[512,1536]{1,0:T(8,128)(2,1)S(1)} %get-tuple-element.59.refs_6_.refs_2_, ...), custom_call_target="tpu_custom_call" | custom-call | flops 1811939328 | bytes 4000000 | tf_op jit(solution)/shard_map/pallas_call | solution.py:211
  145.5 2.5 %shard_map.70 = f32[384,512]{1,0:T(8,128)S(1)} custom-call(s32[4]{0:T(128)S(1)} %get-tuple-element.81.target_ref, bf16[1536,512]{1,0:T(8,128)(2,1)S(1)} %get-tuple-element.72.refs_0_, bf16[1536,512]{1,0:T(8,128)(2,1)S(1)} %get-tuple-element.73.refs_1_, bf16[512,1536]{1,0:T(8,128)(2,1)S(1)} %get-tuple-element.59.refs_6_.refs_2_, ...), custom_call_target="tpu_custom_call" | custom-call | flops 1811939328 | bytes 4000000 | tf_op jit(solution)/shard_map/pallas_call | solution.py:211
  156.0 26.9 %collective-permute-done.29 = f32[768,128]{1,0:T(8,128)S(1)} collective-permute-done((f32[768,128]{1,0:T(8,128)S(1)}, f32[768,128]{1,0:T(8,128)S(1)}, u32[]{:S(2)}, u32[]{:S(2)}) %collective-permute-start.29) | collective-permute-done | bytes 393248 | tf_op jit(solution)/shard_map/ppermute | solution.py:297
  184.9 6.0 %collective-permute-start.32 = (f32[256,128]{1,0:T(8,128)S(1)}, f32[256,128]{1,0:T(8,128)S(1)}, u32[]{:S(2)}, u32[]{:S(2)}) collective-permute-start(f32[256,128]{1,0:T(8,128)S(1)} %slice.21), channel_id=1, source_target_pairs={{4,4},{5,12},{6,20},{7,28},{12,5},{13,13},{14,21},{15,29},{20,6},{... | collective-permute-start | bytes 393224 | tf_op jit(solution)/shard_map/ppermute | solution.py:297
  194.3 4.9 %collective-permute-done.31.turn_e_ref = f32[128,128]{1,0:T(8,128)S(1)} collective-permute-done((f32[128,128]{1,0:T(8,128)S(1)}, f32[128,128]{1,0:T(8,128)S(1)}, u32[]{:S(2)}, u32[]{:S(2)}) %collective-permute-start.31) | collective-permute-done | bytes 65568 | tf_op jit(solution)/shard_map/ppermute | solution.py:297
  (78 shorter events, 35.3 us)
Async XLA Ops:
  1.8 18.3 %collective-permute-start = (f32[1536,128]{1,0:T(8,128)S(1)}, f32[1536,128]{1,0:T(8,128)S(1)}, u32[]{:S(2)}, u32[]{:S(2)}) collective-permute-start(f32[1536,128]{1,0:T(8,128)S(1)} %slice.15.own_ref.rest_0_), channel_id=1, source_target_pairs={{0,4},{4,0},{8,12},{12,8},{16,20},{20,16},{24,28},{28,24},{1,5},{5... | collective-permute-start | bytes 2359304 | tf_op jit(solution)/shard_map/ppermute | solution.py:131
  2.6 20.7 %collective-permute-start.1 = (f32[1536,128]{1,0:T(8,128)S(1)}, f32[1536,128]{1,0:T(8,128)S(1)}, u32[]{:S(2)}, u32[]{:S(2)}) collective-permute-start(f32[1536,128]{1,0:T(8,128)S(1)} %slice.15.own_ref.rest_0_), channel_id=1, source_target_pairs={{0,28},{4,8},{8,4},{12,16},{16,12},{20,24},{24,20},{28,0},{1,29},{... | collective-permute-start | bytes 2359304 | tf_op jit(solution)/shard_map/ppermute | solution.py:131
  5.7 25.7 %collective-permute-start.4 = (f32[1536,128]{1,0:T(8,128)S(1)}, f32[1536,128]{1,0:T(8,128)S(1)}, u32[]{:S(2)}, u32[]{:S(2)}) collective-permute-start(f32[1536,128]{1,0:T(8,128)S(1)} %get-tuple-element.88.own_ref.rest_0_), channel_id=1, source_target_pairs={{0,4},{4,0},{8,12},{12,8},{16,20},{20,16},{24,28},{28,24},{1,5},{5... | collective-permute-start | bytes 2359304 | tf_op jit(solution)/shard_map/ppermute | solution.py:131
  5.8 34.3 %collective-permute-start.5 = (f32[1536,128]{1,0:T(8,128)S(1)}, f32[1536,128]{1,0:T(8,128)S(1)}, u32[]{:S(2)}, u32[]{:S(2)}) collective-permute-start(f32[1536,128]{1,0:T(8,128)S(1)} %get-tuple-element.88.own_ref.rest_0_), channel_id=1, source_target_pairs={{0,28},{4,8},{8,4},{12,16},{16,12},{20,24},{24,20},{28,0},{1,29},{... | collective-permute-start | bytes 2359304 | tf_op jit(solution)/shard_map/ppermute | solution.py:131
  30.1 16.9 %collective-permute-start.2 = (f32[1536,128]{1,0:T(8,128)S(1)}, f32[1536,128]{1,0:T(8,128)S(1)}, u32[]{:S(2)}, u32[]{:S(2)}) collective-permute-start(f32[1536,128]{1,0:T(8,128)S(1)} %shard_map.60.own_ref), channel_id=1, source_target_pairs={{0,4},{4,0},{8,12},{12,8},{16,20},{20,16},{24,28},{28,24},{1,5},{5... | collective-permute-start | bytes 2359304 | tf_op jit(solution)/shard_map/ppermute | solution.py:131
  30.2 26.8 %collective-permute-start.3 = (f32[1536,128]{1,0:T(8,128)S(1)}, f32[1536,128]{1,0:T(8,128)S(1)}, u32[]{:S(2)}, u32[]{:S(2)}) collective-permute-start(f32[1536,128]{1,0:T(8,128)S(1)} %shard_map.60.own_ref), channel_id=1, source_target_pairs={{0,28},{4,8},{8,4},{12,16},{16,12},{20,24},{24,20},{28,0},{1,29},{... | collective-permute-start | bytes 2359304 | tf_op jit(solution)/shard_map/ppermute | solution.py:131
  31.5 33.1 %collective-permute-start.8 = (f32[1536,128]{1,0:T(8,128)S(1)}, f32[1536,128]{1,0:T(8,128)S(1)}, u32[]{:S(2)}, u32[]{:S(2)}) collective-permute-start(f32[1536,128]{1,0:T(8,128)S(1)} %get-tuple-element.89.own_ref.rest_0_), channel_id=1, source_target_pairs={{0,4},{4,0},{8,12},{12,8},{16,20},{20,16},{24,28},{28,24},{1,5},{5... | collective-permute-start | bytes 2359304 | tf_op jit(solution)/shard_map/ppermute | solution.py:131
  31.5 42.4 %collective-permute-start.9 = (f32[1536,128]{1,0:T(8,128)S(1)}, f32[1536,128]{1,0:T(8,128)S(1)}, u32[]{:S(2)}, u32[]{:S(2)}) collective-permute-start(f32[1536,128]{1,0:T(8,128)S(1)} %get-tuple-element.89.own_ref.rest_0_), channel_id=1, source_target_pairs={{0,28},{4,8},{8,4},{12,16},{16,12},{20,24},{24,20},{28,0},{1,29},{... | collective-permute-start | bytes 2359304 | tf_op jit(solution)/shard_map/ppermute | solution.py:131
  46.9 37.0 %collective-permute-start.6 = (f32[1536,128]{1,0:T(8,128)S(1)}, f32[1536,128]{1,0:T(8,128)S(1)}, u32[]{:S(2)}, u32[]{:S(2)}) collective-permute-start(f32[1536,128]{1,0:T(8,128)S(1)} %shard_map.62.own_ref), channel_id=1, source_target_pairs={{0,4},{4,0},{8,12},{12,8},{16,20},{20,16},{24,28},{28,24},{1,5},{5... | collective-permute-start | bytes 2359304 | tf_op jit(solution)/shard_map/ppermute | solution.py:131
  47.0 43.6 %collective-permute-start.7 = (f32[1536,128]{1,0:T(8,128)S(1)}, f32[1536,128]{1,0:T(8,128)S(1)}, u32[]{:S(2)}, u32[]{:S(2)}) collective-permute-start(f32[1536,128]{1,0:T(8,128)S(1)} %shard_map.62.own_ref), channel_id=1, source_target_pairs={{0,28},{4,8},{8,4},{12,16},{16,12},{20,24},{24,20},{28,0},{1,29},{... | collective-permute-start | bytes 2359304 | tf_op jit(solution)/shard_map/ppermute | solution.py:131
  63.8 33.7 %collective-permute-start.12 = (f32[1536,128]{1,0:T(8,128)S(1)}, f32[1536,128]{1,0:T(8,128)S(1)}, u32[]{:S(2)}, u32[]{:S(2)}) collective-permute-start(f32[1536,128]{1,0:T(8,128)S(1)} %shard_map.61.refs_0_), channel_id=1, source_target_pairs={{0,2},{7,5},{8,10},{15,13},{16,18},{23,21},{24,26},{31,29}} | collective-permute-start | bytes 2359304 | tf_op jit(solution)/shard_map/ppermute | solution.py:297
  64.5 33.7 %collective-permute-start.13 = (f32[1536,128]{1,0:T(8,128)S(1)}, f32[1536,128]{1,0:T(8,128)S(1)}, u32[]{:S(2)}, u32[]{:S(2)}) collective-permute-start(f32[1536,128]{1,0:T(8,128)S(1)} %shard_map.61.refs_0_), channel_id=1, source_target_pairs={{1,2},{6,5},{9,10},{14,13},{17,18},{22,21},{25,26},{30,29}} | collective-permute-start | bytes 2359304 | tf_op jit(solution)/shard_map/ppermute | solution.py:297
  73.8 25.2 %collective-permute-start.14 = (f32[1536,128]{1,0:T(8,128)S(1)}, f32[1536,128]{1,0:T(8,128)S(1)}, u32[]{:S(2)}, u32[]{:S(2)}) collective-permute-start(f32[1536,128]{1,0:T(8,128)S(1)} %shard_map.61.refs_0_), channel_id=1, source_target_pairs={{3,2},{4,5},{11,10},{12,13},{19,18},{20,21},{27,26},{28,29}} | collective-permute-start | bytes 2359304 | tf_op jit(solution)/shard_map/ppermute | solution.py:297
  83.9 24.1 %collective-permute-start.10 = (f32[1536,128]{1,0:T(8,128)S(1)}, f32[1536,128]{1,0:T(8,128)S(1)}, u32[]{:S(2)}, u32[]{:S(2)}) collective-permute-start(f32[1536,128]{1,0:T(8,128)S(1)} %shard_map.64.own_ref), channel_id=1, source_target_pairs={{0,28},{4,8},{8,4},{12,16},{16,12},{20,24},{24,20},{28,0},{1,29},{... | collective-permute-start | bytes 2359304 | tf_op jit(solution)/shard_map/ppermute | solution.py:131
  90.7 17.3 %collective-permute-start.11 = (f32[1536,128]{1,0:T(8,128)S(1)}, f32[1536,128]{1,0:T(8,128)S(1)}, u32[]{:S(2)}, u32[]{:S(2)}) collective-permute-start(f32[1536,128]{1,0:T(8,128)S(1)} %shard_map.64.own_ref), channel_id=1, source_target_pairs={{0,4},{4,0},{8,12},{12,8},{16,20},{20,16},{24,28},{28,24},{1,5},{5... | collective-permute-start | bytes 2359304 | tf_op jit(solution)/shard_map/ppermute | solution.py:131
  97.5 18.8 %collective-permute-start.15 = (f32[1536,128]{1,0:T(8,128)S(1)}, f32[1536,128]{1,0:T(8,128)S(1)}, u32[]{:S(2)}, u32[]{:S(2)}) collective-permute-start(f32[1536,128]{1,0:T(8,128)S(1)} %shard_map.63.refs_0_), channel_id=1, source_target_pairs={{0,2},{7,5},{8,10},{15,13},{16,18},{23,21},{24,26},{31,29}} | collective-permute-start | bytes 2359304 | tf_op jit(solution)/shard_map/ppermute | solution.py:297
  98.3 21.5 %collective-permute-start.16 = (f32[1536,128]{1,0:T(8,128)S(1)}, f32[1536,128]{1,0:T(8,128)S(1)}, u32[]{:S(2)}, u32[]{:S(2)}) collective-permute-start(f32[1536,128]{1,0:T(8,128)S(1)} %shard_map.63.refs_0_), channel_id=1, source_target_pairs={{1,2},{6,5},{9,10},{14,13},{17,18},{22,21},{25,26},{30,29}} | collective-permute-start | bytes 2359304 | tf_op jit(solution)/shard_map/ppermute | solution.py:297
  99.0 21.7 %collective-permute-start.17 = (f32[1536,128]{1,0:T(8,128)S(1)}, f32[1536,128]{1,0:T(8,128)S(1)}, u32[]{:S(2)}, u32[]{:S(2)}) collective-permute-start(f32[1536,128]{1,0:T(8,128)S(1)} %shard_map.63.refs_0_), channel_id=1, source_target_pairs={{3,2},{4,5},{11,10},{12,13},{19,18},{20,21},{27,26},{28,29}} | collective-permute-start | bytes 2359304 | tf_op jit(solution)/shard_map/ppermute | solution.py:297
  116.3 20.6 %collective-permute-start.21 = (f32[1536,128]{1,0:T(8,128)S(1)}, f32[1536,128]{1,0:T(8,128)S(1)}, u32[]{:S(2)}, u32[]{:S(2)}) collective-permute-start(f32[1536,128]{1,0:T(8,128)S(1)} %shard_map.66.refs_0_), channel_id=1, source_target_pairs={{3,2},{4,5},{11,10},{12,13},{19,18},{20,21},{27,26},{28,29}} | collective-permute-start | bytes 2359304 | tf_op jit(solution)/shard_map/ppermute | solution.py:297
  127.4 21.3 %collective-permute-start.18 = (f32[384,512]{1,0:T(8,128)S(1)}, f32[384,512]{1,0:T(8,128)S(1)}, u32[]{:S(2)}, u32[]{:S(2)}) collective-permute-start(f32[384,512]{1,0:T(8,128)S(1)} %get-tuple-element.64), channel_id=1, source_target_pairs={{2,26},{5,29},{10,18},{13,21},{18,10},{21,13},{26,2},{29,5}} | collective-permute-start | bytes 2359304 | tf_op jit(solution)/shard_map/ppermute | solution.py:297
  128.2 21.3 %collective-permute-start.22 = (f32[384,512]{1,0:T(8,128)S(1)}, f32[384,512]{1,0:T(8,128)S(1)}, u32[]{:S(2)}, u32[]{:S(2)}) collective-permute-start(f32[384,512]{1,0:T(8,128)S(1)} %get-tuple-element.78), channel_id=1, source_target_pairs={{2,10},{5,13},{10,2},{13,5},{18,26},{21,29},{26,18},{29,21}} | collective-permute-start | bytes 2359304 | tf_op jit(solution)/shard_map/ppermute | solution.py:297
  128.9 20.6 %collective-permute-start.23 = (f32[384,512]{1,0:T(8,128)S(1)}, f32[384,512]{1,0:T(8,128)S(1)}, u32[]{:S(2)}, u32[]{:S(2)}) collective-permute-start(f32[384,512]{1,0:T(8,128)S(1)} %get-tuple-element.79), channel_id=1, source_target_pairs={{2,18},{5,21},{10,26},{13,29},{18,2},{21,5},{26,10},{29,13}} | collective-permute-start | bytes 2359304 | tf_op jit(solution)/shard_map/ppermute | solution.py:297
  154.7 28.2 %collective-permute-start.29 = (f32[768,128]{1,0:T(8,128)S(1)}, f32[768,128]{1,0:T(8,128)S(1)}, u32[]{:S(2)}, u32[]{:S(2)}) collective-permute-start(f32[768,128]{1,0:T(8,128)S(1)} %get-tuple-element.87), channel_id=1, source_target_pairs={{2,3},{5,4},{10,11},{13,12},{18,19},{21,20},{26,27},{29,28}} | collective-permute-start | bytes 1179656 | tf_op jit(solution)/shard_map/ppermute | solution.py:297
  184.9 14.3 %collective-permute-start.32 = (f32[256,128]{1,0:T(8,128)S(1)}, f32[256,128]{1,0:T(8,128)S(1)}, u32[]{:S(2)}, u32[]{:S(2)}) collective-permute-start(f32[256,128]{1,0:T(8,128)S(1)} %slice.21), channel_id=1, source_target_pairs={{4,4},{5,12},{6,20},{7,28},{12,5},{13,13},{14,21},{15,29},{20,6},{... | collective-permute-start | bytes 393224 | tf_op jit(solution)/shard_map/ppermute | solution.py:297
  (13 other events, 78.5 us)

commit v8 on v7

--- a/solution.py
+++ b/solution.py
@@ -10,7 +10,7 @@
 GROUP = 4
 LANES = 128
 MIB = 1024 * 1024
-APPLY_MIB = 14
+APPLY_MIB = 10
 
 
 def split(x):
@@ -189,7 +189,7 @@
         in_specs=[smem, smem] + [vmem] * len(ins),
         out_specs=[vmem] * (4 + len(places)),
         out_shape=[plain, plain, turned, turned] + [product] * len(places),
-        compiler_params=pltpu.CompilerParams(vmem_limit_bytes=18 * MIB),
+        compiler_params=pltpu.CompilerParams(vmem_limit_bytes=14 * MIB),
         cost_estimate=pl.CostEstimate(
             flops=24 * len(places) * high * width * rows, bytes_accessed=8_000_000, transcendentals=0
         ),
@@ -220,49 +220,28 @@
     )(targets, *ins)
 
 
-def sum_kernel(*refs):
-    *ins, out_ref = refs
-    out_ref[...] = (ins[0][...] + ins[1][...]) + (ins[2][...] + ins[3][...])
-
-
-def sum_parts(*parts):
-    vmem = pl.BlockSpec(memory_space=pltpu.VMEM)
-    return pl.pallas_call(
-        sum_kernel,
-        in_specs=[vmem] * 4,
-        out_specs=vmem,
-        out_shape=jax.ShapeDtypeStruct(parts[0].shape, jnp.float32),
-        compiler_params=pltpu.CompilerParams(vmem_limit_bytes=12 * MIB),
-        cost_estimate=pl.CostEstimate(flops=0, bytes_accessed=4_000_000, transcendentals=0),
-    )(*parts)
-
-
-def pick_kernel(goal_ref, early_ref, *refs):
+def pick_kernel(goal_ref, *refs):
     ins, outs = refs[:4], refs[4:]
-    rows, width = early_ref.shape[0], early_ref.shape[1] // 4
+    width = ins[0].shape[1] // 4
     for k, out in enumerate(outs):
         there = pl.ds(pl.multiple_of(goal_ref[k] * width, width), width)
         x, y, u, v = (ref[:, there] for ref in ins)
-        late = (x + y) + (u + v)
-        early = early_ref[:, there]
-        if k == 3:
-            early, late = (jnp.where(goal_ref[4] > 0, x, 0.0) for x in (early, late))
-        out[pl.ds(0, rows), :] = early
-        out[pl.ds(rows, rows), :] = late
-
-
-def pick(goals, early, *late):
-    rows, size = early.shape
-    shape = jax.ShapeDtypeStruct((2 * rows, size // 4), jnp.float32)
+        total = (x + y) + (u + v)
+        out[...] = jnp.where(goal_ref[4] > 0, total, 0.0) if k == 3 else total
+
+
+def pick(goals, parts):
+    rows, size = parts[0].shape
+    shape = jax.ShapeDtypeStruct((rows, size // 4), jnp.float32)
     vmem = pl.BlockSpec(memory_space=pltpu.VMEM)
     return pl.pallas_call(
         pick_kernel,
-        in_specs=[pl.BlockSpec(memory_space=pltpu.SMEM)] + [vmem] * 5,
+        in_specs=[pl.BlockSpec(memory_space=pltpu.SMEM)] + [vmem] * 4,
         out_specs=[vmem] * 4,
         out_shape=[shape] * 4,
-        compiler_params=pltpu.CompilerParams(vmem_limit_bytes=12 * MIB),
+        compiler_params=pltpu.CompilerParams(vmem_limit_bytes=8 * MIB),
         cost_estimate=pl.CostEstimate(flops=0, bytes_accessed=3_000_000, transcendentals=0),
-    )(goals, early, *late)
+    )(goals, *parts)
 
 
 def assemble_kernel(core_ref, piece_ref, turn_e_ref, turn_l_ref, out_ref, *, scale):
@@ -376,19 +355,24 @@
     g2 = one(after_that(f2, upper[0]), hf2, v2, turned=True)
     z2 = gather_bands(g2)
     c1, early = chunk(bands, targets, [after_that(z1[0], g2)] + z1[1:], [c0], ALL, upper)
-    early = [send(x, over_chips(flip)) if flip else x for x, flip in zip(early, FLIPS)]
+    early[0] = send(early[0], over_chips(FLIPS[0]))
+    early[1] = send(early[1], over_chips(FLIPS[1]))
     c2, late = chunk(bands, targets, [after_that(z2[0], c1[0])] + z2[1:], [c0, c1], (0,))
-    for k in (1, 2):
-        late.append(product(after_that(targets, late[-1]), k, [c0, c1, c2]))
-    last = late[-1]
-    late = [send(x, over_chips(flip)) for x, flip in zip(late, FLIPS)]
-    early_sum = sum_parts(after_that(early[0], last), *early[1:])
-    late.append(product(after_that(targets, early_sum, late[0]), 3, [c0, c1, c2]))
-    moved = pick(goals, early_sum, *late)
-    piece = moved[3]
-    for k, x in zip((0, 1, 3), moved):
-        piece = piece + send(x, mirrored([(2, k)]))
+    early[2] = send(after_that(early[2], late[0]), over_chips(FLIPS[2]))
+    late.append(product(after_that(targets, late[0], early[0], early[1]), 1, [c0, c1, c2]))
+    late.append(product(after_that(targets, late[1]), 2, [c0, c1, c2]))
+
+    def deliver(parts):
+        moved = pick(goals, parts)
+        return [moved[3]] + [send(x, mirrored([(2, k)])) for k, x in zip((0, 1, 3), moved)]
+
+    late[0] = send(late[0], over_chips(FLIPS[0]))
+    arrived = [deliver([after_that(early[0], late[2], late[0])] + early[1:])]
+    late[1:] = [send(x, over_chips(flip)) for x, flip in zip(late[1:], FLIPS[1:])]
+    late.append(product(after_that(targets, arrived[0][0], late[1]), 3, [c0, c1, c2]))
+    arrived.append(deliver(late))
     filtered = jnp.concatenate([g0, g1, after_that(g2, late[3])], axis=1)
+    piece = jnp.concatenate([(x[0] + x[1]) + (x[2] + x[3]) for x in arrived], axis=0)
     piece = piece + send(piece, SWAP)
     w = v0.shape[1]
     turn_e = send(piece[w : 2 * w], TURN)

time: 201 us -> 203 us (level)
    ppermute x21 -> x24, starting transfers between devices: 30.7 us -> 31.7 us  [send(): return lax.ppermute(x, ('orb', 'band'), pairs)]
    ppermute x21 -> x24, waiting for transfers between devices: 41.7 us -> 42.1 us  [send(): return lax.ppermute(x, ('orb', 'band'), pairs)]
  transfers between devices with their start and end apart: 33 -> 36, of which waited for: 10 -> 11; matrix products, arithmetic and copies ran while one was open for 2% -> 2% of each run, Pallas kernels for 38% -> 39%
where the time goes in v8:
time: 203 us; the launch traced here: 201 us
  Pallas kernels  79 us (39%)
  waiting for transfers between devices  75.6 us (37%)
  starting transfers between devices  40.2 us (20%)
  local copies, waits for them, and re-layouts  2.8 us (1%)
  other arithmetic  2.07 us (1%)
    ppermute x24, waiting for transfers between devices, send(): return lax.ppermute(x, ('orb', 'band'), pairs)  42.1 us
    pallas_call x6, Pallas kernels, apply_step(): pl.pallas_call(functools.partial(apply_kernel, second=second, turned=turn...  41 us
    ppermute x12, waiting for transfers between devices, neighbours(): return (lax.ppermute(x, 'orb', inside), lax.ppermute(x, 'orb', across))  33.6 us
    ppermute x24, starting transfers between devices, send(): return lax.ppermute(x, ('orb', 'band'), pairs)  31.7 us
    pallas_call x3, Pallas kernels, chunk(): pl.pallas_call(functools.partial(chunk_kernel, before=len(olds) // 4, pla...  14.9 us
    pallas_call x1, Pallas kernels, densify(): pl.pallas_call(functools.partial(densify_kernel, spread=spread, reach=row...  12.8 us
    ppermute x12, starting transfers between devices, neighbours(): return (lax.ppermute(x, 'orb', inside), lax.ppermute(x, 'orb', across))  8.42 us
    pallas_call x3, Pallas kernels, product(): pl.pallas_call(functools.partial(product_kernel, place=place), in_specs=[...  7.56 us
  transfers between devices with their start and end apart: 36, of which 11 were waited for; matrix products, arithmetic and copies ran while one was open for 2% of the time, Pallas kernels for 39%

profile of v8, /device:TPU:3, one launch (start us, length us, event | category | flops | bytes accessed | tf_op | source)
XLA Modules:
  0.0 200.9 jit_solution(6471122436367424910)
XLA Ops:
  7.4 12.8 %shard_map.59 = (bf16[1536,3328]{1,0:T(8,128)(2,1)S(1)}, bf16[1536,3328]{1,0:T(8,128)(2,1)S(1)}) custom-call(s32[24,52]{1,0:T(8,128)S(1)} %select_reduce_fusion.slot_ref, f32[24,32,64,64]{3,2,1,0:T(8,128)} %blocks_ref.1), custom_call_target="tpu_custom_call" | custom-call | bytes 60000000 | tf_op jit(solution)/shard_map/pallas_call | solution.py:52
  20.2 3.1 %collective-permute-done.1.far_ref = f32[1536,128]{1,0:T(8,128)S(1)} collective-permute-done((f32[1536,128]{1,0:T(8,128)S(1)}, f32[1536,128]{1,0:T(8,128)S(1)}, u32[]{:S(2)}, u32[]{:S(2)}) %collective-permute-start.1) | collective-permute-done | bytes 786464 | tf_op jit(solution)/shard_map/ppermute | solution.py:131
  23.3 6.8 %shard_map.60.own_ref = f32[1536,128]{1,0:T(8,128)S(1)} custom-call(s32[1]{0:T(128)} %bitcast.10.core_ref, bf16[1536,3328]{1,0:T(8,128)(2,1)S(1)} %get-tuple-element.52.hi_ref, bf16[1536,3328]{1,0:T(8,128)(2,1)S(1)} %get-tuple-element.53.lo_ref, f32[1536,128]{1,0:T(8,128)S(1)} %collective-permute-done.near_ref, ...), custom_call_target="tpu_custom_call" | custom-call | flops 5234491392 | bytes 20447232 | tf_op jit(solution)/shard_map/pallas_call | solution.py:101
  33.5 6.6 %collective-permute-done.5.far_ref = f32[1536,128]{1,0:T(8,128)S(1)} collective-permute-done((f32[1536,128]{1,0:T(8,128)S(1)}, f32[1536,128]{1,0:T(8,128)S(1)}, u32[]{:S(2)}, u32[]{:S(2)}) %collective-permute-start.5) | collective-permute-done | bytes 786464 | tf_op jit(solution)/shard_map/ppermute | solution.py:131
  40.1 6.8 %shard_map.62.own_ref = f32[1536,128]{1,0:T(8,128)S(1)} custom-call(s32[1]{0:T(128)} %bitcast.10.core_ref, bf16[1536,3328]{1,0:T(8,128)(2,1)S(1)} %get-tuple-element.52.hi_ref, bf16[1536,3328]{1,0:T(8,128)(2,1)S(1)} %get-tuple-element.53.lo_ref, f32[1536,128]{1,0:T(8,128)S(1)} %collective-permute-done.4.near_ref, ...), custom_call_target="tpu_custom_call" | custom-call | flops 5234491392 | bytes 20447232 | tf_op jit(solution)/shard_map/pallas_call | solution.py:101
  48.3 8.6 %collective-permute-done.3.far_ref = f32[1536,128]{1,0:T(8,128)S(1)} collective-permute-done((f32[1536,128]{1,0:T(8,128)S(1)}, f32[1536,128]{1,0:T(8,128)S(1)}, u32[]{:S(2)}, u32[]{:S(2)}) %collective-permute-start.3) | collective-permute-done | bytes 786464 | tf_op jit(solution)/shard_map/ppermute | solution.py:131
  57.0 6.8 %shard_map.61.refs_0_ = f32[1536,128]{1,0:T(8,128)S(1)} custom-call(s32[1]{0:T(128)} %bitcast.10.core_ref, bf16[1536,3328]{1,0:T(8,128)(2,1)S(1)} %get-tuple-element.52.hi_ref, bf16[1536,3328]{1,0:T(8,128)(2,1)S(1)} %get-tuple-element.53.lo_ref, f32[1536,128]{1,0:T(8,128)S(1)} %collective-permute-done.2.near_ref, ...), custom_call_target="tpu_custom_call" | custom-call | flops 5234491392 | bytes 20447232 | tf_op jit(solution)/shard_map/pallas_call | solution.py:101
  65.3 8.6 %collective-permute-done.9.far_ref = f32[1536,128]{1,0:T(8,128)S(1)} collective-permute-done((f32[1536,128]{1,0:T(8,128)S(1)}, f32[1536,128]{1,0:T(8,128)S(1)}, u32[]{:S(2)}, u32[]{:S(2)}) %collective-permute-start.9) | collective-permute-done | bytes 786464 | tf_op jit(solution)/shard_map/ppermute | solution.py:131
  73.8 3.2 %collective-permute-start.14 = (f32[1536,128]{1,0:T(8,128)S(1)}, f32[1536,128]{1,0:T(8,128)S(1)}, u32[]{:S(2)}, u32[]{:S(2)}) collective-permute-start(f32[1536,128]{1,0:T(8,128)S(1)} %shard_map.61.refs_0_), channel_id=1, source_target_pairs={{3,2},{4,5},{11,10},{12,13},{19,18},{20,21},{27,26},{28,29}} | collective-permute-start | bytes 2359304 | tf_op jit(solution)/shard_map/ppermute | solution.py:276
  77.1 6.8 %shard_map.64.own_ref = f32[1536,128]{1,0:T(8,128)S(1)} custom-call(s32[1]{0:T(128)} %bitcast.10.core_ref, bf16[1536,3328]{1,0:T(8,128)(2,1)S(1)} %get-tuple-element.52.hi_ref, bf16[1536,3328]{1,0:T(8,128)(2,1)S(1)} %get-tuple-element.53.lo_ref, f32[1536,128]{1,0:T(8,128)S(1)} %collective-permute-done.8.near_ref, ...), custom_call_target="tpu_custom_call" | custom-call | flops 5234491392 | bytes 20447232 | tf_op jit(solution)/shard_map/pallas_call | solution.py:101
  84.0 6.7 %collective-permute-done.7.far_ref = f32[1536,128]{1,0:T(8,128)S(1)} collective-permute-done((f32[1536,128]{1,0:T(8,128)S(1)}, f32[1536,128]{1,0:T(8,128)S(1)}, u32[]{:S(2)}, u32[]{:S(2)}) %collective-permute-start.7) | collective-permute-done | bytes 786464 | tf_op jit(solution)/shard_map/ppermute | solution.py:131
  90.7 6.8 %shard_map.63.refs_0_ = f32[1536,128]{1,0:T(8,128)S(1)} custom-call(s32[1]{0:T(128)} %bitcast.10.core_ref, bf16[1536,3328]{1,0:T(8,128)(2,1)S(1)} %get-tuple-element.52.hi_ref, bf16[1536,3328]{1,0:T(8,128)(2,1)S(1)} %get-tuple-element.53.lo_ref, f32[1536,128]{1,0:T(8,128)S(1)} %collective-permute-done.6.near_ref, ...), custom_call_target="tpu_custom_call" | custom-call | flops 5234491392 | bytes 20447232 | tf_op jit(solution)/shard_map/pallas_call | solution.py:101
  99.0 4.6 %collective-permute-start.17 = (f32[1536,128]{1,0:T(8,128)S(1)}, f32[1536,128]{1,0:T(8,128)S(1)}, u32[]{:S(2)}, u32[]{:S(2)}) collective-permute-start(f32[1536,128]{1,0:T(8,128)S(1)} %shard_map.63.refs_0_), channel_id=1, source_target_pairs={{3,2},{4,5},{11,10},{12,13},{19,18},{20,21},{27,26},{28,29}} | collective-permute-start | bytes 2359304 | tf_op jit(solution)/shard_map/ppermute | solution.py:276
  103.6 4.4 %shard_map.65 = (bf16[1536,512]{1,0:T(8,128)(2,1)S(1)}, bf16[1536,512]{1,0:T(8,128)(2,1)S(1)}, bf16[512,1536]{1,0:T(8,128)(2,1)S(1)}, bf16[512,1536]{1,0:T(8,128...) custom-call(s32[4]{0:T(128)S(1)} %get-tuple-element.56.band_ref, ...), custom_call_target="tpu_custom_call" | custom-call | flops 2415919104 | bytes 8000000 | tf_op jit(solution)/shard_map/pallas_call | solution.py:185
  108.0 6.8 %shard_map.66.refs_0_ = f32[1536,128]{1,0:T(8,128)S(1)} custom-call(s32[1]{0:T(128)} %bitcast.10.core_ref, bf16[1536,3328]{1,0:T(8,128)(2,1)S(1)} %get-tuple-element.52.hi_ref, bf16[1536,3328]{1,0:T(8,128)(2,1)S(1)} %get-tuple-element.53.lo_ref, f32[1536,128]{1,0:T(8,128)S(1)} %collective-permute-done.10.near_ref, ...), custom_call_target="tpu_custom_call" | custom-call | flops 5234491392 | bytes 20447232 | tf_op jit(solution)/shard_map/pallas_call | solution.py:101
  116.3 3.4 %collective-permute-start.21 = (f32[1536,128]{1,0:T(8,128)S(1)}, f32[1536,128]{1,0:T(8,128)S(1)}, u32[]{:S(2)}, u32[]{:S(2)}) collective-permute-start(f32[1536,128]{1,0:T(8,128)S(1)} %shard_map.66.refs_0_), channel_id=1, source_target_pairs={{3,2},{4,5},{11,10},{12,13},{19,18},{20,21},{27,26},{28,29}} | collective-permute-start | bytes 2359304 | tf_op jit(solution)/shard_map/ppermute | solution.py:276
  120.6 6.8 %shard_map.67 = (bf16[1536,512]{1,0:T(8,128)(2,1)S(1)}, bf16[1536,512]{1,0:T(8,128)(2,1)S(1)}, bf16[512,1536]{1,0:T(8,128)(2,1)S(1)}, bf16[512,1536]{1,0:T(8,128...) custom-call(s32[4]{0:T(128)S(1)} %get-tuple-element.56.band_ref, ...), custom_call_target="tpu_custom_call" | custom-call | flops 7247757312 | bytes 8000000 | tf_op jit(solution)/shard_map/pallas_call | solution.py:185
  128.9 8.0 %collective-permute-done.21.refs_3_ = f32[1536,128]{1,0:T(8,128)S(1)} collective-permute-done((f32[1536,128]{1,0:T(8,128)S(1)}, f32[1536,128]{1,0:T(8,128)S(1)}, u32[]{:S(2)}, u32[]{:S(2)}) %collective-permute-start.21) | collective-permute-done | bytes 786464 | tf_op jit(solution)/shard_map/ppermute | solution.py:276
  136.9 3.7 %shard_map.68 = (bf16[1536,512]{1,0:T(8,128)(2,1)S(1)}, bf16[1536,512]{1,0:T(8,128)(2,1)S(1)}, bf16[512,1536]{1,0:T(8,128)(2,1)S(1)}, bf16[512,1536]{1,0:T(8,128)(2,1)S(1)}, f32[384,512]{1,0:T(8,128)S(1)}) custom-call(s32[4]{0:T(128)S(1)} %get-tuple-element.56.band_ref, s32[4]{0:T(128)S(1)} %get-tuple-element.89.target_ref, ...), custom_call_target="tpu_custom_call" | custom-call | flops 1811939328 | bytes 8000000 | tf_op jit(solution)/shard_map/pallas_call | solution.py:185
  142.3 2.5 %shard_map.69 = f32[384,512]{1,0:T(8,128)S(1)} custom-call(s32[4]{0:T(128)S(1)} %get-tuple-element.89.target_ref, bf16[1536,512]{1,0:T(8,128)(2,1)S(1)} %get-tuple-element.79.refs_0_, bf16[1536,512]{1,0:T(8,128)(2,1)S(1)} %get-tuple-element.80.refs_1_, bf16[512,1536]{1,0:T(8,128)(2,1)S(1)} %get-tuple-element.65.refs_6_.refs_2_, ...), custom_call_target="tpu_custom_call" | custom-call | flops 1811939328 | bytes 4000000 | tf_op jit(solution)/shard_map/pallas_call | solution.py:211
  158.6 17.8 %collective-permute-done.28 = f32[384,128]{1,0:T(8,128)S(1)} collective-permute-done((f32[384,128]{1,0:T(8,128)S(1)}, f32[384,128]{1,0:T(8,128)S(1)}, u32[]{:S(2)}, u32[]{:S(2)}) %collective-permute-start.28) | collective-permute-done | bytes 196640 | tf_op jit(solution)/shard_map/ppermute | solution.py:276
  176.5 8.4 %collective-permute-done.32 = f32[384,128]{1,0:T(8,128)S(1)} collective-permute-done((f32[384,128]{1,0:T(8,128)S(1)}, f32[384,128]{1,0:T(8,128)S(1)}, u32[]{:S(2)}, u32[]{:S(2)}) %collective-permute-start.32) | collective-permute-done | bytes 196640 | tf_op jit(solution)/shard_map/ppermute | solution.py:276
  186.8 4.5 %collective-permute-start.35 = (f32[256,128]{1,0:T(8,128)S(1)}, f32[256,128]{1,0:T(8,128)S(1)}, u32[]{:S(2)}, u32[]{:S(2)}) collective-permute-start(f32[256,128]{1,0:T(8,128)S(1)} %slice.21), channel_id=1, source_target_pairs={{4,4},{5,12},{6,20},{7,28},{12,5},{13,13},{14,21},{15,29},{20,6},{... | collective-permute-start | bytes 393224 | tf_op jit(solution)/shard_map/ppermute | solution.py:276
  194.8 5.2 %collective-permute-done.34.turn_e_ref = f32[128,128]{1,0:T(8,128)S(1)} collective-permute-done((f32[128,128]{1,0:T(8,128)S(1)}, f32[128,128]{1,0:T(8,128)S(1)}, u32[]{:S(2)}, u32[]{:S(2)}) %collective-permute-start.34) | collective-permute-done | bytes 65568 | tf_op jit(solution)/shard_map/ppermute | solution.py:276
  (82 shorter events, 39.8 us)
Async XLA Ops:
  1.8 18.3 %collective-permute-start = (f32[1536,128]{1,0:T(8,128)S(1)}, f32[1536,128]{1,0:T(8,128)S(1)}, u32[]{:S(2)}, u32[]{:S(2)}) collective-permute-start(f32[1536,128]{1,0:T(8,128)S(1)} %slice.15.own_ref.rest_0_), channel_id=1, source_target_pairs={{0,4},{4,0},{8,12},{12,8},{16,20},{20,16},{24,28},{28,24},{1,5},{5... | collective-permute-start | bytes 2359304 | tf_op jit(solution)/shard_map/ppermute | solution.py:131
  2.6 20.7 %collective-permute-start.1 = (f32[1536,128]{1,0:T(8,128)S(1)}, f32[1536,128]{1,0:T(8,128)S(1)}, u32[]{:S(2)}, u32[]{:S(2)}) collective-permute-start(f32[1536,128]{1,0:T(8,128)S(1)} %slice.15.own_ref.rest_0_), channel_id=1, source_target_pairs={{0,28},{4,8},{8,4},{12,16},{16,12},{20,24},{24,20},{28,0},{1,29},{... | collective-permute-start | bytes 2359304 | tf_op jit(solution)/shard_map/ppermute | solution.py:131
  5.7 25.7 %collective-permute-start.4 = (f32[1536,128]{1,0:T(8,128)S(1)}, f32[1536,128]{1,0:T(8,128)S(1)}, u32[]{:S(2)}, u32[]{:S(2)}) collective-permute-start(f32[1536,128]{1,0:T(8,128)S(1)} %get-tuple-element.98.own_ref.rest_0_), channel_id=1, source_target_pairs={{0,4},{4,0},{8,12},{12,8},{16,20},{20,16},{24,28},{28,24},{1,5},{5... | collective-permute-start | bytes 2359304 | tf_op jit(solution)/shard_map/ppermute | solution.py:131
  5.8 34.3 %collective-permute-start.5 = (f32[1536,128]{1,0:T(8,128)S(1)}, f32[1536,128]{1,0:T(8,128)S(1)}, u32[]{:S(2)}, u32[]{:S(2)}) collective-permute-start(f32[1536,128]{1,0:T(8,128)S(1)} %get-tuple-element.98.own_ref.rest_0_), channel_id=1, source_target_pairs={{0,28},{4,8},{8,4},{12,16},{16,12},{20,24},{24,20},{28,0},{1,29},{... | collective-permute-start | bytes 2359304 | tf_op jit(solution)/shard_map/ppermute | solution.py:131
  30.1 16.9 %collective-permute-start.2 = (f32[1536,128]{1,0:T(8,128)S(1)}, f32[1536,128]{1,0:T(8,128)S(1)}, u32[]{:S(2)}, u32[]{:S(2)}) collective-permute-start(f32[1536,128]{1,0:T(8,128)S(1)} %shard_map.60.own_ref), channel_id=1, source_target_pairs={{0,4},{4,0},{8,12},{12,8},{16,20},{20,16},{24,28},{28,24},{1,5},{5... | collective-permute-start | bytes 2359304 | tf_op jit(solution)/shard_map/ppermute | solution.py:131
  30.2 26.8 %collective-permute-start.3 = (f32[1536,128]{1,0:T(8,128)S(1)}, f32[1536,128]{1,0:T(8,128)S(1)}, u32[]{:S(2)}, u32[]{:S(2)}) collective-permute-start(f32[1536,128]{1,0:T(8,128)S(1)} %shard_map.60.own_ref), channel_id=1, source_target_pairs={{0,28},{4,8},{8,4},{12,16},{16,12},{20,24},{24,20},{28,0},{1,29},{... | collective-permute-start | bytes 2359304 | tf_op jit(solution)/shard_map/ppermute | solution.py:131
  31.5 33.1 %collective-permute-start.8 = (f32[1536,128]{1,0:T(8,128)S(1)}, f32[1536,128]{1,0:T(8,128)S(1)}, u32[]{:S(2)}, u32[]{:S(2)}) collective-permute-start(f32[1536,128]{1,0:T(8,128)S(1)} %get-tuple-element.99.own_ref.rest_0_), channel_id=1, source_target_pairs={{0,4},{4,0},{8,12},{12,8},{16,20},{20,16},{24,28},{28,24},{1,5},{5... | collective-permute-start | bytes 2359304 | tf_op jit(solution)/shard_map/ppermute | solution.py:131
  31.5 42.4 %collective-permute-start.9 = (f32[1536,128]{1,0:T(8,128)S(1)}, f32[1536,128]{1,0:T(8,128)S(1)}, u32[]{:S(2)}, u32[]{:S(2)}) collective-permute-start(f32[1536,128]{1,0:T(8,128)S(1)} %get-tuple-element.99.own_ref.rest_0_), channel_id=1, source_target_pairs={{0,28},{4,8},{8,4},{12,16},{16,12},{20,24},{24,20},{28,0},{1,29},{... | collective-permute-start | bytes 2359304 | tf_op jit(solution)/shard_map/ppermute | solution.py:131
  46.9 37.0 %collective-permute-start.6 = (f32[1536,128]{1,0:T(8,128)S(1)}, f32[1536,128]{1,0:T(8,128)S(1)}, u32[]{:S(2)}, u32[]{:S(2)}) collective-permute-start(f32[1536,128]{1,0:T(8,128)S(1)} %shard_map.62.own_ref), channel_id=1, source_target_pairs={{0,4},{4,0},{8,12},{12,8},{16,20},{20,16},{24,28},{28,24},{1,5},{5... | collective-permute-start | bytes 2359304 | tf_op jit(solution)/shard_map/ppermute | solution.py:131
  47.0 43.6 %collective-permute-start.7 = (f32[1536,128]{1,0:T(8,128)S(1)}, f32[1536,128]{1,0:T(8,128)S(1)}, u32[]{:S(2)}, u32[]{:S(2)}) collective-permute-start(f32[1536,128]{1,0:T(8,128)S(1)} %shard_map.62.own_ref), channel_id=1, source_target_pairs={{0,28},{4,8},{8,4},{12,16},{16,12},{20,24},{24,20},{28,0},{1,29},{... | collective-permute-start | bytes 2359304 | tf_op jit(solution)/shard_map/ppermute | solution.py:131
  63.8 33.7 %collective-permute-start.12 = (f32[1536,128]{1,0:T(8,128)S(1)}, f32[1536,128]{1,0:T(8,128)S(1)}, u32[]{:S(2)}, u32[]{:S(2)}) collective-permute-start(f32[1536,128]{1,0:T(8,128)S(1)} %shard_map.61.refs_0_), channel_id=1, source_target_pairs={{0,2},{7,5},{8,10},{15,13},{16,18},{23,21},{24,26},{31,29}} | collective-permute-start | bytes 2359304 | tf_op jit(solution)/shard_map/ppermute | solution.py:276
  64.5 33.7 %collective-permute-start.13 = (f32[1536,128]{1,0:T(8,128)S(1)}, f32[1536,128]{1,0:T(8,128)S(1)}, u32[]{:S(2)}, u32[]{:S(2)}) collective-permute-start(f32[1536,128]{1,0:T(8,128)S(1)} %shard_map.61.refs_0_), channel_id=1, source_target_pairs={{1,2},{6,5},{9,10},{14,13},{17,18},{22,21},{25,26},{30,29}} | collective-permute-start | bytes 2359304 | tf_op jit(solution)/shard_map/ppermute | solution.py:276
  73.8 25.2 %collective-permute-start.14 = (f32[1536,128]{1,0:T(8,128)S(1)}, f32[1536,128]{1,0:T(8,128)S(1)}, u32[]{:S(2)}, u32[]{:S(2)}) collective-permute-start(f32[1536,128]{1,0:T(8,128)S(1)} %shard_map.61.refs_0_), channel_id=1, source_target_pairs={{3,2},{4,5},{11,10},{12,13},{19,18},{20,21},{27,26},{28,29}} | collective-permute-start | bytes 2359304 | tf_op jit(solution)/shard_map/ppermute | solution.py:276
  83.9 24.1 %collective-permute-start.10 = (f32[1536,128]{1,0:T(8,128)S(1)}, f32[1536,128]{1,0:T(8,128)S(1)}, u32[]{:S(2)}, u32[]{:S(2)}) collective-permute-start(f32[1536,128]{1,0:T(8,128)S(1)} %shard_map.64.own_ref), channel_id=1, source_target_pairs={{0,28},{4,8},{8,4},{12,16},{16,12},{20,24},{24,20},{28,0},{1,29},{... | collective-permute-start | bytes 2359304 | tf_op jit(solution)/shard_map/ppermute | solution.py:131
  90.7 17.3 %collective-permute-start.11 = (f32[1536,128]{1,0:T(8,128)S(1)}, f32[1536,128]{1,0:T(8,128)S(1)}, u32[]{:S(2)}, u32[]{:S(2)}) collective-permute-start(f32[1536,128]{1,0:T(8,128)S(1)} %shard_map.64.own_ref), channel_id=1, source_target_pairs={{0,4},{4,0},{8,12},{12,8},{16,20},{20,16},{24,28},{28,24},{1,5},{5... | collective-permute-start | bytes 2359304 | tf_op jit(solution)/shard_map/ppermute | solution.py:131
  97.5 18.8 %collective-permute-start.15 = (f32[1536,128]{1,0:T(8,128)S(1)}, f32[1536,128]{1,0:T(8,128)S(1)}, u32[]{:S(2)}, u32[]{:S(2)}) collective-permute-start(f32[1536,128]{1,0:T(8,128)S(1)} %shard_map.63.refs_0_), channel_id=1, source_target_pairs={{0,2},{7,5},{8,10},{15,13},{16,18},{23,21},{24,26},{31,29}} | collective-permute-start | bytes 2359304 | tf_op jit(solution)/shard_map/ppermute | solution.py:276
  98.3 21.5 %collective-permute-start.16 = (f32[1536,128]{1,0:T(8,128)S(1)}, f32[1536,128]{1,0:T(8,128)S(1)}, u32[]{:S(2)}, u32[]{:S(2)}) collective-permute-start(f32[1536,128]{1,0:T(8,128)S(1)} %shard_map.63.refs_0_), channel_id=1, source_target_pairs={{1,2},{6,5},{9,10},{14,13},{17,18},{22,21},{25,26},{30,29}} | collective-permute-start | bytes 2359304 | tf_op jit(solution)/shard_map/ppermute | solution.py:276
  99.0 21.7 %collective-permute-start.17 = (f32[1536,128]{1,0:T(8,128)S(1)}, f32[1536,128]{1,0:T(8,128)S(1)}, u32[]{:S(2)}, u32[]{:S(2)}) collective-permute-start(f32[1536,128]{1,0:T(8,128)S(1)} %shard_map.63.refs_0_), channel_id=1, source_target_pairs={{3,2},{4,5},{11,10},{12,13},{19,18},{20,21},{27,26},{28,29}} | collective-permute-start | bytes 2359304 | tf_op jit(solution)/shard_map/ppermute | solution.py:276
  116.3 20.6 %collective-permute-start.21 = (f32[1536,128]{1,0:T(8,128)S(1)}, f32[1536,128]{1,0:T(8,128)S(1)}, u32[]{:S(2)}, u32[]{:S(2)}) collective-permute-start(f32[1536,128]{1,0:T(8,128)S(1)} %shard_map.66.refs_0_), channel_id=1, source_target_pairs={{3,2},{4,5},{11,10},{12,13},{19,18},{20,21},{27,26},{28,29}} | collective-permute-start | bytes 2359304 | tf_op jit(solution)/shard_map/ppermute | solution.py:276
  127.5 14.8 %collective-permute-start.18 = (f32[384,512]{1,0:T(8,128)S(1)}, f32[384,512]{1,0:T(8,128)S(1)}, u32[]{:S(2)}, u32[]{:S(2)}) collective-permute-start(f32[384,512]{1,0:T(8,128)S(1)} %get-tuple-element.70), channel_id=1, source_target_pairs={{2,26},{5,29},{10,18},{13,21},{18,10},{21,13},{26,2},{29,5}} | collective-permute-start | bytes 2359304 | tf_op jit(solution)/shard_map/ppermute | solution.py:276
  151.1 25.3 %collective-permute-start.28 = (f32[384,128]{1,0:T(8,128)S(1)}, f32[384,128]{1,0:T(8,128)S(1)}, u32[]{:S(2)}, u32[]{:S(2)}) collective-permute-start(f32[384,128]{1,0:T(8,128)S(1)} %get-tuple-element.93), channel_id=1, source_target_pairs={{2,3},{5,4},{10,11},{13,12},{18,19},{21,20},{26,27},{29,28}} | collective-permute-start | bytes 589832 | tf_op jit(solution)/shard_map/ppermute | solution.py:276
  156.0 20.6 %collective-permute-start.30 = (f32[384,128]{1,0:T(8,128)S(1)}, f32[384,128]{1,0:T(8,128)S(1)}, u32[]{:S(2)}, u32[]{:S(2)}) collective-permute-start(f32[384,128]{1,0:T(8,128)S(1)} %get-tuple-element.95), channel_id=1, source_target_pairs={{2,0},{5,7},{10,8},{13,15},{18,16},{21,23},{26,24},{29,31}} | collective-permute-start | bytes 589832 | tf_op jit(solution)/shard_map/ppermute | solution.py:276
  156.6 19.9 %collective-permute-start.31 = (f32[384,128]{1,0:T(8,128)S(1)}, f32[384,128]{1,0:T(8,128)S(1)}, u32[]{:S(2)}, u32[]{:S(2)}) collective-permute-start(f32[384,128]{1,0:T(8,128)S(1)} %get-tuple-element.96), channel_id=1, source_target_pairs={{2,1},{5,6},{10,9},{13,14},{18,17},{21,22},{26,25},{29,30}} | collective-permute-start | bytes 589832 | tf_op jit(solution)/shard_map/ppermute | solution.py:276
  157.3 27.6 %collective-permute-start.32 = (f32[384,128]{1,0:T(8,128)S(1)}, f32[384,128]{1,0:T(8,128)S(1)}, u32[]{:S(2)}, u32[]{:S(2)}) collective-permute-start(f32[384,128]{1,0:T(8,128)S(1)} %get-tuple-element.97), channel_id=1, source_target_pairs={{2,3},{5,4},{10,11},{13,12},{18,19},{21,20},{26,27},{29,28}} | collective-permute-start | bytes 589832 | tf_op jit(solution)/shard_map/ppermute | solution.py:276
  (14 other events, 117.4 us)

commit v9 on v8

--- a/solution.py
+++ b/solution.py
@@ -355,21 +355,19 @@
     g2 = one(after_that(f2, upper[0]), hf2, v2, turned=True)
     z2 = gather_bands(g2)
     c1, early = chunk(bands, targets, [after_that(z1[0], g2)] + z1[1:], [c0], ALL, upper)
-    early[0] = send(early[0], over_chips(FLIPS[0]))
-    early[1] = send(early[1], over_chips(FLIPS[1]))
+    early = [send(x, over_chips(flip)) if flip else x for x, flip in zip(early, FLIPS)]
     c2, late = chunk(bands, targets, [after_that(z2[0], c1[0])] + z2[1:], [c0, c1], (0,))
-    early[2] = send(after_that(early[2], late[0]), over_chips(FLIPS[2]))
-    late.append(product(after_that(targets, late[0], early[0], early[1]), 1, [c0, c1, c2]))
-    late.append(product(after_that(targets, late[1]), 2, [c0, c1, c2]))
+    for k in (1, 2):
+        late.append(product(after_that(targets, late[-1]), k, [c0, c1, c2]))
+    last = late[-1]
+    late = [send(x, over_chips(flip)) for x, flip in zip(late, FLIPS)]
 
     def deliver(parts):
         moved = pick(goals, parts)
         return [moved[3]] + [send(x, mirrored([(2, k)])) for k, x in zip((0, 1, 3), moved)]
 
-    late[0] = send(late[0], over_chips(FLIPS[0]))
-    arrived = [deliver([after_that(early[0], late[2], late[0])] + early[1:])]
-    late[1:] = [send(x, over_chips(flip)) for x, flip in zip(late[1:], FLIPS[1:])]
-    late.append(product(after_that(targets, arrived[0][0], late[1]), 3, [c0, c1, c2]))
+    arrived = [deliver([after_that(early[0], last)] + early[1:])]
+    late.append(product(after_that(targets, arrived[0][0], late[0]), 3, [c0, c1, c2]))
     arrived.append(deliver(late))
     filtered = jnp.concatenate([g0, g1, after_that(g2, late[3])], axis=1)
     piece = jnp.concatenate([(x[0] + x[1]) + (x[2] + x[3]) for x in arrived], axis=0)

time: 203 us -> 197 us (0.970)
  waiting for transfers between devices: 75.6 us -> 69.6 us
    ppermute x24, waiting for transfers between devices: 42.1 us -> 36 us  [send(): return lax.ppermute(x, ('orb', 'band'), pairs)]
  transfers between devices with their start and end apart: 36 -> 36, of which waited for: 11 -> 11; matrix products, arithmetic and copies ran while one was open for 2% -> 2% of each run, Pallas kernels for 39% -> 40%
where the time goes in v9:
time: 197 us; the launch traced here: 195 us
  Pallas kernels  79 us (40%)
  waiting for transfers between devices  69.6 us (35%)
  starting transfers between devices  40 us (20%)
  local copies, waits for them, and re-layouts  2.8 us (1%)
  other arithmetic  2.07 us (1%)
    pallas_call x6, Pallas kernels, apply_step(): pl.pallas_call(functools.partial(apply_kernel, second=second, turned=turn...  41 us
    ppermute x24, waiting for transfers between devices, send(): return lax.ppermute(x, ('orb', 'band'), pairs)  36 us
    ppermute x12, waiting for transfers between devices, neighbours(): return (lax.ppermute(x, 'orb', inside), lax.ppermute(x, 'orb', across))  33.6 us
    ppermute x24, starting transfers between devices, send(): return lax.ppermute(x, ('orb', 'band'), pairs)  31.5 us
    pallas_call x3, Pallas kernels, chunk(): pl.pallas_call(functools.partial(chunk_kernel, before=len(olds) // 4, pla...  14.9 us
    pallas_call x1, Pallas kernels, densify(): pl.pallas_call(functools.partial(densify_kernel, spread=spread, reach=row...  12.8 us
    ppermute x12, starting transfers between devices, neighbours(): return (lax.ppermute(x, 'orb', inside), lax.ppermute(x, 'orb', across))  8.42 us
    pallas_call x3, Pallas kernels, product(): pl.pallas_call(functools.partial(product_kernel, place=place), in_specs=[...  7.56 us
  transfers between devices with their start and end apart: 36, of which 11 were waited for; matrix products, arithmetic and copies ran while one was open for 2% of the time, Pallas kernels for 40%

profile of v9, /device:TPU:3, one launch (start us, length us, event | category | flops | bytes accessed | tf_op | source)
XLA Modules:
  0.0 194.6 jit_solution(2965213042889868392)
XLA Ops:
  7.4 12.8 %shard_map.59 = (bf16[1536,3328]{1,0:T(8,128)(2,1)S(1)}, bf16[1536,3328]{1,0:T(8,128)(2,1)S(1)}) custom-call(s32[24,52]{1,0:T(8,128)S(1)} %select_reduce_fusion.slot_ref, f32[24,32,64,64]{3,2,1,0:T(8,128)} %blocks_ref.1), custom_call_target="tpu_custom_call" | custom-call | bytes 60000000 | tf_op jit(solution)/shard_map/pallas_call | solution.py:52
  20.2 3.1 %collective-permute-done.1.far_ref = f32[1536,128]{1,0:T(8,128)S(1)} collective-permute-done((f32[1536,128]{1,0:T(8,128)S(1)}, f32[1536,128]{1,0:T(8,128)S(1)}, u32[]{:S(2)}, u32[]{:S(2)}) %collective-permute-start.1) | collective-permute-done | bytes 786464 | tf_op jit(solution)/shard_map/ppermute | solution.py:131
  23.3 6.8 %shard_map.60.own_ref = f32[1536,128]{1,0:T(8,128)S(1)} custom-call(s32[1]{0:T(128)} %bitcast.10.core_ref, bf16[1536,3328]{1,0:T(8,128)(2,1)S(1)} %get-tuple-element.51.hi_ref, bf16[1536,3328]{1,0:T(8,128)(2,1)S(1)} %get-tuple-element.52.lo_ref, f32[1536,128]{1,0:T(8,128)S(1)} %collective-permute-done.near_ref, ...), custom_call_target="tpu_custom_call" | custom-call | flops 5234491392 | bytes 20447232 | tf_op jit(solution)/shard_map/pallas_call | solution.py:101
  33.5 6.6 %collective-permute-done.5.far_ref = f32[1536,128]{1,0:T(8,128)S(1)} collective-permute-done((f32[1536,128]{1,0:T(8,128)S(1)}, f32[1536,128]{1,0:T(8,128)S(1)}, u32[]{:S(2)}, u32[]{:S(2)}) %collective-permute-start.5) | collective-permute-done | bytes 786464 | tf_op jit(solution)/shard_map/ppermute | solution.py:131
  40.1 6.8 %shard_map.62.own_ref = f32[1536,128]{1,0:T(8,128)S(1)} custom-call(s32[1]{0:T(128)} %bitcast.10.core_ref, bf16[1536,3328]{1,0:T(8,128)(2,1)S(1)} %get-tuple-element.51.hi_ref, bf16[1536,3328]{1,0:T(8,128)(2,1)S(1)} %get-tuple-element.52.lo_ref, f32[1536,128]{1,0:T(8,128)S(1)} %collective-permute-done.4.near_ref, ...), custom_call_target="tpu_custom_call" | custom-call | flops 5234491392 | bytes 20447232 | tf_op jit(solution)/shard_map/pallas_call | solution.py:101
  48.3 8.6 %collective-permute-done.3.far_ref = f32[1536,128]{1,0:T(8,128)S(1)} collective-permute-done((f32[1536,128]{1,0:T(8,128)S(1)}, f32[1536,128]{1,0:T(8,128)S(1)}, u32[]{:S(2)}, u32[]{:S(2)}) %collective-permute-start.3) | collective-permute-done | bytes 786464 | tf_op jit(solution)/shard_map/ppermute | solution.py:131
  57.0 6.8 %shard_map.61.refs_0_ = f32[1536,128]{1,0:T(8,128)S(1)} custom-call(s32[1]{0:T(128)} %bitcast.10.core_ref, bf16[1536,3328]{1,0:T(8,128)(2,1)S(1)} %get-tuple-element.51.hi_ref, bf16[1536,3328]{1,0:T(8,128)(2,1)S(1)} %get-tuple-element.52.lo_ref, f32[1536,128]{1,0:T(8,128)S(1)} %collective-permute-done.2.near_ref, ...), custom_call_target="tpu_custom_call" | custom-call | flops 5234491392 | bytes 20447232 | tf_op jit(solution)/shard_map/pallas_call | solution.py:101
  65.3 8.6 %collective-permute-done.9.far_ref = f32[1536,128]{1,0:T(8,128)S(1)} collective-permute-done((f32[1536,128]{1,0:T(8,128)S(1)}, f32[1536,128]{1,0:T(8,128)S(1)}, u32[]{:S(2)}, u32[]{:S(2)}) %collective-permute-start.9) | collective-permute-done | bytes 786464 | tf_op jit(solution)/shard_map/ppermute | solution.py:131
  73.8 3.2 %collective-permute-start.14 = (f32[1536,128]{1,0:T(8,128)S(1)}, f32[1536,128]{1,0:T(8,128)S(1)}, u32[]{:S(2)}, u32[]{:S(2)}) collective-permute-start(f32[1536,128]{1,0:T(8,128)S(1)} %shard_map.61.refs_0_), channel_id=1, source_target_pairs={{3,2},{4,5},{11,10},{12,13},{19,18},{20,21},{27,26},{28,29}} | collective-permute-start | bytes 2359304 | tf_op jit(solution)/shard_map/ppermute | solution.py:276
  77.1 6.8 %shard_map.64.own_ref = f32[1536,128]{1,0:T(8,128)S(1)} custom-call(s32[1]{0:T(128)} %bitcast.10.core_ref, bf16[1536,3328]{1,0:T(8,128)(2,1)S(1)} %get-tuple-element.51.hi_ref, bf16[1536,3328]{1,0:T(8,128)(2,1)S(1)} %get-tuple-element.52.lo_ref, f32[1536,128]{1,0:T(8,128)S(1)} %collective-permute-done.8.near_ref, ...), custom_call_target="tpu_custom_call" | custom-call | flops 5234491392 | bytes 20447232 | tf_op jit(solution)/shard_map/pallas_call | solution.py:101
  84.0 6.7 %collective-permute-done.7.far_ref = f32[1536,128]{1,0:T(8,128)S(1)} collective-permute-done((f32[1536,128]{1,0:T(8,128)S(1)}, f32[1536,128]{1,0:T(8,128)S(1)}, u32[]{:S(2)}, u32[]{:S(2)}) %collective-permute-start.7) | collective-permute-done | bytes 786464 | tf_op jit(solution)/shard_map/ppermute | solution.py:131
  90.7 6.8 %shard_map.63.refs_0_ = f32[1536,128]{1,0:T(8,128)S(1)} custom-call(s32[1]{0:T(128)} %bitcast.10.core_ref, bf16[1536,3328]{1,0:T(8,128)(2,1)S(1)} %get-tuple-element.51.hi_ref, bf16[1536,3328]{1,0:T(8,128)(2,1)S(1)} %get-tuple-element.52.lo_ref, f32[1536,128]{1,0:T(8,128)S(1)} %collective-permute-done.6.near_ref, ...), custom_call_target="tpu_custom_call" | custom-call | flops 5234491392 | bytes 20447232 | tf_op jit(solution)/shard_map/pallas_call | solution.py:101
  99.0 4.6 %collective-permute-start.17 = (f32[1536,128]{1,0:T(8,128)S(1)}, f32[1536,128]{1,0:T(8,128)S(1)}, u32[]{:S(2)}, u32[]{:S(2)}) collective-permute-start(f32[1536,128]{1,0:T(8,128)S(1)} %shard_map.63.refs_0_), channel_id=1, source_target_pairs={{3,2},{4,5},{11,10},{12,13},{19,18},{20,21},{27,26},{28,29}} | collective-permute-start | bytes 2359304 | tf_op jit(solution)/shard_map/ppermute | solution.py:276
  103.6 4.4 %shard_map.65 = (bf16[1536,512]{1,0:T(8,128)(2,1)S(1)}, bf16[1536,512]{1,0:T(8,128)(2,1)S(1)}, bf16[512,1536]{1,0:T(8,128)(2,1)S(1)}, bf16[512,1536]{1,0:T(8,128...) custom-call(s32[4]{0:T(128)S(1)} %get-tuple-element.55.band_ref, ...), custom_call_target="tpu_custom_call" | custom-call | flops 2415919104 | bytes 8000000 | tf_op jit(solution)/shard_map/pallas_call | solution.py:185
  108.0 6.8 %shard_map.66.refs_0_ = f32[1536,128]{1,0:T(8,128)S(1)} custom-call(s32[1]{0:T(128)} %bitcast.10.core_ref, bf16[1536,3328]{1,0:T(8,128)(2,1)S(1)} %get-tuple-element.51.hi_ref, bf16[1536,3328]{1,0:T(8,128)(2,1)S(1)} %get-tuple-element.52.lo_ref, f32[1536,128]{1,0:T(8,128)S(1)} %collective-permute-done.10.near_ref, ...), custom_call_target="tpu_custom_call" | custom-call | flops 5234491392 | bytes 20447232 | tf_op jit(solution)/shard_map/pallas_call | solution.py:101
  116.3 3.4 %collective-permute-start.21 = (f32[1536,128]{1,0:T(8,128)S(1)}, f32[1536,128]{1,0:T(8,128)S(1)}, u32[]{:S(2)}, u32[]{:S(2)}) collective-permute-start(f32[1536,128]{1,0:T(8,128)S(1)} %shard_map.66.refs_0_), channel_id=1, source_target_pairs={{3,2},{4,5},{11,10},{12,13},{19,18},{20,21},{27,26},{28,29}} | collective-permute-start | bytes 2359304 | tf_op jit(solution)/shard_map/ppermute | solution.py:276
  120.6 6.8 %shard_map.67 = (bf16[1536,512]{1,0:T(8,128)(2,1)S(1)}, bf16[1536,512]{1,0:T(8,128)(2,1)S(1)}, bf16[512,1536]{1,0:T(8,128)(2,1)S(1)}, bf16[512,1536]{1,0:T(8,128...) custom-call(s32[4]{0:T(128)S(1)} %get-tuple-element.55.band_ref, ...), custom_call_target="tpu_custom_call" | custom-call | flops 7247757312 | bytes 8000000 | tf_op jit(solution)/shard_map/pallas_call | solution.py:185
  129.6 7.3 %collective-permute-done.21.refs_3_ = f32[1536,128]{1,0:T(8,128)S(1)} collective-permute-done((f32[1536,128]{1,0:T(8,128)S(1)}, f32[1536,128]{1,0:T(8,128)S(1)}, u32[]{:S(2)}, u32[]{:S(2)}) %collective-permute-start.21) | collective-permute-done | bytes 786464 | tf_op jit(solution)/shard_map/ppermute | solution.py:276
  136.9 3.7 %shard_map.68 = (bf16[1536,512]{1,0:T(8,128)(2,1)S(1)}, bf16[1536,512]{1,0:T(8,128)(2,1)S(1)}, bf16[512,1536]{1,0:T(8,128)(2,1)S(1)}, bf16[512,1536]{1,0:T(8,128)(2,1)S(1)}, f32[384,512]{1,0:T(8,128)S(1)}) custom-call(s32[4]{0:T(128)S(1)} %get-tuple-element.55.band_ref, s32[4]{0:T(128)S(1)} %get-tuple-element.87.target_ref, ...), custom_call_target="tpu_custom_call" | custom-call | flops 1811939328 | bytes 8000000 | tf_op jit(solution)/shard_map/pallas_call | solution.py:185
  151.7 2.5 %shard_map.72.refs_3_ = f32[384,512]{1,0:T(8,128)S(1)} custom-call(s32[4]{0:T(128)S(1)} %get-tuple-element.87.target_ref, bf16[1536,512]{1,0:T(8,128)(2,1)S(1)} %get-tuple-element.77.refs_0_, bf16[1536,512]{1,0:T(8,128)(2,1)S(1)} %get-tuple-element.78.refs_1_, bf16[512,1536]{1,0:T(8,128)(2,1)S(1)} %get-tuple-element.64.refs_6_.refs_2_, ...), custom_call_target="tpu_custom_call" | custom-call | flops 1811939328 | bytes 4000000 | tf_op jit(solution)/shard_map/pallas_call | solution.py:211
  157.9 6.4 %collective-permute-done.27 = f32[384,128]{1,0:T(8,128)S(1)} collective-permute-done((f32[384,128]{1,0:T(8,128)S(1)}, f32[384,128]{1,0:T(8,128)S(1)}, u32[]{:S(2)}, u32[]{:S(2)}) %collective-permute-start.27) | collective-permute-done | bytes 196640 | tf_op jit(solution)/shard_map/ppermute | solution.py:276
  164.4 14.5 %collective-permute-done.32 = f32[384,128]{1,0:T(8,128)S(1)} collective-permute-done((f32[384,128]{1,0:T(8,128)S(1)}, f32[384,128]{1,0:T(8,128)S(1)}, u32[]{:S(2)}, u32[]{:S(2)}) %collective-permute-start.32) | collective-permute-done | bytes 196640 | tf_op jit(solution)/shard_map/ppermute | solution.py:276
  180.8 4.3 %collective-permute-start.35 = (f32[256,128]{1,0:T(8,128)S(1)}, f32[256,128]{1,0:T(8,128)S(1)}, u32[]{:S(2)}, u32[]{:S(2)}) collective-permute-start(f32[256,128]{1,0:T(8,128)S(1)} %slice.21), channel_id=1, source_target_pairs={{4,4},{5,12},{6,20},{7,28},{12,5},{13,13},{14,21},{15,29},{20,6},{... | collective-permute-start | bytes 393224 | tf_op jit(solution)/shard_map/ppermute | solution.py:276
  188.6 5.2 %collective-permute-done.34.turn_e_ref = f32[128,128]{1,0:T(8,128)S(1)} collective-permute-done((f32[128,128]{1,0:T(8,128)S(1)}, f32[128,128]{1,0:T(8,128)S(1)}, u32[]{:S(2)}, u32[]{:S(2)}) %collective-permute-start.34) | collective-permute-done | bytes 65568 | tf_op jit(solution)/shard_map/ppermute | solution.py:276
  (82 shorter events, 39.8 us)
Async XLA Ops:
  1.8 18.3 %collective-permute-start = (f32[1536,128]{1,0:T(8,128)S(1)}, f32[1536,128]{1,0:T(8,128)S(1)}, u32[]{:S(2)}, u32[]{:S(2)}) collective-permute-start(f32[1536,128]{1,0:T(8,128)S(1)} %slice.15.own_ref.rest_0_), channel_id=1, source_target_pairs={{0,4},{4,0},{8,12},{12,8},{16,20},{20,16},{24,28},{28,24},{1,5},{5... | collective-permute-start | bytes 2359304 | tf_op jit(solution)/shard_map/ppermute | solution.py:131
  2.6 20.7 %collective-permute-start.1 = (f32[1536,128]{1,0:T(8,128)S(1)}, f32[1536,128]{1,0:T(8,128)S(1)}, u32[]{:S(2)}, u32[]{:S(2)}) collective-permute-start(f32[1536,128]{1,0:T(8,128)S(1)} %slice.15.own_ref.rest_0_), channel_id=1, source_target_pairs={{0,28},{4,8},{8,4},{12,16},{16,12},{20,24},{24,20},{28,0},{1,29},{... | collective-permute-start | bytes 2359304 | tf_op jit(solution)/shard_map/ppermute | solution.py:131
  5.7 25.7 %collective-permute-start.4 = (f32[1536,128]{1,0:T(8,128)S(1)}, f32[1536,128]{1,0:T(8,128)S(1)}, u32[]{:S(2)}, u32[]{:S(2)}) collective-permute-start(f32[1536,128]{1,0:T(8,128)S(1)} %get-tuple-element.96.own_ref.rest_0_), channel_id=1, source_target_pairs={{0,4},{4,0},{8,12},{12,8},{16,20},{20,16},{24,28},{28,24},{1,5},{5... | collective-permute-start | bytes 2359304 | tf_op jit(solution)/shard_map/ppermute | solution.py:131
  5.8 34.3 %collective-permute-start.5 = (f32[1536,128]{1,0:T(8,128)S(1)}, f32[1536,128]{1,0:T(8,128)S(1)}, u32[]{:S(2)}, u32[]{:S(2)}) collective-permute-start(f32[1536,128]{1,0:T(8,128)S(1)} %get-tuple-element.96.own_ref.rest_0_), channel_id=1, source_target_pairs={{0,28},{4,8},{8,4},{12,16},{16,12},{20,24},{24,20},{28,0},{1,29},{... | collective-permute-start | bytes 2359304 | tf_op jit(solution)/shard_map/ppermute | solution.py:131
  30.1 16.9 %collective-permute-start.2 = (f32[1536,128]{1,0:T(8,128)S(1)}, f32[1536,128]{1,0:T(8,128)S(1)}, u32[]{:S(2)}, u32[]{:S(2)}) collective-permute-start(f32[1536,128]{1,0:T(8,128)S(1)} %shard_map.60.own_ref), channel_id=1, source_target_pairs={{0,4},{4,0},{8,12},{12,8},{16,20},{20,16},{24,28},{28,24},{1,5},{5... | collective-permute-start | bytes 2359304 | tf_op jit(solution)/shard_map/ppermute | solution.py:131
  30.2 26.8 %collective-permute-start.3 = (f32[1536,128]{1,0:T(8,128)S(1)}, f32[1536,128]{1,0:T(8,128)S(1)}, u32[]{:S(2)}, u32[]{:S(2)}) collective-permute-start(f32[1536,128]{1,0:T(8,128)S(1)} %shard_map.60.own_ref), channel_id=1, source_target_pairs={{0,28},{4,8},{8,4},{12,16},{16,12},{20,24},{24,20},{28,0},{1,29},{... | collective-permute-start | bytes 2359304 | tf_op jit(solution)/shard_map/ppermute | solution.py:131
  31.5 33.1 %collective-permute-start.8 = (f32[1536,128]{1,0:T(8,128)S(1)}, f32[1536,128]{1,0:T(8,128)S(1)}, u32[]{:S(2)}, u32[]{:S(2)}) collective-permute-start(f32[1536,128]{1,0:T(8,128)S(1)} %get-tuple-element.97.own_ref.rest_0_), channel_id=1, source_target_pairs={{0,4},{4,0},{8,12},{12,8},{16,20},{20,16},{24,28},{28,24},{1,5},{5... | collective-permute-start | bytes 2359304 | tf_op jit(solution)/shard_map/ppermute | solution.py:131
  31.5 42.4 %collective-permute-start.9 = (f32[1536,128]{1,0:T(8,128)S(1)}, f32[1536,128]{1,0:T(8,128)S(1)}, u32[]{:S(2)}, u32[]{:S(2)}) collective-permute-start(f32[1536,128]{1,0:T(8,128)S(1)} %get-tuple-element.97.own_ref.rest_0_), channel_id=1, source_target_pairs={{0,28},{4,8},{8,4},{12,16},{16,12},{20,24},{24,20},{28,0},{1,29},{... | collective-permute-start | bytes 2359304 | tf_op jit(solution)/shard_map/ppermute | solution.py:131
  46.9 37.0 %collective-permute-start.6 = (f32[1536,128]{1,0:T(8,128)S(1)}, f32[1536,128]{1,0:T(8,128)S(1)}, u32[]{:S(2)}, u32[]{:S(2)}) collective-permute-start(f32[1536,128]{1,0:T(8,128)S(1)} %shard_map.62.own_ref), channel_id=1, source_target_pairs={{0,4},{4,0},{8,12},{12,8},{16,20},{20,16},{24,28},{28,24},{1,5},{5... | collective-permute-start | bytes 2359304 | tf_op jit(solution)/shard_map/ppermute | solution.py:131
  47.0 43.6 %collective-permute-start.7 = (f32[1536,128]{1,0:T(8,128)S(1)}, f32[1536,128]{1,0:T(8,128)S(1)}, u32[]{:S(2)}, u32[]{:S(2)}) collective-permute-start(f32[1536,128]{1,0:T(8,128)S(1)} %shard_map.62.own_ref), channel_id=1, source_target_pairs={{0,28},{4,8},{8,4},{12,16},{16,12},{20,24},{24,20},{28,0},{1,29},{... | collective-permute-start | bytes 2359304 | tf_op jit(solution)/shard_map/ppermute | solution.py:131
  63.8 33.7 %collective-permute-start.12 = (f32[1536,128]{1,0:T(8,128)S(1)}, f32[1536,128]{1,0:T(8,128)S(1)}, u32[]{:S(2)}, u32[]{:S(2)}) collective-permute-start(f32[1536,128]{1,0:T(8,128)S(1)} %shard_map.61.refs_0_), channel_id=1, source_target_pairs={{0,2},{7,5},{8,10},{15,13},{16,18},{23,21},{24,26},{31,29}} | collective-permute-start | bytes 2359304 | tf_op jit(solution)/shard_map/ppermute | solution.py:276
  64.5 33.7 %collective-permute-start.13 = (f32[1536,128]{1,0:T(8,128)S(1)}, f32[1536,128]{1,0:T(8,128)S(1)}, u32[]{:S(2)}, u32[]{:S(2)}) collective-permute-start(f32[1536,128]{1,0:T(8,128)S(1)} %shard_map.61.refs_0_), channel_id=1, source_target_pairs={{1,2},{6,5},{9,10},{14,13},{17,18},{22,21},{25,26},{30,29}} | collective-permute-start | bytes 2359304 | tf_op jit(solution)/shard_map/ppermute | solution.py:276
  73.8 25.2 %collective-permute-start.14 = (f32[1536,128]{1,0:T(8,128)S(1)}, f32[1536,128]{1,0:T(8,128)S(1)}, u32[]{:S(2)}, u32[]{:S(2)}) collective-permute-start(f32[1536,128]{1,0:T(8,128)S(1)} %shard_map.61.refs_0_), channel_id=1, source_target_pairs={{3,2},{4,5},{11,10},{12,13},{19,18},{20,21},{27,26},{28,29}} | collective-permute-start | bytes 2359304 | tf_op jit(solution)/shard_map/ppermute | solution.py:276
  83.9 24.1 %collective-permute-start.10 = (f32[1536,128]{1,0:T(8,128)S(1)}, f32[1536,128]{1,0:T(8,128)S(1)}, u32[]{:S(2)}, u32[]{:S(2)}) collective-permute-start(f32[1536,128]{1,0:T(8,128)S(1)} %shard_map.64.own_ref), channel_id=1, source_target_pairs={{0,28},{4,8},{8,4},{12,16},{16,12},{20,24},{24,20},{28,0},{1,29},{... | collective-permute-start | bytes 2359304 | tf_op jit(solution)/shard_map/ppermute | solution.py:131
  90.7 17.3 %collective-permute-start.11 = (f32[1536,128]{1,0:T(8,128)S(1)}, f32[1536,128]{1,0:T(8,128)S(1)}, u32[]{:S(2)}, u32[]{:S(2)}) collective-permute-start(f32[1536,128]{1,0:T(8,128)S(1)} %shard_map.64.own_ref), channel_id=1, source_target_pairs={{0,4},{4,0},{8,12},{12,8},{16,20},{20,16},{24,28},{28,24},{1,5},{5... | collective-permute-start | bytes 2359304 | tf_op jit(solution)/shard_map/ppermute | solution.py:131
  97.5 18.8 %collective-permute-start.15 = (f32[1536,128]{1,0:T(8,128)S(1)}, f32[1536,128]{1,0:T(8,128)S(1)}, u32[]{:S(2)}, u32[]{:S(2)}) collective-permute-start(f32[1536,128]{1,0:T(8,128)S(1)} %shard_map.63.refs_0_), channel_id=1, source_target_pairs={{0,2},{7,5},{8,10},{15,13},{16,18},{23,21},{24,26},{31,29}} | collective-permute-start | bytes 2359304 | tf_op jit(solution)/shard_map/ppermute | solution.py:276
  98.3 21.5 %collective-permute-start.16 = (f32[1536,128]{1,0:T(8,128)S(1)}, f32[1536,128]{1,0:T(8,128)S(1)}, u32[]{:S(2)}, u32[]{:S(2)}) collective-permute-start(f32[1536,128]{1,0:T(8,128)S(1)} %shard_map.63.refs_0_), channel_id=1, source_target_pairs={{1,2},{6,5},{9,10},{14,13},{17,18},{22,21},{25,26},{30,29}} | collective-permute-start | bytes 2359304 | tf_op jit(solution)/shard_map/ppermute | solution.py:276
  99.0 21.7 %collective-permute-start.17 = (f32[1536,128]{1,0:T(8,128)S(1)}, f32[1536,128]{1,0:T(8,128)S(1)}, u32[]{:S(2)}, u32[]{:S(2)}) collective-permute-start(f32[1536,128]{1,0:T(8,128)S(1)} %shard_map.63.refs_0_), channel_id=1, source_target_pairs={{3,2},{4,5},{11,10},{12,13},{19,18},{20,21},{27,26},{28,29}} | collective-permute-start | bytes 2359304 | tf_op jit(solution)/shard_map/ppermute | solution.py:276
  115.6 14.1 %collective-permute-start.20 = (f32[1536,128]{1,0:T(8,128)S(1)}, f32[1536,128]{1,0:T(8,128)S(1)}, u32[]{:S(2)}, u32[]{:S(2)}) collective-permute-start(f32[1536,128]{1,0:T(8,128)S(1)} %shard_map.66.refs_0_), channel_id=1, source_target_pairs={{1,2},{6,5},{9,10},{14,13},{17,18},{22,21},{25,26},{30,29}} | collective-permute-start | bytes 2359304 | tf_op jit(solution)/shard_map/ppermute | solution.py:276
  116.3 20.6 %collective-permute-start.21 = (f32[1536,128]{1,0:T(8,128)S(1)}, f32[1536,128]{1,0:T(8,128)S(1)}, u32[]{:S(2)}, u32[]{:S(2)}) collective-permute-start(f32[1536,128]{1,0:T(8,128)S(1)} %shard_map.66.refs_0_), channel_id=1, source_target_pairs={{3,2},{4,5},{11,10},{12,13},{19,18},{20,21},{27,26},{28,29}} | collective-permute-start | bytes 2359304 | tf_op jit(solution)/shard_map/ppermute | solution.py:276
  127.5 19.9 %collective-permute-start.18 = (f32[384,512]{1,0:T(8,128)S(1)}, f32[384,512]{1,0:T(8,128)S(1)}, u32[]{:S(2)}, u32[]{:S(2)}) collective-permute-start(f32[384,512]{1,0:T(8,128)S(1)} %get-tuple-element.69), channel_id=1, source_target_pairs={{2,26},{5,29},{10,18},{13,21},{18,10},{21,13},{26,2},{29,5}} | collective-permute-start | bytes 2359304 | tf_op jit(solution)/shard_map/ppermute | solution.py:276
  128.2 19.9 %collective-permute-start.22 = (f32[384,512]{1,0:T(8,128)S(1)}, f32[384,512]{1,0:T(8,128)S(1)}, u32[]{:S(2)}, u32[]{:S(2)}) collective-permute-start(f32[384,512]{1,0:T(8,128)S(1)} %get-tuple-element.83), channel_id=1, source_target_pairs={{2,10},{5,13},{10,2},{13,5},{18,26},{21,29},{26,18},{29,21}} | collective-permute-start | bytes 2359304 | tf_op jit(solution)/shard_map/ppermute | solution.py:276
  128.9 19.2 %collective-permute-start.23 = (f32[384,512]{1,0:T(8,128)S(1)}, f32[384,512]{1,0:T(8,128)S(1)}, u32[]{:S(2)}, u32[]{:S(2)}) collective-permute-start(f32[384,512]{1,0:T(8,128)S(1)} %get-tuple-element.84), channel_id=1, source_target_pairs={{2,18},{5,21},{10,26},{13,29},{18,2},{21,5},{26,10},{29,13}} | collective-permute-start | bytes 2359304 | tf_op jit(solution)/shard_map/ppermute | solution.py:276
  156.6 22.3 %collective-permute-start.32 = (f32[384,128]{1,0:T(8,128)S(1)}, f32[384,128]{1,0:T(8,128)S(1)}, u32[]{:S(2)}, u32[]{:S(2)}) collective-permute-start(f32[384,128]{1,0:T(8,128)S(1)} %get-tuple-element.95), channel_id=1, source_target_pairs={{2,3},{5,4},{10,11},{13,12},{18,19},{21,20},{26,27},{29,28}} | collective-permute-start | bytes 589832 | tf_op jit(solution)/shard_map/ppermute | solution.py:276
  (14 other events, 115.3 us)
